TPU v7x, 32 devices: a whole 2x2x4 slice. The times are simulated.
32 devices in a mesh: gx: 8 (over z, y), gy: 4 (over x, core).
Axes of the slice: x: 2, y: 2, z: 4, core: 2. Of those that a mesh axis runs over, the one named last changes fastest.
Arguments:
- density0: float32 [96, 48, 128], P('gx', 'gy'), may hold values from 0.5 to 2
- energy0: float32 [96, 48, 128], P('gx', 'gy'), may hold values from 0.5 to 4.5
- x_velocity: float32 [96, 48, 128], P('gx', 'gy'), may hold values from -1 to 1.5
- y_velocity: float32 [96, 48, 128], P('gx', 'gy'), may hold values from -1 to 1.5
- z_velocity: float32 [96, 48, 128], P('gx', 'gy'), may hold values from -1 to 1.5
- time_increment: float32 [], replicated, may hold values from 0.02 to 0.05
Outputs:
- density_out: float32 [96, 48, 128], P('gx', 'gy')
- energy_out: float32 [96, 48, 128], P('gx', 'gy')
- x_flow: float32 [96, 48, 128], P('gx', 'gy')
- y_flow: float32 [96, 48, 128], P('gx', 'gy')
- z_flow: float32 [96, 48, 128], P('gx', 'gy')
- next_step: float32 [], replicated
All inputs are finite; a program needn't handle non-finite values.
Results may differ from a plain program's by a relative error of at most 0.0003.
Values sent between devices are 32-bit elements; how exact they have to be, the bound alone decides.
No kernel may reach another device: no remote copies, remote signals or barrier semaphores. Data moves between devices by JAX's collectives and lax.ppermute only.
A program may use at most 64 MiB of HBM per device.

v0:
```python
import jax
import jax.numpy as jnp
from jax import lax
from jax.sharding import PartitionSpec as P


def extended(cells, sides, width):
    for axis, dim in sides:
        count = lax.axis_size(axis)
        head = lax.slice_in_dim(cells, 0, width, axis=dim)
        tail = lax.slice_in_dim(cells, cells.shape[dim] - width, cells.shape[dim], axis=dim)
        cells = jnp.concatenate(
            [
                lax.ppermute(tail, axis, [(i, (i + 1) % count) for i in range(count)]),
                cells,
                lax.ppermute(head, axis, [((i + 1) % count, i) for i in range(count)]),
            ],
            axis=dim,
        )
    return cells


def minmod(first, second):
    return 0.5 * (jnp.sign(first) + jnp.sign(second)) * jnp.minimum(jnp.abs(first), jnp.abs(second))


def face_flux(minus_two, minus_one, centre, plus_one, courant_number):
    from_below = minus_one + 0.5 * (1.0 - courant_number) * minmod(
        centre - minus_one, minus_one - minus_two
    )
    from_above = centre - 0.5 * (1.0 + courant_number) * minmod(
        plus_one - centre, centre - minus_one
    )
    return courant_number * jnp.where(courant_number > 0.0, from_below, from_above)


def window(field, along_x, along_y, margin_cut):
    extent_x = field.shape[0]
    extent_y = field.shape[1]
    return field[
        margin_cut + along_x : extent_x - margin_cut + along_x,
        margin_cut + along_y : extent_y - margin_cut + along_y,
    ]


def roll_z(field, shift):
    return jnp.roll(field, -shift, 2)


def lagrange(padded, time_increment):
    density0 = padded[0]
    energy0 = padded[1]
    x_velocity = padded[2]
    y_velocity = padded[3]
    z_velocity = padded[4]
    z_inner = window(z_velocity, 0, 0, 1)
    divergence = 0.5 * (
        window(x_velocity, 1, 0, 1)
        - window(x_velocity, -1, 0, 1)
        + (window(y_velocity, 0, 1, 1) - window(y_velocity, 0, -1, 1))
        + (roll_z(z_inner, 1) - roll_z(z_inner, -1))
    )
    density_a = window(density0, 0, 0, 1)
    energy_a = window(energy0, 0, 0, 1)
    pressure = 0.4 * density_a * energy_a
    viscosity = 0.5 * density_a * jnp.square(jnp.minimum(divergence, 0.0))
    stress = pressure + viscosity
    density_b = window(density0, 0, 0, 2)
    energy_b = window(energy0, 0, 0, 2)
    divergence_b = window(divergence, 0, 0, 1)
    stress_b = window(stress, 0, 0, 1)
    density1 = density_b / (1.0 + time_increment * divergence_b)
    energy1 = energy_b - time_increment * stress_b * divergence_b / density_b
    x_one = (
        window(x_velocity, 0, 0, 2)
        - time_increment * (0.5 * (window(stress, 1, 0, 1) - window(stress, -1, 0, 1))) / density_b
    )
    y_one = (
        window(y_velocity, 0, 0, 2)
        - time_increment * (0.5 * (window(stress, 0, 1, 1) - window(stress, 0, -1, 1))) / density_b
    )
    z_one = (
        window(z_velocity, 0, 0, 2)
        - time_increment * (0.5 * (roll_z(stress_b, 1) - roll_z(stress_b, -1))) / density_b
    )
    return (jnp.stack([density1, density1 * energy1, x_one, y_one, z_one]), energy1)


def edge_sweep(field_stack, stacking_axis, time_increment):
    length = field_stack.shape[stacking_axis]

    def cell_shift(array, shift):
        return lax.slice_in_dim(array, shift, shift + length - 3, axis=stacking_axis)

    transport_field = field_stack[stacking_axis + 1 : stacking_axis + 2]
    courant_number = time_increment * (
        0.5 * (cell_shift(transport_field, 1) + cell_shift(transport_field, 2))
    )
    fluxes = face_flux(
        cell_shift(field_stack, 0),
        cell_shift(field_stack, 1),
        cell_shift(field_stack, 2),
        cell_shift(field_stack, 3),
        courant_number,
    )
    inner = lax.slice_in_dim(field_stack, 2, length - 2, axis=stacking_axis)
    upper = lax.slice_in_dim(fluxes, 1, length - 3, axis=stacking_axis)
    lower = lax.slice_in_dim(fluxes, 0, length - 4, axis=stacking_axis)
    return inner - (upper - lower)


def roll_sweep(field_stack, time_increment):
    transport_field = field_stack[4:5]
    courant_number = time_increment * (0.5 * (jnp.roll(transport_field, 1, 3) + transport_field))
    fluxes = face_flux(
        jnp.roll(field_stack, 2, 3),
        jnp.roll(field_stack, 1, 3),
        field_stack,
        jnp.roll(field_stack, -1, 3),
        courant_number,
    )
    return field_stack - (jnp.roll(fluxes, -1, 3) - fluxes)


def body(density0, energy0, x_velocity, y_velocity, z_velocity, time_increment):
    field_stack = jnp.stack([density0, energy0, x_velocity, y_velocity, z_velocity])
    padded = extended(field_stack, (("gx", 1), ("gy", 2)), 2)
    field_stack, energy1 = lagrange(padded, time_increment)
    field_stack = extended(field_stack, (("gx", 1),), 2)
    field_stack = edge_sweep(field_stack, 1, time_increment)
    field_stack = extended(field_stack, (("gy", 2),), 2)
    field_stack = edge_sweep(field_stack, 2, time_increment)
    field_stack = roll_sweep(field_stack, time_increment)
    signal = (
        jnp.sqrt(0.56 * energy1)
        + jnp.abs(field_stack[2])
        + jnp.abs(field_stack[3])
        + jnp.abs(field_stack[4])
    )
    local_min = jnp.min(0.3 / signal)
    next_step = lax.pmin(local_min, ("gx", "gy"))
    return (
        field_stack[0],
        field_stack[1],
        field_stack[2],
        field_stack[3],
        field_stack[4],
        next_step,
    )


def solution(mesh):
    return jax.shard_map(
        body,
        mesh=mesh,
        in_specs=(
            P("gx", "gy", None),
            P("gx", "gy", None),
            P("gx", "gy", None),
            P("gx", "gy", None),
            P("gx", "gy", None),
            P(),
        ),
        out_specs=(
            P("gx", "gy", None),
            P("gx", "gy", None),
            P("gx", "gy", None),
            P("gx", "gy", None),
            P("gx", "gy", None),
            P(),
        ),
        check_vma=False,
    )
```

profile of v0, /device:TPU:0, one launch (start us, length us, event | category | flops | bytes accessed | tf_op | source)
XLA Modules:
  0.0 76.2 jit_solution(9872154022511754580)
XLA Ops:
  0.6 0.0 copy-start
  0.6 0.9 %bitcast_dynamic-update-slice_fusion.6 = f32[5,12,12,128]{3,2,1,0:T(8,128)S(1)} fusion(f32[12,12,128]{2,1,0:T(8,128)} %param.6), kind=kLoop, calls=%fused_computation.84 | loop fusion | bytes 172032
  1.6 0.0 copy-done
  1.6 0.0 copy-start.1
  1.6 0.9 %copy-done.1 = f32[12,12,128]{2,1,0:T(8,128)S(1)} copy-done((f32[12,12,128]{2,1,0:T(8,128)S(1)}, f32[12,12,128]{2,1,0:T(8,128)}, u32[]{:S(2)}) %copy-start.1) | copy-done | bytes 73752
  2.5 0.0 copy-start.2
  2.5 0.9 %copy-done.2 = f32[12,12,128]{2,1,0:T(8,128)S(1)} copy-done((f32[12,12,128]{2,1,0:T(8,128)S(1)}, f32[12,12,128]{2,1,0:T(8,128)}, u32[]{:S(2)}) %copy-start.2) | copy-done | bytes 73752
  3.4 0.0 copy-start.3
  3.4 0.9 %copy-done.3 = f32[12,12,128]{2,1,0:T(8,128)S(1)} copy-done((f32[12,12,128]{2,1,0:T(8,128)S(1)}, f32[12,12,128]{2,1,0:T(8,128)}, u32[]{:S(2)}) %copy-start.3) | copy-done | bytes 73752
  4.3 3.0 %collective-permute-start = (f32[5,2,12,128]{3,2,1,0:T(8,128)S(1)}, f32[5,2,12,128]{3,2,1,0:T(8,128)S(1)}, u32[]{:S(2)}, u32[]{:S(2)}) collective-permute-start(f32[5,2,12,128]{3,2,1,0:T(8,128)S(1)} %get-tuple-element.37), channel_id=1, source_target_pairs={{0,4},{4,8},{8,12},{12,16},{16,20},{20,24},{24,28},{28,0},{1,5},{5... | collective-permute-start | bytes 184328 | tf_op jit(solution)/shard_map/ppermute | solution.py:14
  7.3 3.1 %collective-permute-start.1 = (f32[5,2,12,128]{3,2,1,0:T(8,128)S(1)}, f32[5,2,12,128]{3,2,1,0:T(8,128)S(1)}, u32[]{:S(2)}, u32[]{:S(2)}) collective-permute-start(f32[5,2,12,128]{3,2,1,0:T(8,128)S(1)} %get-tuple-element.38), channel_id=1, source_target_pairs={{4,0},{8,4},{12,8},{16,12},{20,16},{24,20},{28,24},{0,28},{5,1},{9... | collective-permute-start | bytes 184328 | tf_op jit(solution)/shard_map/ppermute | solution.py:16
  10.4 2.5 %collective-permute-done = f32[5,2,12,128]{3,2,1,0:T(8,128)S(1)} collective-permute-done((f32[5,2,12,128]{3,2,1,0:T(8,128)S(1)}, f32[5,2,12,128]{3,2,1,0:T(8,128)S(1)}, u32[]{:S(2)}, u32[]{:S(2)}) %collective-permute-start) | collective-permute-done | bytes 61472 | tf_op jit(solution)/shard_map/ppermute | solution.py:14
  12.9 0.6 collective-permute-done.1
  13.5 0.1 pad_maximum_fusion.8
  13.6 0.1 collective-permute-start.2
  13.6 1.7 %collective-permute-start.3 = (f32[5,16,2,128]{3,2,1,0:T(2,128)S(1)}, f32[5,16,2,128]{3,2,1,0:T(2,128)S(1)}, u32[]{:S(2)}, u32[]{:S(2)}) collective-permute-start(f32[5,16,2,128]{3,2,1,0:T(2,128)S(1)} %get-tuple-element.26), channel_id=1, source_target_pairs={{1,0},{2,1},{3,2},{0,3},{5,4},{6,5},{7,6},{4,7},{9,8},{10,9},{11,1... | collective-permute-start | bytes 245768 | tf_op jit(solution)/shard_map/ppermute | solution.py:16
  16.0 1.5 %collective-permute-done.2 = f32[5,16,2,128]{3,2,1,0:T(2,128)S(1)} collective-permute-done((f32[5,16,2,128]{3,2,1,0:T(2,128)S(1)}, f32[5,16,2,128]{3,2,1,0:T(2,128)S(1)}, u32[]{:S(2)}, u32[]{:S(2)}) %collective-permute-start.2) | collective-permute-done | bytes 81952 | tf_op jit(solution)/shard_map/ppermute | solution.py:14
  17.5 0.0 collective-permute-done.3
  17.5 0.1 pad_maximum_fusion
  17.7 0.1 fusion.45
  17.8 0.1 fusion.44
  17.9 0.1 fusion.9
  18.0 0.1 fusion.47
  18.1 0.1 fusion.46
  18.3 0.1 bitcast_dynamic-update-slice_fusion
  18.4 0.1 fusion.27
  18.5 0.1 fusion.17
  18.6 0.7 collective-permute-start.4
  19.3 4.1 %collective-permute-start.5 = (f32[5,2,12,128]{3,2,1,0:T(8,128)S(1)}, f32[5,2,12,128]{3,2,1,0:T(8,128)S(1)}, u32[]{:S(2)}, u32[]{:S(2)}) collective-permute-start(f32[5,2,12,128]{3,2,1,0:T(8,128)S(1)} %get-tuple-element.36), channel_id=1, source_target_pairs={{4,0},{8,4},{12,8},{16,12},{20,16},{24,20},{28,24},{0,28},{5,1},{9... | collective-permute-start | bytes 184328 | tf_op jit(solution)/shard_map/ppermute | solution.py:16
  23.4 2.7 %collective-permute-done.4 = f32[5,2,12,128]{3,2,1,0:T(8,128)S(1)} collective-permute-done((f32[5,2,12,128]{3,2,1,0:T(8,128)S(1)}, f32[5,2,12,128]{3,2,1,0:T(8,128)S(1)}, u32[]{:S(2)}, u32[]{:S(2)}) %collective-permute-start.4) | collective-permute-done | bytes 61472 | tf_op jit(solution)/shard_map/ppermute | solution.py:14
  26.1 0.0 collective-permute-done.5
  26.2 0.6 select_multiply_fusion
  26.7 0.1 fusion.7
  26.9 0.5 collective-permute-start.6
  27.3 1.3 %collective-permute-start.7 = (f32[5,12,2,128]{3,2,1,0:T(2,128)S(1)}, f32[5,12,2,128]{3,2,1,0:T(2,128)S(1)}, u32[]{:S(2)}, u32[]{:S(2)}) collective-permute-start(f32[5,12,2,128]{3,2,1,0:T(2,128)S(1)} %get-tuple-element.34), channel_id=1, source_target_pairs={{1,0},{2,1},{3,2},{0,3},{5,4},{6,5},{7,6},{4,7},{9,8},{10,9},{11,1... | collective-permute-start | bytes 184328 | tf_op jit(solution)/shard_map/ppermute | solution.py:16
  28.7 1.9 %collective-permute-done.6 = f32[5,12,2,128]{3,2,1,0:T(2,128)S(1)} collective-permute-done((f32[5,12,2,128]{3,2,1,0:T(2,128)S(1)}, f32[5,12,2,128]{3,2,1,0:T(2,128)S(1)}, u32[]{:S(2)}, u32[]{:S(2)}) %collective-permute-start.6) | collective-permute-done | bytes 61472 | tf_op jit(solution)/shard_map/ppermute | solution.py:14
  30.6 0.0 collective-permute-done.7
  30.6 0.1 compare_bitcast_fusion.2
  30.6 0.9 %select_multiply_fusion.2 = f32[5,12,13,128]{3,2,1,0:T(8,128)S(1)} fusion(f32[5,12,2,128]{3,2,1,0:T(2,128)S(1)} %collective-permute-done.7, f32[5,12,12,128]{3,2,1,0:T(8,128)S(1)} %fusion.7, f32[5,12,2,128]{3,2,1,0:T(2,128)S(1)} %collective-permute-done.6, f32[12,13,128]{2,1,0:T(8,128)S(1)} %get-tuple-element.52, f32[12,13,128]{2,1,0:T(8,128)S(1)} %get-tuple-element.51, ...), kind=kLoop, calls=%fused_computation.28 | loop fusion | flops 2695680 | bytes 1150464 | tf_op jit(solution)/shard_map/mul | solution.py:34
  31.5 0.1 fusion.4
  31.6 0.1 slice.376
  31.7 0.2 slice.381
  31.9 0.2 fusion.40
  32.1 0.2 fusion.39
  32.3 0.1 compare_bitcast_fusion.1
  32.4 1.0 %select_multiply_fusion.1 = f32[5,12,12,128]{3,2,1,0:T(8,128)S(1)} fusion(f32[5,12,12,128]{3,2,1,0:T(8,128)S(1)} %fusion.4, f32[5,12,12,1]{3,2,1,0:T(8,128)S(1)} %get-tuple-element.30, f32[5,12,12,127]{3,2,1,0:T(8,128)S(1)} %get-tuple-element.32, f32[5,12,12,126]{3,2,1,0:T(8,128)S(1)} %bitcast.72, f32[5,12,12,2]{3,2,1,0:T(8,128)S(1)} %slice.381, ...), kind=kLoop, calls=%fused_computation.27 | loop fusion | flops 2396160 | bytes 2082816 | tf_op jit(solution)/shard_map/mul | solution.py:34
  33.4 0.2 slice.385
  33.6 0.2 fusion.8
  33.9 0.7 slice_bitcast_fusion.8
  34.5 1.3 %fusion.33 = (f32[]{:T(128)}, f32[12,12,128]{2,1,0:T(8,128)}, f32[12,12,128]{2,1,0:T(8,128)}, f32[12,12,128]{2,1,0:T(8,128)}) fusion(f32[12,12,128]{2,1,0:T(8,128)S(1)} %get-tuple-element.17, f32[5,12,12,128]{3,2,1,0:T(8,128)S(1)} %fusion.8), kind=kLoop, calls=%fused_computation.91 | loop fusion | flops 165887 | bytes 516100 | tf_op jit(solution)/shard_map/reduce_min | solution.py:140
  35.9 40.4 %pmin.7 = f32[]{:T(128)} all-reduce(f32[]{:T(128)} %get-tuple-element.6), channel_id=1, replica_groups=mesh['gx'=8,'gy'=4] {'gx','gy'}, use_global_device_ids=true, to_apply=%region_1.2 | all-reduce | flops 1 | bytes 8 | tf_op jit(solution)/shard_map/pmin | solution.py:141
  (15 shorter events, 0.3 us)
Async XLA Ops:
  0.6 0.9 %copy-start = (f32[12,12,128]{2,1,0:T(8,128)S(1)}, f32[12,12,128]{2,1,0:T(8,128)}, u32[]{:S(2)}) copy-start(f32[12,12,128]{2,1,0:T(8,128)} %param.7) | copy-start | bytes 221188
  1.6 0.9 %copy-start.1 = (f32[12,12,128]{2,1,0:T(8,128)S(1)}, f32[12,12,128]{2,1,0:T(8,128)}, u32[]{:S(2)}) copy-start(f32[12,12,128]{2,1,0:T(8,128)} %param.8) | copy-start | bytes 221188
  2.5 0.9 %copy-start.2 = (f32[12,12,128]{2,1,0:T(8,128)S(1)}, f32[12,12,128]{2,1,0:T(8,128)}, u32[]{:S(2)}) copy-start(f32[12,12,128]{2,1,0:T(8,128)} %param.9) | copy-start | bytes 221188
  3.4 0.9 %copy-start.3 = (f32[12,12,128]{2,1,0:T(8,128)S(1)}, f32[12,12,128]{2,1,0:T(8,128)}, u32[]{:S(2)}) copy-start(f32[12,12,128]{2,1,0:T(8,128)} %param.10) | copy-start | bytes 221188
  4.3 8.6 %collective-permute-start = (f32[5,2,12,128]{3,2,1,0:T(8,128)S(1)}, f32[5,2,12,128]{3,2,1,0:T(8,128)S(1)}, u32[]{:S(2)}, u32[]{:S(2)}) collective-permute-start(f32[5,2,12,128]{3,2,1,0:T(8,128)S(1)} %get-tuple-element.37), channel_id=1, source_target_pairs={{0,4},{4,8},{8,12},{12,16},{16,20},{20,24},{24,28},{28,0},{1,5},{5... | collective-permute-start | bytes 184328 | tf_op jit(solution)/shard_map/ppermute | solution.py:14
  7.3 6.2 %collective-permute-start.1 = (f32[5,2,12,128]{3,2,1,0:T(8,128)S(1)}, f32[5,2,12,128]{3,2,1,0:T(8,128)S(1)}, u32[]{:S(2)}, u32[]{:S(2)}) collective-permute-start(f32[5,2,12,128]{3,2,1,0:T(8,128)S(1)} %get-tuple-element.38), channel_id=1, source_target_pairs={{4,0},{8,4},{12,8},{16,12},{20,16},{24,20},{28,24},{0,28},{5,1},{9... | collective-permute-start | bytes 184328 | tf_op jit(solution)/shard_map/ppermute | solution.py:16
  13.6 3.9 %collective-permute-start.2 = (f32[5,16,2,128]{3,2,1,0:T(2,128)S(1)}, f32[5,16,2,128]{3,2,1,0:T(2,128)S(1)}, u32[]{:S(2)}, u32[]{:S(2)}) collective-permute-start(f32[5,16,2,128]{3,2,1,0:T(2,128)S(1)} %get-tuple-element.25), channel_id=1, source_target_pairs={{0,1},{1,2},{2,3},{3,0},{4,5},{5,6},{6,7},{7,4},{8,9},{9,10},{10,1... | collective-permute-start | bytes 245768 | tf_op jit(solution)/shard_map/ppermute | solution.py:14
  13.6 3.9 %collective-permute-start.3 = (f32[5,16,2,128]{3,2,1,0:T(2,128)S(1)}, f32[5,16,2,128]{3,2,1,0:T(2,128)S(1)}, u32[]{:S(2)}, u32[]{:S(2)}) collective-permute-start(f32[5,16,2,128]{3,2,1,0:T(2,128)S(1)} %get-tuple-element.26), channel_id=1, source_target_pairs={{1,0},{2,1},{3,2},{0,3},{5,4},{6,5},{7,6},{4,7},{9,8},{10,9},{11,1... | collective-permute-start | bytes 245768 | tf_op jit(solution)/shard_map/ppermute | solution.py:16
  18.6 7.5 %collective-permute-start.4 = (f32[5,2,12,128]{3,2,1,0:T(8,128)S(1)}, f32[5,2,12,128]{3,2,1,0:T(8,128)S(1)}, u32[]{:S(2)}, u32[]{:S(2)}) collective-permute-start(f32[5,2,12,128]{3,2,1,0:T(8,128)S(1)} %get-tuple-element.35), channel_id=1, source_target_pairs={{0,4},{4,8},{8,12},{12,16},{16,20},{20,24},{24,28},{28,0},{1,5},{5... | collective-permute-start | bytes 184328 | tf_op jit(solution)/shard_map/ppermute | solution.py:14
  19.3 6.8 %collective-permute-start.5 = (f32[5,2,12,128]{3,2,1,0:T(8,128)S(1)}, f32[5,2,12,128]{3,2,1,0:T(8,128)S(1)}, u32[]{:S(2)}, u32[]{:S(2)}) collective-permute-start(f32[5,2,12,128]{3,2,1,0:T(8,128)S(1)} %get-tuple-element.36), channel_id=1, source_target_pairs={{4,0},{8,4},{12,8},{16,12},{20,16},{24,20},{28,24},{0,28},{5,1},{9... | collective-permute-start | bytes 184328 | tf_op jit(solution)/shard_map/ppermute | solution.py:16
  26.9 3.7 %collective-permute-start.6 = (f32[5,12,2,128]{3,2,1,0:T(2,128)S(1)}, f32[5,12,2,128]{3,2,1,0:T(2,128)S(1)}, u32[]{:S(2)}, u32[]{:S(2)}) collective-permute-start(f32[5,12,2,128]{3,2,1,0:T(2,128)S(1)} %get-tuple-element.33), channel_id=1, source_target_pairs={{0,1},{1,2},{2,3},{3,0},{4,5},{5,6},{6,7},{7,4},{8,9},{9,10},{10,1... | collective-permute-start | bytes 184328 | tf_op jit(solution)/shard_map/ppermute | solution.py:14
  27.3 3.2 %collective-permute-start.7 = (f32[5,12,2,128]{3,2,1,0:T(2,128)S(1)}, f32[5,12,2,128]{3,2,1,0:T(2,128)S(1)}, u32[]{:S(2)}, u32[]{:S(2)}) collective-permute-start(f32[5,12,2,128]{3,2,1,0:T(2,128)S(1)} %get-tuple-element.34), channel_id=1, source_target_pairs={{1,0},{2,1},{3,2},{0,3},{5,4},{6,5},{7,6},{4,7},{9,8},{10,9},{11,1... | collective-permute-start | bytes 184328 | tf_op jit(solution)/shard_map/ppermute | solution.py:16
where the time goes:
time: 76.6 us; the launch traced here: 76.2 us
  blocking collectives  40.4 us (53%)
  starting transfers between devices  14.5 us (19%)
  waiting for transfers between devices  9.18 us (12%)
  local copies, waits for them, and re-layouts  5.64 us (7%)
  other arithmetic  5.02 us (7%)
  between operations  1.52 us (2%)
    pmin x1, blocking collectives, body(): next_step = lax.pmin(local_min, ('gx', 'gy'))  40.4 us
    ppermute x4, starting transfers between devices, extended(): lax.ppermute(head, axis, [((i + 1) % count, i) for i in range(count)])  10.2 us
    ppermute x4, waiting for transfers between devices, extended(): lax.ppermute(tail, axis, [(i, (i + 1) % count) for i in range(count)])  8.56 us
    ppermute x4, starting transfers between devices, extended(): lax.ppermute(tail, axis, [(i, (i + 1) % count) for i in range(count)])  4.24 us
    unnamed x12, local copies, waits for them, and re-layouts  3.6 us
    mul x3, other arithmetic, face_flux(): courant_number * jnp.where(courant_number > 0.0, from_below, from_above)  2.44 us
  transfers between devices with their start and end apart: 8, of which 5 were waited for; matrix products, arithmetic and copies ran while one was open for 0% of the time, Pallas kernels for 0%

commit v1 on v0

--- a/solution.py
+++ b/solution.py
@@ -122,6 +122,13 @@
     return field_stack - (jnp.roll(fluxes, -1, 3) - fluxes)
 
 
+def global_min(local_min, axes):
+    count = lax.axis_size(axes[0]) * lax.axis_size(axes[1])
+    copies = jnp.broadcast_to(local_min, (count, 1, 128))
+    gathered = lax.all_to_all(copies, axes, 0, 0, tiled=True)
+    return jnp.min(gathered)
+
+
 def body(density0, energy0, x_velocity, y_velocity, z_velocity, time_increment):
     field_stack = jnp.stack([density0, energy0, x_velocity, y_velocity, z_velocity])
     padded = extended(field_stack, (("gx", 1), ("gy", 2)), 2)
@@ -138,7 +145,7 @@
         + jnp.abs(field_stack[4])
     )
     local_min = jnp.min(0.3 / signal)
-    next_step = lax.pmin(local_min, ("gx", "gy"))
+    next_step = global_min(local_min, ("gx", "gy"))
     return (
         field_stack[0],
         field_stack[1],

time: 76.6 us -> 51 us (0.67)
  blocking collectives: 40.4 us -> 0 us
  starting transfers between devices: 14.5 us -> 21.1 us
  waiting for transfers between devices: 9.18 us -> 15.6 us
  local copies, waits for them, and re-layouts: 5.64 us -> 6.89 us
    pmin x1 -> x0, blocking collectives: 40.4 us -> none  [body(): next_step = lax.pmin(local_min, ('gx', 'gy'))]
    all_to_all x0 -> x1, starting transfers between devices: none -> 6.58 us  [global_min(): gathered = lax.all_to_all(copies, axes, 0, 0, tiled=True)]
    all_to_all x0 -> x1, waiting for transfers between devices: none -> 6.46 us  [global_min(): gathered = lax.all_to_all(copies, axes, 0, 0, tiled=True)]
    broadcast_in_dim x0 -> x1, local copies, waits for them, and re-layouts: none -> 1.25 us  [global_min(): copies = jnp.broadcast_to(local_min, (count, 1, 128))]
  transfers between devices with their start and end apart: 8 -> 9, of which waited for: 5 -> 6; matrix products, arithmetic and copies ran while one was open for 0% -> 1% of each run, Pallas kernels for 0% -> 0%
where the time goes in v1:
time: 51 us; the launch traced here: 50.8 us
  starting transfers between devices  21.1 us (41%)
  waiting for transfers between devices  15.6 us (31%)
  local copies, waits for them, and re-layouts  6.89 us (14%)
  other arithmetic  5.63 us (11%)
  between operations  1.53 us (3%)
    ppermute x4, starting transfers between devices, extended(): lax.ppermute(head, axis, [((i + 1) % count, i) for i in range(count)])  10.2 us
    ppermute x4, waiting for transfers between devices, extended(): lax.ppermute(tail, axis, [(i, (i + 1) % count) for i in range(count)])  8.56 us
    all_to_all x1, starting transfers between devices, global_min(): gathered = lax.all_to_all(copies, axes, 0, 0, tiled=True)  6.58 us
    all_to_all x1, waiting for transfers between devices, global_min(): gathered = lax.all_to_all(copies, axes, 0, 0, tiled=True)  6.46 us
    ppermute x4, starting transfers between devices, extended(): lax.ppermute(tail, axis, [(i, (i + 1) % count) for i in range(count)])  4.24 us
    unnamed x12, local copies, waits for them, and re-layouts  3.6 us
    mul x3, other arithmetic, face_flux(): courant_number * jnp.where(courant_number > 0.0, from_below, from_above)  2.44 us
    reduce_min x1, other arithmetic, body(): local_min = jnp.min(0.3 / signal)  1.31 us
  transfers between devices with their start and end apart: 9, of which 6 were waited for; matrix products, arithmetic and copies ran while one was open for 1% of the time, Pallas kernels for 0%

profile of v1, /device:TPU:0, one launch (start us, length us, event | category | flops | bytes accessed | tf_op | source)
XLA Modules:
  0.0 50.8 jit_solution(11435969933767738244)
XLA Ops:
  0.6 0.0 copy-start
  0.6 0.9 %bitcast_dynamic-update-slice_fusion.6 = f32[5,12,12,128]{3,2,1,0:T(8,128)S(1)} fusion(f32[12,12,128]{2,1,0:T(8,128)} %param.6), kind=kLoop, calls=%fused_computation.84 | loop fusion | bytes 172032
  1.6 0.0 copy-done
  1.6 0.0 copy-start.1
  1.6 0.9 %copy-done.1 = f32[12,12,128]{2,1,0:T(8,128)S(1)} copy-done((f32[12,12,128]{2,1,0:T(8,128)S(1)}, f32[12,12,128]{2,1,0:T(8,128)}, u32[]{:S(2)}) %copy-start.1) | copy-done | bytes 73752
  2.5 0.0 copy-start.2
  2.5 0.9 %copy-done.2 = f32[12,12,128]{2,1,0:T(8,128)S(1)} copy-done((f32[12,12,128]{2,1,0:T(8,128)S(1)}, f32[12,12,128]{2,1,0:T(8,128)}, u32[]{:S(2)}) %copy-start.2) | copy-done | bytes 73752
  3.4 0.0 copy-start.3
  3.4 0.9 %copy-done.3 = f32[12,12,128]{2,1,0:T(8,128)S(1)} copy-done((f32[12,12,128]{2,1,0:T(8,128)S(1)}, f32[12,12,128]{2,1,0:T(8,128)}, u32[]{:S(2)}) %copy-start.3) | copy-done | bytes 73752
  4.3 3.0 %collective-permute-start = (f32[5,2,12,128]{3,2,1,0:T(8,128)S(1)}, f32[5,2,12,128]{3,2,1,0:T(8,128)S(1)}, u32[]{:S(2)}, u32[]{:S(2)}) collective-permute-start(f32[5,2,12,128]{3,2,1,0:T(8,128)S(1)} %get-tuple-element.37), channel_id=1, source_target_pairs={{0,4},{4,8},{8,12},{12,16},{16,20},{20,24},{24,28},{28,0},{1,5},{5... | collective-permute-start | bytes 184328 | tf_op jit(solution)/shard_map/ppermute | solution.py:14
  7.3 3.1 %collective-permute-start.1 = (f32[5,2,12,128]{3,2,1,0:T(8,128)S(1)}, f32[5,2,12,128]{3,2,1,0:T(8,128)S(1)}, u32[]{:S(2)}, u32[]{:S(2)}) collective-permute-start(f32[5,2,12,128]{3,2,1,0:T(8,128)S(1)} %get-tuple-element.38), channel_id=1, source_target_pairs={{4,0},{8,4},{12,8},{16,12},{20,16},{24,20},{28,24},{0,28},{5,1},{9... | collective-permute-start | bytes 184328 | tf_op jit(solution)/shard_map/ppermute | solution.py:16
  10.4 2.5 %collective-permute-done = f32[5,2,12,128]{3,2,1,0:T(8,128)S(1)} collective-permute-done((f32[5,2,12,128]{3,2,1,0:T(8,128)S(1)}, f32[5,2,12,128]{3,2,1,0:T(8,128)S(1)}, u32[]{:S(2)}, u32[]{:S(2)}) %collective-permute-start) | collective-permute-done | bytes 61472 | tf_op jit(solution)/shard_map/ppermute | solution.py:14
  12.9 0.6 %collective-permute-done.1 = f32[5,2,12,128]{3,2,1,0:T(8,128)S(1)} collective-permute-done((f32[5,2,12,128]{3,2,1,0:T(8,128)S(1)}, f32[5,2,12,128]{3,2,1,0:T(8,128)S(1)}, u32[]{:S(2)}, u32[]{:S(2)}) %collective-permute-start.1) | collective-permute-done | bytes 61472 | tf_op jit(solution)/shard_map/ppermute | solution.py:16
  13.5 0.1 pad_maximum_fusion.8
  13.6 0.1 collective-permute-start.2
  13.6 1.7 %collective-permute-start.3 = (f32[5,16,2,128]{3,2,1,0:T(2,128)S(1)}, f32[5,16,2,128]{3,2,1,0:T(2,128)S(1)}, u32[]{:S(2)}, u32[]{:S(2)}) collective-permute-start(f32[5,16,2,128]{3,2,1,0:T(2,128)S(1)} %get-tuple-element.26), channel_id=1, source_target_pairs={{1,0},{2,1},{3,2},{0,3},{5,4},{6,5},{7,6},{4,7},{9,8},{10,9},{11,1... | collective-permute-start | bytes 245768 | tf_op jit(solution)/shard_map/ppermute | solution.py:16
  16.0 1.5 %collective-permute-done.2 = f32[5,16,2,128]{3,2,1,0:T(2,128)S(1)} collective-permute-done((f32[5,16,2,128]{3,2,1,0:T(2,128)S(1)}, f32[5,16,2,128]{3,2,1,0:T(2,128)S(1)}, u32[]{:S(2)}, u32[]{:S(2)}) %collective-permute-start.2) | collective-permute-done | bytes 81952 | tf_op jit(solution)/shard_map/ppermute | solution.py:14
  17.5 0.0 collective-permute-done.3
  17.5 0.1 pad_maximum_fusion
  17.7 0.1 fusion.45
  17.8 0.1 fusion.44
  17.9 0.1 fusion.9
  18.0 0.1 fusion.47
  18.1 0.1 fusion.46
  18.3 0.1 bitcast_dynamic-update-slice_fusion
  18.4 0.1 fusion.27
  18.5 0.1 fusion.17
  18.6 0.7 %collective-permute-start.4 = (f32[5,2,12,128]{3,2,1,0:T(8,128)S(1)}, f32[5,2,12,128]{3,2,1,0:T(8,128)S(1)}, u32[]{:S(2)}, u32[]{:S(2)}) collective-permute-start(f32[5,2,12,128]{3,2,1,0:T(8,128)S(1)} %get-tuple-element.35), channel_id=1, source_target_pairs={{0,4},{4,8},{8,12},{12,16},{16,20},{20,24},{24,28},{28,0},{1,5},{5... | collective-permute-start | bytes 184328 | tf_op jit(solution)/shard_map/ppermute | solution.py:14
  19.3 4.1 %collective-permute-start.5 = (f32[5,2,12,128]{3,2,1,0:T(8,128)S(1)}, f32[5,2,12,128]{3,2,1,0:T(8,128)S(1)}, u32[]{:S(2)}, u32[]{:S(2)}) collective-permute-start(f32[5,2,12,128]{3,2,1,0:T(8,128)S(1)} %get-tuple-element.36), channel_id=1, source_target_pairs={{4,0},{8,4},{12,8},{16,12},{20,16},{24,20},{28,24},{0,28},{5,1},{9... | collective-permute-start | bytes 184328 | tf_op jit(solution)/shard_map/ppermute | solution.py:16
  23.4 2.7 %collective-permute-done.4 = f32[5,2,12,128]{3,2,1,0:T(8,128)S(1)} collective-permute-done((f32[5,2,12,128]{3,2,1,0:T(8,128)S(1)}, f32[5,2,12,128]{3,2,1,0:T(8,128)S(1)}, u32[]{:S(2)}, u32[]{:S(2)}) %collective-permute-start.4) | collective-permute-done | bytes 61472 | tf_op jit(solution)/shard_map/ppermute | solution.py:14
  26.1 0.0 collective-permute-done.5
  26.2 0.6 %select_multiply_fusion = f32[5,13,12,128]{3,2,1,0:T(8,128)S(1)} fusion(f32[5,2,12,128]{3,2,1,0:T(8,128)S(1)} %collective-permute-done.5, f32[5,12,12,128]{3,2,1,0:T(8,128)S(1)} %fusion.17, f32[5,2,12,128]{3,2,1,0:T(8,128)S(1)} %collective-permute-done.4, f32[13,12,128]{2,1,0:T(8,128)S(1)} %get-tuple-element.48, f32[13,12,128]{2,1,0:T(8,128)S(1)} %get-tuple-element.47, ...), kind=kLoop, calls=%fused_computation.11 | loop fusion | flops 2695680 | bytes 1150464 | tf_op jit(solution)/shard_map/mul | solution.py:34
  26.7 0.1 fusion.7
  26.9 0.5 collective-permute-start.6
  27.3 1.3 %collective-permute-start.7 = (f32[5,12,2,128]{3,2,1,0:T(2,128)S(1)}, f32[5,12,2,128]{3,2,1,0:T(2,128)S(1)}, u32[]{:S(2)}, u32[]{:S(2)}) collective-permute-start(f32[5,12,2,128]{3,2,1,0:T(2,128)S(1)} %get-tuple-element.34), channel_id=1, source_target_pairs={{1,0},{2,1},{3,2},{0,3},{5,4},{6,5},{7,6},{4,7},{9,8},{10,9},{11,1... | collective-permute-start | bytes 184328 | tf_op jit(solution)/shard_map/ppermute | solution.py:16
  28.7 1.9 %collective-permute-done.6 = f32[5,12,2,128]{3,2,1,0:T(2,128)S(1)} collective-permute-done((f32[5,12,2,128]{3,2,1,0:T(2,128)S(1)}, f32[5,12,2,128]{3,2,1,0:T(2,128)S(1)}, u32[]{:S(2)}, u32[]{:S(2)}) %collective-permute-start.6) | collective-permute-done | bytes 61472 | tf_op jit(solution)/shard_map/ppermute | solution.py:14
  30.6 0.0 collective-permute-done.7
  30.6 0.1 compare_bitcast_fusion.2
  30.6 0.9 %select_multiply_fusion.2 = f32[5,12,13,128]{3,2,1,0:T(8,128)S(1)} fusion(f32[5,12,2,128]{3,2,1,0:T(2,128)S(1)} %collective-permute-done.7, f32[5,12,12,128]{3,2,1,0:T(8,128)S(1)} %fusion.7, f32[5,12,2,128]{3,2,1,0:T(2,128)S(1)} %collective-permute-done.6, f32[12,13,128]{2,1,0:T(8,128)S(1)} %get-tuple-element.52, f32[12,13,128]{2,1,0:T(8,128)S(1)} %get-tuple-element.51, ...), kind=kLoop, calls=%fused_computation.28 | loop fusion | flops 2695680 | bytes 1150464 | tf_op jit(solution)/shard_map/mul | solution.py:34
  31.5 0.1 fusion.4
  31.6 0.1 slice.376
  31.7 0.2 slice.381
  31.9 0.2 fusion.40
  32.1 0.2 fusion.39
  32.3 0.1 compare_bitcast_fusion.1
  32.4 1.0 %select_multiply_fusion.1 = f32[5,12,12,128]{3,2,1,0:T(8,128)S(1)} fusion(f32[5,12,12,128]{3,2,1,0:T(8,128)S(1)} %fusion.4, f32[5,12,12,1]{3,2,1,0:T(8,128)S(1)} %get-tuple-element.30, f32[5,12,12,127]{3,2,1,0:T(8,128)S(1)} %get-tuple-element.32, f32[5,12,12,126]{3,2,1,0:T(8,128)S(1)} %bitcast.73, f32[5,12,12,2]{3,2,1,0:T(8,128)S(1)} %slice.381, ...), kind=kLoop, calls=%fused_computation.27 | loop fusion | flops 2396160 | bytes 2082816 | tf_op jit(solution)/shard_map/mul | solution.py:34
  33.4 0.2 slice.385
  33.6 0.2 fusion.8
  33.9 1.3 %fusion.33 = (f32[]{:T(128)}, f32[12,12,128]{2,1,0:T(8,128)}, f32[12,12,128]{2,1,0:T(8,128)}, f32[12,12,128]{2,1,0:T(8,128)}) fusion(f32[12,12,128]{2,1,0:T(8,128)S(1)} %get-tuple-element.17, f32[5,12,12,128]{3,2,1,0:T(8,128)S(1)} %fusion.8), kind=kLoop, calls=%fused_computation.91 | loop fusion | flops 165887 | bytes 516100 | tf_op jit(solution)/shard_map/reduce_min | solution.py:147
  35.2 1.2 %broadcast_in_dim.39 = f32[32,1,128]{2,1,0:T(1,128)} broadcast(f32[]{:T(128)} %get-tuple-element.6), dimensions={} | broadcast | bytes 16388 | tf_op jit(solution)/shard_map/broadcast_in_dim | solution.py:127
  36.4 6.6 %all-to-all-start = ((f32[32,1,128]{2,1,0:T(1,128)}), f32[32,1,128]{2,1,0:T(1,128)S(1)}, u32[]{:S(2)}, u32[]{:S(2)}) async-start(f32[32,1,128]{2,1,0:T(1,128)} %broadcast_in_dim.39), calls=%async_computation | async-start | bytes 32768 | tf_op jit(solution)/shard_map/all_to_all | solution.py:128
  43.0 0.7 %slice_bitcast_fusion.8 = (f32[12,12,128]{2,1,0:T(8,128)}, f32[12,12,128]{2,1,0:T(8,128)}) fusion(f32[5,12,12,128]{3,2,1,0:T(8,128)S(1)} %fusion.8), kind=kLoop, calls=%fused_computation.50 | loop fusion | bytes 294912 | tf_op jit(solution)/shard_map/squeeze | solution.py:151
  43.7 6.5 %all-to-all-done = f32[32,1,128]{2,1,0:T(1,128)S(1)} async-done(((f32[32,1,128]{2,1,0:T(1,128)}), f32[32,1,128]{2,1,0:T(1,128)S(1)}, u32[]{:S(2)}, u32[]{:S(2)}) %all-to-all-start) | async-done | bytes 16416 | tf_op jit(solution)/shard_map/all_to_all | solution.py:128
  50.2 0.6 %reduce_min.19 = f32[]{:T(128)} reduce(f32[32,1,128]{2,0,1:T(8,128)S(1)} %bitcast.78, f32[]{:T(128)} %constant.13.clone.1), dimensions={0,1,2}, to_apply=%region_1.2 | reduce | flops 4095 | bytes 16392 | tf_op jit(solution)/shard_map/reduce_min | solution.py:129
  (15 shorter events, 0.3 us)
Async XLA Ops:
  0.6 0.9 %copy-start = (f32[12,12,128]{2,1,0:T(8,128)S(1)}, f32[12,12,128]{2,1,0:T(8,128)}, u32[]{:S(2)}) copy-start(f32[12,12,128]{2,1,0:T(8,128)} %param.7) | copy-start | bytes 221188
  1.6 0.9 %copy-start.1 = (f32[12,12,128]{2,1,0:T(8,128)S(1)}, f32[12,12,128]{2,1,0:T(8,128)}, u32[]{:S(2)}) copy-start(f32[12,12,128]{2,1,0:T(8,128)} %param.8) | copy-start | bytes 221188
  2.5 0.9 %copy-start.2 = (f32[12,12,128]{2,1,0:T(8,128)S(1)}, f32[12,12,128]{2,1,0:T(8,128)}, u32[]{:S(2)}) copy-start(f32[12,12,128]{2,1,0:T(8,128)} %param.9) | copy-start | bytes 221188
  3.4 0.9 %copy-start.3 = (f32[12,12,128]{2,1,0:T(8,128)S(1)}, f32[12,12,128]{2,1,0:T(8,128)}, u32[]{:S(2)}) copy-start(f32[12,12,128]{2,1,0:T(8,128)} %param.10) | copy-start | bytes 221188
  4.3 8.6 %collective-permute-start = (f32[5,2,12,128]{3,2,1,0:T(8,128)S(1)}, f32[5,2,12,128]{3,2,1,0:T(8,128)S(1)}, u32[]{:S(2)}, u32[]{:S(2)}) collective-permute-start(f32[5,2,12,128]{3,2,1,0:T(8,128)S(1)} %get-tuple-element.37), channel_id=1, source_target_pairs={{0,4},{4,8},{8,12},{12,16},{16,20},{20,24},{24,28},{28,0},{1,5},{5... | collective-permute-start | bytes 184328 | tf_op jit(solution)/shard_map/ppermute | solution.py:14
  7.3 6.2 %collective-permute-start.1 = (f32[5,2,12,128]{3,2,1,0:T(8,128)S(1)}, f32[5,2,12,128]{3,2,1,0:T(8,128)S(1)}, u32[]{:S(2)}, u32[]{:S(2)}) collective-permute-start(f32[5,2,12,128]{3,2,1,0:T(8,128)S(1)} %get-tuple-element.38), channel_id=1, source_target_pairs={{4,0},{8,4},{12,8},{16,12},{20,16},{24,20},{28,24},{0,28},{5,1},{9... | collective-permute-start | bytes 184328 | tf_op jit(solution)/shard_map/ppermute | solution.py:16
  13.6 3.9 %collective-permute-start.2 = (f32[5,16,2,128]{3,2,1,0:T(2,128)S(1)}, f32[5,16,2,128]{3,2,1,0:T(2,128)S(1)}, u32[]{:S(2)}, u32[]{:S(2)}) collective-permute-start(f32[5,16,2,128]{3,2,1,0:T(2,128)S(1)} %get-tuple-element.25), channel_id=1, source_target_pairs={{0,1},{1,2},{2,3},{3,0},{4,5},{5,6},{6,7},{7,4},{8,9},{9,10},{10,1... | collective-permute-start | bytes 245768 | tf_op jit(solution)/shard_map/ppermute | solution.py:14
  13.6 3.9 %collective-permute-start.3 = (f32[5,16,2,128]{3,2,1,0:T(2,128)S(1)}, f32[5,16,2,128]{3,2,1,0:T(2,128)S(1)}, u32[]{:S(2)}, u32[]{:S(2)}) collective-permute-start(f32[5,16,2,128]{3,2,1,0:T(2,128)S(1)} %get-tuple-element.26), channel_id=1, source_target_pairs={{1,0},{2,1},{3,2},{0,3},{5,4},{6,5},{7,6},{4,7},{9,8},{10,9},{11,1... | collective-permute-start | bytes 245768 | tf_op jit(solution)/shard_map/ppermute | solution.py:16
  18.6 7.5 %collective-permute-start.4 = (f32[5,2,12,128]{3,2,1,0:T(8,128)S(1)}, f32[5,2,12,128]{3,2,1,0:T(8,128)S(1)}, u32[]{:S(2)}, u32[]{:S(2)}) collective-permute-start(f32[5,2,12,128]{3,2,1,0:T(8,128)S(1)} %get-tuple-element.35), channel_id=1, source_target_pairs={{0,4},{4,8},{8,12},{12,16},{16,20},{20,24},{24,28},{28,0},{1,5},{5... | collective-permute-start | bytes 184328 | tf_op jit(solution)/shard_map/ppermute | solution.py:14
  19.3 6.8 %collective-permute-start.5 = (f32[5,2,12,128]{3,2,1,0:T(8,128)S(1)}, f32[5,2,12,128]{3,2,1,0:T(8,128)S(1)}, u32[]{:S(2)}, u32[]{:S(2)}) collective-permute-start(f32[5,2,12,128]{3,2,1,0:T(8,128)S(1)} %get-tuple-element.36), channel_id=1, source_target_pairs={{4,0},{8,4},{12,8},{16,12},{20,16},{24,20},{28,24},{0,28},{5,1},{9... | collective-permute-start | bytes 184328 | tf_op jit(solution)/shard_map/ppermute | solution.py:16
  26.9 3.7 %collective-permute-start.6 = (f32[5,12,2,128]{3,2,1,0:T(2,128)S(1)}, f32[5,12,2,128]{3,2,1,0:T(2,128)S(1)}, u32[]{:S(2)}, u32[]{:S(2)}) collective-permute-start(f32[5,12,2,128]{3,2,1,0:T(2,128)S(1)} %get-tuple-element.33), channel_id=1, source_target_pairs={{0,1},{1,2},{2,3},{3,0},{4,5},{5,6},{6,7},{7,4},{8,9},{9,10},{10,1... | collective-permute-start | bytes 184328 | tf_op jit(solution)/shard_map/ppermute | solution.py:14
  27.3 3.2 %collective-permute-start.7 = (f32[5,12,2,128]{3,2,1,0:T(2,128)S(1)}, f32[5,12,2,128]{3,2,1,0:T(2,128)S(1)}, u32[]{:S(2)}, u32[]{:S(2)}) collective-permute-start(f32[5,12,2,128]{3,2,1,0:T(2,128)S(1)} %get-tuple-element.34), channel_id=1, source_target_pairs={{1,0},{2,1},{3,2},{0,3},{5,4},{6,5},{7,6},{4,7},{9,8},{10,9},{11,1... | collective-permute-start | bytes 184328 | tf_op jit(solution)/shard_map/ppermute | solution.py:16
  36.4 13.7 %all-to-all-start = ((f32[32,1,128]{2,1,0:T(1,128)}), f32[32,1,128]{2,1,0:T(1,128)S(1)}, u32[]{:S(2)}, u32[]{:S(2)}) async-start(f32[32,1,128]{2,1,0:T(1,128)} %broadcast_in_dim.39), calls=%async_computation | async-start | bytes 32768 | tf_op jit(solution)/shard_map/all_to_all | solution.py:128

commit v2 on v0

v2 whole, which is shorter than its diff:
```python
import functools

import jax
import jax.numpy as jnp
from jax import lax
from jax.experimental import pallas as pl
from jax.experimental.pallas import tpu as pltpu
from jax.sharding import PartitionSpec as P

DENSITY, ENERGY, XV, YV, ZV = range(5)
REACH = 4
SIDES = ((-1, 0), (1, 0), (0, -1), (0, 1), (-1, -1), (-1, 1), (1, -1), (1, 1))
TOP = 8
VMEM = pl.BlockSpec(memory_space=pltpu.VMEM)
SMEM = pl.BlockSpec(memory_space=pltpu.SMEM)


def rows_needed(field, a, nx, ny):
    past = max(-a, a - nx + 1, 0)
    if field == XV:
        reach = {0: 3, 1: 3, 2: 3, 3: 3, 4: 2}.get(past, -1)
    elif field == YV:
        reach = {0: 4, 1: 4, 2: 4, 3: 3}.get(past, -1)
    else:
        reach = {0: 3, 1: 3, 2: 3, 3: 2}.get(past, -1)
    return (-reach, ny + reach) if reach >= 0 else (0, 0)


def segments(side, nx, ny):
    columns = {-1: range(-REACH, 0), 0: range(nx), 1: range(nx, nx + REACH)}[side[0]]
    low, high = {-1: (-REACH, 0), 0: (0, ny), 1: (ny, ny + REACH)}[side[1]]
    found, offset = [], 0
    for a in columns:
        for field in range(5):
            first, last = rows_needed(field, a, nx, ny)
            first, last = max(first, low), min(last, high)
            if last > first:
                found.append((field, a, first, last - first, offset))
                offset += last - first
    return found, -(-offset // 8) * 8


def pack_kernel(nx, ny, zero_ref, *refs):
    fields, halos = refs[:5], refs[5:]
    zero = zero_ref[0]
    for side, halo in zip(SIDES, halos):
        for field, a, b, count, offset in segments(side, nx, ny)[0]:
            halo[pl.ds(zero + offset, count), :] = fields[field][
                a - side[0] * nx, pl.ds(zero + (b - side[1] * ny), count), :
            ]


def limited(above, below):
    return jnp.minimum(jnp.maximum(above, jnp.minimum(below, 0.0)), jnp.maximum(below, 0.0))


def face_factors(v_minus, v, half_increment):
    courant = half_increment * (v_minus + v)
    size = jnp.abs(courant)
    return courant, 0.5 * size * (1.0 - size), courant > 0.0


def face_flux(factors, f_minus, f, s_minus, s):
    courant, slope_factor, upward = factors
    return courant * jnp.where(upward, f_minus, f) + slope_factor * jnp.where(upward, s_minus, s)


def step_kernel(nx, ny, zero_ref, dt_ref, *refs):
    fields, halos, outs, peak_ref = refs[:5], refs[5:13], refs[13:18], refs[18]
    cells, stress, growth, heat, state, energy_one, swept, work = refs[19:]
    zero = zero_ref[0]
    dt = dt_ref[0]
    half = 0.5 * dt
    wide = ny + 4
    tall = ny + 12

    for field in range(5):
        for a in range(nx):
            cells[field, a + REACH, pl.ds(TOP, ny), :] = fields[field][a]
    for side, halo in zip(SIDES, halos):
        for field, a, b, count, offset in segments(side, nx, ny)[0]:
            cells[field, a + REACH, pl.ds(zero + (b + TOP), count), :] = halo[pl.ds(zero + offset, count), :]

    def at(ref, *index, start, count):
        return ref[(*index, pl.ds(zero + start, count), slice(None))]

    def up(value):
        return pltpu.roll(value, value.shape[-1] - 1, value.ndim - 1)

    def down(value):
        return pltpu.roll(value, 1, value.ndim - 1)

    for a in range(-3, nx + 3):
        get = functools.partial(at, cells, start=TOP - 4, count=tall)
        z = get(ZV, a + REACH)
        divergence = 0.5 * (
            get(XV, a + REACH + 1)
            - get(XV, a + REACH - 1)
            + (at(cells, YV, a + REACH, start=TOP - 3, count=tall) - at(cells, YV, a + REACH, start=TOP - 5, count=tall))
            + (up(z) - down(z))
        )
        per_mass = 0.4 * get(ENERGY, a + REACH) + 0.5 * jnp.square(jnp.minimum(divergence, 0.0))
        stress[a + 3] = get(DENSITY, a + REACH) * per_mass
        if -2 <= a < nx + 2:
            growth[a + 2] = dt * divergence
            heat[a + 2] = per_mass

    for a in range(-2, nx + 2):
        get = functools.partial(at, cells, start=TOP - 2, count=wide)
        density = get(DENSITY, a + REACH)
        grown = at(growth, a + 2, start=2, count=wide)
        centre = at(stress, a + 3, start=2, count=wide)
        scale = half / density
        density_one = density / (1.0 + grown)
        energy = get(ENERGY, a + REACH) - at(heat, a + 2, start=2, count=wide) * grown
        state[DENSITY, a + 2] = density_one
        state[ENERGY, a + 2] = density_one * energy
        state[XV, a + 2] = get(XV, a + REACH) - scale * (
            at(stress, a + 4, start=2, count=wide) - at(stress, a + 2, start=2, count=wide)
        )
        state[YV, a + 2] = get(YV, a + REACH) - scale * (
            at(stress, a + 3, start=3, count=wide) - at(stress, a + 3, start=1, count=wide)
        )
        state[ZV, a + 2] = get(ZV, a + REACH) - scale * (up(centre) - down(centre))
        if 0 <= a < nx:
            energy_one[a, 0:wide] = energy

    for part in range(0, wide, 8):
        rows = pl.ds(part, 8)
        before = [state[field, 1, rows] for field in range(5)]
        here = [state[field, 2, rows] for field in range(5)]
        steps = [h - b for h, b in zip(here, before)]
        slopes = [limited(st, b - state[field, 0, rows]) for field, (st, b) in enumerate(zip(steps, before))]
        lower = None
        for a in range(nx + 1):
            factors = face_factors(before[XV], here[XV], half)
            fluxes = []
            for field in range(5):
                after = state[field, a + 3, rows]
                step = after - here[field]
                slope = limited(step, steps[field])
                fluxes.append(face_flux(factors, before[field], here[field], slopes[field], slope))
                if lower is not None:
                    swept[field, a - 1, rows] = before[field] - (fluxes[field] - lower[field])
                before[field], here[field], steps[field], slopes[field] = here[field], after, step, slope
            lower = fluxes

    peak = jnp.zeros((wide, swept.shape[-1]), jnp.float32)
    for a in range(nx):
        below = [at(swept, field, a, start=1, count=wide) for field in range(5)]
        here = [at(swept, field, a, start=2, count=wide) for field in range(5)]
        factors = face_factors(below[YV], here[YV], half)
        moved = []
        for field in range(5):
            step = below[field] - swept[field, a, 0:wide]
            slope = limited(here[field] - below[field], step)
            work[field, a, 0:wide] = slope
            flux = face_flux(factors, below[field], here[field], slope, at(work, field, a, start=1, count=wide))
            work[5 + field, a, 0:wide] = flux
            moved.append(here[field] - (at(work, 5 + field, a, start=1, count=wide) - flux))
        below = [down(value) for value in moved]
        factors = face_factors(below[ZV], moved[ZV], half)
        final = []
        for field in range(5):
            step = moved[field] - below[field]
            slope = limited(up(step), step)
            flux = face_flux(factors, below[field], moved[field], down(slope), slope)
            final.append(moved[field] - (up(flux) - flux))
            outs[field][a] = final[field][:ny]
        peak = jnp.maximum(
            peak,
            jnp.sqrt(0.56 * at(energy_one, a, start=2, count=wide))
            + jnp.abs(final[XV])
            + jnp.abs(final[YV])
            + jnp.abs(final[ZV]),
        )
    row = lax.broadcasted_iota(jnp.int32, peak.shape, 0)
    peak = jnp.where(row < ny, peak, 0.0)
    peak_ref[...] = functools.reduce(jnp.maximum, [peak[part : part + 8] for part in range(0, wide, 8)])


def over(value, axis, offset):
    count = lax.axis_size(axis)
    return lax.ppermute(value, axis, [(i, (i + offset) % count) for i in range(count)])


def shifted(value, side):
    gx, gy = lax.axis_size("gx"), lax.axis_size("gy")
    pairs = [
        (((i + side[0]) % gx) * gy + (j + side[1]) % gy, i * gy + j) for i in range(gx) for j in range(gy)
    ]
    return lax.ppermute(value, ("gx", "gy"), pairs)


def all_max(value, axis, radix):
    count, stride = lax.axis_size(axis), 1
    while stride < count:
        offsets = [k * stride for k in range(1, radix) if k * stride < count]
        value = functools.reduce(jnp.maximum, [over(value, axis, offset) for offset in offsets], value)
        stride *= radix
    return value


def body(density0, energy0, x_velocity, y_velocity, z_velocity, time_increment):
    nx, ny, nz = density0.shape
    fields = (density0, energy0, x_velocity, y_velocity, z_velocity)
    zero = jnp.zeros((1,), jnp.int32)
    sizes = [segments(side, nx, ny)[1] for side in SIDES]
    halos = pl.pallas_call(
        functools.partial(pack_kernel, nx, ny),
        out_shape=[jax.ShapeDtypeStruct((size, nz), jnp.float32) for size in sizes],
        in_specs=[SMEM] + [VMEM] * 5,
        out_specs=[VMEM] * len(SIDES),
        name="pack",
    )(zero, *fields)
    halos = [shifted(halo, side) for halo, side in zip(halos, SIDES)]
    wide, tall = ny + 4, ny + 12

    def scratch(*shape):
        return pltpu.VMEM((*shape, nz), jnp.float32)

    *outs, peak = pl.pallas_call(
        functools.partial(step_kernel, nx, ny),
        out_shape=[jax.ShapeDtypeStruct((nx, ny, nz), jnp.float32)] * 5 + [jax.ShapeDtypeStruct((8, nz), jnp.float32)],
        in_specs=[SMEM, SMEM] + [VMEM] * 13,
        out_specs=[VMEM] * 6,
        scratch_shapes=[
            scratch(5, nx + 8, ny + 20),
            scratch(nx + 6, tall),
            scratch(nx + 4, tall),
            scratch(nx + 4, tall),
            scratch(5, nx + 4, wide),
            scratch(nx, wide + 8),
            scratch(5, nx, wide + 8),
            scratch(10, nx, wide + 8),
        ],
        compiler_params=pltpu.CompilerParams(vmem_limit_bytes=32 * 1024 * 1024),
        name="step",
    )(zero, time_increment.reshape(1), *fields, *halos)
    peak = all_max(all_max(peak, "gy", 4), "gx", 8)
    return (*outs, 0.3 / jnp.max(peak))


def solution(mesh):
    cells = P("gx", "gy", None)
    return jax.shard_map(
        body,
        mesh=mesh,
        in_specs=(cells,) * 5 + (P(),),
        out_specs=(cells,) * 5 + (P(),),
        check_vma=False,
    )
```

time: 76.6 us -> 53.2 us (0.69)
  blocking collectives: 40.4 us -> 0 us
  starting transfers between devices: 14.5 us -> 25.6 us
  waiting for transfers between devices: 9.18 us -> 19.1 us
  local copies, waits for them, and re-layouts: 5.64 us -> 0.02 us
  Pallas kernels: 0 us -> 4.5 us
  other arithmetic: 5.02 us -> 0.61 us
  between operations: 1.52 us -> 3.21 us
    pmin x1 -> x0, blocking collectives: 40.4 us -> none  [body(): next_step = lax.pmin(local_min, ('gx', 'gy'))]
    ppermute x8 -> x18, starting transfers between devices: 14.5 us -> 25.6 us  [the longest x10 13.2 us: over(): lax.ppermute(value, axis, [(i, (i + offset) % count) for i in range(count)])]
    ppermute x8 -> x18, waiting for transfers between devices: 9.18 us -> 19.1 us  [the longest x8 11.2 us: shifted(): return lax.ppermute(value, ('gx', 'gy'), pairs)]
    pallas_call x0 -> x2, Pallas kernels: none -> 4.5 us  [the longest x1 2.49 us: body(): pl.pallas_call(functools.partial(step_kernel, nx, ny), out_shape=[jax.Sha...]
    unnamed x12 -> x10, local copies, waits for them, and re-layouts: 3.6 us -> 0.02 us
    mul x6 -> x0, other arithmetic: 2.5 us -> none  [the longest x3 2.44 us: face_flux(): courant_number * jnp.where(courant_number > 0.0, from_below, from_above)]
    reduce_min x1 -> x0, other arithmetic: 1.31 us -> none  [body(): local_min = jnp.min(0.3 / signal)]
    slice x13 -> x0, local copies, waits for them, and re-layouts: 1.31 us -> none  [the longest x2 0.39 us: roll_sweep(): jnp.roll(field_stack, 1, 3)]
  transfers between devices with their start and end apart: 8 -> 18, of which waited for: 5 -> 9; matrix products, arithmetic and copies ran while one was open for 0% -> 0% of each run, Pallas kernels for 0% -> 0%
where the time goes in v2:
time: 53.2 us; the launch traced here: 53 us
  starting transfers between devices  25.6 us (48%)
  waiting for transfers between devices  19.1 us (36%)
  Pallas kernels  4.5 us (8%)
  between operations  3.21 us (6%)
  other arithmetic  0.61 us (1%)
    ppermute x10, starting transfers between devices, over(): lax.ppermute(value, axis, [(i, (i + offset) % count) for i in range(count)])  13.2 us
    ppermute x8, starting transfers between devices, shifted(): return lax.ppermute(value, ('gx', 'gy'), pairs)  12.4 us
    ppermute x8, waiting for transfers between devices, shifted(): return lax.ppermute(value, ('gx', 'gy'), pairs)  11.2 us
    ppermute x10, waiting for transfers between devices, over(): lax.ppermute(value, axis, [(i, (i + offset) % count) for i in range(count)])  7.87 us
    pallas_call x1, Pallas kernels, body(): pl.pallas_call(functools.partial(step_kernel, nx, ny), out_shape=[jax.Sha...  2.49 us
    pallas_call x1, Pallas kernels, body(): pl.pallas_call(functools.partial(pack_kernel, nx, ny), out_shape=[jax.Sha...  2.01 us
  transfers between devices with their start and end apart: 18, of which 9 were waited for; matrix products, arithmetic and copies ran while one was open for 0% of the time, Pallas kernels for 0%

profile of v2, /device:TPU:0, one launch (start us, length us, event | category | flops | bytes accessed | tf_op | source)
XLA Modules:
  0.0 53.0 jit_solution(1870018381620585171)
XLA Ops:
  0.6 0.0 copy-start.4
  0.6 0.0 copy-start.3
  0.7 0.0 copy-start.2
  0.7 0.0 copy-start.1
  0.7 0.0 copy-start
  0.7 2.0 %pack.1 = (f32[192,128]{1,0:T(8,128)}, f32[192,128]{1,0:T(8,128)}, f32[192,128]{1,0:T(8,128)}, f32[192,128]{1,0:T(8,128)}, f32[48,128]{1,0:T(8,128)}, /*index=5*...) custom-call(s32[1]{0:T(128)} %constant.0.clone.1.zero_ref, f32[12,12,128]{2,1,0:T(8,128)} %refs_0_.3, ...), custom_call_target="tpu_custom_call" | custom-call | tf_op jit(solution)/shard_map/pack/pallas_call | solution.py:209
  2.7 2.4 %collective-permute-start.4 = (f32[48,128]{1,0:T(8,128)}, f32[48,128]{1,0:T(8,128)S(1)}, u32[]{:S(2)}, u32[]{:S(2)}) collective-permute-start(f32[48,128]{1,0:T(8,128)} %get-tuple-element.24), channel_id=1, source_target_pairs={{31,0},{28,1},{29,2},{30,3},{3,4},{0,5},{1,6},{2,7},{7,8},{4,9},{5... | collective-permute-start | bytes 73736 | tf_op jit(solution)/shard_map/ppermute | solution.py:192
  5.1 1.5 %collective-permute-start = (f32[192,128]{1,0:T(8,128)}, f32[192,128]{1,0:T(8,128)S(1)}, u32[]{:S(2)}, u32[]{:S(2)}) collective-permute-start(f32[192,128]{1,0:T(8,128)} %get-tuple-element.20), channel_id=1, source_target_pairs={{28,0},{29,1},{30,2},{31,3},{0,4},{1,5},{2,6},{3,7},{4,8},{5,9},{6... | collective-permute-start | bytes 294920 | tf_op jit(solution)/shard_map/ppermute | solution.py:192
  6.6 3.2 %collective-permute-start.1 = (f32[192,128]{1,0:T(8,128)}, f32[192,128]{1,0:T(8,128)S(1)}, u32[]{:S(2)}, u32[]{:S(2)}) collective-permute-start(f32[192,128]{1,0:T(8,128)} %get-tuple-element.21), channel_id=1, source_target_pairs={{4,0},{5,1},{6,2},{7,3},{8,4},{9,5},{10,6},{11,7},{12,8},{13,9},{1... | collective-permute-start | bytes 294920 | tf_op jit(solution)/shard_map/ppermute | solution.py:192
  9.8 1.0 %collective-permute-start.2 = (f32[192,128]{1,0:T(8,128)}, f32[192,128]{1,0:T(8,128)S(1)}, u32[]{:S(2)}, u32[]{:S(2)}) collective-permute-start(f32[192,128]{1,0:T(8,128)} %get-tuple-element.22), channel_id=1, source_target_pairs={{3,0},{0,1},{1,2},{2,3},{7,4},{4,5},{5,6},{6,7},{11,8},{8,9},{9,10... | collective-permute-start | bytes 294920 | tf_op jit(solution)/shard_map/ppermute | solution.py:192
  10.9 0.7 %collective-permute-start.3 = (f32[192,128]{1,0:T(8,128)}, f32[192,128]{1,0:T(8,128)S(1)}, u32[]{:S(2)}, u32[]{:S(2)}) collective-permute-start(f32[192,128]{1,0:T(8,128)} %get-tuple-element.23), channel_id=1, source_target_pairs={{1,0},{2,1},{3,2},{0,3},{5,4},{6,5},{7,6},{4,7},{9,8},{10,9},{11,1... | collective-permute-start | bytes 294920 | tf_op jit(solution)/shard_map/ppermute | solution.py:192
  11.6 0.0 collective-permute-done.4.refs_9_
  11.6 0.0 collective-permute-start.5
  11.6 6.2 %collective-permute-done.5.refs_10_ = f32[48,128]{1,0:T(8,128)S(1)} collective-permute-done((f32[48,128]{1,0:T(8,128)}, f32[48,128]{1,0:T(8,128)S(1)}, u32[]{:S(2)}, u32[]{:S(2)}) %collective-permute-start.5) | collective-permute-done | bytes 24608 | tf_op jit(solution)/shard_map/ppermute | solution.py:192
  17.8 0.5 collective-permute-start.6
  18.3 3.9 %collective-permute-done.6.refs_11_ = f32[48,128]{1,0:T(8,128)S(1)} collective-permute-done((f32[48,128]{1,0:T(8,128)}, f32[48,128]{1,0:T(8,128)S(1)}, u32[]{:S(2)}, u32[]{:S(2)}) %collective-permute-start.6) | collective-permute-done | bytes 24608 | tf_op jit(solution)/shard_map/ppermute | solution.py:192
  22.2 3.0 %collective-permute-start.7 = (f32[48,128]{1,0:T(8,128)}, f32[48,128]{1,0:T(8,128)S(1)}, u32[]{:S(2)}, u32[]{:S(2)}) collective-permute-start(f32[48,128]{1,0:T(8,128)} %get-tuple-element.27), channel_id=1, source_target_pairs={{5,0},{6,1},{7,2},{4,3},{9,4},{10,5},{11,6},{8,7},{13,8},{14,9},{1... | collective-permute-start | bytes 73736 | tf_op jit(solution)/shard_map/ppermute | solution.py:192
  25.8 1.1 %collective-permute-done.7.refs_12_ = f32[48,128]{1,0:T(8,128)S(1)} collective-permute-done((f32[48,128]{1,0:T(8,128)}, f32[48,128]{1,0:T(8,128)S(1)}, u32[]{:S(2)}, u32[]{:S(2)}) %collective-permute-start.7) | collective-permute-done | bytes 24608 | tf_op jit(solution)/shard_map/ppermute | solution.py:192
  26.9 0.0 collective-permute-done.refs_5_
  26.9 0.0 collective-permute-done.1.refs_6_
  26.9 0.0 collective-permute-done.2.refs_7_
  26.9 0.0 collective-permute-done.3.refs_8_
  26.9 0.0 copy-done.4
  26.9 0.0 copy-done.3
  27.0 0.0 copy-done.2
  27.0 0.0 copy-done.1
  27.0 0.0 copy-done
  27.0 2.5 %step.1 = (f32[12,12,128]{2,1,0:T(8,128)}, f32[12,12,128]{2,1,0:T(8,128)}, f32[12,12,128]{2,1,0:T(8,128)}, f32[12,12,128]{2,1,0:T(8,128)}, f32[12,12,128]{2,1,0:T(8,128)}, /*index=5*/f32[8,128]{1,0:T(8,128)S(1)}) custom-call(s32[1]{0:T(128)} %constant.0.clone.1.zero_ref, f32[1]{0:T(128)} %bitcast.1.dt_ref, f32[12,12,128]{2,1,0:T(8,128)S(1)} %copy-done, ...), custom_call_target="tpu_custom_call" | custom-call | tf_op jit(solution)/shard_map/step/pallas_call | solution.py:222
  29.5 0.8 %collective-permute-start.10 = (f32[8,128]{1,0:T(8,128)S(1)}, f32[8,128]{1,0:T(8,128)S(1)}, u32[]{:S(2)}, u32[]{:S(2)}) collective-permute-start(f32[8,128]{1,0:T(8,128)S(1)} %get-tuple-element.33), channel_id=1, source_target_pairs={{0,3},{1,0},{2,1},{3,2},{4,7},{5,4},{6,5},{7,6},{8,11},{9,8},{10,9... | collective-permute-start | bytes 12296 | tf_op jit(solution)/shard_map/ppermute | solution.py:184
  30.3 1.2 %collective-permute-start.9 = (f32[8,128]{1,0:T(8,128)S(1)}, f32[8,128]{1,0:T(8,128)S(1)}, u32[]{:S(2)}, u32[]{:S(2)}) collective-permute-start(f32[8,128]{1,0:T(8,128)S(1)} %get-tuple-element.33), channel_id=1, source_target_pairs={{0,2},{1,3},{2,0},{3,1},{4,6},{5,7},{6,4},{7,5},{8,10},{9,11},{10,... | collective-permute-start | bytes 12296 | tf_op jit(solution)/shard_map/ppermute | solution.py:184
  31.5 0.0 collective-permute-start.8
  31.5 0.2 collective-permute-done.10
  31.7 2.3 %collective-permute-done.9 = f32[8,128]{1,0:T(8,128)S(1)} collective-permute-done((f32[8,128]{1,0:T(8,128)S(1)}, f32[8,128]{1,0:T(8,128)S(1)}, u32[]{:S(2)}, u32[]{:S(2)}) %collective-permute-start.9) | collective-permute-done | bytes 4128 | tf_op jit(solution)/shard_map/ppermute | solution.py:184
  33.9 0.6 %collective-permute-done.8 = f32[8,128]{1,0:T(8,128)S(1)} collective-permute-done((f32[8,128]{1,0:T(8,128)S(1)}, f32[8,128]{1,0:T(8,128)S(1)}, u32[]{:S(2)}, u32[]{:S(2)}) %collective-permute-start.8) | collective-permute-done | bytes 4128 | tf_op jit(solution)/shard_map/ppermute | solution.py:184
  34.5 4.8 %collective-permute-start.17 = (f32[8,128]{1,0:T(8,128)S(1)}, f32[8,128]{1,0:T(8,128)S(1)}, u32[]{:S(2)}, u32[]{:S(2)}) collective-permute-start(f32[8,128]{1,0:T(8,128)S(1)} %maximum_maximum_fusion), channel_id=1, source_target_pairs={{0,28},{4,0},{8,4},{12,8},{16,12},{20,16},{24,20},{28,24},{1,29},{... | collective-permute-start | bytes 12296 | tf_op jit(solution)/shard_map/ppermute | solution.py:184
  39.3 0.0 collective-permute-start.16
  39.3 0.0 collective-permute-start.15
  39.3 3.0 %collective-permute-start.14 = (f32[8,128]{1,0:T(8,128)S(1)}, f32[8,128]{1,0:T(8,128)S(1)}, u32[]{:S(2)}, u32[]{:S(2)}) collective-permute-start(f32[8,128]{1,0:T(8,128)S(1)} %maximum_maximum_fusion), channel_id=1, source_target_pairs={{0,16},{4,20},{8,24},{12,28},{16,0},{20,4},{24,8},{28,12},{1,17},{... | collective-permute-start | bytes 12296 | tf_op jit(solution)/shard_map/ppermute | solution.py:184
  42.3 0.0 collective-permute-start.13
  42.3 0.0 collective-permute-done.17
  42.3 2.0 %collective-permute-start.12 = (f32[8,128]{1,0:T(8,128)S(1)}, f32[8,128]{1,0:T(8,128)S(1)}, u32[]{:S(2)}, u32[]{:S(2)}) collective-permute-start(f32[8,128]{1,0:T(8,128)S(1)} %maximum_maximum_fusion), channel_id=1, source_target_pairs={{0,8},{4,12},{8,16},{12,20},{16,24},{20,28},{24,0},{28,4},{1,9},{5... | collective-permute-start | bytes 12296 | tf_op jit(solution)/shard_map/ppermute | solution.py:184
  44.3 0.0 collective-permute-done.16
  44.3 1.5 %collective-permute-start.11 = (f32[8,128]{1,0:T(8,128)S(1)}, f32[8,128]{1,0:T(8,128)S(1)}, u32[]{:S(2)}, u32[]{:S(2)}) collective-permute-start(f32[8,128]{1,0:T(8,128)S(1)} %maximum_maximum_fusion), channel_id=1, source_target_pairs={{0,4},{4,8},{8,12},{12,16},{16,20},{20,24},{24,28},{28,0},{1,5},{5... | collective-permute-start | bytes 12296 | tf_op jit(solution)/shard_map/ppermute | solution.py:184
  45.8 0.0 collective-permute-done.15
  45.8 0.0 collective-permute-done.14
  45.8 2.0 %collective-permute-done.13 = f32[8,128]{1,0:T(8,128)S(1)} collective-permute-done((f32[8,128]{1,0:T(8,128)S(1)}, f32[8,128]{1,0:T(8,128)S(1)}, u32[]{:S(2)}, u32[]{:S(2)}) %collective-permute-start.13) | collective-permute-done | bytes 4128 | tf_op jit(solution)/shard_map/ppermute | solution.py:184
  47.7 1.4 %collective-permute-done.12 = f32[8,128]{1,0:T(8,128)S(1)} collective-permute-done((f32[8,128]{1,0:T(8,128)S(1)}, f32[8,128]{1,0:T(8,128)S(1)}, u32[]{:S(2)}, u32[]{:S(2)}) %collective-permute-start.12) | collective-permute-done | bytes 4128 | tf_op jit(solution)/shard_map/ppermute | solution.py:184
  49.2 1.4 %collective-permute-done.11 = f32[8,128]{1,0:T(8,128)S(1)} collective-permute-done((f32[8,128]{1,0:T(8,128)S(1)}, f32[8,128]{1,0:T(8,128)S(1)}, u32[]{:S(2)}, u32[]{:S(2)}) %collective-permute-start.11) | collective-permute-done | bytes 4128 | tf_op jit(solution)/shard_map/ppermute | solution.py:184
  50.6 0.6 %maximum_reduce_fusion = f32[]{:T(128)} fusion(f32[8,128]{1,0:T(8,128)S(1)} %collective-permute-done.17, f32[8,128]{1,0:T(8,128)S(1)} %collective-permute-done.16, f32[8,128]{1,0:T(8,128)S(1)} %collective-permute-done.15, f32[8,128]{1,0:T(8,128)S(1)} %collective-permute-done.14, f32[8,128]{1,0:T(8,128)S(1)} %collective-permute-done.13, ...), kind=kLoop, calls=%fused_computation | loop fusion | flops 8191 | bytes 32772 | tf_op jit(solution)/shard_map/reduce_max | solution.py:241
  (1 shorter events, 0.0 us)
Async XLA Ops:
  0.6 26.3 %copy-start.4 = (f32[12,12,128]{2,1,0:T(8,128)S(1)}, f32[12,12,128]{2,1,0:T(8,128)}, u32[]{:S(2)}) copy-start(f32[12,12,128]{2,1,0:T(8,128)} %refs_4_.3) | copy-start | bytes 221188
  0.6 26.3 %copy-start.3 = (f32[12,12,128]{2,1,0:T(8,128)S(1)}, f32[12,12,128]{2,1,0:T(8,128)}, u32[]{:S(2)}) copy-start(f32[12,12,128]{2,1,0:T(8,128)} %refs_3_.3) | copy-start | bytes 221188
  0.7 26.3 %copy-start.2 = (f32[12,12,128]{2,1,0:T(8,128)S(1)}, f32[12,12,128]{2,1,0:T(8,128)}, u32[]{:S(2)}) copy-start(f32[12,12,128]{2,1,0:T(8,128)} %refs_2_.3) | copy-start | bytes 221188
  0.7 26.3 %copy-start.1 = (f32[12,12,128]{2,1,0:T(8,128)S(1)}, f32[12,12,128]{2,1,0:T(8,128)}, u32[]{:S(2)}) copy-start(f32[12,12,128]{2,1,0:T(8,128)} %refs_1_.3) | copy-start | bytes 221188
  0.7 26.3 %copy-start = (f32[12,12,128]{2,1,0:T(8,128)S(1)}, f32[12,12,128]{2,1,0:T(8,128)}, u32[]{:S(2)}) copy-start(f32[12,12,128]{2,1,0:T(8,128)} %refs_0_.3) | copy-start | bytes 221188
  2.7 8.9 %collective-permute-start.4 = (f32[48,128]{1,0:T(8,128)}, f32[48,128]{1,0:T(8,128)S(1)}, u32[]{:S(2)}, u32[]{:S(2)}) collective-permute-start(f32[48,128]{1,0:T(8,128)} %get-tuple-element.24), channel_id=1, source_target_pairs={{31,0},{28,1},{29,2},{30,3},{3,4},{0,5},{1,6},{2,7},{7,8},{4,9},{5... | collective-permute-start | bytes 73736 | tf_op jit(solution)/shard_map/ppermute | solution.py:192
  5.1 21.8 %collective-permute-start = (f32[192,128]{1,0:T(8,128)}, f32[192,128]{1,0:T(8,128)S(1)}, u32[]{:S(2)}, u32[]{:S(2)}) collective-permute-start(f32[192,128]{1,0:T(8,128)} %get-tuple-element.20), channel_id=1, source_target_pairs={{28,0},{29,1},{30,2},{31,3},{0,4},{1,5},{2,6},{3,7},{4,8},{5,9},{6... | collective-permute-start | bytes 294920 | tf_op jit(solution)/shard_map/ppermute | solution.py:192
  6.6 20.3 %collective-permute-start.1 = (f32[192,128]{1,0:T(8,128)}, f32[192,128]{1,0:T(8,128)S(1)}, u32[]{:S(2)}, u32[]{:S(2)}) collective-permute-start(f32[192,128]{1,0:T(8,128)} %get-tuple-element.21), channel_id=1, source_target_pairs={{4,0},{5,1},{6,2},{7,3},{8,4},{9,5},{10,6},{11,7},{12,8},{13,9},{1... | collective-permute-start | bytes 294920 | tf_op jit(solution)/shard_map/ppermute | solution.py:192
  9.8 17.1 %collective-permute-start.2 = (f32[192,128]{1,0:T(8,128)}, f32[192,128]{1,0:T(8,128)S(1)}, u32[]{:S(2)}, u32[]{:S(2)}) collective-permute-start(f32[192,128]{1,0:T(8,128)} %get-tuple-element.22), channel_id=1, source_target_pairs={{3,0},{0,1},{1,2},{2,3},{7,4},{4,5},{5,6},{6,7},{11,8},{8,9},{9,10... | collective-permute-start | bytes 294920 | tf_op jit(solution)/shard_map/ppermute | solution.py:192
  10.9 16.1 %collective-permute-start.3 = (f32[192,128]{1,0:T(8,128)}, f32[192,128]{1,0:T(8,128)S(1)}, u32[]{:S(2)}, u32[]{:S(2)}) collective-permute-start(f32[192,128]{1,0:T(8,128)} %get-tuple-element.23), channel_id=1, source_target_pairs={{1,0},{2,1},{3,2},{0,3},{5,4},{6,5},{7,6},{4,7},{9,8},{10,9},{11,1... | collective-permute-start | bytes 294920 | tf_op jit(solution)/shard_map/ppermute | solution.py:192
  11.6 6.2 %collective-permute-start.5 = (f32[48,128]{1,0:T(8,128)}, f32[48,128]{1,0:T(8,128)S(1)}, u32[]{:S(2)}, u32[]{:S(2)}) collective-permute-start(f32[48,128]{1,0:T(8,128)} %get-tuple-element.25), channel_id=1, source_target_pairs={{29,0},{30,1},{31,2},{28,3},{1,4},{2,5},{3,6},{0,7},{5,8},{6,9},{7... | collective-permute-start | bytes 73736 | tf_op jit(solution)/shard_map/ppermute | solution.py:192
  17.8 4.4 %collective-permute-start.6 = (f32[48,128]{1,0:T(8,128)}, f32[48,128]{1,0:T(8,128)S(1)}, u32[]{:S(2)}, u32[]{:S(2)}) collective-permute-start(f32[48,128]{1,0:T(8,128)} %get-tuple-element.26), channel_id=1, source_target_pairs={{7,0},{4,1},{5,2},{6,3},{11,4},{8,5},{9,6},{10,7},{15,8},{12,9},{1... | collective-permute-start | bytes 73736 | tf_op jit(solution)/shard_map/ppermute | solution.py:192
  22.2 4.7 %collective-permute-start.7 = (f32[48,128]{1,0:T(8,128)}, f32[48,128]{1,0:T(8,128)S(1)}, u32[]{:S(2)}, u32[]{:S(2)}) collective-permute-start(f32[48,128]{1,0:T(8,128)} %get-tuple-element.27), channel_id=1, source_target_pairs={{5,0},{6,1},{7,2},{4,3},{9,4},{10,5},{11,6},{8,7},{13,8},{14,9},{1... | collective-permute-start | bytes 73736 | tf_op jit(solution)/shard_map/ppermute | solution.py:192
  29.5 2.2 %collective-permute-start.10 = (f32[8,128]{1,0:T(8,128)S(1)}, f32[8,128]{1,0:T(8,128)S(1)}, u32[]{:S(2)}, u32[]{:S(2)}) collective-permute-start(f32[8,128]{1,0:T(8,128)S(1)} %get-tuple-element.33), channel_id=1, source_target_pairs={{0,3},{1,0},{2,1},{3,2},{4,7},{5,4},{6,5},{7,6},{8,11},{9,8},{10,9... | collective-permute-start | bytes 12296 | tf_op jit(solution)/shard_map/ppermute | solution.py:184
  30.3 3.6 %collective-permute-start.9 = (f32[8,128]{1,0:T(8,128)S(1)}, f32[8,128]{1,0:T(8,128)S(1)}, u32[]{:S(2)}, u32[]{:S(2)}) collective-permute-start(f32[8,128]{1,0:T(8,128)S(1)} %get-tuple-element.33), channel_id=1, source_target_pairs={{0,2},{1,3},{2,0},{3,1},{4,6},{5,7},{6,4},{7,5},{8,10},{9,11},{10,... | collective-permute-start | bytes 12296 | tf_op jit(solution)/shard_map/ppermute | solution.py:184
  31.5 3.0 %collective-permute-start.8 = (f32[8,128]{1,0:T(8,128)S(1)}, f32[8,128]{1,0:T(8,128)S(1)}, u32[]{:S(2)}, u32[]{:S(2)}) collective-permute-start(f32[8,128]{1,0:T(8,128)S(1)} %get-tuple-element.33), channel_id=1, source_target_pairs={{0,1},{1,2},{2,3},{3,0},{4,5},{5,6},{6,7},{7,4},{8,9},{9,10},{10,1... | collective-permute-start | bytes 12296 | tf_op jit(solution)/shard_map/ppermute | solution.py:184
  34.5 7.8 %collective-permute-start.17 = (f32[8,128]{1,0:T(8,128)S(1)}, f32[8,128]{1,0:T(8,128)S(1)}, u32[]{:S(2)}, u32[]{:S(2)}) collective-permute-start(f32[8,128]{1,0:T(8,128)S(1)} %maximum_maximum_fusion), channel_id=1, source_target_pairs={{0,28},{4,0},{8,4},{12,8},{16,12},{20,16},{24,20},{28,24},{1,29},{... | collective-permute-start | bytes 12296 | tf_op jit(solution)/shard_map/ppermute | solution.py:184
  39.3 5.0 %collective-permute-start.16 = (f32[8,128]{1,0:T(8,128)S(1)}, f32[8,128]{1,0:T(8,128)S(1)}, u32[]{:S(2)}, u32[]{:S(2)}) collective-permute-start(f32[8,128]{1,0:T(8,128)S(1)} %maximum_maximum_fusion), channel_id=1, source_target_pairs={{0,24},{4,28},{8,0},{12,4},{16,8},{20,12},{24,16},{28,20},{1,25},{... | collective-permute-start | bytes 12296 | tf_op jit(solution)/shard_map/ppermute | solution.py:184
  39.3 6.4 %collective-permute-start.15 = (f32[8,128]{1,0:T(8,128)S(1)}, f32[8,128]{1,0:T(8,128)S(1)}, u32[]{:S(2)}, u32[]{:S(2)}) collective-permute-start(f32[8,128]{1,0:T(8,128)S(1)} %maximum_maximum_fusion), channel_id=1, source_target_pairs={{0,20},{4,24},{8,28},{12,0},{16,4},{20,8},{24,12},{28,16},{1,21},{... | collective-permute-start | bytes 12296 | tf_op jit(solution)/shard_map/ppermute | solution.py:184
  39.3 6.4 %collective-permute-start.14 = (f32[8,128]{1,0:T(8,128)S(1)}, f32[8,128]{1,0:T(8,128)S(1)}, u32[]{:S(2)}, u32[]{:S(2)}) collective-permute-start(f32[8,128]{1,0:T(8,128)S(1)} %maximum_maximum_fusion), channel_id=1, source_target_pairs={{0,16},{4,20},{8,24},{12,28},{16,0},{20,4},{24,8},{28,12},{1,17},{... | collective-permute-start | bytes 12296 | tf_op jit(solution)/shard_map/ppermute | solution.py:184
  42.3 5.4 %collective-permute-start.13 = (f32[8,128]{1,0:T(8,128)S(1)}, f32[8,128]{1,0:T(8,128)S(1)}, u32[]{:S(2)}, u32[]{:S(2)}) collective-permute-start(f32[8,128]{1,0:T(8,128)S(1)} %maximum_maximum_fusion), channel_id=1, source_target_pairs={{0,12},{4,16},{8,20},{12,24},{16,28},{20,0},{24,4},{28,8},{1,13},{... | collective-permute-start | bytes 12296 | tf_op jit(solution)/shard_map/ppermute | solution.py:184
  42.3 6.8 %collective-permute-start.12 = (f32[8,128]{1,0:T(8,128)S(1)}, f32[8,128]{1,0:T(8,128)S(1)}, u32[]{:S(2)}, u32[]{:S(2)}) collective-permute-start(f32[8,128]{1,0:T(8,128)S(1)} %maximum_maximum_fusion), channel_id=1, source_target_pairs={{0,8},{4,12},{8,16},{12,20},{16,24},{20,28},{24,0},{28,4},{1,9},{5... | collective-permute-start | bytes 12296 | tf_op jit(solution)/shard_map/ppermute | solution.py:184
  44.3 6.3 %collective-permute-start.11 = (f32[8,128]{1,0:T(8,128)S(1)}, f32[8,128]{1,0:T(8,128)S(1)}, u32[]{:S(2)}, u32[]{:S(2)}) collective-permute-start(f32[8,128]{1,0:T(8,128)S(1)} %maximum_maximum_fusion), channel_id=1, source_target_pairs={{0,4},{4,8},{8,12},{12,16},{16,20},{20,24},{24,28},{28,0},{1,5},{5... | collective-permute-start | bytes 12296 | tf_op jit(solution)/shard_map/ppermute | solution.py:184

commit v3 on v2

--- a/solution.py
+++ b/solution.py
@@ -9,7 +9,7 @@
 
 DENSITY, ENERGY, XV, YV, ZV = range(5)
 REACH = 4
-SIDES = ((-1, 0), (1, 0), (0, -1), (0, 1), (-1, -1), (-1, 1), (1, -1), (1, 1))
+SIDES = ((-1, 0), (1, 0), (0, -1), (0, 1))
 TOP = 8
 VMEM = pl.BlockSpec(memory_space=pltpu.VMEM)
 SMEM = pl.BlockSpec(memory_space=pltpu.SMEM)
@@ -40,6 +40,15 @@
     return found, -(-offset // 8) * 8
 
 
+def corner_segments(side_y, nx, ny):
+    found, offset = [], 0
+    for side_x in (-1, 1):
+        for field, a, first, count, _ in segments((side_x, side_y), nx, ny)[0]:
+            found.append((side_x, field, a, first, count, offset))
+            offset += count
+    return found, -(-offset // 8) * 8
+
+
 def pack_kernel(nx, ny, zero_ref, *refs):
     fields, halos = refs[:5], refs[5:]
     zero = zero_ref[0]
@@ -50,6 +59,19 @@
             ]
 
 
+def corner_kernel(nx, ny, zero_ref, below_ref, above_ref, low_ref, high_ref):
+    zero = zero_ref[0]
+    held = {
+        (side_x, field, a): (ref, offset)
+        for side_x, ref in ((-1, below_ref), (1, above_ref))
+        for field, a, _, _, offset in segments((side_x, 0), nx, ny)[0]
+    }
+    for side_y, out in ((-1, low_ref), (1, high_ref)):
+        for side_x, field, a, b, count, offset in corner_segments(side_y, nx, ny)[0]:
+            ref, start = held[side_x, field, a]
+            out[pl.ds(zero + offset, count), :] = ref[pl.ds(zero + (start + b - side_y * ny), count), :]
+
+
 def limited(above, below):
     return jnp.minimum(jnp.maximum(above, jnp.minimum(below, 0.0)), jnp.maximum(below, 0.0))
 
@@ -66,8 +88,8 @@
 
 
 def step_kernel(nx, ny, zero_ref, dt_ref, *refs):
-    fields, halos, outs, peak_ref = refs[:5], refs[5:13], refs[13:18], refs[18]
-    cells, stress, growth, heat, state, energy_one, swept, work = refs[19:]
+    fields, halos, outs, peak_ref = refs[:5], refs[5:11], refs[11:16], refs[16]
+    cells, stress, growth, heat, state, energy_one, swept, work = refs[17:]
     zero = zero_ref[0]
     dt = dt_ref[0]
     half = 0.5 * dt
@@ -79,6 +101,9 @@
             cells[field, a + REACH, pl.ds(TOP, ny), :] = fields[field][a]
     for side, halo in zip(SIDES, halos):
         for field, a, b, count, offset in segments(side, nx, ny)[0]:
+            cells[field, a + REACH, pl.ds(zero + (b + TOP), count), :] = halo[pl.ds(zero + offset, count), :]
+    for side_y, halo in zip((-1, 1), halos[len(SIDES) :]):
+        for _, field, a, b, count, offset in corner_segments(side_y, nx, ny)[0]:
             cells[field, a + REACH, pl.ds(zero + (b + TOP), count), :] = halo[pl.ds(zero + offset, count), :]
 
     def at(ref, *index, start, count):
@@ -176,29 +201,13 @@
         )
     row = lax.broadcasted_iota(jnp.int32, peak.shape, 0)
     peak = jnp.where(row < ny, peak, 0.0)
-    peak_ref[...] = functools.reduce(jnp.maximum, [peak[part : part + 8] for part in range(0, wide, 8)])
-
-
-def over(value, axis, offset):
+    peak_ref[...] = jnp.max(peak, axis=0, keepdims=True)
+
+
+def shifted(value, side):
+    axis, step = ("gx", side[0]) if side[0] else ("gy", side[1])
     count = lax.axis_size(axis)
-    return lax.ppermute(value, axis, [(i, (i + offset) % count) for i in range(count)])
-
-
-def shifted(value, side):
-    gx, gy = lax.axis_size("gx"), lax.axis_size("gy")
-    pairs = [
-        (((i + side[0]) % gx) * gy + (j + side[1]) % gy, i * gy + j) for i in range(gx) for j in range(gy)
-    ]
-    return lax.ppermute(value, ("gx", "gy"), pairs)
-
-
-def all_max(value, axis, radix):
-    count, stride = lax.axis_size(axis), 1
-    while stride < count:
-        offsets = [k * stride for k in range(1, radix) if k * stride < count]
-        value = functools.reduce(jnp.maximum, [over(value, axis, offset) for offset in offsets], value)
-        stride *= radix
-    return value
+    return lax.ppermute(value, axis, [((i + step) % count, i) for i in range(count)])
 
 
 def body(density0, energy0, x_velocity, y_velocity, z_velocity, time_increment):
@@ -214,6 +223,15 @@
         name="pack",
     )(zero, *fields)
     halos = [shifted(halo, side) for halo, side in zip(halos, SIDES)]
+    corner_rows = corner_segments(1, nx, ny)[1]
+    corners = pl.pallas_call(
+        functools.partial(corner_kernel, nx, ny),
+        out_shape=[jax.ShapeDtypeStruct((corner_rows, nz), jnp.float32)] * 2,
+        in_specs=[SMEM] + [VMEM] * 2,
+        out_specs=[VMEM] * 2,
+        name="corners",
+    )(zero, halos[0], halos[1])
+    halos += [shifted(corner, (0, side_y)) for corner, side_y in zip(corners, (-1, 1))]
     wide, tall = ny + 4, ny + 12
 
     def scratch(*shape):
@@ -221,8 +239,8 @@
 
     *outs, peak = pl.pallas_call(
         functools.partial(step_kernel, nx, ny),
-        out_shape=[jax.ShapeDtypeStruct((nx, ny, nz), jnp.float32)] * 5 + [jax.ShapeDtypeStruct((8, nz), jnp.float32)],
-        in_specs=[SMEM, SMEM] + [VMEM] * 13,
+        out_shape=[jax.ShapeDtypeStruct((nx, ny, nz), jnp.float32)] * 5 + [jax.ShapeDtypeStruct((1, nz), jnp.float32)],
+        in_specs=[SMEM, SMEM] + [VMEM] * 11,
         out_specs=[VMEM] * 6,
         scratch_shapes=[
             scratch(5, nx + 8, ny + 20),
@@ -237,7 +255,7 @@
         compiler_params=pltpu.CompilerParams(vmem_limit_bytes=32 * 1024 * 1024),
         name="step",
     )(zero, time_increment.reshape(1), *fields, *halos)
-    peak = all_max(all_max(peak, "gy", 4), "gx", 8)
+    peak = lax.all_gather(peak, ("gx", "gy"), tiled=True)
     return (*outs, 0.3 / jnp.max(peak))
 
 

time: 53.2 us -> 66.4 us (1.25)
  blocking collectives: 0 us -> 40.8 us
  starting transfers between devices: 25.6 us -> 9.5 us
  waiting for transfers between devices: 19.1 us -> 3.54 us
  local copies, waits for them, and re-layouts: 0.02 us -> 2.44 us
  Pallas kernels: 4.5 us -> 6.04 us
    all_gather x0 -> x1, blocking collectives: none -> 40.8 us  [body(): peak = lax.all_gather(peak, ('gx', 'gy'), tiled=True)]
    ppermute x18 -> x6, starting transfers between devices: 25.6 us -> 9.5 us  [shifted(): lax.ppermute(value, axis, [((i + step) % count, i) for i in range(count)])]
    ppermute x18 -> x6, waiting for transfers between devices: 19.1 us -> 3.54 us  [shifted(): lax.ppermute(value, axis, [((i + step) % count, i) for i in range(count)])]
    unnamed x10 -> x18, local copies, waits for them, and re-layouts: 0.02 us -> 2.44 us
    pallas_call x0 -> x1, Pallas kernels: none -> 1.6 us  [body(): pl.pallas_call(functools.partial(corner_kernel, nx, ny), out_shape=[jax.S...]
  transfers between devices with their start and end apart: 18 -> 6, of which waited for: 9 -> 4; matrix products, arithmetic and copies ran while one was open for 0% -> 0% of each run, Pallas kernels for 0% -> 2%
where the time goes in v3:
time: 66.4 us; the launch traced here: 66.1 us
  blocking collectives  40.8 us (61%)
  starting transfers between devices  9.5 us (14%)
  Pallas kernels  6.04 us (9%)
  waiting for transfers between devices  3.54 us (5%)
  between operations  3.17 us (5%)
  local copies, waits for them, and re-layouts  2.44 us (4%)
    all_gather x1, blocking collectives, body(): peak = lax.all_gather(peak, ('gx', 'gy'), tiled=True)  40.8 us
    ppermute x6, starting transfers between devices, shifted(): lax.ppermute(value, axis, [((i + step) % count, i) for i in range(count)])  9.5 us
    ppermute x6, waiting for transfers between devices, shifted(): lax.ppermute(value, axis, [((i + step) % count, i) for i in range(count)])  3.54 us
    pallas_call x1, Pallas kernels, body(): pl.pallas_call(functools.partial(step_kernel, nx, ny), out_shape=[jax.Sha...  2.51 us
    unnamed x18, local copies, waits for them, and re-layouts  2.44 us
    pallas_call x1, Pallas kernels, body(): pl.pallas_call(functools.partial(pack_kernel, nx, ny), out_shape=[jax.Sha...  1.93 us
    pallas_call x1, Pallas kernels, body(): pl.pallas_call(functools.partial(corner_kernel, nx, ny), out_shape=[jax.S...  1.6 us
  transfers between devices with their start and end apart: 6, of which 4 were waited for; matrix products, arithmetic and copies ran while one was open for 0% of the time, Pallas kernels for 2%

profile of v3, /device:TPU:0, one launch (start us, length us, event | category | flops | bytes accessed | tf_op | source)
XLA Modules:
  0.0 66.1 jit_solution(15415107422778190297)
XLA Ops:
  0.6 0.0 copy-start.2
  0.6 0.0 copy-start.3
  0.7 0.0 copy-start.4
  0.7 1.9 %pack.1 = (f32[192,128]{1,0:T(8,128)}, f32[192,128]{1,0:T(8,128)}, f32[192,128]{1,0:T(8,128)}, f32[192,128]{1,0:T(8,128)}) custom-call(s32[1]{0:T(128)} %constant.0.clone.1.zero_ref, f32[12,12,128]{2,1,0:T(8,128)} %refs_0_.3, f32[12,12,128]{2,1,0:T(8,128)} %refs_1_.3, f32[12,12,128]{2,1,0:T(8,128)} %refs_2_.3, f32[12,12,128]{2,1,0:T(8,128)} %refs_3_.3, ...), custom_call_target="tpu_custom_call" | custom-call | tf_op jit(solution)/shard_map/pack/pallas_call | solution.py:218
  2.6 3.0 %collective-permute-start = (f32[192,128]{1,0:T(8,128)}, f32[192,128]{1,0:T(8,128)S(1)}, u32[]{:S(2)}, u32[]{:S(2)}) collective-permute-start(f32[192,128]{1,0:T(8,128)} %get-tuple-element.18), channel_id=1, source_target_pairs={{28,0},{0,4},{4,8},{8,12},{12,16},{16,20},{20,24},{24,28},{29,1},{... | collective-permute-start | bytes 294920 | tf_op jit(solution)/shard_map/ppermute | solution.py:210
  5.6 3.0 %collective-permute-start.1 = (f32[192,128]{1,0:T(8,128)}, f32[192,128]{1,0:T(8,128)S(1)}, u32[]{:S(2)}, u32[]{:S(2)}) collective-permute-start(f32[192,128]{1,0:T(8,128)} %get-tuple-element.19), channel_id=1, source_target_pairs={{4,0},{8,4},{12,8},{16,12},{20,16},{24,20},{28,24},{0,28},{5,1},{9... | collective-permute-start | bytes 294920 | tf_op jit(solution)/shard_map/ppermute | solution.py:210
  8.6 0.0 collective-permute-start.2
  8.6 0.0 copy-start
  8.6 0.0 copy-start.1
  8.6 1.7 %collective-permute-start.3 = (f32[192,128]{1,0:T(8,128)}, f32[192,128]{1,0:T(8,128)S(1)}, u32[]{:S(2)}, u32[]{:S(2)}) collective-permute-start(f32[192,128]{1,0:T(8,128)} %get-tuple-element.21), channel_id=1, source_target_pairs={{1,0},{2,1},{3,2},{0,3},{5,4},{6,5},{7,6},{4,7},{9,8},{10,9},{11,1... | collective-permute-start | bytes 294920 | tf_op jit(solution)/shard_map/ppermute | solution.py:210
  10.4 1.4 %collective-permute-done.below_ref.refs_5_ = f32[192,128]{1,0:T(8,128)S(1)} collective-permute-done((f32[192,128]{1,0:T(8,128)}, f32[192,128]{1,0:T(8,128)S(1)}, u32[]{:S(2)}, u32[]{:S(2)}) %collective-permute-start) | collective-permute-done | bytes 98336 | tf_op jit(solution)/shard_map/ppermute | solution.py:210
  11.7 0.0 copy-start.5
  11.7 0.8 %collective-permute-done.1.above_ref.refs_6_ = f32[192,128]{1,0:T(8,128)S(1)} collective-permute-done((f32[192,128]{1,0:T(8,128)}, f32[192,128]{1,0:T(8,128)S(1)}, u32[]{:S(2)}, u32[]{:S(2)}) %collective-permute-start.1) | collective-permute-done | bytes 98336 | tf_op jit(solution)/shard_map/ppermute | solution.py:210
  12.5 0.0 copy-done.5
  12.5 0.0 copy-start.7
  12.5 0.6 copy-done.7
  13.1 1.6 %corners.1 = (f32[96,128]{1,0:T(8,128)}, f32[96,128]{1,0:T(8,128)}) custom-call(s32[1]{0:T(128)} %constant.0.clone.1.zero_ref, f32[192,128]{1,0:T(8,128)} %copy-done.5, f32[192,128]{1,0:T(8,128)} %copy-done.7), custom_call_target="tpu_custom_call" | custom-call | tf_op jit(solution)/shard_map/corners/pallas_call | solution.py:227
  14.7 0.0 collective-permute-start.4
  14.7 1.7 %collective-permute-start.5 = (f32[96,128]{1,0:T(8,128)}, f32[96,128]{1,0:T(8,128)S(1)}, u32[]{:S(2)}, u32[]{:S(2)}) collective-permute-start(f32[96,128]{1,0:T(8,128)} %get-tuple-element.23), channel_id=1, source_target_pairs={{1,0},{2,1},{3,2},{0,3},{5,4},{6,5},{7,6},{4,7},{9,8},{10,9},{11,1... | collective-permute-start | bytes 147464 | tf_op jit(solution)/shard_map/ppermute | solution.py:210
  17.1 0.0 collective-permute-done.2.refs_7_
  17.1 0.0 collective-permute-done.3.refs_8_
  17.2 1.3 %collective-permute-done.4.refs_9_ = f32[96,128]{1,0:T(8,128)S(1)} collective-permute-done((f32[96,128]{1,0:T(8,128)}, f32[96,128]{1,0:T(8,128)S(1)}, u32[]{:S(2)}, u32[]{:S(2)}) %collective-permute-start.4) | collective-permute-done | bytes 49184 | tf_op jit(solution)/shard_map/ppermute | solution.py:210
  18.5 0.1 collective-permute-done.5.refs_10_
  18.6 0.0 copy-done.2
  18.6 0.0 copy-done.3
  18.6 0.0 copy-done.4
  18.6 0.0 copy-done
  18.6 0.0 copy-done.1
  18.6 0.0 copy-start.6
  18.6 0.9 %copy-done.6 = f32[192,128]{1,0:T(8,128)S(1)} copy-done((f32[192,128]{1,0:T(8,128)S(1)}, f32[192,128]{1,0:T(8,128)}, u32[]{:S(2)}) %copy-start.6) | copy-done | bytes 98328
  19.5 0.0 copy-start.8
  19.5 0.9 %copy-done.8 = f32[192,128]{1,0:T(8,128)S(1)} copy-done((f32[192,128]{1,0:T(8,128)S(1)}, f32[192,128]{1,0:T(8,128)}, u32[]{:S(2)}) %copy-start.8) | copy-done | bytes 98328
  20.4 2.5 %step.1 = (f32[12,12,128]{2,1,0:T(8,128)}, f32[12,12,128]{2,1,0:T(8,128)}, f32[12,12,128]{2,1,0:T(8,128)}, f32[12,12,128]{2,1,0:T(8,128)}, f32[12,12,128]{2,1,0:T(8,128)}, /*index=5*/f32[1,128]{1,0:T(1,128)S(1)}) custom-call(s32[1]{0:T(128)} %constant.0.clone.1.zero_ref, f32[1]{0:T(128)} %bitcast.2.dt_ref, f32[12,12,128]{2,1,0:T(8,128)S(1)} %copy-done, ...), custom_call_target="tpu_custom_call" | custom-call | tf_op jit(solution)/shard_map/step/pallas_call | solution.py:240
  22.9 40.8 %all-gather = f32[32,1,128]{2,1,0:T(1,128)S(1)} all-gather(f32[1,1,128]{2,1,0:T(1,128)S(1)} %bitcast.3), channel_id=1, replica_groups=mesh['gx'=8,'gy'=4] {'gx','gy'}, dimensions={0}, use_global_device_ids=true | all-gather | bytes 16896 | tf_op jit(solution)/shard_map/all_gather | solution.py:258
  63.7 0.6 reduce_max.9
Async XLA Ops:
  0.6 17.9 %copy-start.2 = (f32[12,12,128]{2,1,0:T(8,128)S(1)}, f32[12,12,128]{2,1,0:T(8,128)}, u32[]{:S(2)}) copy-start(f32[12,12,128]{2,1,0:T(8,128)} %refs_2_.3) | copy-start | bytes 221188
  0.6 17.9 %copy-start.3 = (f32[12,12,128]{2,1,0:T(8,128)S(1)}, f32[12,12,128]{2,1,0:T(8,128)}, u32[]{:S(2)}) copy-start(f32[12,12,128]{2,1,0:T(8,128)} %refs_3_.3) | copy-start | bytes 221188
  0.7 17.9 %copy-start.4 = (f32[12,12,128]{2,1,0:T(8,128)S(1)}, f32[12,12,128]{2,1,0:T(8,128)}, u32[]{:S(2)}) copy-start(f32[12,12,128]{2,1,0:T(8,128)} %refs_4_.3) | copy-start | bytes 221188
  2.6 9.1 %collective-permute-start = (f32[192,128]{1,0:T(8,128)}, f32[192,128]{1,0:T(8,128)S(1)}, u32[]{:S(2)}, u32[]{:S(2)}) collective-permute-start(f32[192,128]{1,0:T(8,128)} %get-tuple-element.18), channel_id=1, source_target_pairs={{28,0},{0,4},{4,8},{8,12},{12,16},{16,20},{20,24},{24,28},{29,1},{... | collective-permute-start | bytes 294920 | tf_op jit(solution)/shard_map/ppermute | solution.py:210
  5.6 6.9 %collective-permute-start.1 = (f32[192,128]{1,0:T(8,128)}, f32[192,128]{1,0:T(8,128)S(1)}, u32[]{:S(2)}, u32[]{:S(2)}) collective-permute-start(f32[192,128]{1,0:T(8,128)} %get-tuple-element.19), channel_id=1, source_target_pairs={{4,0},{8,4},{12,8},{16,12},{20,16},{24,20},{28,24},{0,28},{5,1},{9... | collective-permute-start | bytes 294920 | tf_op jit(solution)/shard_map/ppermute | solution.py:210
  8.6 8.5 %collective-permute-start.2 = (f32[192,128]{1,0:T(8,128)}, f32[192,128]{1,0:T(8,128)S(1)}, u32[]{:S(2)}, u32[]{:S(2)}) collective-permute-start(f32[192,128]{1,0:T(8,128)} %get-tuple-element.20), channel_id=1, source_target_pairs={{3,0},{0,1},{1,2},{2,3},{7,4},{4,5},{5,6},{6,7},{11,8},{8,9},{9,10... | collective-permute-start | bytes 294920 | tf_op jit(solution)/shard_map/ppermute | solution.py:210
  8.6 10.0 %copy-start = (f32[12,12,128]{2,1,0:T(8,128)S(1)}, f32[12,12,128]{2,1,0:T(8,128)}, u32[]{:S(2)}) copy-start(f32[12,12,128]{2,1,0:T(8,128)} %refs_0_.3) | copy-start | bytes 221188
  8.6 10.0 %copy-start.1 = (f32[12,12,128]{2,1,0:T(8,128)S(1)}, f32[12,12,128]{2,1,0:T(8,128)}, u32[]{:S(2)}) copy-start(f32[12,12,128]{2,1,0:T(8,128)} %refs_1_.3) | copy-start | bytes 221188
  8.6 8.5 %collective-permute-start.3 = (f32[192,128]{1,0:T(8,128)}, f32[192,128]{1,0:T(8,128)S(1)}, u32[]{:S(2)}, u32[]{:S(2)}) collective-permute-start(f32[192,128]{1,0:T(8,128)} %get-tuple-element.21), channel_id=1, source_target_pairs={{1,0},{2,1},{3,2},{0,3},{5,4},{6,5},{7,6},{4,7},{9,8},{10,9},{11,1... | collective-permute-start | bytes 294920 | tf_op jit(solution)/shard_map/ppermute | solution.py:210
  11.7 0.8 %copy-start.5 = (f32[192,128]{1,0:T(8,128)}, f32[192,128]{1,0:T(8,128)S(1)}, u32[]{:S(2)}) copy-start(f32[192,128]{1,0:T(8,128)S(1)} %collective-permute-done.below_ref.refs_5_) | copy-start | bytes 294916
  12.5 0.6 copy-start.7
  14.7 3.7 %collective-permute-start.4 = (f32[96,128]{1,0:T(8,128)}, f32[96,128]{1,0:T(8,128)S(1)}, u32[]{:S(2)}, u32[]{:S(2)}) collective-permute-start(f32[96,128]{1,0:T(8,128)} %get-tuple-element.22), channel_id=1, source_target_pairs={{3,0},{0,1},{1,2},{2,3},{7,4},{4,5},{5,6},{6,7},{11,8},{8,9},{9,10... | collective-permute-start | bytes 147464 | tf_op jit(solution)/shard_map/ppermute | solution.py:210
  14.7 3.8 %collective-permute-start.5 = (f32[96,128]{1,0:T(8,128)}, f32[96,128]{1,0:T(8,128)S(1)}, u32[]{:S(2)}, u32[]{:S(2)}) collective-permute-start(f32[96,128]{1,0:T(8,128)} %get-tuple-element.23), channel_id=1, source_target_pairs={{1,0},{2,1},{3,2},{0,3},{5,4},{6,5},{7,6},{4,7},{9,8},{10,9},{11,1... | collective-permute-start | bytes 147464 | tf_op jit(solution)/shard_map/ppermute | solution.py:210
  18.6 0.9 %copy-start.6 = (f32[192,128]{1,0:T(8,128)S(1)}, f32[192,128]{1,0:T(8,128)}, u32[]{:S(2)}) copy-start(f32[192,128]{1,0:T(8,128)} %copy-done.5) | copy-start | bytes 294916
  19.5 0.9 %copy-start.8 = (f32[192,128]{1,0:T(8,128)S(1)}, f32[192,128]{1,0:T(8,128)}, u32[]{:S(2)}) copy-start(f32[192,128]{1,0:T(8,128)} %copy-done.7) | copy-start | bytes 294916

commit v4 on v3

--- a/solution.py
+++ b/solution.py
@@ -12,6 +12,7 @@
 SIDES = ((-1, 0), (1, 0), (0, -1), (0, 1))
 TOP = 8
 VMEM = pl.BlockSpec(memory_space=pltpu.VMEM)
+HBM = pl.BlockSpec(memory_space=pltpu.HBM)
 SMEM = pl.BlockSpec(memory_space=pltpu.SMEM)
 
 
@@ -50,13 +51,19 @@
 
 
 def pack_kernel(nx, ny, zero_ref, *refs):
-    fields, halos = refs[:5], refs[5:]
+    fields, own, edges, arrived = refs[:5], refs[5], refs[6 : 6 + len(SIDES)], refs[-1]
     zero = zero_ref[0]
-    for side, halo in zip(SIDES, halos):
-        for field, a, b, count, offset in segments(side, nx, ny)[0]:
-            halo[pl.ds(zero + offset, count), :] = fields[field][
-                a - side[0] * nx, pl.ds(zero + (b - side[1] * ny), count), :
-            ]
+    copies = [pltpu.make_async_copy(fields[field], own.at[field], arrived.at[field]) for field in range(5)]
+    for copy in copies:
+        copy.start()
+    for current, copy in enumerate(copies):
+        copy.wait()
+        for side, edge in zip(SIDES, edges):
+            for field, a, b, count, offset in segments(side, nx, ny)[0]:
+                if field == current:
+                    edge[pl.ds(zero + offset, count), :] = own[
+                        field, a - side[0] * nx, pl.ds(zero + (b - side[1] * ny), count), :
+                    ]
 
 
 def corner_kernel(nx, ny, zero_ref, below_ref, above_ref, low_ref, high_ref):
@@ -88,8 +95,8 @@
 
 
 def step_kernel(nx, ny, zero_ref, dt_ref, *refs):
-    fields, halos, outs, peak_ref = refs[:5], refs[5:11], refs[11:16], refs[16]
-    cells, stress, growth, heat, state, energy_one, swept, work = refs[17:]
+    own, halos, outs, peak_ref = refs[0], refs[1:7], refs[7:12], refs[12]
+    cells, stress, growth, heat, state, energy_one, swept, work = refs[13:]
     zero = zero_ref[0]
     dt = dt_ref[0]
     half = 0.5 * dt
@@ -98,7 +105,7 @@
 
     for field in range(5):
         for a in range(nx):
-            cells[field, a + REACH, pl.ds(TOP, ny), :] = fields[field][a]
+            cells[field, a + REACH, pl.ds(TOP, ny), :] = own[field, a]
     for side, halo in zip(SIDES, halos):
         for field, a, b, count, offset in segments(side, nx, ny)[0]:
             cells[field, a + REACH, pl.ds(zero + (b + TOP), count), :] = halo[pl.ds(zero + offset, count), :]
@@ -201,7 +208,9 @@
         )
     row = lax.broadcasted_iota(jnp.int32, peak.shape, 0)
     peak = jnp.where(row < ny, peak, 0.0)
-    peak_ref[...] = jnp.max(peak, axis=0, keepdims=True)
+    peak = jnp.max(peak, axis=0, keepdims=True)
+    for copy in range(peak_ref.shape[0]):
+        peak_ref[copy] = peak
 
 
 def shifted(value, side):
@@ -210,37 +219,48 @@
     return lax.ppermute(value, axis, [((i + step) % count, i) for i in range(count)])
 
 
+def all_max(copies, axis):
+    return jnp.max(lax.all_to_all(copies, axis, 0, 0, tiled=True), axis=0)
+
+
 def body(density0, energy0, x_velocity, y_velocity, z_velocity, time_increment):
     nx, ny, nz = density0.shape
     fields = (density0, energy0, x_velocity, y_velocity, z_velocity)
     zero = jnp.zeros((1,), jnp.int32)
-    sizes = [segments(side, nx, ny)[1] for side in SIDES]
-    halos = pl.pallas_call(
+    wide, tall = ny + 4, ny + 12
+
+    def array(*shape):
+        return jax.ShapeDtypeStruct((*shape, nz), jnp.float32)
+
+    def scratch(*shape):
+        return pltpu.VMEM((*shape, nz), jnp.float32)
+
+    def limit(mebibytes):
+        return pltpu.CompilerParams(vmem_limit_bytes=mebibytes * 1024 * 1024)
+
+    own, *edges = pl.pallas_call(
         functools.partial(pack_kernel, nx, ny),
-        out_shape=[jax.ShapeDtypeStruct((size, nz), jnp.float32) for size in sizes],
-        in_specs=[SMEM] + [VMEM] * 5,
-        out_specs=[VMEM] * len(SIDES),
+        out_shape=[array(5, nx, ny)] + [array(segments(side, nx, ny)[1]) for side in SIDES],
+        in_specs=[SMEM] + [HBM] * 5,
+        out_specs=[VMEM] * (1 + len(SIDES)),
+        scratch_shapes=[pltpu.SemaphoreType.DMA((5,))],
+        compiler_params=limit(4),
         name="pack",
-    )(zero, *fields)
-    halos = [shifted(halo, side) for halo, side in zip(halos, SIDES)]
-    corner_rows = corner_segments(1, nx, ny)[1]
+    )(zero, *[pltpu.with_memory_space_constraint(field, pltpu.HBM) for field in fields])
+    edges = [shifted(edge, side) for edge, side in zip(edges, SIDES)]
     corners = pl.pallas_call(
         functools.partial(corner_kernel, nx, ny),
-        out_shape=[jax.ShapeDtypeStruct((corner_rows, nz), jnp.float32)] * 2,
+        out_shape=[array(corner_segments(1, nx, ny)[1])] * 2,
         in_specs=[SMEM] + [VMEM] * 2,
         out_specs=[VMEM] * 2,
+        compiler_params=limit(4),
         name="corners",
-    )(zero, halos[0], halos[1])
-    halos += [shifted(corner, (0, side_y)) for corner, side_y in zip(corners, (-1, 1))]
-    wide, tall = ny + 4, ny + 12
-
-    def scratch(*shape):
-        return pltpu.VMEM((*shape, nz), jnp.float32)
-
+    )(zero, edges[0], edges[1])
+    corners = [shifted(corner, (0, side_y)) for corner, side_y in zip(corners, (-1, 1))]
     *outs, peak = pl.pallas_call(
         functools.partial(step_kernel, nx, ny),
-        out_shape=[jax.ShapeDtypeStruct((nx, ny, nz), jnp.float32)] * 5 + [jax.ShapeDtypeStruct((1, nz), jnp.float32)],
-        in_specs=[SMEM, SMEM] + [VMEM] * 11,
+        out_shape=[array(nx, ny)] * 5 + [array(lax.axis_size("gy"), 1)],
+        in_specs=[SMEM, SMEM] + [VMEM] * 7,
         out_specs=[VMEM] * 6,
         scratch_shapes=[
             scratch(5, nx + 8, ny + 20),
@@ -252,10 +272,11 @@
             scratch(5, nx, wide + 8),
             scratch(10, nx, wide + 8),
         ],
-        compiler_params=pltpu.CompilerParams(vmem_limit_bytes=32 * 1024 * 1024),
+        compiler_params=limit(12),
         name="step",
-    )(zero, time_increment.reshape(1), *fields, *halos)
-    peak = lax.all_gather(peak, ("gx", "gy"), tiled=True)
+    )(zero, time_increment.reshape(1), own, *edges, *corners)
+    peak = all_max(peak, "gy")
+    peak = all_max(jnp.broadcast_to(peak, (lax.axis_size("gx"), 1, nz)), "gx")
     return (*outs, 0.3 / jnp.max(peak))
 
 

time: 66.4 us -> 38.1 us (0.57)
  blocking collectives: 40.8 us -> 17.8 us
  Pallas kernels: 6.04 us -> 3.61 us
  local copies, waits for them, and re-layouts: 2.44 us -> 0.01 us
    all_gather x1 -> x0, blocking collectives: 40.8 us -> none  [body(): peak = lax.all_gather(peak, ('gx', 'gy'), tiled=True)]
    all_to_all x0 -> x2, blocking collectives: none -> 17.8 us  [all_max(): return jnp.max(lax.all_to_all(copies, axis, 0, 0, tiled=True), axis=0)]
    unnamed x18 -> x0, local copies, waits for them, and re-layouts: 2.44 us -> none
    pallas_call x3, Pallas kernels: 6.04 us -> 3.61 us  [the longest x1 2.5 us: body(): pl.pallas_call(functools.partial(step_kernel, nx, ny), out_shape=[array(n...]
  transfers between devices with their start and end apart: 6 -> 6, of which waited for: 4 -> 3; matrix products, arithmetic and copies ran while one was open for 0% -> 0% of each run, Pallas kernels for 2% -> 0%
where the time goes in v4:
time: 38.1 us; the launch traced here: 37.8 us
  blocking collectives  17.8 us (47%)
  starting transfers between devices  9.66 us (25%)
  Pallas kernels  3.61 us (9%)
  between operations  3.14 us (8%)
  waiting for transfers between devices  2.98 us (8%)
  other arithmetic  0.62 us (2%)
    all_to_all x2, blocking collectives, all_max(): return jnp.max(lax.all_to_all(copies, axis, 0, 0, tiled=True), axis=0)  17.8 us
    ppermute x6, starting transfers between devices, shifted(): lax.ppermute(value, axis, [((i + step) % count, i) for i in range(count)])  9.66 us
    ppermute x6, waiting for transfers between devices, shifted(): lax.ppermute(value, axis, [((i + step) % count, i) for i in range(count)])  2.98 us
    pallas_call x1, Pallas kernels, body(): pl.pallas_call(functools.partial(step_kernel, nx, ny), out_shape=[array(n...  2.5 us
    pallas_call x1, Pallas kernels, body(): pl.pallas_call(functools.partial(pack_kernel, nx, ny), out_shape=[array(5...  1.08 us
  transfers between devices with their start and end apart: 6, of which 3 were waited for; matrix products, arithmetic and copies ran while one was open for 0% of the time, Pallas kernels for 0%

profile of v4, /device:TPU:0, one launch (start us, length us, event | category | flops | bytes accessed | tf_op | source)
XLA Modules:
  0.0 37.8 jit_solution(338696894264365047)
XLA Ops:
  0.6 1.1 %pack.1 = (f32[5,12,12,128]{3,2,1,0:T(8,128)S(1)}, f32[192,128]{1,0:T(8,128)S(1)}, f32[192,128]{1,0:T(8,128)S(1)}, f32[192,128]{1,0:T(8,128)S(1)}, f32[192,128]{1,0:T(8,128)S(1)}) custom-call(s32[1]{0:T(128)} %constant.0.clone.1.zero_ref, f32[12,12,128]{2,1,0:T(8,128)} %refs_0_.1, f32[12,12,128]{2,1,0:T(8,128)} %refs_1_.1, f32[12,12,128]{2,1,0:T(8,128)} %refs_2_.1, ...), custom_call_target="tpu_custom_call" | custom-call | tf_op jit(solution)/shard_map/pack/pallas_call | solution.py:241
  1.7 3.0 %collective-permute-start = (f32[192,128]{1,0:T(8,128)S(1)}, f32[192,128]{1,0:T(8,128)S(1)}, u32[]{:S(2)}, u32[]{:S(2)}) collective-permute-start(f32[192,128]{1,0:T(8,128)S(1)} %get-tuple-element.20), channel_id=1, source_target_pairs={{28,0},{0,4},{4,8},{8,12},{12,16},{16,20},{20,24},{24,28},{29,1},{... | collective-permute-start | bytes 294920 | tf_op jit(solution)/shard_map/ppermute | solution.py:219
  4.7 3.1 %collective-permute-start.1 = (f32[192,128]{1,0:T(8,128)S(1)}, f32[192,128]{1,0:T(8,128)S(1)}, u32[]{:S(2)}, u32[]{:S(2)}) collective-permute-start(f32[192,128]{1,0:T(8,128)S(1)} %get-tuple-element.21), channel_id=1, source_target_pairs={{4,0},{8,4},{12,8},{16,12},{20,16},{24,20},{28,24},{0,28},{5,1},{9... | collective-permute-start | bytes 294920 | tf_op jit(solution)/shard_map/ppermute | solution.py:219
  7.8 0.0 collective-permute-start.2
  7.9 1.7 %collective-permute-start.3 = (f32[192,128]{1,0:T(8,128)S(1)}, f32[192,128]{1,0:T(8,128)S(1)}, u32[]{:S(2)}, u32[]{:S(2)}) collective-permute-start(f32[192,128]{1,0:T(8,128)S(1)} %get-tuple-element.23), channel_id=1, source_target_pairs={{1,0},{2,1},{3,2},{0,3},{5,4},{6,5},{7,6},{4,7},{9,8},{10,9},{11,1... | collective-permute-start | bytes 294920 | tf_op jit(solution)/shard_map/ppermute | solution.py:219
  9.6 1.1 %collective-permute-done.below_ref.refs_1_ = f32[192,128]{1,0:T(8,128)S(1)} collective-permute-done((f32[192,128]{1,0:T(8,128)S(1)}, f32[192,128]{1,0:T(8,128)S(1)}, u32[]{:S(2)}, u32[]{:S(2)}) %collective-permute-start) | collective-permute-done | bytes 98336 | tf_op jit(solution)/shard_map/ppermute | solution.py:219
  10.7 0.8 %collective-permute-done.1.above_ref.refs_2_ = f32[192,128]{1,0:T(8,128)S(1)} collective-permute-done((f32[192,128]{1,0:T(8,128)S(1)}, f32[192,128]{1,0:T(8,128)S(1)}, u32[]{:S(2)}, u32[]{:S(2)}) %collective-permute-start.1) | collective-permute-done | bytes 98336 | tf_op jit(solution)/shard_map/ppermute | solution.py:219
  11.5 0.1 collective-permute-start.4
  11.6 1.7 %collective-permute-start.5 = (f32[96,128]{1,0:T(8,128)S(1)}, f32[96,128]{1,0:T(8,128)S(1)}, u32[]{:S(2)}, u32[]{:S(2)}) collective-permute-start(f32[96,128]{1,0:T(8,128)S(1)} %get-tuple-element.25), channel_id=1, source_target_pairs={{1,0},{2,1},{3,2},{0,3},{5,4},{6,5},{7,6},{4,7},{9,8},{10,9},{11,1... | collective-permute-start | bytes 147464 | tf_op jit(solution)/shard_map/ppermute | solution.py:219
  13.9 0.0 collective-permute-done.2.refs_3_
  14.0 0.0 collective-permute-done.3.refs_4_
  14.0 1.1 %collective-permute-done.4.refs_5_ = f32[96,128]{1,0:T(8,128)S(1)} collective-permute-done((f32[96,128]{1,0:T(8,128)S(1)}, f32[96,128]{1,0:T(8,128)S(1)}, u32[]{:S(2)}, u32[]{:S(2)}) %collective-permute-start.4) | collective-permute-done | bytes 49184 | tf_op jit(solution)/shard_map/ppermute | solution.py:219
  15.1 0.0 collective-permute-done.5.refs_6_
  15.1 2.5 %step.1 = (f32[12,12,128]{2,1,0:T(8,128)}, f32[12,12,128]{2,1,0:T(8,128)}, f32[12,12,128]{2,1,0:T(8,128)}, f32[12,12,128]{2,1,0:T(8,128)}, f32[12,12,128]{2,1,0:T(8,128)}, /*index=5*/f32[4,1,128]{2,1,0:T(1,128)S(1)}) custom-call(s32[1]{0:T(128)} %constant.0.clone.1.zero_ref, f32[1]{0:T(128)} %bitcast.2.dt_ref, ...), custom_call_target="tpu_custom_call" | custom-call | tf_op jit(solution)/shard_map/step/pallas_call | solution.py:260
  17.6 6.6 %all_to_all.10 = f32[4,1,128]{2,1,0:T(1,128)S(1)} all-to-all(f32[4,1,128]{2,1,0:T(1,128)S(1)} %get-tuple-element.31), channel_id=1, replica_groups=mesh['gx'=8,'gy'=4] {'gy'}, dimensions={0} | all-to-all | bytes 4096 | tf_op jit(solution)/shard_map/all_to_all | solution.py:223
  24.2 11.2 %all_to_all.11 = f32[8,1,128]{2,1,0:T(1,128)S(1)} all-to-all(f32[8,1,128]{2,1,0:T(1,128)S(1)} %broadcast_in_dim.3), channel_id=1, replica_groups=mesh['gx'=8,'gy'=4] {'gx'}, dimensions={0} | all-to-all | bytes 8192 | tf_op jit(solution)/shard_map/all_to_all | solution.py:223
  35.4 0.6 %reduce_max.20 = f32[]{:T(128)} reduce(f32[8,1,128]{2,0,1:T(8,128)S(1)} %bitcast.3, f32[]{:T(128)} %constant.2.clone.1), dimensions={0,1,2}, to_apply=%region_1.0 | reduce | flops 1023 | bytes 4104 | tf_op jit(solution)/shard_map/reduce_max | solution.py:280
  (3 shorter events, 0.1 us)
Async XLA Ops:
  1.7 9.0 %collective-permute-start = (f32[192,128]{1,0:T(8,128)S(1)}, f32[192,128]{1,0:T(8,128)S(1)}, u32[]{:S(2)}, u32[]{:S(2)}) collective-permute-start(f32[192,128]{1,0:T(8,128)S(1)} %get-tuple-element.20), channel_id=1, source_target_pairs={{28,0},{0,4},{4,8},{8,12},{12,16},{16,20},{20,24},{24,28},{29,1},{... | collective-permute-start | bytes 294920 | tf_op jit(solution)/shard_map/ppermute | solution.py:219
  4.7 6.7 %collective-permute-start.1 = (f32[192,128]{1,0:T(8,128)S(1)}, f32[192,128]{1,0:T(8,128)S(1)}, u32[]{:S(2)}, u32[]{:S(2)}) collective-permute-start(f32[192,128]{1,0:T(8,128)S(1)} %get-tuple-element.21), channel_id=1, source_target_pairs={{4,0},{8,4},{12,8},{16,12},{20,16},{24,20},{28,24},{0,28},{5,1},{9... | collective-permute-start | bytes 294920 | tf_op jit(solution)/shard_map/ppermute | solution.py:219
  7.8 6.1 %collective-permute-start.2 = (f32[192,128]{1,0:T(8,128)S(1)}, f32[192,128]{1,0:T(8,128)S(1)}, u32[]{:S(2)}, u32[]{:S(2)}) collective-permute-start(f32[192,128]{1,0:T(8,128)S(1)} %get-tuple-element.22), channel_id=1, source_target_pairs={{3,0},{0,1},{1,2},{2,3},{7,4},{4,5},{5,6},{6,7},{11,8},{8,9},{9,10... | collective-permute-start | bytes 294920 | tf_op jit(solution)/shard_map/ppermute | solution.py:219
  7.9 6.1 %collective-permute-start.3 = (f32[192,128]{1,0:T(8,128)S(1)}, f32[192,128]{1,0:T(8,128)S(1)}, u32[]{:S(2)}, u32[]{:S(2)}) collective-permute-start(f32[192,128]{1,0:T(8,128)S(1)} %get-tuple-element.23), channel_id=1, source_target_pairs={{1,0},{2,1},{3,2},{0,3},{5,4},{6,5},{7,6},{4,7},{9,8},{10,9},{11,1... | collective-permute-start | bytes 294920 | tf_op jit(solution)/shard_map/ppermute | solution.py:219
  11.5 3.6 %collective-permute-start.4 = (f32[96,128]{1,0:T(8,128)S(1)}, f32[96,128]{1,0:T(8,128)S(1)}, u32[]{:S(2)}, u32[]{:S(2)}) collective-permute-start(f32[96,128]{1,0:T(8,128)S(1)} %get-tuple-element.24), channel_id=1, source_target_pairs={{3,0},{0,1},{1,2},{2,3},{7,4},{4,5},{5,6},{6,7},{11,8},{8,9},{9,10... | collective-permute-start | bytes 147464 | tf_op jit(solution)/shard_map/ppermute | solution.py:219
  11.6 3.5 %collective-permute-start.5 = (f32[96,128]{1,0:T(8,128)S(1)}, f32[96,128]{1,0:T(8,128)S(1)}, u32[]{:S(2)}, u32[]{:S(2)}) collective-permute-start(f32[96,128]{1,0:T(8,128)S(1)} %get-tuple-element.25), channel_id=1, source_target_pairs={{1,0},{2,1},{3,2},{0,3},{5,4},{6,5},{7,6},{4,7},{9,8},{10,9},{11,1... | collective-permute-start | bytes 147464 | tf_op jit(solution)/shard_map/ppermute | solution.py:219

commit v5 on v4

--- a/solution.py
+++ b/solution.py
@@ -208,9 +208,7 @@
         )
     row = lax.broadcasted_iota(jnp.int32, peak.shape, 0)
     peak = jnp.where(row < ny, peak, 0.0)
-    peak = jnp.max(peak, axis=0, keepdims=True)
-    for copy in range(peak_ref.shape[0]):
-        peak_ref[copy] = peak
+    peak_ref[...] = jnp.max(peak, axis=0, keepdims=True)
 
 
 def shifted(value, side):
@@ -219,8 +217,30 @@
     return lax.ppermute(value, axis, [((i + step) % count, i) for i in range(count)])
 
 
-def all_max(copies, axis):
-    return jnp.max(lax.all_to_all(copies, axis, 0, 0, tiled=True), axis=0)
+def tree(count, fan):
+    nodes, levels = list(range(count)), []
+    while len(nodes) > 1:
+        groups = [nodes[i : i + fan] for i in range(0, len(nodes), fan)]
+        nodes = [group[min(2, len(group) - 1)] for group in groups]
+        members = [[node for node in group if node != hub] for group, hub in zip(groups, nodes)]
+        levels.append(
+            [
+                [(group[k], hub) for group, hub in zip(members, nodes) if k < len(group)]
+                for k in range(max(map(len, members)))
+            ]
+        )
+    return levels
+
+
+def all_max(row):
+    axes = ("gx", "gy")
+    levels = tree(lax.axis_size(axes), 6)
+    for level in levels:
+        row = functools.reduce(jnp.maximum, [lax.ppermute(row, axes, pairs) for pairs in level], row)
+    for level in reversed(levels):
+        arrived = [lax.ppermute(row, axes, [(hub, member) for member, hub in pairs]) for pairs in level]
+        row = functools.reduce(jnp.maximum, arrived, row)
+    return row
 
 
 def body(density0, energy0, x_velocity, y_velocity, z_velocity, time_increment):
@@ -259,7 +279,7 @@
     corners = [shifted(corner, (0, side_y)) for corner, side_y in zip(corners, (-1, 1))]
     *outs, peak = pl.pallas_call(
         functools.partial(step_kernel, nx, ny),
-        out_shape=[array(nx, ny)] * 5 + [array(lax.axis_size("gy"), 1)],
+        out_shape=[array(nx, ny)] * 5 + [array(1)],
         in_specs=[SMEM, SMEM] + [VMEM] * 7,
         out_specs=[VMEM] * 6,
         scratch_shapes=[
@@ -275,9 +295,7 @@
         compiler_params=limit(12),
         name="step",
     )(zero, time_increment.reshape(1), own, *edges, *corners)
-    peak = all_max(peak, "gy")
-    peak = all_max(jnp.broadcast_to(peak, (lax.axis_size("gx"), 1, nz)), "gx")
-    return (*outs, 0.3 / jnp.max(peak))
+    return (*outs, 0.3 / jnp.max(all_max(peak)))
 
 
 def solution(mesh):

time: 38.1 us -> 61.4 us (1.61)
  waiting for transfers between devices: 2.98 us -> 24.5 us
  starting transfers between devices: 9.66 us -> 28.8 us
  blocking collectives: 17.8 us -> 0 us
    ppermute x0 -> x20, waiting for transfers between devices: none -> 21.5 us  [the longest x10 20.2 us: all_max(): lax.ppermute(row, axes, [(hub, member) for member, hub in pairs])]
    ppermute x0 -> x20, starting transfers between devices: none -> 19.1 us  [the longest x10 11.8 us: all_max(): lax.ppermute(row, axes, pairs)]
    all_to_all x2 -> x0, blocking collectives: 17.8 us -> none  [all_max(): return jnp.max(lax.all_to_all(copies, axis, 0, 0, tiled=True), axis=0)]
  transfers between devices with their start and end apart: 6 -> 26, of which waited for: 3 -> 5; matrix products, arithmetic and copies ran while one was open for 0% -> 0% of each run, Pallas kernels for 0% -> 0%
where the time goes in v5:
time: 61.4 us; the launch traced here: 60.9 us
  starting transfers between devices  28.8 us (47%)
  waiting for transfers between devices  24.5 us (40%)
  Pallas kernels  3.61 us (6%)
  between operations  3.46 us (6%)
  other arithmetic  0.63 us (1%)
    ppermute x10, waiting for transfers between devices, all_max(): lax.ppermute(row, axes, [(hub, member) for member, hub in pairs])  20.2 us
    ppermute x10, starting transfers between devices, all_max(): lax.ppermute(row, axes, pairs)  11.8 us
    ppermute x6, starting transfers between devices, shifted(): lax.ppermute(value, axis, [((i + step) % count, i) for i in range(count)])  9.66 us
    ppermute x10, starting transfers between devices, all_max(): lax.ppermute(row, axes, [(hub, member) for member, hub in pairs])  7.25 us
    ppermute x6, waiting for transfers between devices, shifted(): lax.ppermute(value, axis, [((i + step) % count, i) for i in range(count)])  2.98 us
    pallas_call x1, Pallas kernels, body(): pl.pallas_call(functools.partial(step_kernel, nx, ny), out_shape=[array(n...  2.5 us
    ppermute x10, waiting for transfers between devices, all_max(): lax.ppermute(row, axes, pairs)  1.26 us
  transfers between devices with their start and end apart: 26, of which 5 were waited for; matrix products, arithmetic and copies ran while one was open for 0% of the time, Pallas kernels for 0%

profile of v5, /device:TPU:0, one launch (start us, length us, event | category | flops | bytes accessed | tf_op | source)
XLA Modules:
  0.0 60.9 jit_solution(2563720279635658096)
XLA Ops:
  0.6 1.1 %pack.1 = (f32[5,12,12,128]{3,2,1,0:T(8,128)S(1)}, f32[192,128]{1,0:T(8,128)S(1)}, f32[192,128]{1,0:T(8,128)S(1)}, f32[192,128]{1,0:T(8,128)S(1)}, f32[192,128]{1,0:T(8,128)S(1)}) custom-call(s32[1]{0:T(128)} %constant.0.clone.1.zero_ref, f32[12,12,128]{2,1,0:T(8,128)} %refs_0_.1, f32[12,12,128]{2,1,0:T(8,128)} %refs_1_.1, f32[12,12,128]{2,1,0:T(8,128)} %refs_2_.1, ...), custom_call_target="tpu_custom_call" | custom-call | tf_op jit(solution)/shard_map/pack/pallas_call | solution.py:261
  1.7 3.0 %collective-permute-start = (f32[192,128]{1,0:T(8,128)S(1)}, f32[192,128]{1,0:T(8,128)S(1)}, u32[]{:S(2)}, u32[]{:S(2)}) collective-permute-start(f32[192,128]{1,0:T(8,128)S(1)} %get-tuple-element.20), channel_id=1, source_target_pairs={{28,0},{0,4},{4,8},{8,12},{12,16},{16,20},{20,24},{24,28},{29,1},{... | collective-permute-start | bytes 294920 | tf_op jit(solution)/shard_map/ppermute | solution.py:217
  4.7 3.1 %collective-permute-start.1 = (f32[192,128]{1,0:T(8,128)S(1)}, f32[192,128]{1,0:T(8,128)S(1)}, u32[]{:S(2)}, u32[]{:S(2)}) collective-permute-start(f32[192,128]{1,0:T(8,128)S(1)} %get-tuple-element.21), channel_id=1, source_target_pairs={{4,0},{8,4},{12,8},{16,12},{20,16},{24,20},{28,24},{0,28},{5,1},{9... | collective-permute-start | bytes 294920 | tf_op jit(solution)/shard_map/ppermute | solution.py:217
  7.8 0.0 collective-permute-start.2
  7.9 1.7 %collective-permute-start.3 = (f32[192,128]{1,0:T(8,128)S(1)}, f32[192,128]{1,0:T(8,128)S(1)}, u32[]{:S(2)}, u32[]{:S(2)}) collective-permute-start(f32[192,128]{1,0:T(8,128)S(1)} %get-tuple-element.23), channel_id=1, source_target_pairs={{1,0},{2,1},{3,2},{0,3},{5,4},{6,5},{7,6},{4,7},{9,8},{10,9},{11,1... | collective-permute-start | bytes 294920 | tf_op jit(solution)/shard_map/ppermute | solution.py:217
  9.6 1.1 %collective-permute-done.below_ref.refs_1_ = f32[192,128]{1,0:T(8,128)S(1)} collective-permute-done((f32[192,128]{1,0:T(8,128)S(1)}, f32[192,128]{1,0:T(8,128)S(1)}, u32[]{:S(2)}, u32[]{:S(2)}) %collective-permute-start) | collective-permute-done | bytes 98336 | tf_op jit(solution)/shard_map/ppermute | solution.py:217
  10.7 0.8 %collective-permute-done.1.above_ref.refs_2_ = f32[192,128]{1,0:T(8,128)S(1)} collective-permute-done((f32[192,128]{1,0:T(8,128)S(1)}, f32[192,128]{1,0:T(8,128)S(1)}, u32[]{:S(2)}, u32[]{:S(2)}) %collective-permute-start.1) | collective-permute-done | bytes 98336 | tf_op jit(solution)/shard_map/ppermute | solution.py:217
  11.5 0.1 collective-permute-start.4
  11.6 1.7 %collective-permute-start.5 = (f32[96,128]{1,0:T(8,128)S(1)}, f32[96,128]{1,0:T(8,128)S(1)}, u32[]{:S(2)}, u32[]{:S(2)}) collective-permute-start(f32[96,128]{1,0:T(8,128)S(1)} %get-tuple-element.25), channel_id=1, source_target_pairs={{1,0},{2,1},{3,2},{0,3},{5,4},{6,5},{7,6},{4,7},{9,8},{10,9},{11,1... | collective-permute-start | bytes 147464 | tf_op jit(solution)/shard_map/ppermute | solution.py:217
  13.9 0.0 collective-permute-done.2.refs_3_
  14.0 0.0 collective-permute-done.3.refs_4_
  14.0 1.1 %collective-permute-done.4.refs_5_ = f32[96,128]{1,0:T(8,128)S(1)} collective-permute-done((f32[96,128]{1,0:T(8,128)S(1)}, f32[96,128]{1,0:T(8,128)S(1)}, u32[]{:S(2)}, u32[]{:S(2)}) %collective-permute-start.4) | collective-permute-done | bytes 49184 | tf_op jit(solution)/shard_map/ppermute | solution.py:217
  15.1 0.0 collective-permute-done.5.refs_6_
  15.1 2.5 %step.1 = (f32[12,12,128]{2,1,0:T(8,128)}, f32[12,12,128]{2,1,0:T(8,128)}, f32[12,12,128]{2,1,0:T(8,128)}, f32[12,12,128]{2,1,0:T(8,128)}, f32[12,12,128]{2,1,0:T(8,128)}, /*index=5*/f32[1,128]{1,0:T(1,128)S(1)}) custom-call(s32[1]{0:T(128)} %constant.0.clone.1.zero_ref, f32[1]{0:T(128)} %bitcast.1.dt_ref, f32[5,12,12,128]{3,2,1,0:T(8,128)S(1)} %get-tuple-element.19.refs_0_, ...), custom_call_target="tpu_custom_call" | custom-call | tf_op jit(solution)/shard_map/step/pallas_call | solution.py:280
  17.6 0.7 %collective-permute-start.10 = (f32[1,128]{1,0:T(1,128)S(1)}, f32[1,128]{1,0:T(1,128)S(1)}, u32[]{:S(2)}, u32[]{:S(2)}) collective-permute-start(f32[1,128]{1,0:T(1,128)S(1)} %get-tuple-element.31), channel_id=1, source_target_pairs={{5,2},{11,8},{17,14},{23,20},{29,26}} | collective-permute-start | bytes 1544 | tf_op jit(solution)/shard_map/ppermute | solution.py:239
  18.2 0.7 %collective-permute-start.9 = (f32[1,128]{1,0:T(1,128)S(1)}, f32[1,128]{1,0:T(1,128)S(1)}, u32[]{:S(2)}, u32[]{:S(2)}) collective-permute-start(f32[1,128]{1,0:T(1,128)S(1)} %get-tuple-element.31), channel_id=1, source_target_pairs={{4,2},{10,8},{16,14},{22,20},{28,26}} | collective-permute-start | bytes 1544 | tf_op jit(solution)/shard_map/ppermute | solution.py:239
  18.9 0.7 %collective-permute-start.8 = (f32[1,128]{1,0:T(1,128)S(1)}, f32[1,128]{1,0:T(1,128)S(1)}, u32[]{:S(2)}, u32[]{:S(2)}) collective-permute-start(f32[1,128]{1,0:T(1,128)S(1)} %get-tuple-element.31), channel_id=1, source_target_pairs={{3,2},{9,8},{15,14},{21,20},{27,26}} | collective-permute-start | bytes 1544 | tf_op jit(solution)/shard_map/ppermute | solution.py:239
  19.6 0.7 %collective-permute-start.7 = (f32[1,128]{1,0:T(1,128)S(1)}, f32[1,128]{1,0:T(1,128)S(1)}, u32[]{:S(2)}, u32[]{:S(2)}) collective-permute-start(f32[1,128]{1,0:T(1,128)S(1)} %get-tuple-element.31), channel_id=1, source_target_pairs={{1,2},{7,8},{13,14},{19,20},{25,26}} | collective-permute-start | bytes 1544 | tf_op jit(solution)/shard_map/ppermute | solution.py:239
  20.2 5.9 %collective-permute-start.6 = (f32[1,128]{1,0:T(1,128)S(1)}, f32[1,128]{1,0:T(1,128)S(1)}, u32[]{:S(2)}, u32[]{:S(2)}) collective-permute-start(f32[1,128]{1,0:T(1,128)S(1)} %get-tuple-element.31), channel_id=1, source_target_pairs={{0,2},{6,8},{12,14},{18,20},{24,26},{30,31}} | collective-permute-start | bytes 1544 | tf_op jit(solution)/shard_map/ppermute | solution.py:239
  26.2 0.0 collective-permute-done.10
  26.2 0.0 collective-permute-done.9
  26.2 0.0 collective-permute-done.8
  26.2 0.0 collective-permute-done.7
  26.2 1.2 %collective-permute-done.6 = f32[1,128]{1,0:T(1,128)S(1)} collective-permute-done((f32[1,128]{1,0:T(1,128)S(1)}, f32[1,128]{1,0:T(1,128)S(1)}, u32[]{:S(2)}, u32[]{:S(2)}) %collective-permute-start.6) | collective-permute-done | bytes 544 | tf_op jit(solution)/shard_map/ppermute | solution.py:239
  27.4 0.6 %collective-permute-start.15 = (f32[1,128]{1,0:T(1,128)S(1)}, f32[1,128]{1,0:T(1,128)S(1)}, u32[]{:S(2)}, u32[]{:S(2)}) collective-permute-start(f32[1,128]{1,0:T(1,128)S(1)} %maximum_maximum_fusion.2), channel_id=1, source_target_pairs={{31,14}} | collective-permute-start | bytes 1544 | tf_op jit(solution)/shard_map/ppermute | solution.py:239
  28.1 0.7 %collective-permute-start.14 = (f32[1,128]{1,0:T(1,128)S(1)}, f32[1,128]{1,0:T(1,128)S(1)}, u32[]{:S(2)}, u32[]{:S(2)}) collective-permute-start(f32[1,128]{1,0:T(1,128)S(1)} %maximum_maximum_fusion.2), channel_id=1, source_target_pairs={{26,14}} | collective-permute-start | bytes 1544 | tf_op jit(solution)/shard_map/ppermute | solution.py:239
  28.8 0.7 %collective-permute-start.13 = (f32[1,128]{1,0:T(1,128)S(1)}, f32[1,128]{1,0:T(1,128)S(1)}, u32[]{:S(2)}, u32[]{:S(2)}) collective-permute-start(f32[1,128]{1,0:T(1,128)S(1)} %maximum_maximum_fusion.2), channel_id=1, source_target_pairs={{20,14}} | collective-permute-start | bytes 1544 | tf_op jit(solution)/shard_map/ppermute | solution.py:239
  29.4 0.7 %collective-permute-start.12 = (f32[1,128]{1,0:T(1,128)S(1)}, f32[1,128]{1,0:T(1,128)S(1)}, u32[]{:S(2)}, u32[]{:S(2)}) collective-permute-start(f32[1,128]{1,0:T(1,128)S(1)} %maximum_maximum_fusion.2), channel_id=1, source_target_pairs={{8,14}} | collective-permute-start | bytes 1544 | tf_op jit(solution)/shard_map/ppermute | solution.py:239
  30.1 0.7 %collective-permute-start.11 = (f32[1,128]{1,0:T(1,128)S(1)}, f32[1,128]{1,0:T(1,128)S(1)}, u32[]{:S(2)}, u32[]{:S(2)}) collective-permute-start(f32[1,128]{1,0:T(1,128)S(1)} %maximum_maximum_fusion.2), channel_id=1, source_target_pairs={{2,14}} | collective-permute-start | bytes 1544 | tf_op jit(solution)/shard_map/ppermute | solution.py:239
  30.8 0.0 collective-permute-done.15
  30.8 0.0 collective-permute-done.14
  30.8 0.0 collective-permute-done.13
  30.8 0.0 collective-permute-done.12
  30.8 0.0 collective-permute-done.11
  30.9 0.7 %collective-permute-start.20 = (f32[1,128]{1,0:T(1,128)S(1)}, f32[1,128]{1,0:T(1,128)S(1)}, u32[]{:S(2)}, u32[]{:S(2)}) collective-permute-start(f32[1,128]{1,0:T(1,128)S(1)} %maximum_maximum_fusion.1), channel_id=1, source_target_pairs={{14,31}} | collective-permute-start | bytes 1544 | tf_op jit(solution)/shard_map/ppermute | solution.py:241
  31.5 0.7 %collective-permute-start.19 = (f32[1,128]{1,0:T(1,128)S(1)}, f32[1,128]{1,0:T(1,128)S(1)}, u32[]{:S(2)}, u32[]{:S(2)}) collective-permute-start(f32[1,128]{1,0:T(1,128)S(1)} %maximum_maximum_fusion.1), channel_id=1, source_target_pairs={{14,26}} | collective-permute-start | bytes 1544 | tf_op jit(solution)/shard_map/ppermute | solution.py:241
  32.2 0.7 %collective-permute-start.18 = (f32[1,128]{1,0:T(1,128)S(1)}, f32[1,128]{1,0:T(1,128)S(1)}, u32[]{:S(2)}, u32[]{:S(2)}) collective-permute-start(f32[1,128]{1,0:T(1,128)S(1)} %maximum_maximum_fusion.1), channel_id=1, source_target_pairs={{14,20}} | collective-permute-start | bytes 1544 | tf_op jit(solution)/shard_map/ppermute | solution.py:241
  32.9 0.7 %collective-permute-start.17 = (f32[1,128]{1,0:T(1,128)S(1)}, f32[1,128]{1,0:T(1,128)S(1)}, u32[]{:S(2)}, u32[]{:S(2)}) collective-permute-start(f32[1,128]{1,0:T(1,128)S(1)} %maximum_maximum_fusion.1), channel_id=1, source_target_pairs={{14,8}} | collective-permute-start | bytes 1544 | tf_op jit(solution)/shard_map/ppermute | solution.py:241
  33.5 0.7 %collective-permute-start.16 = (f32[1,128]{1,0:T(1,128)S(1)}, f32[1,128]{1,0:T(1,128)S(1)}, u32[]{:S(2)}, u32[]{:S(2)}) collective-permute-start(f32[1,128]{1,0:T(1,128)S(1)} %maximum_maximum_fusion.1), channel_id=1, source_target_pairs={{14,2}} | collective-permute-start | bytes 1544 | tf_op jit(solution)/shard_map/ppermute | solution.py:241
  34.2 0.0 collective-permute-done.20
  34.2 0.0 collective-permute-done.19
  34.2 0.0 collective-permute-done.18
  34.2 0.0 collective-permute-done.17
  34.2 0.0 collective-permute-done.16
  34.3 0.7 %collective-permute-start.25 = (f32[1,128]{1,0:T(1,128)S(1)}, f32[1,128]{1,0:T(1,128)S(1)}, u32[]{:S(2)}, u32[]{:S(2)}) collective-permute-start(f32[1,128]{1,0:T(1,128)S(1)} %maximum_maximum_fusion), channel_id=1, source_target_pairs={{2,5},{8,11},{14,17},{20,23},{26,29}} | collective-permute-start | bytes 1544 | tf_op jit(solution)/shard_map/ppermute | solution.py:241
  34.9 0.7 %collective-permute-start.24 = (f32[1,128]{1,0:T(1,128)S(1)}, f32[1,128]{1,0:T(1,128)S(1)}, u32[]{:S(2)}, u32[]{:S(2)}) collective-permute-start(f32[1,128]{1,0:T(1,128)S(1)} %maximum_maximum_fusion), channel_id=1, source_target_pairs={{2,4},{8,10},{14,16},{20,22},{26,28}} | collective-permute-start | bytes 1544 | tf_op jit(solution)/shard_map/ppermute | solution.py:241
  35.6 0.7 %collective-permute-start.23 = (f32[1,128]{1,0:T(1,128)S(1)}, f32[1,128]{1,0:T(1,128)S(1)}, u32[]{:S(2)}, u32[]{:S(2)}) collective-permute-start(f32[1,128]{1,0:T(1,128)S(1)} %maximum_maximum_fusion), channel_id=1, source_target_pairs={{2,3},{8,9},{14,15},{20,21},{26,27}} | collective-permute-start | bytes 1544 | tf_op jit(solution)/shard_map/ppermute | solution.py:241
  36.3 0.7 %collective-permute-start.22 = (f32[1,128]{1,0:T(1,128)S(1)}, f32[1,128]{1,0:T(1,128)S(1)}, u32[]{:S(2)}, u32[]{:S(2)}) collective-permute-start(f32[1,128]{1,0:T(1,128)S(1)} %maximum_maximum_fusion), channel_id=1, source_target_pairs={{2,1},{8,7},{14,13},{20,19},{26,25}} | collective-permute-start | bytes 1544 | tf_op jit(solution)/shard_map/ppermute | solution.py:241
  36.9 1.3 %collective-permute-start.21 = (f32[1,128]{1,0:T(1,128)S(1)}, f32[1,128]{1,0:T(1,128)S(1)}, u32[]{:S(2)}, u32[]{:S(2)}) collective-permute-start(f32[1,128]{1,0:T(1,128)S(1)} %maximum_maximum_fusion), channel_id=1, source_target_pairs={{2,0},{8,6},{14,12},{20,18},{26,24},{31,30}} | collective-permute-start | bytes 1544 | tf_op jit(solution)/shard_map/ppermute | solution.py:241
  38.2 0.0 collective-permute-done.25
  38.3 0.0 collective-permute-done.24
  38.3 0.0 collective-permute-done.23
  38.3 0.0 collective-permute-done.22
  38.3 20.2 %collective-permute-done.21 = f32[1,128]{1,0:T(1,128)S(1)} collective-permute-done((f32[1,128]{1,0:T(1,128)S(1)}, f32[1,128]{1,0:T(1,128)S(1)}, u32[]{:S(2)}, u32[]{:S(2)}) %collective-permute-start.21) | collective-permute-done | bytes 544 | tf_op jit(solution)/shard_map/ppermute | solution.py:241
  58.5 0.6 maximum_reduce_fusion
  (4 shorter events, 0.1 us)
Async XLA Ops:
  1.7 9.0 %collective-permute-start = (f32[192,128]{1,0:T(8,128)S(1)}, f32[192,128]{1,0:T(8,128)S(1)}, u32[]{:S(2)}, u32[]{:S(2)}) collective-permute-start(f32[192,128]{1,0:T(8,128)S(1)} %get-tuple-element.20), channel_id=1, source_target_pairs={{28,0},{0,4},{4,8},{8,12},{12,16},{16,20},{20,24},{24,28},{29,1},{... | collective-permute-start | bytes 294920 | tf_op jit(solution)/shard_map/ppermute | solution.py:217
  4.7 6.7 %collective-permute-start.1 = (f32[192,128]{1,0:T(8,128)S(1)}, f32[192,128]{1,0:T(8,128)S(1)}, u32[]{:S(2)}, u32[]{:S(2)}) collective-permute-start(f32[192,128]{1,0:T(8,128)S(1)} %get-tuple-element.21), channel_id=1, source_target_pairs={{4,0},{8,4},{12,8},{16,12},{20,16},{24,20},{28,24},{0,28},{5,1},{9... | collective-permute-start | bytes 294920 | tf_op jit(solution)/shard_map/ppermute | solution.py:217
  7.8 6.1 %collective-permute-start.2 = (f32[192,128]{1,0:T(8,128)S(1)}, f32[192,128]{1,0:T(8,128)S(1)}, u32[]{:S(2)}, u32[]{:S(2)}) collective-permute-start(f32[192,128]{1,0:T(8,128)S(1)} %get-tuple-element.22), channel_id=1, source_target_pairs={{3,0},{0,1},{1,2},{2,3},{7,4},{4,5},{5,6},{6,7},{11,8},{8,9},{9,10... | collective-permute-start | bytes 294920 | tf_op jit(solution)/shard_map/ppermute | solution.py:217
  7.9 6.1 %collective-permute-start.3 = (f32[192,128]{1,0:T(8,128)S(1)}, f32[192,128]{1,0:T(8,128)S(1)}, u32[]{:S(2)}, u32[]{:S(2)}) collective-permute-start(f32[192,128]{1,0:T(8,128)S(1)} %get-tuple-element.23), channel_id=1, source_target_pairs={{1,0},{2,1},{3,2},{0,3},{5,4},{6,5},{7,6},{4,7},{9,8},{10,9},{11,1... | collective-permute-start | bytes 294920 | tf_op jit(solution)/shard_map/ppermute | solution.py:217
  11.5 3.6 %collective-permute-start.4 = (f32[96,128]{1,0:T(8,128)S(1)}, f32[96,128]{1,0:T(8,128)S(1)}, u32[]{:S(2)}, u32[]{:S(2)}) collective-permute-start(f32[96,128]{1,0:T(8,128)S(1)} %get-tuple-element.24), channel_id=1, source_target_pairs={{3,0},{0,1},{1,2},{2,3},{7,4},{4,5},{5,6},{6,7},{11,8},{8,9},{9,10... | collective-permute-start | bytes 147464 | tf_op jit(solution)/shard_map/ppermute | solution.py:217
  11.6 3.5 %collective-permute-start.5 = (f32[96,128]{1,0:T(8,128)S(1)}, f32[96,128]{1,0:T(8,128)S(1)}, u32[]{:S(2)}, u32[]{:S(2)}) collective-permute-start(f32[96,128]{1,0:T(8,128)S(1)} %get-tuple-element.25), channel_id=1, source_target_pairs={{1,0},{2,1},{3,2},{0,3},{5,4},{6,5},{7,6},{4,7},{9,8},{10,9},{11,1... | collective-permute-start | bytes 147464 | tf_op jit(solution)/shard_map/ppermute | solution.py:217
  17.6 8.6 %collective-permute-start.10 = (f32[1,128]{1,0:T(1,128)S(1)}, f32[1,128]{1,0:T(1,128)S(1)}, u32[]{:S(2)}, u32[]{:S(2)}) collective-permute-start(f32[1,128]{1,0:T(1,128)S(1)} %get-tuple-element.31), channel_id=1, source_target_pairs={{5,2},{11,8},{17,14},{23,20},{29,26}} | collective-permute-start | bytes 1544 | tf_op jit(solution)/shard_map/ppermute | solution.py:239
  18.2 7.9 %collective-permute-start.9 = (f32[1,128]{1,0:T(1,128)S(1)}, f32[1,128]{1,0:T(1,128)S(1)}, u32[]{:S(2)}, u32[]{:S(2)}) collective-permute-start(f32[1,128]{1,0:T(1,128)S(1)} %get-tuple-element.31), channel_id=1, source_target_pairs={{4,2},{10,8},{16,14},{22,20},{28,26}} | collective-permute-start | bytes 1544 | tf_op jit(solution)/shard_map/ppermute | solution.py:239
  18.9 7.3 %collective-permute-start.8 = (f32[1,128]{1,0:T(1,128)S(1)}, f32[1,128]{1,0:T(1,128)S(1)}, u32[]{:S(2)}, u32[]{:S(2)}) collective-permute-start(f32[1,128]{1,0:T(1,128)S(1)} %get-tuple-element.31), channel_id=1, source_target_pairs={{3,2},{9,8},{15,14},{21,20},{27,26}} | collective-permute-start | bytes 1544 | tf_op jit(solution)/shard_map/ppermute | solution.py:239
  19.6 6.6 %collective-permute-start.7 = (f32[1,128]{1,0:T(1,128)S(1)}, f32[1,128]{1,0:T(1,128)S(1)}, u32[]{:S(2)}, u32[]{:S(2)}) collective-permute-start(f32[1,128]{1,0:T(1,128)S(1)} %get-tuple-element.31), channel_id=1, source_target_pairs={{1,2},{7,8},{13,14},{19,20},{25,26}} | collective-permute-start | bytes 1544 | tf_op jit(solution)/shard_map/ppermute | solution.py:239
  20.2 7.2 %collective-permute-start.6 = (f32[1,128]{1,0:T(1,128)S(1)}, f32[1,128]{1,0:T(1,128)S(1)}, u32[]{:S(2)}, u32[]{:S(2)}) collective-permute-start(f32[1,128]{1,0:T(1,128)S(1)} %get-tuple-element.31), channel_id=1, source_target_pairs={{0,2},{6,8},{12,14},{18,20},{24,26},{30,31}} | collective-permute-start | bytes 1544 | tf_op jit(solution)/shard_map/ppermute | solution.py:239
  27.4 3.3 %collective-permute-start.15 = (f32[1,128]{1,0:T(1,128)S(1)}, f32[1,128]{1,0:T(1,128)S(1)}, u32[]{:S(2)}, u32[]{:S(2)}) collective-permute-start(f32[1,128]{1,0:T(1,128)S(1)} %maximum_maximum_fusion.2), channel_id=1, source_target_pairs={{31,14}} | collective-permute-start | bytes 1544 | tf_op jit(solution)/shard_map/ppermute | solution.py:239
  28.1 2.7 %collective-permute-start.14 = (f32[1,128]{1,0:T(1,128)S(1)}, f32[1,128]{1,0:T(1,128)S(1)}, u32[]{:S(2)}, u32[]{:S(2)}) collective-permute-start(f32[1,128]{1,0:T(1,128)S(1)} %maximum_maximum_fusion.2), channel_id=1, source_target_pairs={{26,14}} | collective-permute-start | bytes 1544 | tf_op jit(solution)/shard_map/ppermute | solution.py:239
  28.8 2.0 %collective-permute-start.13 = (f32[1,128]{1,0:T(1,128)S(1)}, f32[1,128]{1,0:T(1,128)S(1)}, u32[]{:S(2)}, u32[]{:S(2)}) collective-permute-start(f32[1,128]{1,0:T(1,128)S(1)} %maximum_maximum_fusion.2), channel_id=1, source_target_pairs={{20,14}} | collective-permute-start | bytes 1544 | tf_op jit(solution)/shard_map/ppermute | solution.py:239
  29.4 1.4 %collective-permute-start.12 = (f32[1,128]{1,0:T(1,128)S(1)}, f32[1,128]{1,0:T(1,128)S(1)}, u32[]{:S(2)}, u32[]{:S(2)}) collective-permute-start(f32[1,128]{1,0:T(1,128)S(1)} %maximum_maximum_fusion.2), channel_id=1, source_target_pairs={{8,14}} | collective-permute-start | bytes 1544 | tf_op jit(solution)/shard_map/ppermute | solution.py:239
  30.1 0.7 %collective-permute-start.11 = (f32[1,128]{1,0:T(1,128)S(1)}, f32[1,128]{1,0:T(1,128)S(1)}, u32[]{:S(2)}, u32[]{:S(2)}) collective-permute-start(f32[1,128]{1,0:T(1,128)S(1)} %maximum_maximum_fusion.2), channel_id=1, source_target_pairs={{2,14}} | collective-permute-start | bytes 1544 | tf_op jit(solution)/shard_map/ppermute | solution.py:239
  30.9 3.4 %collective-permute-start.20 = (f32[1,128]{1,0:T(1,128)S(1)}, f32[1,128]{1,0:T(1,128)S(1)}, u32[]{:S(2)}, u32[]{:S(2)}) collective-permute-start(f32[1,128]{1,0:T(1,128)S(1)} %maximum_maximum_fusion.1), channel_id=1, source_target_pairs={{14,31}} | collective-permute-start | bytes 1544 | tf_op jit(solution)/shard_map/ppermute | solution.py:241
  31.5 2.7 %collective-permute-start.19 = (f32[1,128]{1,0:T(1,128)S(1)}, f32[1,128]{1,0:T(1,128)S(1)}, u32[]{:S(2)}, u32[]{:S(2)}) collective-permute-start(f32[1,128]{1,0:T(1,128)S(1)} %maximum_maximum_fusion.1), channel_id=1, source_target_pairs={{14,26}} | collective-permute-start | bytes 1544 | tf_op jit(solution)/shard_map/ppermute | solution.py:241
  32.2 2.0 %collective-permute-start.18 = (f32[1,128]{1,0:T(1,128)S(1)}, f32[1,128]{1,0:T(1,128)S(1)}, u32[]{:S(2)}, u32[]{:S(2)}) collective-permute-start(f32[1,128]{1,0:T(1,128)S(1)} %maximum_maximum_fusion.1), channel_id=1, source_target_pairs={{14,20}} | collective-permute-start | bytes 1544 | tf_op jit(solution)/shard_map/ppermute | solution.py:241
  32.9 1.4 %collective-permute-start.17 = (f32[1,128]{1,0:T(1,128)S(1)}, f32[1,128]{1,0:T(1,128)S(1)}, u32[]{:S(2)}, u32[]{:S(2)}) collective-permute-start(f32[1,128]{1,0:T(1,128)S(1)} %maximum_maximum_fusion.1), channel_id=1, source_target_pairs={{14,8}} | collective-permute-start | bytes 1544 | tf_op jit(solution)/shard_map/ppermute | solution.py:241
  33.5 0.7 %collective-permute-start.16 = (f32[1,128]{1,0:T(1,128)S(1)}, f32[1,128]{1,0:T(1,128)S(1)}, u32[]{:S(2)}, u32[]{:S(2)}) collective-permute-start(f32[1,128]{1,0:T(1,128)S(1)} %maximum_maximum_fusion.1), channel_id=1, source_target_pairs={{14,2}} | collective-permute-start | bytes 1544 | tf_op jit(solution)/shard_map/ppermute | solution.py:241
  34.3 4.0 %collective-permute-start.25 = (f32[1,128]{1,0:T(1,128)S(1)}, f32[1,128]{1,0:T(1,128)S(1)}, u32[]{:S(2)}, u32[]{:S(2)}) collective-permute-start(f32[1,128]{1,0:T(1,128)S(1)} %maximum_maximum_fusion), channel_id=1, source_target_pairs={{2,5},{8,11},{14,17},{20,23},{26,29}} | collective-permute-start | bytes 1544 | tf_op jit(solution)/shard_map/ppermute | solution.py:241
  34.9 3.3 %collective-permute-start.24 = (f32[1,128]{1,0:T(1,128)S(1)}, f32[1,128]{1,0:T(1,128)S(1)}, u32[]{:S(2)}, u32[]{:S(2)}) collective-permute-start(f32[1,128]{1,0:T(1,128)S(1)} %maximum_maximum_fusion), channel_id=1, source_target_pairs={{2,4},{8,10},{14,16},{20,22},{26,28}} | collective-permute-start | bytes 1544 | tf_op jit(solution)/shard_map/ppermute | solution.py:241
  35.6 2.7 %collective-permute-start.23 = (f32[1,128]{1,0:T(1,128)S(1)}, f32[1,128]{1,0:T(1,128)S(1)}, u32[]{:S(2)}, u32[]{:S(2)}) collective-permute-start(f32[1,128]{1,0:T(1,128)S(1)} %maximum_maximum_fusion), channel_id=1, source_target_pairs={{2,3},{8,9},{14,15},{20,21},{26,27}} | collective-permute-start | bytes 1544 | tf_op jit(solution)/shard_map/ppermute | solution.py:241
  36.3 2.0 %collective-permute-start.22 = (f32[1,128]{1,0:T(1,128)S(1)}, f32[1,128]{1,0:T(1,128)S(1)}, u32[]{:S(2)}, u32[]{:S(2)}) collective-permute-start(f32[1,128]{1,0:T(1,128)S(1)} %maximum_maximum_fusion), channel_id=1, source_target_pairs={{2,1},{8,7},{14,13},{20,19},{26,25}} | collective-permute-start | bytes 1544 | tf_op jit(solution)/shard_map/ppermute | solution.py:241
  36.9 21.6 %collective-permute-start.21 = (f32[1,128]{1,0:T(1,128)S(1)}, f32[1,128]{1,0:T(1,128)S(1)}, u32[]{:S(2)}, u32[]{:S(2)}) collective-permute-start(f32[1,128]{1,0:T(1,128)S(1)} %maximum_maximum_fusion), channel_id=1, source_target_pairs={{2,0},{8,6},{14,12},{20,18},{26,24},{31,30}} | collective-permute-start | bytes 1544 | tf_op jit(solution)/shard_map/ppermute | solution.py:241

commit v6 on v4

--- a/solution.py
+++ b/solution.py
@@ -94,9 +94,65 @@
     return courant * jnp.where(upward, f_minus, f) + slope_factor * jnp.where(upward, s_minus, s)
 
 
+def up(value):
+    return pltpu.roll(value, value.shape[-1] - 1, value.ndim - 1)
+
+
+def down(value):
+    return pltpu.roll(value, 1, value.ndim - 1)
+
+
+def sweep_x(state, speed, swept, fields, half):
+    for part in range(0, state.shape[2], 8):
+        rows = pl.ds(part, 8)
+        before = [state[field, 1, rows] for field in fields]
+        here = [state[field, 2, rows] for field in fields]
+        steps = [h - b for h, b in zip(here, before)]
+        slopes = [limited(st, b - state[field, 0, rows]) for field, st, b in zip(fields, steps, before)]
+        lower = None
+        for a in range(swept.shape[1] + 1):
+            factors = face_factors(speed[a + 1, rows], speed[a + 2, rows], half)
+            fluxes = []
+            for k, field in enumerate(fields):
+                after = state[field, a + 3, rows]
+                step = after - here[k]
+                slope = limited(step, steps[k])
+                fluxes.append(face_flux(factors, before[k], here[k], slopes[k], slope))
+                if lower is not None:
+                    swept[field, a - 1, rows] = before[k] - (fluxes[k] - lower[k])
+                before[k], here[k], steps[k], slopes[k] = here[k], after, step, slope
+            lower = fluxes
+
+
+def sweep_y(zero, swept, work, a, fields, factors, wide):
+    moved = []
+    for field in fields:
+        below = swept[field, a, pl.ds(zero + 1, wide)]
+        here = swept[field, a, pl.ds(zero + 2, wide)]
+        slope = limited(here - below, below - swept[field, a, 0:wide])
+        work[0, field, a, 0:wide] = slope
+        flux = face_flux(factors, below, here, slope, work[0, field, a, pl.ds(zero + 1, wide)])
+        work[1, field, a, 0:wide] = flux
+        moved.append(here - (work[1, field, a, pl.ds(zero + 1, wide)] - flux))
+    return moved
+
+
+def sweep_z(moved, factors):
+    final = []
+    for value in moved:
+        below = down(value)
+        step = value - below
+        slope = limited(up(step), step)
+        flux = face_flux(factors, below, value, down(slope), slope)
+        final.append(value - (up(flux) - flux))
+    return final
+
+
 def step_kernel(nx, ny, zero_ref, dt_ref, *refs):
-    own, halos, outs, peak_ref = refs[0], refs[1:7], refs[7:12], refs[12]
+    own, halos = refs[0], refs[1:7]
+    passive, speed, speed_y, speed_z, flows, peak_ref = refs[7:13]
     cells, stress, growth, heat, state, energy_one, swept, work = refs[13:]
+    nz = own.shape[-1]
     zero = zero_ref[0]
     dt = dt_ref[0]
     half = 0.5 * dt
@@ -115,12 +171,6 @@
 
     def at(ref, *index, start, count):
         return ref[(*index, pl.ds(zero + start, count), slice(None))]
-
-    def up(value):
-        return pltpu.roll(value, value.shape[-1] - 1, value.ndim - 1)
-
-    def down(value):
-        return pltpu.roll(value, 1, value.ndim - 1)
 
     for a in range(-3, nx + 3):
         get = functools.partial(at, cells, start=TOP - 4, count=tall)
@@ -145,82 +195,68 @@
         scale = half / density
         density_one = density / (1.0 + grown)
         energy = get(ENERGY, a + REACH) - at(heat, a + 2, start=2, count=wide) * grown
-        state[DENSITY, a + 2] = density_one
-        state[ENERGY, a + 2] = density_one * energy
-        state[XV, a + 2] = get(XV, a + REACH) - scale * (
+        passive[0, a + 2] = density_one
+        passive[1, a + 2] = density_one * energy
+        x_one = get(XV, a + REACH) - scale * (
             at(stress, a + 4, start=2, count=wide) - at(stress, a + 2, start=2, count=wide)
         )
-        state[YV, a + 2] = get(YV, a + REACH) - scale * (
+        state[0, a + 2] = x_one
+        speed[a + 2] = x_one
+        state[1, a + 2] = get(YV, a + REACH) - scale * (
             at(stress, a + 3, start=3, count=wide) - at(stress, a + 3, start=1, count=wide)
         )
-        state[ZV, a + 2] = get(ZV, a + REACH) - scale * (up(centre) - down(centre))
+        state[2, a + 2] = get(ZV, a + REACH) - scale * (up(centre) - down(centre))
         if 0 <= a < nx:
             energy_one[a, 0:wide] = energy
 
-    for part in range(0, wide, 8):
-        rows = pl.ds(part, 8)
-        before = [state[field, 1, rows] for field in range(5)]
-        here = [state[field, 2, rows] for field in range(5)]
-        steps = [h - b for h, b in zip(here, before)]
-        slopes = [limited(st, b - state[field, 0, rows]) for field, (st, b) in enumerate(zip(steps, before))]
-        lower = None
-        for a in range(nx + 1):
-            factors = face_factors(before[XV], here[XV], half)
-            fluxes = []
-            for field in range(5):
-                after = state[field, a + 3, rows]
-                step = after - here[field]
-                slope = limited(step, steps[field])
-                fluxes.append(face_flux(factors, before[field], here[field], slopes[field], slope))
-                if lower is not None:
-                    swept[field, a - 1, rows] = before[field] - (fluxes[field] - lower[field])
-                before[field], here[field], steps[field], slopes[field] = here[field], after, step, slope
-            lower = fluxes
-
-    peak = jnp.zeros((wide, swept.shape[-1]), jnp.float32)
+    sweep_x(state, speed, swept, (0, 1, 2), half)
     for a in range(nx):
-        below = [at(swept, field, a, start=1, count=wide) for field in range(5)]
-        here = [at(swept, field, a, start=2, count=wide) for field in range(5)]
-        factors = face_factors(below[YV], here[YV], half)
-        moved = []
-        for field in range(5):
-            step = below[field] - swept[field, a, 0:wide]
-            slope = limited(here[field] - below[field], step)
-            work[field, a, 0:wide] = slope
-            flux = face_flux(factors, below[field], here[field], slope, at(work, field, a, start=1, count=wide))
-            work[5 + field, a, 0:wide] = flux
-            moved.append(here[field] - (at(work, 5 + field, a, start=1, count=wide) - flux))
-        below = [down(value) for value in moved]
-        factors = face_factors(below[ZV], moved[ZV], half)
-        final = []
-        for field in range(5):
-            step = moved[field] - below[field]
-            slope = limited(up(step), step)
-            flux = face_flux(factors, below[field], moved[field], down(slope), slope)
-            final.append(moved[field] - (up(flux) - flux))
-            outs[field][a] = final[field][:ny]
+        speed_y[a, 0:wide] = swept[1, a, 0:wide]
+
+    peak = jnp.zeros((wide, nz), jnp.float32)
+    for a in range(nx):
+        below, here = at(swept, 1, a, start=1, count=wide), at(swept, 1, a, start=2, count=wide)
+        moved = sweep_y(zero, swept, work, a, (0, 1, 2), face_factors(below, here, half), wide)
+        speed_z[a] = moved[2]
+        final = sweep_z(moved, face_factors(down(moved[2]), moved[2], half))
+        for field in range(3):
+            flows[field, a] = final[field][:ny]
         peak = jnp.maximum(
             peak,
             jnp.sqrt(0.56 * at(energy_one, a, start=2, count=wide))
-            + jnp.abs(final[XV])
-            + jnp.abs(final[YV])
-            + jnp.abs(final[ZV]),
+            + jnp.abs(final[0])
+            + jnp.abs(final[1])
+            + jnp.abs(final[2]),
         )
     row = lax.broadcasted_iota(jnp.int32, peak.shape, 0)
-    peak = jnp.where(row < ny, peak, 0.0)
-    peak = jnp.max(peak, axis=0, keepdims=True)
-    for copy in range(peak_ref.shape[0]):
-        peak_ref[copy] = peak
+    peak = jnp.max(jnp.where(row < ny, peak, 0.0), axis=0, keepdims=True)
+    peak_ref[...] = jnp.broadcast_to(peak, peak_ref.shape)
+
+
+def carry_kernel(nx, ny, zero_ref, dt_ref, *refs):
+    state, speed, speed_y, speed_z, flows, density_out, energy_out = refs[:7]
+    flow_outs, swept, work, written = refs[7:10], refs[10], refs[11], refs[12]
+    zero = zero_ref[0]
+    half = 0.5 * dt_ref[0]
+    wide = ny + 4
+    copies = [pltpu.make_async_copy(flows.at[k], flow_outs[k], written.at[k]) for k in range(3)]
+    for copy in copies:
+        copy.start()
+    sweep_x(state, speed, swept, (0, 1), half)
+    for a in range(nx):
+        below, here = speed_y[a, pl.ds(zero + 1, wide)], speed_y[a, pl.ds(zero + 2, wide)]
+        moved = sweep_y(zero, swept, work, a, (0, 1), face_factors(below, here, half), wide)
+        final = sweep_z(moved, face_factors(down(speed_z[a]), speed_z[a], half))
+        density_out[a] = final[0][:ny]
+        energy_out[a] = final[1][:ny]
+    for copy in copies:
+        copy.wait()
 
 
 def shifted(value, side):
     axis, step = ("gx", side[0]) if side[0] else ("gy", side[1])
     count = lax.axis_size(axis)
     return lax.ppermute(value, axis, [((i + step) % count, i) for i in range(count)])
-
-
-def all_max(copies, axis):
-    return jnp.max(lax.all_to_all(copies, axis, 0, 0, tiled=True), axis=0)
 
 
 def body(density0, energy0, x_velocity, y_velocity, z_velocity, time_increment):
@@ -257,9 +293,12 @@
         name="corners",
     )(zero, edges[0], edges[1])
     corners = [shifted(corner, (0, side_y)) for corner, side_y in zip(corners, (-1, 1))]
-    *outs, peak = pl.pallas_call(
+    count = lax.axis_size(("gx", "gy"))
+    increment = time_increment.reshape(1)
+    passed = [array(2, nx + 4, wide), array(nx + 4, wide), array(nx, wide + 8), array(nx, wide), array(3, nx, ny)]
+    *passed, peak = pl.pallas_call(
         functools.partial(step_kernel, nx, ny),
-        out_shape=[array(nx, ny)] * 5 + [array(lax.axis_size("gy"), 1)],
+        out_shape=passed + [array(count)],
         in_specs=[SMEM, SMEM] + [VMEM] * 7,
         out_specs=[VMEM] * 6,
         scratch_shapes=[
@@ -267,16 +306,29 @@
             scratch(nx + 6, tall),
             scratch(nx + 4, tall),
             scratch(nx + 4, tall),
-            scratch(5, nx + 4, wide),
+            scratch(3, nx + 4, wide),
             scratch(nx, wide + 8),
-            scratch(5, nx, wide + 8),
-            scratch(10, nx, wide + 8),
+            scratch(3, nx, wide + 8),
+            scratch(2, 3, nx, wide + 8),
         ],
         compiler_params=limit(12),
         name="step",
-    )(zero, time_increment.reshape(1), own, *edges, *corners)
-    peak = all_max(peak, "gy")
-    peak = all_max(jnp.broadcast_to(peak, (lax.axis_size("gx"), 1, nz)), "gx")
+    )(zero, increment, own, *edges, *corners)
+    outs = pl.pallas_call(
+        functools.partial(carry_kernel, nx, ny),
+        out_shape=[array(nx, ny)] * 5,
+        in_specs=[SMEM, SMEM] + [VMEM] * 5,
+        out_specs=[VMEM] * 2 + [HBM] * 3,
+        scratch_shapes=[
+            scratch(2, nx, wide + 8),
+            scratch(2, 2, nx, wide + 8),
+            pltpu.SemaphoreType.DMA((3,)),
+        ],
+        compiler_params=limit(8),
+        cost_estimate=pl.CostEstimate(flops=10**7, bytes_accessed=4 * 10**6, transcendentals=0),
+        name="carry",
+    )(zero, increment, *passed)
+    peak = lax.all_to_all(peak, ("gx", "gy"), 0, 0, tiled=True)
     return (*outs, 0.3 / jnp.max(peak))
 
 

time: 38.1 us -> 32.2 us (0.85)
  blocking collectives: 17.8 us -> 0 us
  starting transfers between devices: 9.66 us -> 15 us
  waiting for transfers between devices: 2.98 us -> 8.08 us
  Pallas kernels: 3.61 us -> 5.04 us
    all_to_all x2 -> x0, blocking collectives: 17.8 us -> none  [all_max(): return jnp.max(lax.all_to_all(copies, axis, 0, 0, tiled=True), axis=0)]
    all_to_all x0 -> x1, starting transfers between devices: none -> 5.37 us  [body(): peak = lax.all_to_all(peak, ('gx', 'gy'), 0, 0, tiled=True)]
    all_to_all x0 -> x1, waiting for transfers between devices: none -> 5.1 us  [body(): peak = lax.all_to_all(peak, ('gx', 'gy'), 0, 0, tiled=True)]
    pallas_call x1 -> x2, Pallas kernels: 2.5 us -> 3.93 us  [the longest x1 2.03 us: body(): pl.pallas_call(functools.partial(carry_kernel, nx, ny), out_shape=[array(...]
  transfers between devices with their start and end apart: 6 -> 7, of which waited for: 3 -> 4; matrix products, arithmetic and copies ran while one was open for 0% -> 0% of each run, Pallas kernels for 0% -> 6%
where the time goes in v6:
time: 32.2 us; the launch traced here: 31.9 us
  starting transfers between devices  15 us (47%)
  waiting for transfers between devices  8.08 us (25%)
  Pallas kernels  5.04 us (16%)
  between operations  3.16 us (10%)
  other arithmetic  0.63 us (2%)
    ppermute x6, starting transfers between devices, shifted(): lax.ppermute(value, axis, [((i + step) % count, i) for i in range(count)])  9.66 us
    all_to_all x1, starting transfers between devices, body(): peak = lax.all_to_all(peak, ('gx', 'gy'), 0, 0, tiled=True)  5.37 us
    all_to_all x1, waiting for transfers between devices, body(): peak = lax.all_to_all(peak, ('gx', 'gy'), 0, 0, tiled=True)  5.1 us
    ppermute x6, waiting for transfers between devices, shifted(): lax.ppermute(value, axis, [((i + step) % count, i) for i in range(count)])  2.98 us
    pallas_call x1, Pallas kernels, body(): pl.pallas_call(functools.partial(carry_kernel, nx, ny), out_shape=[array(...  2.03 us
    pallas_call x1, Pallas kernels, body(): pl.pallas_call(functools.partial(step_kernel, nx, ny), out_shape=passed +...  1.9 us
    pallas_call x1, Pallas kernels, body(): pl.pallas_call(functools.partial(pack_kernel, nx, ny), out_shape=[array(5...  1.08 us
  transfers between devices with their start and end apart: 7, of which 4 were waited for; matrix products, arithmetic and copies ran while one was open for 0% of the time, Pallas kernels for 6%

profile of v6, /device:TPU:0, one launch (start us, length us, event | category | flops | bytes accessed | tf_op | source)
XLA Modules:
  0.0 31.9 jit_solution(9274591581061212333)
XLA Ops:
  0.6 1.1 %pack.1 = (f32[5,12,12,128]{3,2,1,0:T(8,128)S(1)}, f32[192,128]{1,0:T(8,128)S(1)}, f32[192,128]{1,0:T(8,128)S(1)}, f32[192,128]{1,0:T(8,128)S(1)}, f32[192,128]{1,0:T(8,128)S(1)}) custom-call(s32[1]{0:T(128)} %constant.0.clone.1.zero_ref, f32[12,12,128]{2,1,0:T(8,128)} %refs_0_.1, f32[12,12,128]{2,1,0:T(8,128)} %refs_1_.1, f32[12,12,128]{2,1,0:T(8,128)} %refs_2_.1, ...), custom_call_target="tpu_custom_call" | custom-call | tf_op jit(solution)/shard_map/pack/pallas_call | solution.py:277
  1.7 3.0 %collective-permute-start = (f32[192,128]{1,0:T(8,128)S(1)}, f32[192,128]{1,0:T(8,128)S(1)}, u32[]{:S(2)}, u32[]{:S(2)}) collective-permute-start(f32[192,128]{1,0:T(8,128)S(1)} %get-tuple-element.25), channel_id=1, source_target_pairs={{28,0},{0,4},{4,8},{8,12},{12,16},{16,20},{20,24},{24,28},{29,1},{... | collective-permute-start | bytes 294920 | tf_op jit(solution)/shard_map/ppermute | solution.py:259
  4.7 3.1 %collective-permute-start.1 = (f32[192,128]{1,0:T(8,128)S(1)}, f32[192,128]{1,0:T(8,128)S(1)}, u32[]{:S(2)}, u32[]{:S(2)}) collective-permute-start(f32[192,128]{1,0:T(8,128)S(1)} %get-tuple-element.26), channel_id=1, source_target_pairs={{4,0},{8,4},{12,8},{16,12},{20,16},{24,20},{28,24},{0,28},{5,1},{9... | collective-permute-start | bytes 294920 | tf_op jit(solution)/shard_map/ppermute | solution.py:259
  7.8 0.0 collective-permute-start.2
  7.9 1.7 %collective-permute-start.3 = (f32[192,128]{1,0:T(8,128)S(1)}, f32[192,128]{1,0:T(8,128)S(1)}, u32[]{:S(2)}, u32[]{:S(2)}) collective-permute-start(f32[192,128]{1,0:T(8,128)S(1)} %get-tuple-element.28), channel_id=1, source_target_pairs={{1,0},{2,1},{3,2},{0,3},{5,4},{6,5},{7,6},{4,7},{9,8},{10,9},{11,1... | collective-permute-start | bytes 294920 | tf_op jit(solution)/shard_map/ppermute | solution.py:259
  9.6 1.1 %collective-permute-done.below_ref.refs_1_ = f32[192,128]{1,0:T(8,128)S(1)} collective-permute-done((f32[192,128]{1,0:T(8,128)S(1)}, f32[192,128]{1,0:T(8,128)S(1)}, u32[]{:S(2)}, u32[]{:S(2)}) %collective-permute-start) | collective-permute-done | bytes 98336 | tf_op jit(solution)/shard_map/ppermute | solution.py:259
  10.7 0.8 %collective-permute-done.1.above_ref.refs_2_ = f32[192,128]{1,0:T(8,128)S(1)} collective-permute-done((f32[192,128]{1,0:T(8,128)S(1)}, f32[192,128]{1,0:T(8,128)S(1)}, u32[]{:S(2)}, u32[]{:S(2)}) %collective-permute-start.1) | collective-permute-done | bytes 98336 | tf_op jit(solution)/shard_map/ppermute | solution.py:259
  11.5 0.1 collective-permute-start.4
  11.6 1.7 %collective-permute-start.5 = (f32[96,128]{1,0:T(8,128)S(1)}, f32[96,128]{1,0:T(8,128)S(1)}, u32[]{:S(2)}, u32[]{:S(2)}) collective-permute-start(f32[96,128]{1,0:T(8,128)S(1)} %get-tuple-element.30), channel_id=1, source_target_pairs={{1,0},{2,1},{3,2},{0,3},{5,4},{6,5},{7,6},{4,7},{9,8},{10,9},{11,1... | collective-permute-start | bytes 147464 | tf_op jit(solution)/shard_map/ppermute | solution.py:259
  13.9 0.0 collective-permute-done.2.refs_3_
  14.0 0.0 collective-permute-done.3.refs_4_
  14.0 1.1 %collective-permute-done.4.refs_5_ = f32[96,128]{1,0:T(8,128)S(1)} collective-permute-done((f32[96,128]{1,0:T(8,128)S(1)}, f32[96,128]{1,0:T(8,128)S(1)}, u32[]{:S(2)}, u32[]{:S(2)}) %collective-permute-start.4) | collective-permute-done | bytes 49184 | tf_op jit(solution)/shard_map/ppermute | solution.py:259
  15.1 0.0 collective-permute-done.5.refs_6_
  15.1 1.9 %step.1 = (f32[2,16,16,128]{3,2,1,0:T(8,128)S(1)}, f32[16,16,128]{2,1,0:T(8,128)S(1)}, f32[12,24,128]{2,1,0:T(8,128)S(1)}, f32[12,16,128]{2,1,0:T(8,128)S(1)}, f...) custom-call(s32[1]{0:T(128)} %constant.0.clone.1.zero_ref, f32[1]{0:T(128)} %bitcast.4.dt_ref, ...), custom_call_target="tpu_custom_call" | custom-call | tf_op jit(solution)/shard_map/step/pallas_call | solution.py:299
  17.0 5.4 %all-to-all-start = ((f32[32,1,128]{2,1,0:T(1,128)}), f32[32,1,128]{2,1,0:T(1,128)S(1)}, u32[]{:S(2)}, u32[]{:S(2)}) async-start(f32[32,1,128]{2,1,0:T(1,128)} %bitcast.2), calls=%async_computation | async-start | bytes 32768 | tf_op jit(solution)/shard_map/all_to_all | solution.py:331
  22.3 2.0 %carry.1 = (f32[12,12,128]{2,1,0:T(8,128)}, f32[12,12,128]{2,1,0:T(8,128)}, f32[12,12,128]{2,1,0:T(8,128)}, f32[12,12,128]{2,1,0:T(8,128)}, f32[12,12,128]{2,1,0:T(8,128)}) custom-call(s32[1]{0:T(128)} %constant.0.clone.1.zero_ref, f32[1]{0:T(128)} %bitcast.5.dt_ref, f32[2,16,16,128]{3,2,1,0:T(8,128)S(1)} %get-tuple-element.31.refs_0_, ...), custom_call_target="tpu_custom_call" | custom-call | flops 10000000 | bytes 4000000 | tf_op jit(solution)/shard_map/carry/pallas_call | solution.py:317
  24.4 5.1 %all-to-all-done = f32[32,1,128]{2,1,0:T(1,128)S(1)} async-done(((f32[32,1,128]{2,1,0:T(1,128)}), f32[32,1,128]{2,1,0:T(1,128)S(1)}, u32[]{:S(2)}, u32[]{:S(2)}) %all-to-all-start) | async-done | bytes 16416 | tf_op jit(solution)/shard_map/all_to_all | solution.py:331
  29.5 0.6 %reduce_max.9 = f32[]{:T(128)} reduce(f32[32,1,128]{2,1,0:T(1,128)S(1)} %all-to-all-done, f32[]{:T(128)} %constant.2.clone.1), dimensions={0,1,2}, to_apply=%region_0.0 | reduce | flops 4095 | bytes 16392 | tf_op jit(solution)/shard_map/reduce_max | solution.py:332
  (1 shorter events, 0.0 us)
Async XLA Ops:
  1.7 9.0 %collective-permute-start = (f32[192,128]{1,0:T(8,128)S(1)}, f32[192,128]{1,0:T(8,128)S(1)}, u32[]{:S(2)}, u32[]{:S(2)}) collective-permute-start(f32[192,128]{1,0:T(8,128)S(1)} %get-tuple-element.25), channel_id=1, source_target_pairs={{28,0},{0,4},{4,8},{8,12},{12,16},{16,20},{20,24},{24,28},{29,1},{... | collective-permute-start | bytes 294920 | tf_op jit(solution)/shard_map/ppermute | solution.py:259
  4.7 6.7 %collective-permute-start.1 = (f32[192,128]{1,0:T(8,128)S(1)}, f32[192,128]{1,0:T(8,128)S(1)}, u32[]{:S(2)}, u32[]{:S(2)}) collective-permute-start(f32[192,128]{1,0:T(8,128)S(1)} %get-tuple-element.26), channel_id=1, source_target_pairs={{4,0},{8,4},{12,8},{16,12},{20,16},{24,20},{28,24},{0,28},{5,1},{9... | collective-permute-start | bytes 294920 | tf_op jit(solution)/shard_map/ppermute | solution.py:259
  7.8 6.1 %collective-permute-start.2 = (f32[192,128]{1,0:T(8,128)S(1)}, f32[192,128]{1,0:T(8,128)S(1)}, u32[]{:S(2)}, u32[]{:S(2)}) collective-permute-start(f32[192,128]{1,0:T(8,128)S(1)} %get-tuple-element.27), channel_id=1, source_target_pairs={{3,0},{0,1},{1,2},{2,3},{7,4},{4,5},{5,6},{6,7},{11,8},{8,9},{9,10... | collective-permute-start | bytes 294920 | tf_op jit(solution)/shard_map/ppermute | solution.py:259
  7.9 6.1 %collective-permute-start.3 = (f32[192,128]{1,0:T(8,128)S(1)}, f32[192,128]{1,0:T(8,128)S(1)}, u32[]{:S(2)}, u32[]{:S(2)}) collective-permute-start(f32[192,128]{1,0:T(8,128)S(1)} %get-tuple-element.28), channel_id=1, source_target_pairs={{1,0},{2,1},{3,2},{0,3},{5,4},{6,5},{7,6},{4,7},{9,8},{10,9},{11,1... | collective-permute-start | bytes 294920 | tf_op jit(solution)/shard_map/ppermute | solution.py:259
  11.5 3.6 %collective-permute-start.4 = (f32[96,128]{1,0:T(8,128)S(1)}, f32[96,128]{1,0:T(8,128)S(1)}, u32[]{:S(2)}, u32[]{:S(2)}) collective-permute-start(f32[96,128]{1,0:T(8,128)S(1)} %get-tuple-element.29), channel_id=1, source_target_pairs={{3,0},{0,1},{1,2},{2,3},{7,4},{4,5},{5,6},{6,7},{11,8},{8,9},{9,10... | collective-permute-start | bytes 147464 | tf_op jit(solution)/shard_map/ppermute | solution.py:259
  11.6 3.5 %collective-permute-start.5 = (f32[96,128]{1,0:T(8,128)S(1)}, f32[96,128]{1,0:T(8,128)S(1)}, u32[]{:S(2)}, u32[]{:S(2)}) collective-permute-start(f32[96,128]{1,0:T(8,128)S(1)} %get-tuple-element.30), channel_id=1, source_target_pairs={{1,0},{2,1},{3,2},{0,3},{5,4},{6,5},{7,6},{4,7},{9,8},{10,9},{11,1... | collective-permute-start | bytes 147464 | tf_op jit(solution)/shard_map/ppermute | solution.py:259
  17.0 12.5 %all-to-all-start = ((f32[32,1,128]{2,1,0:T(1,128)}), f32[32,1,128]{2,1,0:T(1,128)S(1)}, u32[]{:S(2)}, u32[]{:S(2)}) async-start(f32[32,1,128]{2,1,0:T(1,128)} %bitcast.2), calls=%async_computation | async-start | bytes 32768 | tf_op jit(solution)/shard_map/all_to_all | solution.py:331

commit v7 on v6

--- a/solution.py
+++ b/solution.py
@@ -1,4 +1,5 @@
 import functools
+import itertools
 
 import jax
 import jax.numpy as jnp
@@ -9,74 +10,85 @@
 
 DENSITY, ENERGY, XV, YV, ZV = range(5)
 REACH = 4
-SIDES = ((-1, 0), (1, 0), (0, -1), (0, 1))
+NEAR, FAR = "near", "far"
+LINKS = (FAR, NEAR)
 TOP = 8
 VMEM = pl.BlockSpec(memory_space=pltpu.VMEM)
 HBM = pl.BlockSpec(memory_space=pltpu.HBM)
 SMEM = pl.BlockSpec(memory_space=pltpu.SMEM)
 
 
-def rows_needed(field, a, nx, ny):
-    past = max(-a, a - nx + 1, 0)
-    if field == XV:
-        reach = {0: 3, 1: 3, 2: 3, 3: 3, 4: 2}.get(past, -1)
-    elif field == YV:
-        reach = {0: 4, 1: 4, 2: 4, 3: 3}.get(past, -1)
-    else:
-        reach = {0: 3, 1: 3, 2: 3, 3: 2}.get(past, -1)
-    return (-reach, ny + reach) if reach >= 0 else (0, 0)
-
-
-def segments(side, nx, ny):
-    columns = {-1: range(-REACH, 0), 0: range(nx), 1: range(nx, nx + REACH)}[side[0]]
-    low, high = {-1: (-REACH, 0), 0: (0, ny), 1: (ny, ny + REACH)}[side[1]]
+def ghost_rows(field, past):
+    if field == YV:
+        return (4, 4, 4, 3, 0)[past]
+    return (3, 3, 3, 3, 2)[past] if field == XV else (3, 3, 3, 2, 0)[past]
+
+
+def x_layers():
+    return [(field, past) for field in range(5) for past in range(1, REACH + 1) if ghost_rows(field, past)]
+
+
+def y_layers(nx):
     found, offset = [], 0
-    for a in columns:
+    for a in range(nx):
         for field in range(5):
-            first, last = rows_needed(field, a, nx, ny)
-            first, last = max(first, low), min(last, high)
-            if last > first:
-                found.append((field, a, first, last - first, offset))
-                offset += last - first
+            found.append((field, a, ghost_rows(field, 0), offset))
+            offset += ghost_rows(field, 0)
     return found, -(-offset // 8) * 8
 
 
-def corner_segments(side_y, nx, ny):
+def corner_layers():
     found, offset = [], 0
-    for side_x in (-1, 1):
-        for field, a, first, count, _ in segments((side_x, side_y), nx, ny)[0]:
-            found.append((side_x, field, a, first, count, offset))
-            offset += count
+    for link in LINKS:
+        for number, (field, past) in enumerate(x_layers()):
+            rows = ghost_rows(field, past)
+            found.append((link, number, field, past, rows, offset))
+            offset += rows
     return found, -(-offset // 8) * 8
 
 
+def is_low(axis, link):
+    odd = lax.rem(lax.axis_index(axis), 2)
+    return odd if link == NEAR else 1 - odd
+
+
+def exchanged(value, axis, link):
+    count = lax.axis_size(axis)
+    partner = [i ^ 1 if link == NEAR else ((i - 1) ^ 1) + 1 for i in range(count)]
+    return lax.ppermute(value, axis, [(i, j % count) for i, j in enumerate(partner)])
+
+
+def pick(flag, one, other):
+    return flag * one + (1 - flag) * other
+
+
 def pack_kernel(nx, ny, zero_ref, *refs):
-    fields, own, edges, arrived = refs[:5], refs[5], refs[6 : 6 + len(SIDES)], refs[-1]
+    fields, own, x_edges, y_edges, arrived = refs[:5], refs[5], refs[6:8], refs[8:10], refs[-1]
     zero = zero_ref[0]
     copies = [pltpu.make_async_copy(fields[field], own.at[field], arrived.at[field]) for field in range(5)]
     for copy in copies:
         copy.start()
     for current, copy in enumerate(copies):
         copy.wait()
-        for side, edge in zip(SIDES, edges):
-            for field, a, b, count, offset in segments(side, nx, ny)[0]:
+        for link, edge in zip(LINKS, x_edges):
+            low = is_low("gx", link)
+            for number, (field, past) in enumerate(x_layers()):
                 if field == current:
-                    edge[pl.ds(zero + offset, count), :] = own[
-                        field, a - side[0] * nx, pl.ds(zero + (b - side[1] * ny), count), :
-                    ]
-
-
-def corner_kernel(nx, ny, zero_ref, below_ref, above_ref, low_ref, high_ref):
+                    edge[pl.ds(zero + number * ny, ny), :] = own[field, pick(low, past - 1, nx - past)]
+        for link, edge in zip(LINKS, y_edges):
+            low = is_low("gy", link)
+            for field, a, rows, offset in y_layers(nx)[0]:
+                if field == current:
+                    edge[pl.ds(zero + offset, rows), :] = own[field, a, pl.ds(pick(low, 0, ny - rows), rows), :]
+
+
+def corner_kernel(ny, zero_ref, *refs):
     zero = zero_ref[0]
-    held = {
-        (side_x, field, a): (ref, offset)
-        for side_x, ref in ((-1, below_ref), (1, above_ref))
-        for field, a, _, _, offset in segments((side_x, 0), nx, ny)[0]
-    }
-    for side_y, out in ((-1, low_ref), (1, high_ref)):
-        for side_x, field, a, b, count, offset in corner_segments(side_y, nx, ny)[0]:
-            ref, start = held[side_x, field, a]
-            out[pl.ds(zero + offset, count), :] = ref[pl.ds(zero + (start + b - side_y * ny), count), :]
+    for link_y, out in zip(LINKS, refs[2:]):
+        low = is_low("gy", link_y)
+        for link, number, _, _, rows, offset in corner_layers()[0]:
+            edge = refs[LINKS.index(link)]
+            out[pl.ds(zero + offset, rows), :] = edge[pl.ds(number * ny + pick(low, 0, ny - rows), rows), :]
 
 
 def limited(above, below):
@@ -149,7 +161,7 @@
 
 
 def step_kernel(nx, ny, zero_ref, dt_ref, *refs):
-    own, halos = refs[0], refs[1:7]
+    own, x_edges, y_edges, corners = refs[0], refs[1:3], refs[3:5], refs[5:7]
     passive, speed, speed_y, speed_z, flows, peak_ref = refs[7:13]
     cells, stress, growth, heat, state, energy_one, swept, work = refs[13:]
     nz = own.shape[-1]
@@ -162,12 +174,20 @@
     for field in range(5):
         for a in range(nx):
             cells[field, a + REACH, pl.ds(TOP, ny), :] = own[field, a]
-    for side, halo in zip(SIDES, halos):
-        for field, a, b, count, offset in segments(side, nx, ny)[0]:
-            cells[field, a + REACH, pl.ds(zero + (b + TOP), count), :] = halo[pl.ds(zero + offset, count), :]
-    for side_y, halo in zip((-1, 1), halos[len(SIDES) :]):
-        for _, field, a, b, count, offset in corner_segments(side_y, nx, ny)[0]:
-            cells[field, a + REACH, pl.ds(zero + (b + TOP), count), :] = halo[pl.ds(zero + offset, count), :]
+    for link, edge in zip(LINKS, x_edges):
+        low = is_low("gx", link)
+        for number, (field, past) in enumerate(x_layers()):
+            column = REACH + pick(low, -past, nx - 1 + past)
+            cells[field, column, pl.ds(TOP, ny), :] = edge[pl.ds(zero + number * ny, ny), :]
+    for link_y, edge, corner in zip(LINKS, y_edges, corners):
+        low_y = is_low("gy", link_y)
+        for field, a, rows, offset in y_layers(nx)[0]:
+            to = pl.ds(TOP + pick(low_y, -rows, ny), rows)
+            cells[field, a + REACH, to, :] = edge[pl.ds(zero + offset, rows), :]
+        for link, _, field, past, rows, offset in corner_layers()[0]:
+            column = REACH + pick(is_low("gx", link), -past, nx - 1 + past)
+            to = pl.ds(TOP + pick(low_y, -rows, ny), rows)
+            cells[field, column, to, :] = corner[pl.ds(zero + offset, rows), :]
 
     def at(ref, *index, start, count):
         return ref[(*index, pl.ds(zero + start, count), slice(None))]
@@ -230,7 +250,7 @@
         )
     row = lax.broadcasted_iota(jnp.int32, peak.shape, 0)
     peak = jnp.max(jnp.where(row < ny, peak, 0.0), axis=0, keepdims=True)
-    peak_ref[...] = jnp.broadcast_to(peak, peak_ref.shape)
+    peak_ref[...] = peak
 
 
 def carry_kernel(nx, ny, zero_ref, dt_ref, *refs):
@@ -253,10 +273,17 @@
         copy.wait()
 
 
-def shifted(value, side):
-    axis, step = ("gx", side[0]) if side[0] else ("gy", side[1])
-    count = lax.axis_size(axis)
-    return lax.ppermute(value, axis, [((i + step) % count, i) for i in range(count)])
+def all_max(row):
+    axes = ("gx", "gy")
+    count, stride = lax.axis_size(axes), 1
+    while stride < count:
+        if count & (count - 1):
+            pairs = [(i, (i + stride) % count) for i in range(count)]
+        else:
+            pairs = [(i, i ^ stride) for i in range(count)]
+        row = jnp.maximum(row, lax.ppermute(row, axes, pairs))
+        stride *= 2
+    return row
 
 
 def body(density0, energy0, x_velocity, y_velocity, z_velocity, time_increment):
@@ -274,31 +301,31 @@
     def limit(mebibytes):
         return pltpu.CompilerParams(vmem_limit_bytes=mebibytes * 1024 * 1024)
 
+    x_edge, y_edge = array(len(x_layers()) * ny), array(y_layers(nx)[1])
     own, *edges = pl.pallas_call(
         functools.partial(pack_kernel, nx, ny),
-        out_shape=[array(5, nx, ny)] + [array(segments(side, nx, ny)[1]) for side in SIDES],
+        out_shape=[array(5, nx, ny), x_edge, x_edge, y_edge, y_edge],
         in_specs=[SMEM] + [HBM] * 5,
-        out_specs=[VMEM] * (1 + len(SIDES)),
+        out_specs=[VMEM] * 5,
         scratch_shapes=[pltpu.SemaphoreType.DMA((5,))],
         compiler_params=limit(4),
         name="pack",
     )(zero, *[pltpu.with_memory_space_constraint(field, pltpu.HBM) for field in fields])
-    edges = [shifted(edge, side) for edge, side in zip(edges, SIDES)]
+    edges = [exchanged(edge, axis, link) for edge, (axis, link) in zip(edges, itertools.product(("gx", "gy"), LINKS))]
     corners = pl.pallas_call(
-        functools.partial(corner_kernel, nx, ny),
-        out_shape=[array(corner_segments(1, nx, ny)[1])] * 2,
+        functools.partial(corner_kernel, ny),
+        out_shape=[array(corner_layers()[1])] * 2,
         in_specs=[SMEM] + [VMEM] * 2,
         out_specs=[VMEM] * 2,
         compiler_params=limit(4),
         name="corners",
     )(zero, edges[0], edges[1])
-    corners = [shifted(corner, (0, side_y)) for corner, side_y in zip(corners, (-1, 1))]
-    count = lax.axis_size(("gx", "gy"))
+    corners = [exchanged(corner, "gy", link) for corner, link in zip(corners, LINKS)]
     increment = time_increment.reshape(1)
     passed = [array(2, nx + 4, wide), array(nx + 4, wide), array(nx, wide + 8), array(nx, wide), array(3, nx, ny)]
     *passed, peak = pl.pallas_call(
         functools.partial(step_kernel, nx, ny),
-        out_shape=passed + [array(count)],
+        out_shape=passed + [array(1)],
         in_specs=[SMEM, SMEM] + [VMEM] * 7,
         out_specs=[VMEM] * 6,
         scratch_shapes=[
@@ -328,8 +355,7 @@
         cost_estimate=pl.CostEstimate(flops=10**7, bytes_accessed=4 * 10**6, transcendentals=0),
         name="carry",
     )(zero, increment, *passed)
-    peak = lax.all_to_all(peak, ("gx", "gy"), 0, 0, tiled=True)
-    return (*outs, 0.3 / jnp.max(peak))
+    return (*outs, 0.3 / jnp.max(all_max(peak)))
 
 
 def solution(mesh):

time: 32.2 us -> 37.1 us (1.15)
  waiting for transfers between devices: 8.08 us -> 17.5 us
  starting transfers between devices: 15 us -> 11.1 us
  Pallas kernels: 5.04 us -> 4.56 us
    ppermute x6 -> x11, waiting for transfers between devices: 2.98 us -> 17.5 us  [the longest x5 12.5 us: all_max(): row = jnp.maximum(row, lax.ppermute(row, axes, pairs))]
    all_to_all x1 -> x0, starting transfers between devices: 5.37 us -> none  [body(): peak = lax.all_to_all(peak, ('gx', 'gy'), 0, 0, tiled=True)]
    all_to_all x1 -> x0, waiting for transfers between devices: 5.1 us -> none  [body(): peak = lax.all_to_all(peak, ('gx', 'gy'), 0, 0, tiled=True)]
    ppermute x6 -> x11, starting transfers between devices: 9.66 us -> 11.1 us  [the longest x6 9.35 us: exchanged(): lax.ppermute(value, axis, [(i, j % count) for i, j in enumerate(partner)])]
    pallas_call x1, Pallas kernels: 1.9 us -> 1.43 us  [body(): pl.pallas_call(functools.partial(step_kernel, nx, ny), out_shape=passed +...]
  transfers between devices with their start and end apart: 7 -> 11, of which waited for: 4 -> 8; matrix products, arithmetic and copies ran while one was open for 0% -> 0% of each run, Pallas kernels for 6% -> 6%
where the time goes in v7:
time: 37.1 us; the launch traced here: 36.9 us
  waiting for transfers between devices  17.5 us (47%)
  starting transfers between devices  11.1 us (30%)
  Pallas kernels  4.56 us (12%)
  between operations  3.15 us (8%)
  other arithmetic  0.61 us (2%)
    ppermute x5, waiting for transfers between devices, all_max(): row = jnp.maximum(row, lax.ppermute(row, axes, pairs))  12.5 us
    ppermute x6, starting transfers between devices, exchanged(): lax.ppermute(value, axis, [(i, j % count) for i, j in enumerate(partner)])  9.35 us
    ppermute x6, waiting for transfers between devices, exchanged(): lax.ppermute(value, axis, [(i, j % count) for i, j in enumerate(partner)])  5.01 us
    pallas_call x1, Pallas kernels, body(): pl.pallas_call(functools.partial(carry_kernel, nx, ny), out_shape=[array(...  2.03 us
    ppermute x5, starting transfers between devices, all_max(): row = jnp.maximum(row, lax.ppermute(row, axes, pairs))  1.75 us
    pallas_call x1, Pallas kernels, body(): pl.pallas_call(functools.partial(step_kernel, nx, ny), out_shape=passed +...  1.43 us
    pallas_call x1, Pallas kernels, body(): pl.pallas_call(functools.partial(pack_kernel, nx, ny), out_shape=[array(5...  1.08 us
  transfers between devices with their start and end apart: 11, of which 8 were waited for; matrix products, arithmetic and copies ran while one was open for 0% of the time, Pallas kernels for 6%

profile of v7, /device:TPU:0, one launch (start us, length us, event | category | flops | bytes accessed | tf_op | source)
XLA Modules:
  0.0 36.9 jit_solution(4081526379985669886)
XLA Ops:
  0.6 1.1 %pack.1 = (f32[5,12,12,128]{3,2,1,0:T(8,128)S(1)}, f32[192,128]{1,0:T(8,128)S(1)}, f32[192,128]{1,0:T(8,128)S(1)}, f32[192,128]{1,0:T(8,128)S(1)}, f32[192,128]{1,0:T(8,128)S(1)}) custom-call(s32[1]{0:T(128)} %constant.0.clone.1.zero_ref, f32[12,12,128]{2,1,0:T(8,128)} %refs_0_.1, f32[12,12,128]{2,1,0:T(8,128)} %refs_1_.1, f32[12,12,128]{2,1,0:T(8,128)} %refs_2_.1, ...), custom_call_target="tpu_custom_call" | custom-call | tf_op jit(solution)/shard_map/pack/pallas_call | solution.py:305
  1.7 6.1 %collective-permute-start = (f32[192,128]{1,0:T(8,128)S(1)}, f32[192,128]{1,0:T(8,128)S(1)}, u32[]{:S(2)}, u32[]{:S(2)}) collective-permute-start(f32[192,128]{1,0:T(8,128)S(1)} %get-tuple-element.25), channel_id=1, source_target_pairs={{0,28},{4,8},{8,4},{12,16},{16,12},{20,24},{24,20},{28,0},{1,29},{... | collective-permute-start | bytes 294920 | tf_op jit(solution)/shard_map/ppermute | solution.py:58
  7.8 0.0 collective-permute-start.1
  7.8 0.7 %collective-permute-start.2 = (f32[192,128]{1,0:T(8,128)S(1)}, f32[192,128]{1,0:T(8,128)S(1)}, u32[]{:S(2)}, u32[]{:S(2)}) collective-permute-start(f32[192,128]{1,0:T(8,128)S(1)} %get-tuple-element.27), channel_id=1, source_target_pairs={{0,3},{1,2},{2,1},{3,0},{4,7},{5,6},{6,5},{7,4},{8,11},{9,10},{10,... | collective-permute-start | bytes 294920 | tf_op jit(solution)/shard_map/ppermute | solution.py:58
  8.4 1.0 %collective-permute-start.3 = (f32[192,128]{1,0:T(8,128)S(1)}, f32[192,128]{1,0:T(8,128)S(1)}, u32[]{:S(2)}, u32[]{:S(2)}) collective-permute-start(f32[192,128]{1,0:T(8,128)S(1)} %get-tuple-element.28), channel_id=1, source_target_pairs={{0,1},{1,0},{2,3},{3,2},{4,5},{5,4},{6,7},{7,6},{8,9},{9,8},{10,11... | collective-permute-start | bytes 294920 | tf_op jit(solution)/shard_map/ppermute | solution.py:58
  9.4 1.2 %collective-permute-done.refs_0_.refs_1_ = f32[192,128]{1,0:T(8,128)S(1)} collective-permute-done((f32[192,128]{1,0:T(8,128)S(1)}, f32[192,128]{1,0:T(8,128)S(1)}, u32[]{:S(2)}, u32[]{:S(2)}) %collective-permute-start) | collective-permute-done | bytes 98336 | tf_op jit(solution)/shard_map/ppermute | solution.py:58
  10.7 2.0 %collective-permute-done.1.refs_1_.refs_2_ = f32[192,128]{1,0:T(8,128)S(1)} collective-permute-done((f32[192,128]{1,0:T(8,128)S(1)}, f32[192,128]{1,0:T(8,128)S(1)}, u32[]{:S(2)}, u32[]{:S(2)}) %collective-permute-start.1) | collective-permute-done | bytes 98336 | tf_op jit(solution)/shard_map/ppermute | solution.py:58
  12.7 0.4 %collective-permute-start.4 = (f32[96,128]{1,0:T(8,128)S(1)}, f32[96,128]{1,0:T(8,128)S(1)}, u32[]{:S(2)}, u32[]{:S(2)}) collective-permute-start(f32[96,128]{1,0:T(8,128)S(1)} %get-tuple-element.29), channel_id=1, source_target_pairs={{0,3},{1,2},{2,1},{3,0},{4,7},{5,6},{6,5},{7,4},{8,11},{9,10},{10,... | collective-permute-start | bytes 147464 | tf_op jit(solution)/shard_map/ppermute | solution.py:58
  13.2 1.2 %collective-permute-start.5 = (f32[96,128]{1,0:T(8,128)S(1)}, f32[96,128]{1,0:T(8,128)S(1)}, u32[]{:S(2)}, u32[]{:S(2)}) collective-permute-start(f32[96,128]{1,0:T(8,128)S(1)} %get-tuple-element.30), channel_id=1, source_target_pairs={{0,1},{1,0},{2,3},{3,2},{4,5},{5,4},{6,7},{7,6},{8,9},{9,8},{10,11... | collective-permute-start | bytes 147464 | tf_op jit(solution)/shard_map/ppermute | solution.py:58
  15.0 0.0 collective-permute-done.2.refs_3_
  15.1 0.0 collective-permute-done.3.refs_4_
  15.1 1.7 %collective-permute-done.4.refs_5_ = f32[96,128]{1,0:T(8,128)S(1)} collective-permute-done((f32[96,128]{1,0:T(8,128)S(1)}, f32[96,128]{1,0:T(8,128)S(1)}, u32[]{:S(2)}, u32[]{:S(2)}) %collective-permute-start.4) | collective-permute-done | bytes 49184 | tf_op jit(solution)/shard_map/ppermute | solution.py:58
  16.8 0.0 collective-permute-done.5.refs_6_
  16.8 1.4 %step.1 = (f32[2,16,16,128]{3,2,1,0:T(8,128)S(1)}, f32[16,16,128]{2,1,0:T(8,128)S(1)}, f32[12,24,128]{2,1,0:T(8,128)S(1)}, f32[12,16,128]{2,1,0:T(8,128)S(1)}, f...) custom-call(s32[1]{0:T(128)} %constant.0.clone.1.zero_ref, f32[1]{0:T(128)} %bitcast.1.dt_ref, ...), custom_call_target="tpu_custom_call" | custom-call | tf_op jit(solution)/shard_map/step/pallas_call | solution.py:326
  18.2 0.2 collective-permute-start.6
  18.4 1.0 %collective-permute-done.6 = f32[1,128]{1,0:T(1,128)S(1)} collective-permute-done((f32[1,128]{1,0:T(1,128)S(1)}, f32[1,128]{1,0:T(1,128)S(1)}, u32[]{:S(2)}, u32[]{:S(2)}) %collective-permute-start.6) | collective-permute-done | bytes 544 | tf_op jit(solution)/shard_map/ppermute | solution.py:284
  19.4 1.0 %collective-permute-start.7 = (f32[1,128]{1,0:T(1,128)S(1)}, f32[1,128]{1,0:T(1,128)S(1)}, u32[]{:S(2)}, u32[]{:S(2)}) collective-permute-start(f32[1,128]{1,0:T(1,128)S(1)} %max.15), channel_id=1, source_target_pairs={{0,2},{1,3},{2,0},{3,1},{4,6},{5,7},{6,4},{7,5},{8,10},{9,11},{10,... | collective-permute-start | bytes 1544 | tf_op jit(solution)/shard_map/ppermute | solution.py:284
  20.4 2.5 %collective-permute-done.7 = f32[1,128]{1,0:T(1,128)S(1)} collective-permute-done((f32[1,128]{1,0:T(1,128)S(1)}, f32[1,128]{1,0:T(1,128)S(1)}, u32[]{:S(2)}, u32[]{:S(2)}) %collective-permute-start.7) | collective-permute-done | bytes 544 | tf_op jit(solution)/shard_map/ppermute | solution.py:284
  22.9 0.0 collective-permute-start.8
  22.9 3.5 %collective-permute-done.8 = f32[1,128]{1,0:T(1,128)S(1)} collective-permute-done((f32[1,128]{1,0:T(1,128)S(1)}, f32[1,128]{1,0:T(1,128)S(1)}, u32[]{:S(2)}, u32[]{:S(2)}) %collective-permute-start.8) | collective-permute-done | bytes 544 | tf_op jit(solution)/shard_map/ppermute | solution.py:284
  26.5 0.0 collective-permute-start.9
  26.5 3.5 %collective-permute-done.9 = f32[1,128]{1,0:T(1,128)S(1)} collective-permute-done((f32[1,128]{1,0:T(1,128)S(1)}, f32[1,128]{1,0:T(1,128)S(1)}, u32[]{:S(2)}, u32[]{:S(2)}) %collective-permute-start.9) | collective-permute-done | bytes 544 | tf_op jit(solution)/shard_map/ppermute | solution.py:284
  30.0 0.6 %collective-permute-start.10 = (f32[1,128]{1,0:T(1,128)S(1)}, f32[1,128]{1,0:T(1,128)S(1)}, u32[]{:S(2)}, u32[]{:S(2)}) collective-permute-start(f32[1,128]{1,0:T(1,128)S(1)} %max.18), channel_id=1, source_target_pairs={{0,16},{1,17},{2,18},{3,19},{4,20},{5,21},{6,22},{7,23},{8,24},{9,... | collective-permute-start | bytes 1544 | tf_op jit(solution)/shard_map/ppermute | solution.py:284
  30.6 2.0 %carry.1 = (f32[12,12,128]{2,1,0:T(8,128)}, f32[12,12,128]{2,1,0:T(8,128)}, f32[12,12,128]{2,1,0:T(8,128)}, f32[12,12,128]{2,1,0:T(8,128)}, f32[12,12,128]{2,1,0:T(8,128)}) custom-call(s32[1]{0:T(128)} %constant.0.clone.1.zero_ref, f32[1]{0:T(128)} %bitcast.2.dt_ref, f32[2,16,16,128]{3,2,1,0:T(8,128)S(1)} %get-tuple-element.31.refs_0_, ...), custom_call_target="tpu_custom_call" | custom-call | flops 10000000 | bytes 4000000 | tf_op jit(solution)/shard_map/carry/pallas_call | solution.py:344
  32.6 1.8 %collective-permute-done.10 = f32[1,128]{1,0:T(1,128)S(1)} collective-permute-done((f32[1,128]{1,0:T(1,128)S(1)}, f32[1,128]{1,0:T(1,128)S(1)}, u32[]{:S(2)}, u32[]{:S(2)}) %collective-permute-start.10) | collective-permute-done | bytes 544 | tf_op jit(solution)/shard_map/ppermute | solution.py:284
  34.5 0.6 %maximum_reduce_fusion = f32[]{:T(128)} fusion(f32[1,128]{1,0:T(1,128)S(1)} %max.18, f32[1,128]{1,0:T(1,128)S(1)} %collective-permute-done.10), kind=kLoop, calls=%fused_computation | loop fusion | flops 255 | bytes 1028 | tf_op jit(solution)/shard_map/reduce_max | solution.py:358
  (5 shorter events, 0.0 us)
Async XLA Ops:
  1.7 8.9 %collective-permute-start = (f32[192,128]{1,0:T(8,128)S(1)}, f32[192,128]{1,0:T(8,128)S(1)}, u32[]{:S(2)}, u32[]{:S(2)}) collective-permute-start(f32[192,128]{1,0:T(8,128)S(1)} %get-tuple-element.25), channel_id=1, source_target_pairs={{0,28},{4,8},{8,4},{12,16},{16,12},{20,24},{24,20},{28,0},{1,29},{... | collective-permute-start | bytes 294920 | tf_op jit(solution)/shard_map/ppermute | solution.py:58
  7.8 4.9 %collective-permute-start.1 = (f32[192,128]{1,0:T(8,128)S(1)}, f32[192,128]{1,0:T(8,128)S(1)}, u32[]{:S(2)}, u32[]{:S(2)}) collective-permute-start(f32[192,128]{1,0:T(8,128)S(1)} %get-tuple-element.26), channel_id=1, source_target_pairs={{0,4},{4,0},{8,12},{12,8},{16,20},{20,16},{24,28},{28,24},{1,5},{5... | collective-permute-start | bytes 294920 | tf_op jit(solution)/shard_map/ppermute | solution.py:58
  7.8 7.3 %collective-permute-start.2 = (f32[192,128]{1,0:T(8,128)S(1)}, f32[192,128]{1,0:T(8,128)S(1)}, u32[]{:S(2)}, u32[]{:S(2)}) collective-permute-start(f32[192,128]{1,0:T(8,128)S(1)} %get-tuple-element.27), channel_id=1, source_target_pairs={{0,3},{1,2},{2,1},{3,0},{4,7},{5,6},{6,5},{7,4},{8,11},{9,10},{10,... | collective-permute-start | bytes 294920 | tf_op jit(solution)/shard_map/ppermute | solution.py:58
  8.4 6.6 %collective-permute-start.3 = (f32[192,128]{1,0:T(8,128)S(1)}, f32[192,128]{1,0:T(8,128)S(1)}, u32[]{:S(2)}, u32[]{:S(2)}) collective-permute-start(f32[192,128]{1,0:T(8,128)S(1)} %get-tuple-element.28), channel_id=1, source_target_pairs={{0,1},{1,0},{2,3},{3,2},{4,5},{5,4},{6,7},{7,6},{8,9},{9,8},{10,11... | collective-permute-start | bytes 294920 | tf_op jit(solution)/shard_map/ppermute | solution.py:58
  12.7 4.1 %collective-permute-start.4 = (f32[96,128]{1,0:T(8,128)S(1)}, f32[96,128]{1,0:T(8,128)S(1)}, u32[]{:S(2)}, u32[]{:S(2)}) collective-permute-start(f32[96,128]{1,0:T(8,128)S(1)} %get-tuple-element.29), channel_id=1, source_target_pairs={{0,3},{1,2},{2,1},{3,0},{4,7},{5,6},{6,5},{7,4},{8,11},{9,10},{10,... | collective-permute-start | bytes 147464 | tf_op jit(solution)/shard_map/ppermute | solution.py:58
  13.2 3.6 %collective-permute-start.5 = (f32[96,128]{1,0:T(8,128)S(1)}, f32[96,128]{1,0:T(8,128)S(1)}, u32[]{:S(2)}, u32[]{:S(2)}) collective-permute-start(f32[96,128]{1,0:T(8,128)S(1)} %get-tuple-element.30), channel_id=1, source_target_pairs={{0,1},{1,0},{2,3},{3,2},{4,5},{5,4},{6,7},{7,6},{8,9},{9,8},{10,11... | collective-permute-start | bytes 147464 | tf_op jit(solution)/shard_map/ppermute | solution.py:58
  18.2 1.2 %collective-permute-start.6 = (f32[1,128]{1,0:T(1,128)S(1)}, f32[1,128]{1,0:T(1,128)S(1)}, u32[]{:S(2)}, u32[]{:S(2)}) collective-permute-start(f32[1,128]{1,0:T(1,128)S(1)} %get-tuple-element.41), channel_id=1, source_target_pairs={{0,1},{1,0},{2,3},{3,2},{4,5},{5,4},{6,7},{7,6},{8,9},{9,8},{10,11... | collective-permute-start | bytes 1544 | tf_op jit(solution)/shard_map/ppermute | solution.py:284
  19.4 3.5 %collective-permute-start.7 = (f32[1,128]{1,0:T(1,128)S(1)}, f32[1,128]{1,0:T(1,128)S(1)}, u32[]{:S(2)}, u32[]{:S(2)}) collective-permute-start(f32[1,128]{1,0:T(1,128)S(1)} %max.15), channel_id=1, source_target_pairs={{0,2},{1,3},{2,0},{3,1},{4,6},{5,7},{6,4},{7,5},{8,10},{9,11},{10,... | collective-permute-start | bytes 1544 | tf_op jit(solution)/shard_map/ppermute | solution.py:284
  22.9 3.5 %collective-permute-start.8 = (f32[1,128]{1,0:T(1,128)S(1)}, f32[1,128]{1,0:T(1,128)S(1)}, u32[]{:S(2)}, u32[]{:S(2)}) collective-permute-start(f32[1,128]{1,0:T(1,128)S(1)} %max.16), channel_id=1, source_target_pairs={{0,4},{1,5},{2,6},{3,7},{4,0},{5,1},{6,2},{7,3},{8,12},{9,13},{10,... | collective-permute-start | bytes 1544 | tf_op jit(solution)/shard_map/ppermute | solution.py:284
  26.5 3.5 %collective-permute-start.9 = (f32[1,128]{1,0:T(1,128)S(1)}, f32[1,128]{1,0:T(1,128)S(1)}, u32[]{:S(2)}, u32[]{:S(2)}) collective-permute-start(f32[1,128]{1,0:T(1,128)S(1)} %max.17), channel_id=1, source_target_pairs={{0,8},{1,9},{2,10},{3,11},{4,12},{5,13},{6,14},{7,15},{8,0},{9,1},... | collective-permute-start | bytes 1544 | tf_op jit(solution)/shard_map/ppermute | solution.py:284
  30.0 4.4 %collective-permute-start.10 = (f32[1,128]{1,0:T(1,128)S(1)}, f32[1,128]{1,0:T(1,128)S(1)}, u32[]{:S(2)}, u32[]{:S(2)}) collective-permute-start(f32[1,128]{1,0:T(1,128)S(1)} %max.18), channel_id=1, source_target_pairs={{0,16},{1,17},{2,18},{3,19},{4,20},{5,21},{6,22},{7,23},{8,24},{9,... | collective-permute-start | bytes 1544 | tf_op jit(solution)/shard_map/ppermute | solution.py:284

commit v8 on v7

--- a/solution.py
+++ b/solution.py
@@ -1,5 +1,4 @@
 import functools
-import itertools
 
 import jax
 import jax.numpy as jnp
@@ -37,6 +36,10 @@
     return found, -(-offset // 8) * 8
 
 
+def split_rows(ny):
+    return [(0, REACH), (ny - REACH, REACH)], [(REACH, ny - 2 * REACH)]
+
+
 def corner_layers():
     found, offset = [], 0
     for link in LINKS:
@@ -63,18 +66,23 @@
 
 
 def pack_kernel(nx, ny, zero_ref, *refs):
-    fields, own, x_edges, y_edges, arrived = refs[:5], refs[5], refs[6:8], refs[8:10], refs[-1]
+    fields, own, x_outer, x_inner, y_edges, arrived = refs[:5], refs[5], refs[6:8], refs[8:10], refs[10:12], refs[-1]
     zero = zero_ref[0]
     copies = [pltpu.make_async_copy(fields[field], own.at[field], arrived.at[field]) for field in range(5)]
     for copy in copies:
         copy.start()
     for current, copy in enumerate(copies):
         copy.wait()
-        for link, edge in zip(LINKS, x_edges):
+        for k, link in enumerate(LINKS):
             low = is_low("gx", link)
             for number, (field, past) in enumerate(x_layers()):
                 if field == current:
-                    edge[pl.ds(zero + number * ny, ny), :] = own[field, pick(low, past - 1, nx - past)]
+                    column = pick(low, past - 1, nx - past)
+                    for edge, pieces in zip((x_outer[k], x_inner[k]), split_rows(ny)):
+                        offset = number * sum(rows for _, rows in pieces)
+                        for first, rows in pieces:
+                            edge[pl.ds(zero + offset, rows), :] = own[field, column, pl.ds(zero + first, rows), :]
+                            offset += rows
         for link, edge in zip(LINKS, y_edges):
             low = is_low("gy", link)
             for field, a, rows, offset in y_layers(nx)[0]:
@@ -82,13 +90,16 @@
                     edge[pl.ds(zero + offset, rows), :] = own[field, a, pl.ds(pick(low, 0, ny - rows), rows), :]
 
 
-def corner_kernel(ny, zero_ref, *refs):
+def corner_kernel(zero_ref, far_ref, near_ref, y_near, far_out, near_out):
     zero = zero_ref[0]
-    for link_y, out in zip(LINKS, refs[2:]):
+    start = y_near.shape[0]
+    near_out[0:start, :] = y_near[...]
+    for link_y, out, start in ((FAR, far_out, 0), (NEAR, near_out, start)):
         low = is_low("gy", link_y)
         for link, number, _, _, rows, offset in corner_layers()[0]:
-            edge = refs[LINKS.index(link)]
-            out[pl.ds(zero + offset, rows), :] = edge[pl.ds(number * ny + pick(low, 0, ny - rows), rows), :]
+            edge = far_ref if link == FAR else near_ref
+            first = number * 2 * REACH + pick(low, 0, 2 * REACH - rows)
+            out[pl.ds(zero + (start + offset), rows), :] = edge[pl.ds(first, rows), :]
 
 
 def limited(above, below):
@@ -161,9 +172,9 @@
 
 
 def step_kernel(nx, ny, zero_ref, dt_ref, *refs):
-    own, x_edges, y_edges, corners = refs[0], refs[1:3], refs[3:5], refs[5:7]
-    passive, speed, speed_y, speed_z, flows, peak_ref = refs[7:13]
-    cells, stress, growth, heat, state, energy_one, swept, work = refs[13:]
+    own, x_outer, x_inner, (y_far, far, near) = refs[0], refs[1:3], refs[3:5], refs[5:8]
+    passive, speed, speed_y, speed_z, flows, peak_ref = refs[8:14]
+    cells, stress, growth, heat, state, energy_one, swept, work = refs[14:]
     nz = own.shape[-1]
     zero = zero_ref[0]
     dt = dt_ref[0]
@@ -174,12 +185,16 @@
     for field in range(5):
         for a in range(nx):
             cells[field, a + REACH, pl.ds(TOP, ny), :] = own[field, a]
-    for link, edge in zip(LINKS, x_edges):
+    for k, link in enumerate(LINKS):
         low = is_low("gx", link)
         for number, (field, past) in enumerate(x_layers()):
             column = REACH + pick(low, -past, nx - 1 + past)
-            cells[field, column, pl.ds(TOP, ny), :] = edge[pl.ds(zero + number * ny, ny), :]
-    for link_y, edge, corner in zip(LINKS, y_edges, corners):
+            for edge, pieces in zip((x_outer[k], x_inner[k]), split_rows(ny)):
+                offset = number * sum(rows for _, rows in pieces)
+                for first, rows in pieces:
+                    cells[field, column, pl.ds(zero + (TOP + first), rows), :] = edge[pl.ds(zero + offset, rows), :]
+                    offset += rows
+    for link_y, edge, corner, start in ((FAR, y_far, far, 0), (NEAR, near, near, y_layers(nx)[1])):
         low_y = is_low("gy", link_y)
         for field, a, rows, offset in y_layers(nx)[0]:
             to = pl.ds(TOP + pick(low_y, -rows, ny), rows)
@@ -187,7 +202,7 @@
         for link, _, field, past, rows, offset in corner_layers()[0]:
             column = REACH + pick(is_low("gx", link), -past, nx - 1 + past)
             to = pl.ds(TOP + pick(low_y, -rows, ny), rows)
-            cells[field, column, to, :] = corner[pl.ds(zero + offset, rows), :]
+            cells[field, column, to, :] = corner[pl.ds(zero + (start + offset), rows), :]
 
     def at(ref, *index, start, count):
         return ref[(*index, pl.ds(zero + start, count), slice(None))]
@@ -250,7 +265,7 @@
         )
     row = lax.broadcasted_iota(jnp.int32, peak.shape, 0)
     peak = jnp.max(jnp.where(row < ny, peak, 0.0), axis=0, keepdims=True)
-    peak_ref[...] = peak
+    peak_ref[...] = jnp.broadcast_to(peak, peak_ref.shape)
 
 
 def carry_kernel(nx, ny, zero_ref, dt_ref, *refs):
@@ -273,19 +288,6 @@
         copy.wait()
 
 
-def all_max(row):
-    axes = ("gx", "gy")
-    count, stride = lax.axis_size(axes), 1
-    while stride < count:
-        if count & (count - 1):
-            pairs = [(i, (i + stride) % count) for i in range(count)]
-        else:
-            pairs = [(i, i ^ stride) for i in range(count)]
-        row = jnp.maximum(row, lax.ppermute(row, axes, pairs))
-        stride *= 2
-    return row
-
-
 def body(density0, energy0, x_velocity, y_velocity, z_velocity, time_increment):
     nx, ny, nz = density0.shape
     fields = (density0, energy0, x_velocity, y_velocity, z_velocity)
@@ -301,32 +303,37 @@
     def limit(mebibytes):
         return pltpu.CompilerParams(vmem_limit_bytes=mebibytes * 1024 * 1024)
 
-    x_edge, y_edge = array(len(x_layers()) * ny), array(y_layers(nx)[1])
+    outer, inner = [
+        array(len(x_layers()) * sum(rows for _, rows in pieces)) for pieces in split_rows(ny)
+    ]
+    y_edge, corner = array(y_layers(nx)[1]), array(corner_layers()[1])
     own, *edges = pl.pallas_call(
         functools.partial(pack_kernel, nx, ny),
-        out_shape=[array(5, nx, ny), x_edge, x_edge, y_edge, y_edge],
+        out_shape=[array(5, nx, ny), outer, outer, inner, inner, y_edge, y_edge],
         in_specs=[SMEM] + [HBM] * 5,
-        out_specs=[VMEM] * 5,
+        out_specs=[VMEM] * 7,
         scratch_shapes=[pltpu.SemaphoreType.DMA((5,))],
         compiler_params=limit(4),
         name="pack",
     )(zero, *[pltpu.with_memory_space_constraint(field, pltpu.HBM) for field in fields])
-    edges = [exchanged(edge, axis, link) for edge, (axis, link) in zip(edges, itertools.product(("gx", "gy"), LINKS))]
-    corners = pl.pallas_call(
-        functools.partial(corner_kernel, ny),
-        out_shape=[array(corner_layers()[1])] * 2,
-        in_specs=[SMEM] + [VMEM] * 2,
+    outers = [exchanged(edge, "gx", link) for edge, link in zip(edges[0:2], LINKS)]
+    inners = [exchanged(edge, "gx", link) for edge, link in zip(edges[2:4], LINKS)]
+    y_far = exchanged(edges[4], "gy", FAR)
+    far, near = pl.pallas_call(
+        corner_kernel,
+        out_shape=[corner, array(y_edge.shape[0] + corner.shape[0])],
+        in_specs=[SMEM] + [VMEM] * 3,
         out_specs=[VMEM] * 2,
         compiler_params=limit(4),
         name="corners",
-    )(zero, edges[0], edges[1])
-    corners = [exchanged(corner, "gy", link) for corner, link in zip(corners, LINKS)]
+    )(zero, *outers, edges[5])
+    far, near = exchanged(far, "gy", FAR), exchanged(near, "gy", NEAR)
     increment = time_increment.reshape(1)
     passed = [array(2, nx + 4, wide), array(nx + 4, wide), array(nx, wide + 8), array(nx, wide), array(3, nx, ny)]
     *passed, peak = pl.pallas_call(
         functools.partial(step_kernel, nx, ny),
-        out_shape=passed + [array(1)],
-        in_specs=[SMEM, SMEM] + [VMEM] * 7,
+        out_shape=passed + [pltpu.VMEM((lax.axis_size(("gx", "gy")), nz), jnp.float32)],
+        in_specs=[SMEM, SMEM] + [VMEM] * 8,
         out_specs=[VMEM] * 6,
         scratch_shapes=[
             scratch(5, nx + 8, ny + 20),
@@ -340,7 +347,7 @@
         ],
         compiler_params=limit(12),
         name="step",
-    )(zero, increment, own, *edges, *corners)
+    )(zero, increment, own, *outers, *inners, y_far, far, near)
     outs = pl.pallas_call(
         functools.partial(carry_kernel, nx, ny),
         out_shape=[array(nx, ny)] * 5,
@@ -355,7 +362,8 @@
         cost_estimate=pl.CostEstimate(flops=10**7, bytes_accessed=4 * 10**6, transcendentals=0),
         name="carry",
     )(zero, increment, *passed)
-    return (*outs, 0.3 / jnp.max(all_max(peak)))
+    peak = lax.all_to_all(peak, ("gx", "gy"), 0, 0, tiled=True)
+    return (*outs, 0.3 / jnp.max(peak))
 
 
 def solution(mesh):

time: 37.1 us -> 36.5 us (0.984)
  waiting for transfers between devices: 17.5 us -> 13 us
  starting transfers between devices: 11.1 us -> 14.3 us
  Pallas kernels: 4.56 us -> 5.2 us
    ppermute x5 -> x0, waiting for transfers between devices: 12.5 us -> none  [all_max(): row = jnp.maximum(row, lax.ppermute(row, axes, pairs))]
    all_to_all x0 -> x1, waiting for transfers between devices: none -> 5.11 us  [body(): peak = lax.all_to_all(peak, ('gx', 'gy'), 0, 0, tiled=True)]
    all_to_all x0 -> x1, starting transfers between devices: none -> 3.68 us  [body(): peak = lax.all_to_all(peak, ('gx', 'gy'), 0, 0, tiled=True)]
    ppermute x6 -> x7, waiting for transfers between devices: 5.01 us -> 7.87 us  [exchanged(): lax.ppermute(value, axis, [(i, j % count) for i, j in enumerate(partner)])]
    ppermute x5 -> x0, starting transfers between devices: 1.75 us -> none  [all_max(): row = jnp.maximum(row, lax.ppermute(row, axes, pairs))]
    ppermute x6 -> x7, starting transfers between devices: 9.35 us -> 10.7 us  [exchanged(): lax.ppermute(value, axis, [(i, j % count) for i, j in enumerate(partner)])]
    pallas_call x1, Pallas kernels: 1.43 us -> 2.05 us  [body(): pl.pallas_call(functools.partial(step_kernel, nx, ny), out_shape=passed +...]
  transfers between devices with their start and end apart: 11 -> 8, of which waited for: 8 -> 5; matrix products, arithmetic and copies ran while one was open for 0% -> 0% of each run, Pallas kernels for 6% -> 6%
where the time goes in v8:
time: 36.5 us; the launch traced here: 36.3 us
  starting transfers between devices  14.3 us (39%)
  waiting for transfers between devices  13 us (36%)
  Pallas kernels  5.2 us (14%)
  between operations  3.15 us (9%)
  other arithmetic  0.63 us (2%)
    ppermute x7, starting transfers between devices, exchanged(): lax.ppermute(value, axis, [(i, j % count) for i, j in enumerate(partner)])  10.7 us
    ppermute x7, waiting for transfers between devices, exchanged(): lax.ppermute(value, axis, [(i, j % count) for i, j in enumerate(partner)])  7.87 us
    all_to_all x1, waiting for transfers between devices, body(): peak = lax.all_to_all(peak, ('gx', 'gy'), 0, 0, tiled=True)  5.11 us
    all_to_all x1, starting transfers between devices, body(): peak = lax.all_to_all(peak, ('gx', 'gy'), 0, 0, tiled=True)  3.68 us
    pallas_call x1, Pallas kernels, body(): pl.pallas_call(functools.partial(step_kernel, nx, ny), out_shape=passed +...  2.05 us
    pallas_call x1, Pallas kernels, body(): pl.pallas_call(functools.partial(carry_kernel, nx, ny), out_shape=[array(...  2.03 us
    pallas_call x1, Pallas kernels, body(): pl.pallas_call(functools.partial(pack_kernel, nx, ny), out_shape=[array(5...  1.09 us
  transfers between devices with their start and end apart: 8, of which 5 were waited for; matrix products, arithmetic and copies ran while one was open for 0% of the time, Pallas kernels for 6%

profile of v8, /device:TPU:0, one launch (start us, length us, event | category | flops | bytes accessed | tf_op | source)
XLA Modules:
  0.0 36.3 jit_solution(9974820060134275453)
XLA Ops:
  0.6 1.1 %pack.1 = (f32[5,12,12,128]{3,2,1,0:T(8,128)S(1)}, f32[128,128]{1,0:T(8,128)S(1)}, f32[128,128]{1,0:T(8,128)S(1)}, f32[64,128]{1,0:T(8,128)S(1)}, f32[64,128]{1,...) custom-call(s32[1]{0:T(128)} %constant.0.clone.1.zero_ref, f32[12,12,128]{2,1,0:T(8,128)} %refs_0_.1, ...), custom_call_target="tpu_custom_call" | custom-call | tf_op jit(solution)/shard_map/pack/pallas_call | solution.py:310
  1.7 6.1 %collective-permute-start = (f32[128,128]{1,0:T(8,128)S(1)}, f32[128,128]{1,0:T(8,128)S(1)}, u32[]{:S(2)}, u32[]{:S(2)}) collective-permute-start(f32[128,128]{1,0:T(8,128)S(1)} %get-tuple-element.27), channel_id=1, source_target_pairs={{0,28},{4,8},{8,4},{12,16},{16,12},{20,24},{24,20},{28,0},{1,29},{... | collective-permute-start | bytes 196616 | tf_op jit(solution)/shard_map/ppermute | solution.py:61
  7.8 0.0 collective-permute-start.1
  7.8 2.2 %collective-permute-done.far_ref.refs_1_ = f32[128,128]{1,0:T(8,128)S(1)} collective-permute-done((f32[128,128]{1,0:T(8,128)S(1)}, f32[128,128]{1,0:T(8,128)S(1)}, u32[]{:S(2)}, u32[]{:S(2)}) %collective-permute-start) | collective-permute-done | bytes 65568 | tf_op jit(solution)/shard_map/ppermute | solution.py:61
  10.0 2.0 %collective-permute-done.1.near_ref.refs_2_ = f32[128,128]{1,0:T(8,128)S(1)} collective-permute-done((f32[128,128]{1,0:T(8,128)S(1)}, f32[128,128]{1,0:T(8,128)S(1)}, u32[]{:S(2)}, u32[]{:S(2)}) %collective-permute-start.1) | collective-permute-done | bytes 65568 | tf_op jit(solution)/shard_map/ppermute | solution.py:61
  12.1 0.1 collective-permute-start.6
  12.2 1.6 %collective-permute-start.4 = (f32[192,128]{1,0:T(8,128)S(1)}, f32[192,128]{1,0:T(8,128)S(1)}, u32[]{:S(2)}, u32[]{:S(2)}) collective-permute-start(f32[192,128]{1,0:T(8,128)S(1)} %get-tuple-element.31), channel_id=1, source_target_pairs={{0,3},{1,2},{2,1},{3,0},{4,7},{5,6},{6,5},{7,4},{8,11},{9,10},{10,... | collective-permute-start | bytes 294920 | tf_op jit(solution)/shard_map/ppermute | solution.py:61
  13.8 0.2 collective-permute-start.5
  14.0 2.7 %collective-permute-start.2 = (f32[64,128]{1,0:T(8,128)S(1)}, f32[64,128]{1,0:T(8,128)S(1)}, u32[]{:S(2)}, u32[]{:S(2)}) collective-permute-start(f32[64,128]{1,0:T(8,128)S(1)} %get-tuple-element.29), channel_id=1, source_target_pairs={{0,28},{4,8},{8,4},{12,16},{16,12},{20,24},{24,20},{28,0},{1,29},{... | collective-permute-start | bytes 98312 | tf_op jit(solution)/shard_map/ppermute | solution.py:61
  16.7 0.0 collective-permute-start.3
  17.3 3.3 %collective-permute-done.2.refs_3_ = f32[64,128]{1,0:T(8,128)S(1)} collective-permute-done((f32[64,128]{1,0:T(8,128)S(1)}, f32[64,128]{1,0:T(8,128)S(1)}, u32[]{:S(2)}, u32[]{:S(2)}) %collective-permute-start.2) | collective-permute-done | bytes 32800 | tf_op jit(solution)/shard_map/ppermute | solution.py:61
  20.6 0.3 collective-permute-done.3.refs_4_
  21.0 0.0 collective-permute-done.4.refs_5_
  21.0 0.0 collective-permute-done.5.refs_6_
  21.0 0.0 collective-permute-done.6.refs_7_
  21.0 2.0 %step.1 = (f32[2,16,16,128]{3,2,1,0:T(8,128)S(1)}, f32[16,16,128]{2,1,0:T(8,128)S(1)}, f32[12,24,128]{2,1,0:T(8,128)S(1)}, f32[12,16,128]{2,1,0:T(8,128)S(1)}, f...) custom-call(s32[1]{0:T(128)} %constant.0.clone.1.zero_ref, f32[1]{0:T(128)} %bitcast.4.dt_ref, ...), custom_call_target="tpu_custom_call" | custom-call | tf_op jit(solution)/shard_map/step/pallas_call | solution.py:333
  23.0 3.7 %all-to-all-start = ((f32[32,1,128]{2,1,0:T(1,128)}), f32[32,1,128]{2,1,0:T(1,128)S(1)}, u32[]{:S(2)}, u32[]{:S(2)}) async-start(f32[32,1,128]{2,1,0:T(1,128)} %bitcast.2), calls=%async_computation | async-start | bytes 32768 | tf_op jit(solution)/shard_map/all_to_all | solution.py:365
  26.7 2.0 %carry.1 = (f32[12,12,128]{2,1,0:T(8,128)}, f32[12,12,128]{2,1,0:T(8,128)}, f32[12,12,128]{2,1,0:T(8,128)}, f32[12,12,128]{2,1,0:T(8,128)}, f32[12,12,128]{2,1,0:T(8,128)}) custom-call(s32[1]{0:T(128)} %constant.0.clone.1.zero_ref, f32[1]{0:T(128)} %bitcast.5.dt_ref, f32[2,16,16,128]{3,2,1,0:T(8,128)S(1)} %get-tuple-element.35.refs_0_, ...), custom_call_target="tpu_custom_call" | custom-call | flops 10000000 | bytes 4000000 | tf_op jit(solution)/shard_map/carry/pallas_call | solution.py:351
  28.7 5.1 %all-to-all-done = f32[32,1,128]{2,1,0:T(1,128)S(1)} async-done(((f32[32,1,128]{2,1,0:T(1,128)}), f32[32,1,128]{2,1,0:T(1,128)S(1)}, u32[]{:S(2)}, u32[]{:S(2)}) %all-to-all-start) | async-done | bytes 16416 | tf_op jit(solution)/shard_map/all_to_all | solution.py:365
  33.9 0.6 %reduce_max.9 = f32[]{:T(128)} reduce(f32[32,1,128]{2,1,0:T(1,128)S(1)} %all-to-all-done, f32[]{:T(128)} %constant.2.clone.1), dimensions={0,1,2}, to_apply=%region_0.0 | reduce | flops 4095 | bytes 16392 | tf_op jit(solution)/shard_map/reduce_max | solution.py:366
  (1 shorter events, 0.0 us)
Async XLA Ops:
  1.7 8.3 %collective-permute-start = (f32[128,128]{1,0:T(8,128)S(1)}, f32[128,128]{1,0:T(8,128)S(1)}, u32[]{:S(2)}, u32[]{:S(2)}) collective-permute-start(f32[128,128]{1,0:T(8,128)S(1)} %get-tuple-element.27), channel_id=1, source_target_pairs={{0,28},{4,8},{8,4},{12,16},{16,12},{20,24},{24,20},{28,0},{1,29},{... | collective-permute-start | bytes 196616 | tf_op jit(solution)/shard_map/ppermute | solution.py:61
  7.8 4.3 %collective-permute-start.1 = (f32[128,128]{1,0:T(8,128)S(1)}, f32[128,128]{1,0:T(8,128)S(1)}, u32[]{:S(2)}, u32[]{:S(2)}) collective-permute-start(f32[128,128]{1,0:T(8,128)S(1)} %get-tuple-element.28), channel_id=1, source_target_pairs={{0,4},{4,0},{8,12},{12,8},{16,20},{20,16},{24,28},{28,24},{1,5},{5... | collective-permute-start | bytes 196616 | tf_op jit(solution)/shard_map/ppermute | solution.py:61
  12.1 8.9 %collective-permute-start.6 = (f32[288,128]{1,0:T(8,128)S(1)}, f32[288,128]{1,0:T(8,128)S(1)}, u32[]{:S(2)}, u32[]{:S(2)}) collective-permute-start(f32[288,128]{1,0:T(8,128)S(1)} %get-tuple-element.34), channel_id=1, source_target_pairs={{0,1},{1,0},{2,3},{3,2},{4,5},{5,4},{6,7},{7,6},{8,9},{9,8},{10,11... | collective-permute-start | bytes 442376 | tf_op jit(solution)/shard_map/ppermute | solution.py:61
  12.2 8.8 %collective-permute-start.4 = (f32[192,128]{1,0:T(8,128)S(1)}, f32[192,128]{1,0:T(8,128)S(1)}, u32[]{:S(2)}, u32[]{:S(2)}) collective-permute-start(f32[192,128]{1,0:T(8,128)S(1)} %get-tuple-element.31), channel_id=1, source_target_pairs={{0,3},{1,2},{2,1},{3,0},{4,7},{5,6},{6,5},{7,4},{8,11},{9,10},{10,... | collective-permute-start | bytes 294920 | tf_op jit(solution)/shard_map/ppermute | solution.py:61
  13.8 7.2 %collective-permute-start.5 = (f32[96,128]{1,0:T(8,128)S(1)}, f32[96,128]{1,0:T(8,128)S(1)}, u32[]{:S(2)}, u32[]{:S(2)}) collective-permute-start(f32[96,128]{1,0:T(8,128)S(1)} %get-tuple-element.33), channel_id=1, source_target_pairs={{0,3},{1,2},{2,1},{3,0},{4,7},{5,6},{6,5},{7,4},{8,11},{9,10},{10,... | collective-permute-start | bytes 147464 | tf_op jit(solution)/shard_map/ppermute | solution.py:61
  14.0 6.6 %collective-permute-start.2 = (f32[64,128]{1,0:T(8,128)S(1)}, f32[64,128]{1,0:T(8,128)S(1)}, u32[]{:S(2)}, u32[]{:S(2)}) collective-permute-start(f32[64,128]{1,0:T(8,128)S(1)} %get-tuple-element.29), channel_id=1, source_target_pairs={{0,28},{4,8},{8,4},{12,16},{16,12},{20,24},{24,20},{28,0},{1,29},{... | collective-permute-start | bytes 98312 | tf_op jit(solution)/shard_map/ppermute | solution.py:61
  16.7 4.3 %collective-permute-start.3 = (f32[64,128]{1,0:T(8,128)S(1)}, f32[64,128]{1,0:T(8,128)S(1)}, u32[]{:S(2)}, u32[]{:S(2)}) collective-permute-start(f32[64,128]{1,0:T(8,128)S(1)} %get-tuple-element.30), channel_id=1, source_target_pairs={{0,4},{4,0},{8,12},{12,8},{16,20},{20,16},{24,28},{28,24},{1,5},{5... | collective-permute-start | bytes 98312 | tf_op jit(solution)/shard_map/ppermute | solution.py:61
  23.0 10.8 %all-to-all-start = ((f32[32,1,128]{2,1,0:T(1,128)}), f32[32,1,128]{2,1,0:T(1,128)S(1)}, u32[]{:S(2)}, u32[]{:S(2)}) async-start(f32[32,1,128]{2,1,0:T(1,128)} %bitcast.2), calls=%async_computation | async-start | bytes 32768 | tf_op jit(solution)/shard_map/all_to_all | solution.py:365

commit v9 on v7

--- a/solution.py
+++ b/solution.py
@@ -1,5 +1,4 @@
 import functools
-import itertools
 
 import jax
 import jax.numpy as jnp
@@ -11,7 +10,7 @@
 DENSITY, ENERGY, XV, YV, ZV = range(5)
 REACH = 4
 NEAR, FAR = "near", "far"
-LINKS = (FAR, NEAR)
+SIDES = (-1, 1)
 TOP = 8
 VMEM = pl.BlockSpec(memory_space=pltpu.VMEM)
 HBM = pl.BlockSpec(memory_space=pltpu.HBM)
@@ -39,23 +38,32 @@
 
 def corner_layers():
     found, offset = [], 0
-    for link in LINKS:
-        for number, (field, past) in enumerate(x_layers()):
-            rows = ghost_rows(field, past)
-            found.append((link, number, field, past, rows, offset))
-            offset += rows
+    for number, (field, past) in enumerate(x_layers()):
+        rows = ghost_rows(field, past)
+        found.append((number, field, past, rows, offset))
+        offset += rows
     return found, -(-offset // 8) * 8
 
 
-def is_low(axis, link):
-    odd = lax.rem(lax.axis_index(axis), 2)
+def is_low(link):
+    odd = lax.rem(lax.axis_index("gy"), 2)
     return odd if link == NEAR else 1 - odd
 
 
-def exchanged(value, axis, link):
-    count = lax.axis_size(axis)
-    partner = [i ^ 1 if link == NEAR else ((i - 1) ^ 1) + 1 for i in range(count)]
-    return lax.ppermute(value, axis, [(i, j % count) for i, j in enumerate(partner)])
+def partner(index, link, count):
+    return index ^ 1 if link == NEAR else (((index - 1) ^ 1) + 1) % count
+
+
+def fetched(value, side=0, link=None):
+    gx, gy = lax.axis_size("gx"), lax.axis_size("gy")
+    if link is None:
+        return lax.ppermute(value, "gx", [((i + side) % gx, i) for i in range(gx)])
+    if not side:
+        return lax.ppermute(value, "gy", [(partner(j, link, gy), j) for j in range(gy)])
+    pairs = [
+        ((i + side) % gx * gy + partner(j, link, gy), i * gy + j) for i in range(gx) for j in range(gy)
+    ]
+    return lax.ppermute(value, ("gx", "gy"), pairs)
 
 
 def pick(flag, one, other):
@@ -63,32 +71,36 @@
 
 
 def pack_kernel(nx, ny, zero_ref, *refs):
-    fields, own, x_edges, y_edges, arrived = refs[:5], refs[5], refs[6:8], refs[8:10], refs[-1]
+    fields, own, x_edges, corners, y_edges, arrived = refs[:5], refs[5], refs[6:8], refs[8:10], refs[10:12], refs[-1]
     zero = zero_ref[0]
+    low = is_low(FAR)
     copies = [pltpu.make_async_copy(fields[field], own.at[field], arrived.at[field]) for field in range(5)]
     for copy in copies:
         copy.start()
     for current, copy in enumerate(copies):
         copy.wait()
-        for link, edge in zip(LINKS, x_edges):
-            low = is_low("gx", link)
-            for number, (field, past) in enumerate(x_layers()):
+        for side, edge, corner in zip(SIDES, x_edges, corners):
+            for number, field, past, rows, offset in corner_layers()[0]:
                 if field == current:
-                    edge[pl.ds(zero + number * ny, ny), :] = own[field, pick(low, past - 1, nx - past)]
-        for link, edge in zip(LINKS, y_edges):
-            low = is_low("gy", link)
+                    column = nx - past if side < 0 else past - 1
+                    edge[pl.ds(zero + number * ny, ny), :] = own[field, column]
+                    corner[pl.ds(zero + offset, rows), :] = own[field, column, pl.ds(pick(low, 0, ny - rows), rows), :]
+        for link, edge in zip((FAR, NEAR), y_edges):
             for field, a, rows, offset in y_layers(nx)[0]:
                 if field == current:
-                    edge[pl.ds(zero + offset, rows), :] = own[field, a, pl.ds(pick(low, 0, ny - rows), rows), :]
-
-
-def corner_kernel(ny, zero_ref, *refs):
-    zero = zero_ref[0]
-    for link_y, out in zip(LINKS, refs[2:]):
-        low = is_low("gy", link_y)
-        for link, number, _, _, rows, offset in corner_layers()[0]:
-            edge = refs[LINKS.index(link)]
-            out[pl.ds(zero + offset, rows), :] = edge[pl.ds(number * ny + pick(low, 0, ny - rows), rows), :]
+                    start = pick(is_low(link), 0, ny - rows)
+                    edge[pl.ds(zero + offset, rows), :] = own[field, a, pl.ds(start, rows), :]
+
+
+def near_kernel(ny, zero_ref, low_ref, high_ref, y_near, *refs):
+    zero, out = zero_ref[0], refs[-1]
+    start = y_near.shape[0]
+    out[0:start, :] = y_near[...]
+    for edge in (low_ref, high_ref):
+        for number, _, _, rows, offset in corner_layers()[0]:
+            first = number * ny + pick(is_low(NEAR), 0, ny - rows)
+            out[pl.ds(zero + (start + offset), rows), :] = edge[pl.ds(first, rows), :]
+        start += corner_layers()[1]
 
 
 def limited(above, below):
@@ -161,7 +173,7 @@
 
 
 def step_kernel(nx, ny, zero_ref, dt_ref, *refs):
-    own, x_edges, y_edges, corners = refs[0], refs[1:3], refs[3:5], refs[5:7]
+    own, x_edges, far_corners, (y_far, near) = refs[0], refs[1:3], refs[3:5], refs[5:7]
     passive, speed, speed_y, speed_z, flows, peak_ref = refs[7:13]
     cells, stress, growth, heat, state, energy_one, swept, work = refs[13:]
     nz = own.shape[-1]
@@ -174,20 +186,22 @@
     for field in range(5):
         for a in range(nx):
             cells[field, a + REACH, pl.ds(TOP, ny), :] = own[field, a]
-    for link, edge in zip(LINKS, x_edges):
-        low = is_low("gx", link)
+    for side, edge in zip(SIDES, x_edges):
         for number, (field, past) in enumerate(x_layers()):
-            column = REACH + pick(low, -past, nx - 1 + past)
+            column = REACH + (-past if side < 0 else nx - 1 + past)
             cells[field, column, pl.ds(TOP, ny), :] = edge[pl.ds(zero + number * ny, ny), :]
-    for link_y, edge, corner in zip(LINKS, y_edges, corners):
-        low_y = is_low("gy", link_y)
+    corner_rows, start = corner_layers()[1], y_layers(nx)[1]
+    near_corners = [(near, start), (near, start + corner_rows)]
+    for link, edge, corners in ((FAR, y_far, [(corner, 0) for corner in far_corners]), (NEAR, near, near_corners)):
+        low = is_low(link)
         for field, a, rows, offset in y_layers(nx)[0]:
-            to = pl.ds(TOP + pick(low_y, -rows, ny), rows)
+            to = pl.ds(TOP + pick(low, -rows, ny), rows)
             cells[field, a + REACH, to, :] = edge[pl.ds(zero + offset, rows), :]
-        for link, _, field, past, rows, offset in corner_layers()[0]:
-            column = REACH + pick(is_low("gx", link), -past, nx - 1 + past)
-            to = pl.ds(TOP + pick(low_y, -rows, ny), rows)
-            cells[field, column, to, :] = corner[pl.ds(zero + offset, rows), :]
+        for side, (corner, start) in zip(SIDES, corners):
+            for _, field, past, rows, offset in corner_layers()[0]:
+                column = REACH + (-past if side < 0 else nx - 1 + past)
+                to = pl.ds(TOP + pick(low, -rows, ny), rows)
+                cells[field, column, to, :] = corner[pl.ds(zero + (start + offset), rows), :]
 
     def at(ref, *index, start, count):
         return ref[(*index, pl.ds(zero + start, count), slice(None))]
@@ -250,7 +264,7 @@
         )
     row = lax.broadcasted_iota(jnp.int32, peak.shape, 0)
     peak = jnp.max(jnp.where(row < ny, peak, 0.0), axis=0, keepdims=True)
-    peak_ref[...] = peak
+    peak_ref[...] = jnp.broadcast_to(peak, peak_ref.shape)
 
 
 def carry_kernel(nx, ny, zero_ref, dt_ref, *refs):
@@ -273,19 +287,6 @@
         copy.wait()
 
 
-def all_max(row):
-    axes = ("gx", "gy")
-    count, stride = lax.axis_size(axes), 1
-    while stride < count:
-        if count & (count - 1):
-            pairs = [(i, (i + stride) % count) for i in range(count)]
-        else:
-            pairs = [(i, i ^ stride) for i in range(count)]
-        row = jnp.maximum(row, lax.ppermute(row, axes, pairs))
-        stride *= 2
-    return row
-
-
 def body(density0, energy0, x_velocity, y_velocity, z_velocity, time_increment):
     nx, ny, nz = density0.shape
     fields = (density0, energy0, x_velocity, y_velocity, z_velocity)
@@ -301,31 +302,33 @@
     def limit(mebibytes):
         return pltpu.CompilerParams(vmem_limit_bytes=mebibytes * 1024 * 1024)
 
-    x_edge, y_edge = array(len(x_layers()) * ny), array(y_layers(nx)[1])
+    x_edge, y_edge, corner = array(len(x_layers()) * ny), array(y_layers(nx)[1]), array(corner_layers()[1])
     own, *edges = pl.pallas_call(
         functools.partial(pack_kernel, nx, ny),
-        out_shape=[array(5, nx, ny), x_edge, x_edge, y_edge, y_edge],
+        out_shape=[array(5, nx, ny), x_edge, x_edge, corner, corner, y_edge, y_edge],
         in_specs=[SMEM] + [HBM] * 5,
-        out_specs=[VMEM] * 5,
+        out_specs=[VMEM] * 7,
         scratch_shapes=[pltpu.SemaphoreType.DMA((5,))],
         compiler_params=limit(4),
         name="pack",
     )(zero, *[pltpu.with_memory_space_constraint(field, pltpu.HBM) for field in fields])
-    edges = [exchanged(edge, axis, link) for edge, (axis, link) in zip(edges, itertools.product(("gx", "gy"), LINKS))]
-    corners = pl.pallas_call(
-        functools.partial(corner_kernel, ny),
-        out_shape=[array(corner_layers()[1])] * 2,
-        in_specs=[SMEM] + [VMEM] * 2,
-        out_specs=[VMEM] * 2,
+    x_edges = [fetched(edge, side) for side, edge in zip(SIDES, edges[0:2])]
+    far_corners = [fetched(edge, side, FAR) for side, edge in zip(SIDES, edges[2:4])]
+    y_far = fetched(edges[4], 0, FAR)
+    near = pl.pallas_call(
+        functools.partial(near_kernel, ny),
+        out_shape=array(y_edge.shape[0] + 2 * corner.shape[0]),
+        in_specs=[SMEM] + [VMEM] * 6,
+        out_specs=VMEM,
         compiler_params=limit(4),
-        name="corners",
-    )(zero, edges[0], edges[1])
-    corners = [exchanged(corner, "gy", link) for corner, link in zip(corners, LINKS)]
+        name="near",
+    )(zero, *x_edges, edges[5], *far_corners, y_far)
+    near = fetched(near, 0, NEAR)
     increment = time_increment.reshape(1)
     passed = [array(2, nx + 4, wide), array(nx + 4, wide), array(nx, wide + 8), array(nx, wide), array(3, nx, ny)]
     *passed, peak = pl.pallas_call(
         functools.partial(step_kernel, nx, ny),
-        out_shape=passed + [array(1)],
+        out_shape=passed + [array(lax.axis_size(("gx", "gy")))],
         in_specs=[SMEM, SMEM] + [VMEM] * 7,
         out_specs=[VMEM] * 6,
         scratch_shapes=[
@@ -340,7 +343,7 @@
         ],
         compiler_params=limit(12),
         name="step",
-    )(zero, increment, own, *edges, *corners)
+    )(zero, increment, own, *x_edges, *far_corners, y_far, near)
     outs = pl.pallas_call(
         functools.partial(carry_kernel, nx, ny),
         out_shape=[array(nx, ny)] * 5,
@@ -355,7 +358,8 @@
         cost_estimate=pl.CostEstimate(flops=10**7, bytes_accessed=4 * 10**6, transcendentals=0),
         name="carry",
     )(zero, increment, *passed)
-    return (*outs, 0.3 / jnp.max(all_max(peak)))
+    peak = lax.all_to_all(peak, ("gx", "gy"), 0, 0, tiled=True)
+    return (*outs, 0.3 / jnp.max(peak))
 
 
 def solution(mesh):

time: 37.1 us -> 35.3 us (0.951)
  waiting for transfers between devices: 17.5 us -> 6.99 us
  starting transfers between devices: 11.1 us -> 19.2 us
  Pallas kernels: 4.56 us -> 5.16 us
    ppermute x11 -> x6, waiting for transfers between devices: 17.5 us -> 1.88 us  [the longest x2 1.52 us: fetched(): return lax.ppermute(value, ('gx', 'gy'), pairs)]
    all_to_all x0 -> x1, starting transfers between devices: none -> 5.95 us  [body(): peak = lax.all_to_all(peak, ('gx', 'gy'), 0, 0, tiled=True)]
    all_to_all x0 -> x1, waiting for transfers between devices: none -> 5.1 us  [body(): peak = lax.all_to_all(peak, ('gx', 'gy'), 0, 0, tiled=True)]
    ppermute x11 -> x6, starting transfers between devices: 11.1 us -> 13.2 us  [the longest x2 6.12 us: fetched(): return lax.ppermute(value, 'gx', [((i + side) % gx, i) for i in range(gx)])]
    pallas_call x1, Pallas kernels: 1.43 us -> 2.01 us  [body(): pl.pallas_call(functools.partial(step_kernel, nx, ny), out_shape=passed +...]
  transfers between devices with their start and end apart: 11 -> 7, of which waited for: 8 -> 3; matrix products, arithmetic and copies ran while one was open for 0% -> 0% of each run, Pallas kernels for 6% -> 6%
where the time goes in v9:
time: 35.3 us; the launch traced here: 35.1 us
  starting transfers between devices  19.2 us (54%)
  waiting for transfers between devices  6.99 us (20%)
  Pallas kernels  5.16 us (15%)
  between operations  3.14 us (9%)
  other arithmetic  0.63 us (2%)
    ppermute x2, starting transfers between devices, fetched(): return lax.ppermute(value, 'gx', [((i + side) % gx, i) for i in range(gx)])  6.12 us
    all_to_all x1, starting transfers between devices, body(): peak = lax.all_to_all(peak, ('gx', 'gy'), 0, 0, tiled=True)  5.95 us
    ppermute x2, starting transfers between devices, fetched(): return lax.ppermute(value, ('gx', 'gy'), pairs)  5.34 us
    all_to_all x1, waiting for transfers between devices, body(): peak = lax.all_to_all(peak, ('gx', 'gy'), 0, 0, tiled=True)  5.1 us
    pallas_call x1, Pallas kernels, body(): pl.pallas_call(functools.partial(carry_kernel, nx, ny), out_shape=[array(...  2.03 us
    pallas_call x1, Pallas kernels, body(): pl.pallas_call(functools.partial(step_kernel, nx, ny), out_shape=passed +...  2.01 us
    ppermute x2, starting transfers between devices, fetched(): lax.ppermute(value, 'gy', [(partner(j, link, gy), j) for j in range(gy)])  1.77 us
    ppermute x2, waiting for transfers between devices, fetched(): return lax.ppermute(value, ('gx', 'gy'), pairs)  1.52 us
  transfers between devices with their start and end apart: 7, of which 3 were waited for; matrix products, arithmetic and copies ran while one was open for 0% of the time, Pallas kernels for 6%

profile of v9, /device:TPU:0, one launch (start us, length us, event | category | flops | bytes accessed | tf_op | source)
XLA Modules:
  0.0 35.1 jit_solution(14886658635462583510)
XLA Ops:
  0.6 1.1 %pack.1 = (f32[5,12,12,128]{3,2,1,0:T(8,128)S(1)}, f32[192,128]{1,0:T(8,128)S(1)}, f32[192,128]{1,0:T(8,128)S(1)}, f32[48,128]{1,0:T(8,128)S(1)}, f32[48,128]{1,...) custom-call(s32[1]{0:T(128)} %constant.0.clone.1.zero_ref, f32[12,12,128]{2,1,0:T(8,128)} %refs_0_.1, ...), custom_call_target="tpu_custom_call" | custom-call | tf_op jit(solution)/shard_map/pack/pallas_call | solution.py:306
  1.7 3.0 %collective-permute-start = (f32[192,128]{1,0:T(8,128)S(1)}, f32[192,128]{1,0:T(8,128)S(1)}, u32[]{:S(2)}, u32[]{:S(2)}) collective-permute-start(f32[192,128]{1,0:T(8,128)S(1)} %get-tuple-element.25), channel_id=1, source_target_pairs={{28,0},{0,4},{4,8},{8,12},{12,16},{16,20},{20,24},{24,28},{29,1},{... | collective-permute-start | bytes 294920 | tf_op jit(solution)/shard_map/ppermute | solution.py:60
  4.7 3.1 %collective-permute-start.1 = (f32[192,128]{1,0:T(8,128)S(1)}, f32[192,128]{1,0:T(8,128)S(1)}, u32[]{:S(2)}, u32[]{:S(2)}) collective-permute-start(f32[192,128]{1,0:T(8,128)S(1)} %get-tuple-element.26), channel_id=1, source_target_pairs={{4,0},{8,4},{12,8},{16,12},{20,16},{24,20},{28,24},{0,28},{5,1},{9... | collective-permute-start | bytes 294920 | tf_op jit(solution)/shard_map/ppermute | solution.py:60
  7.9 0.7 %collective-permute-start.4 = (f32[192,128]{1,0:T(8,128)S(1)}, f32[192,128]{1,0:T(8,128)S(1)}, u32[]{:S(2)}, u32[]{:S(2)}) collective-permute-start(f32[192,128]{1,0:T(8,128)S(1)} %get-tuple-element.29), channel_id=1, source_target_pairs={{3,0},{2,1},{1,2},{0,3},{7,4},{6,5},{5,6},{4,7},{11,8},{10,9},{9,1... | collective-permute-start | bytes 294920 | tf_op jit(solution)/shard_map/ppermute | solution.py:62
  8.5 0.0 collective-permute-start.2
  8.5 5.3 %collective-permute-start.3 = (f32[48,128]{1,0:T(8,128)S(1)}, f32[48,128]{1,0:T(8,128)S(1)}, u32[]{:S(2)}, u32[]{:S(2)}) collective-permute-start(f32[48,128]{1,0:T(8,128)S(1)} %get-tuple-element.28), channel_id=1, source_target_pairs={{7,0},{6,1},{5,2},{4,3},{11,4},{10,5},{9,6},{8,7},{15,8},{14,9},{1... | collective-permute-start | bytes 73736 | tf_op jit(solution)/shard_map/ppermute | solution.py:66
  13.8 1.5 %collective-permute-done.2.refs_0_.refs_3_ = f32[48,128]{1,0:T(8,128)S(1)} collective-permute-done((f32[48,128]{1,0:T(8,128)S(1)}, f32[48,128]{1,0:T(8,128)S(1)}, u32[]{:S(2)}, u32[]{:S(2)}) %collective-permute-start.2) | collective-permute-done | bytes 24608 | tf_op jit(solution)/shard_map/ppermute | solution.py:66
  15.4 0.0 collective-permute-done.3.refs_1_.refs_4_
  15.4 0.0 collective-permute-done.low_ref.refs_1_
  15.4 0.0 collective-permute-done.1.high_ref.refs_2_
  15.4 0.0 collective-permute-done.4.refs_2_.refs_5_
  15.4 1.1 %collective-permute-start.5 = (f32[288,128]{1,0:T(8,128)S(1)}, f32[288,128]{1,0:T(8,128)S(1)}, u32[]{:S(2)}, u32[]{:S(2)}) collective-permute-start(f32[288,128]{1,0:T(8,128)S(1)} %near.1), channel_id=1, source_target_pairs={{1,0},{0,1},{3,2},{2,3},{5,4},{4,5},{7,6},{6,7},{9,8},{8,9},{11,10... | collective-permute-start | bytes 442376 | tf_op jit(solution)/shard_map/ppermute | solution.py:62
  17.2 0.4 %collective-permute-done.5.refs_6_ = f32[288,128]{1,0:T(8,128)S(1)} collective-permute-done((f32[288,128]{1,0:T(8,128)S(1)}, f32[288,128]{1,0:T(8,128)S(1)}, u32[]{:S(2)}, u32[]{:S(2)}) %collective-permute-start.5) | collective-permute-done | bytes 147488 | tf_op jit(solution)/shard_map/ppermute | solution.py:62
  17.5 2.0 %step.1 = (f32[2,16,16,128]{3,2,1,0:T(8,128)S(1)}, f32[16,16,128]{2,1,0:T(8,128)S(1)}, f32[12,24,128]{2,1,0:T(8,128)S(1)}, f32[12,16,128]{2,1,0:T(8,128)S(1)}, f...) custom-call(s32[1]{0:T(128)} %constant.0.clone.1.zero_ref, f32[1]{0:T(128)} %bitcast.4.dt_ref, ...), custom_call_target="tpu_custom_call" | custom-call | tf_op jit(solution)/shard_map/step/pallas_call | solution.py:329
  19.6 5.9 %all-to-all-start = ((f32[32,1,128]{2,1,0:T(1,128)}), f32[32,1,128]{2,1,0:T(1,128)S(1)}, u32[]{:S(2)}, u32[]{:S(2)}) async-start(f32[32,1,128]{2,1,0:T(1,128)} %bitcast.2), calls=%async_computation | async-start | bytes 32768 | tf_op jit(solution)/shard_map/all_to_all | solution.py:361
  25.5 2.0 %carry.1 = (f32[12,12,128]{2,1,0:T(8,128)}, f32[12,12,128]{2,1,0:T(8,128)}, f32[12,12,128]{2,1,0:T(8,128)}, f32[12,12,128]{2,1,0:T(8,128)}, f32[12,12,128]{2,1,0:T(8,128)}) custom-call(s32[1]{0:T(128)} %constant.0.clone.1.zero_ref, f32[1]{0:T(128)} %bitcast.5.dt_ref, f32[2,16,16,128]{3,2,1,0:T(8,128)S(1)} %get-tuple-element.31.refs_0_, ...), custom_call_target="tpu_custom_call" | custom-call | flops 10000000 | bytes 4000000 | tf_op jit(solution)/shard_map/carry/pallas_call | solution.py:347
  27.5 5.1 %all-to-all-done = f32[32,1,128]{2,1,0:T(1,128)S(1)} async-done(((f32[32,1,128]{2,1,0:T(1,128)}), f32[32,1,128]{2,1,0:T(1,128)S(1)}, u32[]{:S(2)}, u32[]{:S(2)}) %all-to-all-start) | async-done | bytes 16416 | tf_op jit(solution)/shard_map/all_to_all | solution.py:361
  32.7 0.6 %reduce_max.9 = f32[]{:T(128)} reduce(f32[32,1,128]{2,1,0:T(1,128)S(1)} %all-to-all-done, f32[]{:T(128)} %constant.2.clone.1), dimensions={0,1,2}, to_apply=%region_0.0 | reduce | flops 4095 | bytes 16392 | tf_op jit(solution)/shard_map/reduce_max | solution.py:362
  (1 shorter events, 0.0 us)
Async XLA Ops:
  1.7 13.6 %collective-permute-start = (f32[192,128]{1,0:T(8,128)S(1)}, f32[192,128]{1,0:T(8,128)S(1)}, u32[]{:S(2)}, u32[]{:S(2)}) collective-permute-start(f32[192,128]{1,0:T(8,128)S(1)} %get-tuple-element.25), channel_id=1, source_target_pairs={{28,0},{0,4},{4,8},{8,12},{12,16},{16,20},{20,24},{24,28},{29,1},{... | collective-permute-start | bytes 294920 | tf_op jit(solution)/shard_map/ppermute | solution.py:60
  4.7 10.6 %collective-permute-start.1 = (f32[192,128]{1,0:T(8,128)S(1)}, f32[192,128]{1,0:T(8,128)S(1)}, u32[]{:S(2)}, u32[]{:S(2)}) collective-permute-start(f32[192,128]{1,0:T(8,128)S(1)} %get-tuple-element.26), channel_id=1, source_target_pairs={{4,0},{8,4},{12,8},{16,12},{20,16},{24,20},{28,24},{0,28},{5,1},{9... | collective-permute-start | bytes 294920 | tf_op jit(solution)/shard_map/ppermute | solution.py:60
  7.9 7.5 %collective-permute-start.4 = (f32[192,128]{1,0:T(8,128)S(1)}, f32[192,128]{1,0:T(8,128)S(1)}, u32[]{:S(2)}, u32[]{:S(2)}) collective-permute-start(f32[192,128]{1,0:T(8,128)S(1)} %get-tuple-element.29), channel_id=1, source_target_pairs={{3,0},{2,1},{1,2},{0,3},{7,4},{6,5},{5,6},{4,7},{11,8},{10,9},{9,1... | collective-permute-start | bytes 294920 | tf_op jit(solution)/shard_map/ppermute | solution.py:62
  8.5 6.8 %collective-permute-start.2 = (f32[48,128]{1,0:T(8,128)S(1)}, f32[48,128]{1,0:T(8,128)S(1)}, u32[]{:S(2)}, u32[]{:S(2)}) collective-permute-start(f32[48,128]{1,0:T(8,128)S(1)} %get-tuple-element.27), channel_id=1, source_target_pairs={{31,0},{30,1},{29,2},{28,3},{3,4},{2,5},{1,6},{0,7},{7,8},{6,9},{5... | collective-permute-start | bytes 73736 | tf_op jit(solution)/shard_map/ppermute | solution.py:66
  8.5 6.9 %collective-permute-start.3 = (f32[48,128]{1,0:T(8,128)S(1)}, f32[48,128]{1,0:T(8,128)S(1)}, u32[]{:S(2)}, u32[]{:S(2)}) collective-permute-start(f32[48,128]{1,0:T(8,128)S(1)} %get-tuple-element.28), channel_id=1, source_target_pairs={{7,0},{6,1},{5,2},{4,3},{11,4},{10,5},{9,6},{8,7},{15,8},{14,9},{1... | collective-permute-start | bytes 73736 | tf_op jit(solution)/shard_map/ppermute | solution.py:66
  15.4 2.1 %collective-permute-start.5 = (f32[288,128]{1,0:T(8,128)S(1)}, f32[288,128]{1,0:T(8,128)S(1)}, u32[]{:S(2)}, u32[]{:S(2)}) collective-permute-start(f32[288,128]{1,0:T(8,128)S(1)} %near.1), channel_id=1, source_target_pairs={{1,0},{0,1},{3,2},{2,3},{5,4},{4,5},{7,6},{6,7},{9,8},{8,9},{11,10... | collective-permute-start | bytes 442376 | tf_op jit(solution)/shard_map/ppermute | solution.py:62
  19.6 13.1 %all-to-all-start = ((f32[32,1,128]{2,1,0:T(1,128)}), f32[32,1,128]{2,1,0:T(1,128)S(1)}, u32[]{:S(2)}, u32[]{:S(2)}) async-start(f32[32,1,128]{2,1,0:T(1,128)} %bitcast.2), calls=%async_computation | async-start | bytes 32768 | tf_op jit(solution)/shard_map/all_to_all | solution.py:361

commit v10 on v6

--- a/solution.py
+++ b/solution.py
@@ -50,9 +50,13 @@
     return found, -(-offset // 8) * 8
 
 
-def pack_kernel(nx, ny, zero_ref, *refs):
+def hidden_zero():
+    return lax.shift_right_logical(lax.axis_index("gx"), 20)
+
+
+def pack_kernel(nx, ny, *refs):
     fields, own, edges, arrived = refs[:5], refs[5], refs[6 : 6 + len(SIDES)], refs[-1]
-    zero = zero_ref[0]
+    zero = hidden_zero()
     copies = [pltpu.make_async_copy(fields[field], own.at[field], arrived.at[field]) for field in range(5)]
     for copy in copies:
         copy.start()
@@ -66,8 +70,8 @@
                     ]
 
 
-def corner_kernel(nx, ny, zero_ref, below_ref, above_ref, low_ref, high_ref):
-    zero = zero_ref[0]
+def corner_kernel(nx, ny, below_ref, above_ref, low_ref, high_ref):
+    zero = hidden_zero()
     held = {
         (side_x, field, a): (ref, offset)
         for side_x, ref in ((-1, below_ref), (1, above_ref))
@@ -148,12 +152,12 @@
     return final
 
 
-def step_kernel(nx, ny, zero_ref, dt_ref, *refs):
+def step_kernel(nx, ny, dt_ref, *refs):
     own, halos = refs[0], refs[1:7]
-    passive, speed, speed_y, speed_z, flows, peak_ref = refs[7:13]
+    passive, speed, speed_y, speed_z, flows, increment_ref = refs[7:13]
     cells, stress, growth, heat, state, energy_one, swept, work = refs[13:]
     nz = own.shape[-1]
-    zero = zero_ref[0]
+    zero = hidden_zero()
     dt = dt_ref[0]
     half = 0.5 * dt
     wide = ny + 4
@@ -230,13 +234,13 @@
         )
     row = lax.broadcasted_iota(jnp.int32, peak.shape, 0)
     peak = jnp.max(jnp.where(row < ny, peak, 0.0), axis=0, keepdims=True)
-    peak_ref[...] = jnp.broadcast_to(peak, peak_ref.shape)
-
-
-def carry_kernel(nx, ny, zero_ref, dt_ref, *refs):
+    increment_ref[...] = jnp.broadcast_to(0.3 / peak, increment_ref.shape)
+
+
+def carry_kernel(nx, ny, dt_ref, *refs):
     state, speed, speed_y, speed_z, flows, density_out, energy_out = refs[:7]
     flow_outs, swept, work, written = refs[7:10], refs[10], refs[11], refs[12]
-    zero = zero_ref[0]
+    zero = hidden_zero()
     half = 0.5 * dt_ref[0]
     wide = ny + 4
     copies = [pltpu.make_async_copy(flows.at[k], flow_outs[k], written.at[k]) for k in range(3)]
@@ -262,7 +266,6 @@
 def body(density0, energy0, x_velocity, y_velocity, z_velocity, time_increment):
     nx, ny, nz = density0.shape
     fields = (density0, energy0, x_velocity, y_velocity, z_velocity)
-    zero = jnp.zeros((1,), jnp.int32)
     wide, tall = ny + 4, ny + 12
 
     def array(*shape):
@@ -277,29 +280,29 @@
     own, *edges = pl.pallas_call(
         functools.partial(pack_kernel, nx, ny),
         out_shape=[array(5, nx, ny)] + [array(segments(side, nx, ny)[1]) for side in SIDES],
-        in_specs=[SMEM] + [HBM] * 5,
+        in_specs=[HBM] * 5,
         out_specs=[VMEM] * (1 + len(SIDES)),
         scratch_shapes=[pltpu.SemaphoreType.DMA((5,))],
         compiler_params=limit(4),
         name="pack",
-    )(zero, *[pltpu.with_memory_space_constraint(field, pltpu.HBM) for field in fields])
+    )(*[pltpu.with_memory_space_constraint(field, pltpu.HBM) for field in fields])
     edges = [shifted(edge, side) for edge, side in zip(edges, SIDES)]
     corners = pl.pallas_call(
         functools.partial(corner_kernel, nx, ny),
         out_shape=[array(corner_segments(1, nx, ny)[1])] * 2,
-        in_specs=[SMEM] + [VMEM] * 2,
+        in_specs=[VMEM] * 2,
         out_specs=[VMEM] * 2,
         compiler_params=limit(4),
         name="corners",
-    )(zero, edges[0], edges[1])
+    )(edges[0], edges[1])
     corners = [shifted(corner, (0, side_y)) for corner, side_y in zip(corners, (-1, 1))]
     count = lax.axis_size(("gx", "gy"))
     increment = time_increment.reshape(1)
     passed = [array(2, nx + 4, wide), array(nx + 4, wide), array(nx, wide + 8), array(nx, wide), array(3, nx, ny)]
-    *passed, peak = pl.pallas_call(
+    *passed, smallest = pl.pallas_call(
         functools.partial(step_kernel, nx, ny),
         out_shape=passed + [array(count)],
-        in_specs=[SMEM, SMEM] + [VMEM] * 7,
+        in_specs=[SMEM] + [VMEM] * 7,
         out_specs=[VMEM] * 6,
         scratch_shapes=[
             scratch(5, nx + 8, ny + 20),
@@ -313,11 +316,11 @@
         ],
         compiler_params=limit(12),
         name="step",
-    )(zero, increment, own, *edges, *corners)
+    )(increment, own, *edges, *corners)
     outs = pl.pallas_call(
         functools.partial(carry_kernel, nx, ny),
         out_shape=[array(nx, ny)] * 5,
-        in_specs=[SMEM, SMEM] + [VMEM] * 5,
+        in_specs=[SMEM] + [VMEM] * 5,
         out_specs=[VMEM] * 2 + [HBM] * 3,
         scratch_shapes=[
             scratch(2, nx, wide + 8),
@@ -327,9 +330,8 @@
         compiler_params=limit(8),
         cost_estimate=pl.CostEstimate(flops=10**7, bytes_accessed=4 * 10**6, transcendentals=0),
         name="carry",
-    )(zero, increment, *passed)
-    peak = lax.all_to_all(peak, ("gx", "gy"), 0, 0, tiled=True)
-    return (*outs, 0.3 / jnp.max(peak))
+    )(increment, *passed)
+    return (*outs, jnp.min(lax.all_to_all(smallest, ("gx", "gy"), 0, 0, tiled=True)))
 
 
 def solution(mesh):

time: 32.2 us -> 30.3 us (0.941)
  between operations: 3.16 us -> 1.34 us
    reduce_min x0 -> x1, other arithmetic: none -> 0.63 us  [body(): jnp.min(lax.all_to_all(smallest, ('gx', 'gy'), 0, 0, tiled=True))]
    reduce_max x1 -> x0, other arithmetic: 0.63 us -> none  [body(): return (*outs, 0.3 / jnp.max(peak))]
  transfers between devices with their start and end apart: 7 -> 7, of which waited for: 4 -> 4; matrix products, arithmetic and copies ran while one was open for 0% -> 0% of each run, Pallas kernels for 6% -> 7%
where the time goes in v10:
time: 30.3 us; the launch traced here: 30.1 us
  starting transfers between devices  15 us (50%)
  waiting for transfers between devices  8.08 us (27%)
  Pallas kernels  5.06 us (17%)
  between operations  1.34 us (4%)
  other arithmetic  0.63 us (2%)
    ppermute x6, starting transfers between devices, shifted(): lax.ppermute(value, axis, [((i + step) % count, i) for i in range(count)])  9.66 us
    all_to_all x1, starting transfers between devices, body(): lax.all_to_all(smallest, ('gx', 'gy'), 0, 0, tiled=True)  5.37 us
    all_to_all x1, waiting for transfers between devices, body(): lax.all_to_all(smallest, ('gx', 'gy'), 0, 0, tiled=True)  5.11 us
    ppermute x6, waiting for transfers between devices, shifted(): lax.ppermute(value, axis, [((i + step) % count, i) for i in range(count)])  2.98 us
    pallas_call x1, Pallas kernels, body(): pl.pallas_call(functools.partial(carry_kernel, nx, ny), out_shape=[array(...  2.03 us
    pallas_call x1, Pallas kernels, body(): pl.pallas_call(functools.partial(step_kernel, nx, ny), out_shape=passed +...  1.92 us
    pallas_call x1, Pallas kernels, body(): pl.pallas_call(functools.partial(pack_kernel, nx, ny), out_shape=[array(5...  1.09 us
    reduce_min x1, other arithmetic, body(): jnp.min(lax.all_to_all(smallest, ('gx', 'gy'), 0, 0, tiled=True))  0.63 us
  transfers between devices with their start and end apart: 7, of which 4 were waited for; matrix products, arithmetic and copies ran while one was open for 0% of the time, Pallas kernels for 7%

profile of v10, /device:TPU:0, one launch (start us, length us, event | category | flops | bytes accessed | tf_op | source)
XLA Modules:
  0.0 30.1 jit_solution(16573653664131838775)
XLA Ops:
  0.6 1.1 %pack.1 = (f32[5,12,12,128]{3,2,1,0:T(8,128)S(1)}, f32[192,128]{1,0:T(8,128)S(1)}, f32[192,128]{1,0:T(8,128)S(1)}, f32[192,128]{1,0:T(8,128)S(1)}, f32[192,128]{1,0:T(8,128)S(1)}) custom-call(f32[12,12,128]{2,1,0:T(8,128)} %refs_0_.1, f32[12,12,128]{2,1,0:T(8,128)} %refs_1_.1, f32[12,12,128]{2,1,0:T(8,128)} %refs_2_.1, f32[12,12,128]{2,1,0:T(8,128)} %refs_3_.1, ...), custom_call_target="tpu_custom_call" | custom-call | tf_op jit(solution)/shard_map/pack/pallas_call | solution.py:280
  1.7 3.0 %collective-permute-start = (f32[192,128]{1,0:T(8,128)S(1)}, f32[192,128]{1,0:T(8,128)S(1)}, u32[]{:S(2)}, u32[]{:S(2)}) collective-permute-start(f32[192,128]{1,0:T(8,128)S(1)} %get-tuple-element.25), channel_id=1, source_target_pairs={{28,0},{0,4},{4,8},{8,12},{12,16},{16,20},{20,24},{24,28},{29,1},{... | collective-permute-start | bytes 294920 | tf_op jit(solution)/shard_map/ppermute | solution.py:263
  4.7 3.1 %collective-permute-start.1 = (f32[192,128]{1,0:T(8,128)S(1)}, f32[192,128]{1,0:T(8,128)S(1)}, u32[]{:S(2)}, u32[]{:S(2)}) collective-permute-start(f32[192,128]{1,0:T(8,128)S(1)} %get-tuple-element.26), channel_id=1, source_target_pairs={{4,0},{8,4},{12,8},{16,12},{20,16},{24,20},{28,24},{0,28},{5,1},{9... | collective-permute-start | bytes 294920 | tf_op jit(solution)/shard_map/ppermute | solution.py:263
  7.9 0.0 collective-permute-start.2
  7.9 1.7 %collective-permute-start.3 = (f32[192,128]{1,0:T(8,128)S(1)}, f32[192,128]{1,0:T(8,128)S(1)}, u32[]{:S(2)}, u32[]{:S(2)}) collective-permute-start(f32[192,128]{1,0:T(8,128)S(1)} %get-tuple-element.28), channel_id=1, source_target_pairs={{1,0},{2,1},{3,2},{0,3},{5,4},{6,5},{7,6},{4,7},{9,8},{10,9},{11,1... | collective-permute-start | bytes 294920 | tf_op jit(solution)/shard_map/ppermute | solution.py:263
  9.6 1.1 %collective-permute-done.below_ref.refs_1_ = f32[192,128]{1,0:T(8,128)S(1)} collective-permute-done((f32[192,128]{1,0:T(8,128)S(1)}, f32[192,128]{1,0:T(8,128)S(1)}, u32[]{:S(2)}, u32[]{:S(2)}) %collective-permute-start) | collective-permute-done | bytes 98336 | tf_op jit(solution)/shard_map/ppermute | solution.py:263
  10.7 0.8 %collective-permute-done.1.above_ref.refs_2_ = f32[192,128]{1,0:T(8,128)S(1)} collective-permute-done((f32[192,128]{1,0:T(8,128)S(1)}, f32[192,128]{1,0:T(8,128)S(1)}, u32[]{:S(2)}, u32[]{:S(2)}) %collective-permute-start.1) | collective-permute-done | bytes 98336 | tf_op jit(solution)/shard_map/ppermute | solution.py:263
  11.5 0.1 collective-permute-start.4
  11.6 1.7 %collective-permute-start.5 = (f32[96,128]{1,0:T(8,128)S(1)}, f32[96,128]{1,0:T(8,128)S(1)}, u32[]{:S(2)}, u32[]{:S(2)}) collective-permute-start(f32[96,128]{1,0:T(8,128)S(1)} %get-tuple-element.30), channel_id=1, source_target_pairs={{1,0},{2,1},{3,2},{0,3},{5,4},{6,5},{7,6},{4,7},{9,8},{10,9},{11,1... | collective-permute-start | bytes 147464 | tf_op jit(solution)/shard_map/ppermute | solution.py:263
  13.9 0.0 collective-permute-done.2.refs_3_
  14.0 0.0 collective-permute-done.3.refs_4_
  14.0 1.1 %collective-permute-done.4.refs_5_ = f32[96,128]{1,0:T(8,128)S(1)} collective-permute-done((f32[96,128]{1,0:T(8,128)S(1)}, f32[96,128]{1,0:T(8,128)S(1)}, u32[]{:S(2)}, u32[]{:S(2)}) %collective-permute-start.4) | collective-permute-done | bytes 49184 | tf_op jit(solution)/shard_map/ppermute | solution.py:263
  15.1 0.0 collective-permute-done.5.refs_6_
  15.1 1.9 %step.1 = (f32[2,16,16,128]{3,2,1,0:T(8,128)S(1)}, f32[16,16,128]{2,1,0:T(8,128)S(1)}, f32[12,24,128]{2,1,0:T(8,128)S(1)}, f32[12,16,128]{2,1,0:T(8,128)S(1)}, f...) custom-call(f32[1]{0:T(128)} %bitcast.4.dt_ref, f32[5,12,12,128]{3,2,1,0:T(8,128)S(1)} %get-tuple-element.24.refs_0_, ...), custom_call_target="tpu_custom_call" | custom-call | tf_op jit(solution)/shard_map/step/pallas_call | solution.py:302
  17.0 5.4 %all-to-all-start = ((f32[32,1,128]{2,1,0:T(1,128)}), f32[32,1,128]{2,1,0:T(1,128)S(1)}, u32[]{:S(2)}, u32[]{:S(2)}) async-start(f32[32,1,128]{2,1,0:T(1,128)} %bitcast.2), calls=%async_computation | async-start | bytes 32768 | tf_op jit(solution)/shard_map/all_to_all | solution.py:334
  22.4 2.0 %carry.1 = (f32[12,12,128]{2,1,0:T(8,128)}, f32[12,12,128]{2,1,0:T(8,128)}, f32[12,12,128]{2,1,0:T(8,128)}, f32[12,12,128]{2,1,0:T(8,128)}, f32[12,12,128]{2,1,0:T(8,128)}) custom-call(f32[1]{0:T(128)} %bitcast.5.dt_ref, f32[2,16,16,128]{3,2,1,0:T(8,128)S(1)} %get-tuple-element.31.refs_0_, f32[16,16,128]{2,1,0:T(8,128)S(1)} %get-tuple-element.32.refs_1_, ...), custom_call_target="tpu_custom_call" | custom-call | flops 10000000 | bytes 4000000 | tf_op jit(solution)/shard_map/carry/pallas_call | solution.py:320
  24.4 5.1 %all-to-all-done = f32[32,1,128]{2,1,0:T(1,128)S(1)} async-done(((f32[32,1,128]{2,1,0:T(1,128)}), f32[32,1,128]{2,1,0:T(1,128)S(1)}, u32[]{:S(2)}, u32[]{:S(2)}) %all-to-all-start) | async-done | bytes 16416 | tf_op jit(solution)/shard_map/all_to_all | solution.py:334
  29.5 0.6 %reduce_min.9 = f32[]{:T(128)} reduce(f32[32,1,128]{2,1,0:T(1,128)S(1)} %all-to-all-done, f32[]{:T(128)} %constant.0.clone.1), dimensions={0,1,2}, to_apply=%region_0.0 | reduce | flops 4095 | bytes 16392 | tf_op jit(solution)/shard_map/reduce_min | solution.py:334
  (1 shorter events, 0.0 us)
Async XLA Ops:
  1.7 9.0 %collective-permute-start = (f32[192,128]{1,0:T(8,128)S(1)}, f32[192,128]{1,0:T(8,128)S(1)}, u32[]{:S(2)}, u32[]{:S(2)}) collective-permute-start(f32[192,128]{1,0:T(8,128)S(1)} %get-tuple-element.25), channel_id=1, source_target_pairs={{28,0},{0,4},{4,8},{8,12},{12,16},{16,20},{20,24},{24,28},{29,1},{... | collective-permute-start | bytes 294920 | tf_op jit(solution)/shard_map/ppermute | solution.py:263
  4.7 6.7 %collective-permute-start.1 = (f32[192,128]{1,0:T(8,128)S(1)}, f32[192,128]{1,0:T(8,128)S(1)}, u32[]{:S(2)}, u32[]{:S(2)}) collective-permute-start(f32[192,128]{1,0:T(8,128)S(1)} %get-tuple-element.26), channel_id=1, source_target_pairs={{4,0},{8,4},{12,8},{16,12},{20,16},{24,20},{28,24},{0,28},{5,1},{9... | collective-permute-start | bytes 294920 | tf_op jit(solution)/shard_map/ppermute | solution.py:263
  7.9 6.1 %collective-permute-start.2 = (f32[192,128]{1,0:T(8,128)S(1)}, f32[192,128]{1,0:T(8,128)S(1)}, u32[]{:S(2)}, u32[]{:S(2)}) collective-permute-start(f32[192,128]{1,0:T(8,128)S(1)} %get-tuple-element.27), channel_id=1, source_target_pairs={{3,0},{0,1},{1,2},{2,3},{7,4},{4,5},{5,6},{6,7},{11,8},{8,9},{9,10... | collective-permute-start | bytes 294920 | tf_op jit(solution)/shard_map/ppermute | solution.py:263
  7.9 6.1 %collective-permute-start.3 = (f32[192,128]{1,0:T(8,128)S(1)}, f32[192,128]{1,0:T(8,128)S(1)}, u32[]{:S(2)}, u32[]{:S(2)}) collective-permute-start(f32[192,128]{1,0:T(8,128)S(1)} %get-tuple-element.28), channel_id=1, source_target_pairs={{1,0},{2,1},{3,2},{0,3},{5,4},{6,5},{7,6},{4,7},{9,8},{10,9},{11,1... | collective-permute-start | bytes 294920 | tf_op jit(solution)/shard_map/ppermute | solution.py:263
  11.5 3.6 %collective-permute-start.4 = (f32[96,128]{1,0:T(8,128)S(1)}, f32[96,128]{1,0:T(8,128)S(1)}, u32[]{:S(2)}, u32[]{:S(2)}) collective-permute-start(f32[96,128]{1,0:T(8,128)S(1)} %get-tuple-element.29), channel_id=1, source_target_pairs={{3,0},{0,1},{1,2},{2,3},{7,4},{4,5},{5,6},{6,7},{11,8},{8,9},{9,10... | collective-permute-start | bytes 147464 | tf_op jit(solution)/shard_map/ppermute | solution.py:263
  11.6 3.5 %collective-permute-start.5 = (f32[96,128]{1,0:T(8,128)S(1)}, f32[96,128]{1,0:T(8,128)S(1)}, u32[]{:S(2)}, u32[]{:S(2)}) collective-permute-start(f32[96,128]{1,0:T(8,128)S(1)} %get-tuple-element.30), channel_id=1, source_target_pairs={{1,0},{2,1},{3,2},{0,3},{5,4},{6,5},{7,6},{4,7},{9,8},{10,9},{11,1... | collective-permute-start | bytes 147464 | tf_op jit(solution)/shard_map/ppermute | solution.py:263
  17.0 12.5 %all-to-all-start = ((f32[32,1,128]{2,1,0:T(1,128)}), f32[32,1,128]{2,1,0:T(1,128)S(1)}, u32[]{:S(2)}, u32[]{:S(2)}) async-start(f32[32,1,128]{2,1,0:T(1,128)} %bitcast.2), calls=%async_computation | async-start | bytes 32768 | tf_op jit(solution)/shard_map/all_to_all | solution.py:334

commit v11 on v10

--- a/solution.py
+++ b/solution.py
@@ -234,10 +234,10 @@
         )
     row = lax.broadcasted_iota(jnp.int32, peak.shape, 0)
     peak = jnp.max(jnp.where(row < ny, peak, 0.0), axis=0, keepdims=True)
-    increment_ref[...] = jnp.broadcast_to(0.3 / peak, increment_ref.shape)
-
-
-def carry_kernel(nx, ny, dt_ref, *refs):
+    increment_ref[...] = 0.3 / peak
+
+
+def carry_kernel(nx, ny, dt_ref, _, *refs):
     state, speed, speed_y, speed_z, flows, density_out, energy_out = refs[:7]
     flow_outs, swept, work, written = refs[7:10], refs[10], refs[11], refs[12]
     zero = hidden_zero()
@@ -261,6 +261,19 @@
     axis, step = ("gx", side[0]) if side[0] else ("gy", side[1])
     count = lax.axis_size(axis)
     return lax.ppermute(value, axis, [((i + step) % count, i) for i in range(count)])
+
+
+def pair_min(row):
+    axes = ("gx", "gy")
+    return jnp.minimum(row, lax.ppermute(row, axes, [(i, i ^ 1) for i in range(lax.axis_size(axes))]))
+
+
+def global_min(row):
+    axes = ("gx", "gy")
+    count = lax.axis_size(axes)
+    rows = jnp.broadcast_to(row, (count // 2, row.shape[-1]))
+    groups = [list(range(first, count, 2)) for first in range(2)]
+    return jnp.min(lax.all_to_all(rows, axes, 0, 0, axis_index_groups=groups, tiled=True))
 
 
 def body(density0, energy0, x_velocity, y_velocity, z_velocity, time_increment):
@@ -296,12 +309,11 @@
         name="corners",
     )(edges[0], edges[1])
     corners = [shifted(corner, (0, side_y)) for corner, side_y in zip(corners, (-1, 1))]
-    count = lax.axis_size(("gx", "gy"))
     increment = time_increment.reshape(1)
     passed = [array(2, nx + 4, wide), array(nx + 4, wide), array(nx, wide + 8), array(nx, wide), array(3, nx, ny)]
     *passed, smallest = pl.pallas_call(
         functools.partial(step_kernel, nx, ny),
-        out_shape=passed + [array(count)],
+        out_shape=passed + [array(1)],
         in_specs=[SMEM] + [VMEM] * 7,
         out_specs=[VMEM] * 6,
         scratch_shapes=[
@@ -317,10 +329,11 @@
         compiler_params=limit(12),
         name="step",
     )(increment, own, *edges, *corners)
+    smallest = pair_min(smallest)
     outs = pl.pallas_call(
         functools.partial(carry_kernel, nx, ny),
         out_shape=[array(nx, ny)] * 5,
-        in_specs=[SMEM] + [VMEM] * 5,
+        in_specs=[SMEM] + [VMEM] * 6,
         out_specs=[VMEM] * 2 + [HBM] * 3,
         scratch_shapes=[
             scratch(2, nx, wide + 8),
@@ -330,8 +343,8 @@
         compiler_params=limit(8),
         cost_estimate=pl.CostEstimate(flops=10**7, bytes_accessed=4 * 10**6, transcendentals=0),
         name="carry",
-    )(increment, *passed)
-    return (*outs, jnp.min(lax.all_to_all(smallest, ("gx", "gy"), 0, 0, tiled=True)))
+    )(increment, smallest, *passed)
+    return (*outs, global_min(smallest))
 
 
 def solution(mesh):

time: 30.3 us -> 32.7 us (1.079)
  starting transfers between devices: 15 us -> 16.5 us
  waiting for transfers between devices: 8.08 us -> 9.03 us
  Pallas kernels: 5.06 us -> 4.45 us
  local copies, waits for them, and re-layouts: 0 us -> 0.6 us
    ppermute x0 -> x1, starting transfers between devices: none -> 1.67 us  [pair_min(): lax.ppermute(row, axes, [(i, i ^ 1) for i in range(lax.axis_size(axes))])]
    ppermute x0 -> x1, waiting for transfers between devices: none -> 0.82 us  [pair_min(): lax.ppermute(row, axes, [(i, i ^ 1) for i in range(lax.axis_size(axes))])]
    pallas_call x1, Pallas kernels: 1.92 us -> 1.31 us  [body(): pl.pallas_call(functools.partial(step_kernel, nx, ny), out_shape=passed +...]
    broadcast_in_dim x0 -> x1, local copies, waits for them, and re-layouts: none -> 0.6 us  [global_min(): rows = jnp.broadcast_to(row, (count // 2, row.shape[-1]))]
  transfers between devices with their start and end apart: 7 -> 8, of which waited for: 4 -> 5; matrix products, arithmetic and copies ran while one was open for 0% -> 0% of each run, Pallas kernels for 7% -> 6%
where the time goes in v11:
time: 32.7 us; the launch traced here: 32.5 us
  starting transfers between devices  16.5 us (50%)
  waiting for transfers between devices  9.03 us (28%)
  Pallas kernels  4.45 us (14%)
  between operations  1.35 us (4%)
  other arithmetic  0.6 us (2%)
  local copies, waits for them, and re-layouts  0.6 us (2%)
    ppermute x6, starting transfers between devices, shifted(): lax.ppermute(value, axis, [((i + step) % count, i) for i in range(count)])  9.66 us
    all_to_all x1, waiting for transfers between devices, global_min(): lax.all_to_all(rows, axes, 0, 0, axis_index_groups=groups, tiled=True)  5.23 us
    all_to_all x1, starting transfers between devices, global_min(): lax.all_to_all(rows, axes, 0, 0, axis_index_groups=groups, tiled=True)  5.18 us
    ppermute x6, waiting for transfers between devices, shifted(): lax.ppermute(value, axis, [((i + step) % count, i) for i in range(count)])  2.98 us
    pallas_call x1, Pallas kernels, body(): pl.pallas_call(functools.partial(carry_kernel, nx, ny), out_shape=[array(...  2.03 us
    ppermute x1, starting transfers between devices, pair_min(): lax.ppermute(row, axes, [(i, i ^ 1) for i in range(lax.axis_size(axes))])  1.67 us
    pallas_call x1, Pallas kernels, body(): pl.pallas_call(functools.partial(step_kernel, nx, ny), out_shape=passed +...  1.31 us
    pallas_call x1, Pallas kernels, body(): pl.pallas_call(functools.partial(pack_kernel, nx, ny), out_shape=[array(5...  1.09 us
  transfers between devices with their start and end apart: 8, of which 5 were waited for; matrix products, arithmetic and copies ran while one was open for 0% of the time, Pallas kernels for 6%

profile of v11, /device:TPU:0, one launch (start us, length us, event | category | flops | bytes accessed | tf_op | source)
XLA Modules:
  0.0 32.5 jit_solution(8911834233219186967)
XLA Ops:
  0.6 1.1 %pack.1 = (f32[5,12,12,128]{3,2,1,0:T(8,128)S(1)}, f32[192,128]{1,0:T(8,128)S(1)}, f32[192,128]{1,0:T(8,128)S(1)}, f32[192,128]{1,0:T(8,128)S(1)}, f32[192,128]{1,0:T(8,128)S(1)}) custom-call(f32[12,12,128]{2,1,0:T(8,128)} %refs_0_.1, f32[12,12,128]{2,1,0:T(8,128)} %refs_1_.1, f32[12,12,128]{2,1,0:T(8,128)} %refs_2_.1, f32[12,12,128]{2,1,0:T(8,128)} %refs_3_.1, ...), custom_call_target="tpu_custom_call" | custom-call | tf_op jit(solution)/shard_map/pack/pallas_call | solution.py:293
  1.7 3.0 %collective-permute-start = (f32[192,128]{1,0:T(8,128)S(1)}, f32[192,128]{1,0:T(8,128)S(1)}, u32[]{:S(2)}, u32[]{:S(2)}) collective-permute-start(f32[192,128]{1,0:T(8,128)S(1)} %get-tuple-element.25), channel_id=1, source_target_pairs={{28,0},{0,4},{4,8},{8,12},{12,16},{16,20},{20,24},{24,28},{29,1},{... | collective-permute-start | bytes 294920 | tf_op jit(solution)/shard_map/ppermute | solution.py:263
  4.7 3.1 %collective-permute-start.1 = (f32[192,128]{1,0:T(8,128)S(1)}, f32[192,128]{1,0:T(8,128)S(1)}, u32[]{:S(2)}, u32[]{:S(2)}) collective-permute-start(f32[192,128]{1,0:T(8,128)S(1)} %get-tuple-element.26), channel_id=1, source_target_pairs={{4,0},{8,4},{12,8},{16,12},{20,16},{24,20},{28,24},{0,28},{5,1},{9... | collective-permute-start | bytes 294920 | tf_op jit(solution)/shard_map/ppermute | solution.py:263
  7.9 0.0 collective-permute-start.2
  7.9 1.7 %collective-permute-start.3 = (f32[192,128]{1,0:T(8,128)S(1)}, f32[192,128]{1,0:T(8,128)S(1)}, u32[]{:S(2)}, u32[]{:S(2)}) collective-permute-start(f32[192,128]{1,0:T(8,128)S(1)} %get-tuple-element.28), channel_id=1, source_target_pairs={{1,0},{2,1},{3,2},{0,3},{5,4},{6,5},{7,6},{4,7},{9,8},{10,9},{11,1... | collective-permute-start | bytes 294920 | tf_op jit(solution)/shard_map/ppermute | solution.py:263
  9.6 1.1 %collective-permute-done.below_ref.refs_1_ = f32[192,128]{1,0:T(8,128)S(1)} collective-permute-done((f32[192,128]{1,0:T(8,128)S(1)}, f32[192,128]{1,0:T(8,128)S(1)}, u32[]{:S(2)}, u32[]{:S(2)}) %collective-permute-start) | collective-permute-done | bytes 98336 | tf_op jit(solution)/shard_map/ppermute | solution.py:263
  10.7 0.8 %collective-permute-done.1.above_ref.refs_2_ = f32[192,128]{1,0:T(8,128)S(1)} collective-permute-done((f32[192,128]{1,0:T(8,128)S(1)}, f32[192,128]{1,0:T(8,128)S(1)}, u32[]{:S(2)}, u32[]{:S(2)}) %collective-permute-start.1) | collective-permute-done | bytes 98336 | tf_op jit(solution)/shard_map/ppermute | solution.py:263
  11.5 0.1 collective-permute-start.4
  11.6 1.7 %collective-permute-start.5 = (f32[96,128]{1,0:T(8,128)S(1)}, f32[96,128]{1,0:T(8,128)S(1)}, u32[]{:S(2)}, u32[]{:S(2)}) collective-permute-start(f32[96,128]{1,0:T(8,128)S(1)} %get-tuple-element.30), channel_id=1, source_target_pairs={{1,0},{2,1},{3,2},{0,3},{5,4},{6,5},{7,6},{4,7},{9,8},{10,9},{11,1... | collective-permute-start | bytes 147464 | tf_op jit(solution)/shard_map/ppermute | solution.py:263
  13.9 0.0 collective-permute-done.2.refs_3_
  14.0 0.0 collective-permute-done.3.refs_4_
  14.0 1.1 %collective-permute-done.4.refs_5_ = f32[96,128]{1,0:T(8,128)S(1)} collective-permute-done((f32[96,128]{1,0:T(8,128)S(1)}, f32[96,128]{1,0:T(8,128)S(1)}, u32[]{:S(2)}, u32[]{:S(2)}) %collective-permute-start.4) | collective-permute-done | bytes 49184 | tf_op jit(solution)/shard_map/ppermute | solution.py:263
  15.1 0.0 collective-permute-done.5.refs_6_
  15.1 1.3 %step.1 = (f32[2,16,16,128]{3,2,1,0:T(8,128)S(1)}, f32[16,16,128]{2,1,0:T(8,128)S(1)}, f32[12,24,128]{2,1,0:T(8,128)S(1)}, f32[12,16,128]{2,1,0:T(8,128)S(1)}, f...) custom-call(f32[1]{0:T(128)} %bitcast.3.dt_ref, f32[5,12,12,128]{3,2,1,0:T(8,128)S(1)} %get-tuple-element.24.refs_0_, ...), custom_call_target="tpu_custom_call" | custom-call | tf_op jit(solution)/shard_map/step/pallas_call | solution.py:314
  16.4 1.7 %collective-permute-start.6 = (f32[1,128]{1,0:T(1,128)S(1)}, f32[1,128]{1,0:T(1,128)S(1)}, u32[]{:S(2)}, u32[]{:S(2)}) collective-permute-start(f32[1,128]{1,0:T(1,128)S(1)} %get-tuple-element.31), channel_id=1, source_target_pairs={{0,1},{1,0},{2,3},{3,2},{4,5},{5,4},{6,7},{7,6},{8,9},{9,8},{10,11... | collective-permute-start | bytes 1544 | tf_op jit(solution)/shard_map/ppermute | solution.py:268
  18.0 0.8 %collective-permute-done.6 = f32[1,128]{1,0:T(1,128)S(1)} collective-permute-done((f32[1,128]{1,0:T(1,128)S(1)}, f32[1,128]{1,0:T(1,128)S(1)}, u32[]{:S(2)}, u32[]{:S(2)}) %collective-permute-start.6) | collective-permute-done | bytes 544 | tf_op jit(solution)/shard_map/ppermute | solution.py:268
  18.9 0.6 %broadcast_in_dim.2 = f32[16,1,128]{2,1,0:T(1,128)} broadcast(f32[128]{0:T(128)S(1)} %bitcast.5), dimensions={2} | broadcast | bytes 8704 | tf_op jit(solution)/shard_map/broadcast_in_dim | solution.py:274
  19.5 5.2 %all-to-all-start = ((f32[16,1,128]{2,1,0:T(1,128)}), f32[16,1,128]{2,1,0:T(1,128)S(1)}, u32[]{:S(2)}, u32[]{:S(2)}) async-start(f32[16,1,128]{2,1,0:T(1,128)} %broadcast_in_dim.2), calls=%async_computation | async-start | bytes 16384 | tf_op jit(solution)/shard_map/all_to_all | solution.py:276
  24.7 2.0 %carry.1 = (f32[12,12,128]{2,1,0:T(8,128)}, f32[12,12,128]{2,1,0:T(8,128)}, f32[12,12,128]{2,1,0:T(8,128)}, f32[12,12,128]{2,1,0:T(8,128)}, f32[12,12,128]{2,1,0:T(8,128)}) custom-call(f32[1]{0:T(128)} %bitcast.4.dt_ref, f32[1,128]{1,0:T(1,128)S(1)} %min.5._, f32[2,16,16,128]{3,2,1,0:T(8,128)S(1)} %get-tuple-element.32.refs_0_, ...), custom_call_target="tpu_custom_call" | custom-call | flops 10000000 | bytes 4000000 | tf_op jit(solution)/shard_map/carry/pallas_call | solution.py:333
  26.7 5.2 %all-to-all-done = f32[16,1,128]{2,1,0:T(1,128)S(1)} async-done(((f32[16,1,128]{2,1,0:T(1,128)}), f32[16,1,128]{2,1,0:T(1,128)S(1)}, u32[]{:S(2)}, u32[]{:S(2)}) %all-to-all-start) | async-done | bytes 8224 | tf_op jit(solution)/shard_map/all_to_all | solution.py:276
  31.9 0.6 %reduce_min.9 = f32[]{:T(128)} reduce(f32[16,1,128]{2,0,1:T(8,128)S(1)} %bitcast.6, f32[]{:T(128)} %constant.0.clone.1), dimensions={0,1,2}, to_apply=%region_0.0 | reduce | flops 2047 | bytes 8200 | tf_op jit(solution)/shard_map/reduce_min | solution.py:276
  (2 shorter events, 0.0 us)
Async XLA Ops:
  1.7 9.0 %collective-permute-start = (f32[192,128]{1,0:T(8,128)S(1)}, f32[192,128]{1,0:T(8,128)S(1)}, u32[]{:S(2)}, u32[]{:S(2)}) collective-permute-start(f32[192,128]{1,0:T(8,128)S(1)} %get-tuple-element.25), channel_id=1, source_target_pairs={{28,0},{0,4},{4,8},{8,12},{12,16},{16,20},{20,24},{24,28},{29,1},{... | collective-permute-start | bytes 294920 | tf_op jit(solution)/shard_map/ppermute | solution.py:263
  4.7 6.7 %collective-permute-start.1 = (f32[192,128]{1,0:T(8,128)S(1)}, f32[192,128]{1,0:T(8,128)S(1)}, u32[]{:S(2)}, u32[]{:S(2)}) collective-permute-start(f32[192,128]{1,0:T(8,128)S(1)} %get-tuple-element.26), channel_id=1, source_target_pairs={{4,0},{8,4},{12,8},{16,12},{20,16},{24,20},{28,24},{0,28},{5,1},{9... | collective-permute-start | bytes 294920 | tf_op jit(solution)/shard_map/ppermute | solution.py:263
  7.9 6.1 %collective-permute-start.2 = (f32[192,128]{1,0:T(8,128)S(1)}, f32[192,128]{1,0:T(8,128)S(1)}, u32[]{:S(2)}, u32[]{:S(2)}) collective-permute-start(f32[192,128]{1,0:T(8,128)S(1)} %get-tuple-element.27), channel_id=1, source_target_pairs={{3,0},{0,1},{1,2},{2,3},{7,4},{4,5},{5,6},{6,7},{11,8},{8,9},{9,10... | collective-permute-start | bytes 294920 | tf_op jit(solution)/shard_map/ppermute | solution.py:263
  7.9 6.1 %collective-permute-start.3 = (f32[192,128]{1,0:T(8,128)S(1)}, f32[192,128]{1,0:T(8,128)S(1)}, u32[]{:S(2)}, u32[]{:S(2)}) collective-permute-start(f32[192,128]{1,0:T(8,128)S(1)} %get-tuple-element.28), channel_id=1, source_target_pairs={{1,0},{2,1},{3,2},{0,3},{5,4},{6,5},{7,6},{4,7},{9,8},{10,9},{11,1... | collective-permute-start | bytes 294920 | tf_op jit(solution)/shard_map/ppermute | solution.py:263
  11.5 3.6 %collective-permute-start.4 = (f32[96,128]{1,0:T(8,128)S(1)}, f32[96,128]{1,0:T(8,128)S(1)}, u32[]{:S(2)}, u32[]{:S(2)}) collective-permute-start(f32[96,128]{1,0:T(8,128)S(1)} %get-tuple-element.29), channel_id=1, source_target_pairs={{3,0},{0,1},{1,2},{2,3},{7,4},{4,5},{5,6},{6,7},{11,8},{8,9},{9,10... | collective-permute-start | bytes 147464 | tf_op jit(solution)/shard_map/ppermute | solution.py:263
  11.6 3.5 %collective-permute-start.5 = (f32[96,128]{1,0:T(8,128)S(1)}, f32[96,128]{1,0:T(8,128)S(1)}, u32[]{:S(2)}, u32[]{:S(2)}) collective-permute-start(f32[96,128]{1,0:T(8,128)S(1)} %get-tuple-element.30), channel_id=1, source_target_pairs={{1,0},{2,1},{3,2},{0,3},{5,4},{6,5},{7,6},{4,7},{9,8},{10,9},{11,1... | collective-permute-start | bytes 147464 | tf_op jit(solution)/shard_map/ppermute | solution.py:263
  16.4 2.5 %collective-permute-start.6 = (f32[1,128]{1,0:T(1,128)S(1)}, f32[1,128]{1,0:T(1,128)S(1)}, u32[]{:S(2)}, u32[]{:S(2)}) collective-permute-start(f32[1,128]{1,0:T(1,128)S(1)} %get-tuple-element.31), channel_id=1, source_target_pairs={{0,1},{1,0},{2,3},{3,2},{4,5},{5,4},{6,7},{7,6},{8,9},{9,8},{10,11... | collective-permute-start | bytes 1544 | tf_op jit(solution)/shard_map/ppermute | solution.py:268
  19.5 12.5 %all-to-all-start = ((f32[16,1,128]{2,1,0:T(1,128)}), f32[16,1,128]{2,1,0:T(1,128)S(1)}, u32[]{:S(2)}, u32[]{:S(2)}) async-start(f32[16,1,128]{2,1,0:T(1,128)} %broadcast_in_dim.2), calls=%async_computation | async-start | bytes 16384 | tf_op jit(solution)/shard_map/all_to_all | solution.py:276

commit v12 on v10

--- a/solution.py
+++ b/solution.py
@@ -8,79 +8,124 @@
 from jax.sharding import PartitionSpec as P
 
 DENSITY, ENERGY, XV, YV, ZV = range(5)
-REACH = 4
-SIDES = ((-1, 0), (1, 0), (0, -1), (0, 1))
 TOP = 8
+LEFT = 3
+SIDES = (-1, 1)
+NEAR, FAR = "near", "far"
+LINKS = (FAR, NEAR)
+EDGE_KINDS = 4
 VMEM = pl.BlockSpec(memory_space=pltpu.VMEM)
 HBM = pl.BlockSpec(memory_space=pltpu.HBM)
 SMEM = pl.BlockSpec(memory_space=pltpu.SMEM)
 
 
-def rows_needed(field, a, nx, ny):
-    past = max(-a, a - nx + 1, 0)
-    if field == XV:
-        reach = {0: 3, 1: 3, 2: 3, 3: 3, 4: 2}.get(past, -1)
-    elif field == YV:
-        reach = {0: 4, 1: 4, 2: 4, 3: 3}.get(past, -1)
-    else:
-        reach = {0: 3, 1: 3, 2: 3, 3: 2}.get(past, -1)
-    return (-reach, ny + reach) if reach >= 0 else (0, 0)
-
-
-def segments(side, nx, ny):
-    columns = {-1: range(-REACH, 0), 0: range(nx), 1: range(nx, nx + REACH)}[side[0]]
-    low, high = {-1: (-REACH, 0), 0: (0, ny), 1: (ny, ny + REACH)}[side[1]]
+def ghost_rows(field):
+    return 4 if field == YV else 3
+
+
+def x_layers():
+    return [(field, past) for field in range(5) for past in (1, 2)] + [(XV, 3)]
+
+
+def x_edge_rows(ny):
+    return (len(x_layers()) + 1) * ny + 2 * EDGE_KINDS
+
+
+def y_layers(nx):
     found, offset = [], 0
-    for a in columns:
+    for a in range(nx):
         for field in range(5):
-            first, last = rows_needed(field, a, nx, ny)
-            first, last = max(first, low), min(last, high)
-            if last > first:
-                found.append((field, a, first, last - first, offset))
-                offset += last - first
+            found.append((field, a, ghost_rows(field), offset))
+            offset += ghost_rows(field)
     return found, -(-offset // 8) * 8
 
 
-def corner_segments(side_y, nx, ny):
+def corner_layers():
     found, offset = [], 0
-    for side_x in (-1, 1):
-        for field, a, first, count, _ in segments((side_x, side_y), nx, ny)[0]:
-            found.append((side_x, field, a, first, count, offset))
-            offset += count
-    return found, -(-offset // 8) * 8
+    for number, (field, past) in enumerate(x_layers()):
+        found.append((number, field, past, ghost_rows(field), offset))
+        offset += ghost_rows(field)
+    return found, offset, -(-(offset + 1 + EDGE_KINDS) // 8) * 8
+
+
+def is_low(link):
+    odd = lax.rem(lax.axis_index("gy"), 2)
+    return odd if link == NEAR else 1 - odd
+
+
+def pick(flag, one, other):
+    return flag * one + (1 - flag) * other
+
+
+def along_x(value, side):
+    count = lax.axis_size("gx")
+    return lax.ppermute(value, "gx", [((i + side) % count, i) for i in range(count)])
+
+
+def along_y(value, link):
+    count = lax.axis_size("gy")
+    partners = [i ^ 1 if link == NEAR else (((i - 1) ^ 1) + 1) % count for i in range(count)]
+    return lax.ppermute(value, "gy", list(enumerate(partners)))
 
 
 def hidden_zero():
     return lax.shift_right_logical(lax.axis_index("gx"), 20)
 
 
+def per_mass(energy, spread):
+    return 0.4 * energy + 0.5 * jnp.square(jnp.minimum(0.5 * spread, 0.0))
+
+
 def pack_kernel(nx, ny, *refs):
-    fields, own, edges, arrived = refs[:5], refs[5], refs[6 : 6 + len(SIDES)], refs[-1]
+    fields, own, x_edges, y_edges, padded, arrived = refs[:5], refs[5], refs[6:8], refs[8:10], refs[10], refs[11]
     zero = hidden_zero()
     copies = [pltpu.make_async_copy(fields[field], own.at[field], arrived.at[field]) for field in range(5)]
     for copy in copies:
         copy.start()
     for current, copy in enumerate(copies):
         copy.wait()
-        for side, edge in zip(SIDES, edges):
-            for field, a, b, count, offset in segments(side, nx, ny)[0]:
+        for side, edge in zip(SIDES, x_edges):
+            for number, (field, past) in enumerate(x_layers()):
                 if field == current:
-                    edge[pl.ds(zero + offset, count), :] = own[
-                        field, a - side[0] * nx, pl.ds(zero + (b - side[1] * ny), count), :
-                    ]
-
-
-def corner_kernel(nx, ny, below_ref, above_ref, low_ref, high_ref):
+                    column = nx - past if side < 0 else past - 1
+                    edge[pl.ds(zero + number * ny, ny), :] = own[field, column]
+        for link, edge in zip(LINKS, y_edges):
+            for field, a, rows, offset in y_layers(nx)[0]:
+                if field == current:
+                    start = pick(is_low(link), 0, ny - rows)
+                    edge[pl.ds(zero + offset, rows), :] = own[field, a, pl.ds(start, rows), :]
+    for k, (side, edge) in enumerate(zip(SIDES, x_edges)):
+        a = nx - 3 if side < 0 else 2
+        offset = len(x_layers()) * ny
+        padded[k] = jnp.zeros_like(padded[k])
+        padded[k, pl.ds(TOP, ny), :] = own[YV, a]
+        spread = own[XV, a + 1] - own[XV, a - 1]
+        spread += padded[k, pl.ds(zero + (TOP + 1), ny), :] - padded[k, pl.ds(zero + (TOP - 1), ny), :]
+        spread += up(own[ZV, a]) - down(own[ZV, a])
+        edge[pl.ds(zero + offset, ny), :] = own[DENSITY, a] * per_mass(own[ENERGY, a], spread)
+        offset += ny
+        padded[k, pl.ds(TOP, ny), :] = spread
+        for row in (0, ny - 1):
+            for value in (own[DENSITY, a, pl.ds(row, 1), :], own[ENERGY, a, pl.ds(row, 1), :],
+                          padded[k, pl.ds(TOP + row, 1), :], own[YV, a, pl.ds(row, 1), :]):
+                edge[pl.ds(zero + offset, 1), :] = value
+                offset += 1
+
+
+def corner_kernel(ny, *refs):
+    x_edges, outs = refs[:2], refs[2:]
     zero = hidden_zero()
-    held = {
-        (side_x, field, a): (ref, offset)
-        for side_x, ref in ((-1, below_ref), (1, above_ref))
-        for field, a, _, _, offset in segments((side_x, 0), nx, ny)[0]
-    }
-    for side_y, out in ((-1, low_ref), (1, high_ref)):
-        for side_x, field, a, b, count, offset in corner_segments(side_y, nx, ny)[0]:
-            ref, start = held[side_x, field, a]
-            out[pl.ds(zero + offset, count), :] = ref[pl.ds(zero + (start + b - side_y * ny), count), :]
+    columns, singles, rows_of_corner = corner_layers()
+    for link, out in zip(LINKS, outs):
+        low = is_low(link)
+        for k, edge in enumerate(x_edges):
+            base = zero + k * rows_of_corner
+            for number, _, _, rows, offset in columns:
+                out[pl.ds(base + offset, rows), :] = edge[pl.ds(number * ny + pick(low, 0, ny - rows), rows), :]
+            number = len(x_layers())
+            out[pl.ds(base + singles, 1), :] = edge[pl.ds(number * ny + pick(low, 1, ny - 2), 1), :]
+            first = (number + 1) * ny + pick(low, 0, EDGE_KINDS)
+            out[pl.ds(base + (singles + 1), EDGE_KINDS), :] = edge[pl.ds(first, EDGE_KINDS), :]
 
 
 def limited(above, below):
@@ -153,9 +198,9 @@
 
 
 def step_kernel(nx, ny, dt_ref, *refs):
-    own, halos = refs[0], refs[1:7]
+    own, x_edges, y_edges, corners = refs[0], refs[1:3], refs[3:5], refs[5:7]
     passive, speed, speed_y, speed_z, flows, increment_ref = refs[7:13]
-    cells, stress, growth, heat, state, energy_one, swept, work = refs[13:]
+    cells, third, stress, growth, heat, state, energy_one, swept, work = refs[13:]
     nz = own.shape[-1]
     zero = hidden_zero()
     dt = dt_ref[0]
@@ -165,51 +210,81 @@
 
     for field in range(5):
         for a in range(nx):
-            cells[field, a + REACH, pl.ds(TOP, ny), :] = own[field, a]
-    for side, halo in zip(SIDES, halos):
-        for field, a, b, count, offset in segments(side, nx, ny)[0]:
-            cells[field, a + REACH, pl.ds(zero + (b + TOP), count), :] = halo[pl.ds(zero + offset, count), :]
-    for side_y, halo in zip((-1, 1), halos[len(SIDES) :]):
-        for _, field, a, b, count, offset in corner_segments(side_y, nx, ny)[0]:
-            cells[field, a + REACH, pl.ds(zero + (b + TOP), count), :] = halo[pl.ds(zero + offset, count), :]
+            cells[field, a + LEFT, pl.ds(TOP, ny), :] = own[field, a]
+    columns, singles, rows_of_corner = corner_layers()
+    for k, (side, edge) in enumerate(zip(SIDES, x_edges)):
+        for number, (field, past) in enumerate(x_layers()):
+            column = LEFT + (-past if side < 0 else nx - 1 + past)
+            cells[field, column, pl.ds(TOP, ny), :] = edge[pl.ds(zero + number * ny, ny), :]
+        offset = len(x_layers()) * ny
+        third[k, EDGE_KINDS, pl.ds(TOP, ny), :] = edge[pl.ds(zero + offset, ny), :]
+        offset += ny
+        for row in (0, ny - 1):
+            for kind in range(EDGE_KINDS):
+                third[k, kind, pl.ds(TOP + row, 1), :] = edge[pl.ds(zero + offset, 1), :]
+                offset += 1
+    for link, edge, corner in zip(LINKS, y_edges, corners):
+        low = is_low(link)
+        for field, a, rows, offset in y_layers(nx)[0]:
+            to = pl.ds(TOP + pick(low, -rows, ny), rows)
+            cells[field, a + LEFT, to, :] = edge[pl.ds(zero + offset, rows), :]
+        for k, side in enumerate(SIDES):
+            base = zero + k * rows_of_corner
+            for _, field, past, rows, offset in columns:
+                column = LEFT + (-past if side < 0 else nx - 1 + past)
+                to = pl.ds(TOP + pick(low, -rows, ny), rows)
+                cells[field, column, to, :] = corner[pl.ds(base + offset, rows), :]
+            third[k, EDGE_KINDS, pl.ds(TOP + pick(low, -2, ny + 1), 1), :] = corner[pl.ds(base + singles, 1), :]
+            for kind in range(EDGE_KINDS):
+                to = pl.ds(TOP + pick(low, -1, ny), 1)
+                third[k, kind, to, :] = corner[pl.ds(base + (singles + 1 + kind), 1), :]
 
     def at(ref, *index, start, count):
         return ref[(*index, pl.ds(zero + start, count), slice(None))]
 
-    for a in range(-3, nx + 3):
+    row = lax.broadcasted_iota(jnp.int32, (tall, nz), 0) - 4
+    for k, a in enumerate((-3, nx + 2)):
+        above = at(third, k, 3, start=TOP - 3, count=tall)
+        below = at(third, k, 3, start=TOP - 5, count=tall)
+        spread = at(third, k, 2, start=TOP - 4, count=tall)
+        spread += jnp.where((row == -1) | (row == ny - 1), above, -below)
+        density, energy = [at(third, k, kind, start=TOP - 4, count=tall) for kind in range(2)]
+        split = (row == -1) | (row == 0) | (row == ny - 1) | (row == ny)
+        whole = at(third, k, EDGE_KINDS, start=TOP - 4, count=tall)
+        stress[a + 3] = jnp.where(split, density * per_mass(energy, spread), whole)
+
+    for a in range(-2, nx + 2):
         get = functools.partial(at, cells, start=TOP - 4, count=tall)
-        z = get(ZV, a + REACH)
-        divergence = 0.5 * (
-            get(XV, a + REACH + 1)
-            - get(XV, a + REACH - 1)
-            + (at(cells, YV, a + REACH, start=TOP - 3, count=tall) - at(cells, YV, a + REACH, start=TOP - 5, count=tall))
+        z = get(ZV, a + LEFT)
+        spread = (
+            get(XV, a + LEFT + 1)
+            - get(XV, a + LEFT - 1)
+            + (at(cells, YV, a + LEFT, start=TOP - 3, count=tall) - at(cells, YV, a + LEFT, start=TOP - 5, count=tall))
             + (up(z) - down(z))
         )
-        per_mass = 0.4 * get(ENERGY, a + REACH) + 0.5 * jnp.square(jnp.minimum(divergence, 0.0))
-        stress[a + 3] = get(DENSITY, a + REACH) * per_mass
-        if -2 <= a < nx + 2:
-            growth[a + 2] = dt * divergence
-            heat[a + 2] = per_mass
+        heat[a + 2] = per_mass(get(ENERGY, a + LEFT), spread)
+        stress[a + 3] = get(DENSITY, a + LEFT) * heat[a + 2]
+        growth[a + 2] = half * spread
 
     for a in range(-2, nx + 2):
         get = functools.partial(at, cells, start=TOP - 2, count=wide)
-        density = get(DENSITY, a + REACH)
+        density = get(DENSITY, a + LEFT)
         grown = at(growth, a + 2, start=2, count=wide)
         centre = at(stress, a + 3, start=2, count=wide)
         scale = half / density
         density_one = density / (1.0 + grown)
-        energy = get(ENERGY, a + REACH) - at(heat, a + 2, start=2, count=wide) * grown
+        energy = get(ENERGY, a + LEFT) - at(heat, a + 2, start=2, count=wide) * grown
         passive[0, a + 2] = density_one
         passive[1, a + 2] = density_one * energy
-        x_one = get(XV, a + REACH) - scale * (
+        x_one = get(XV, a + LEFT) - scale * (
             at(stress, a + 4, start=2, count=wide) - at(stress, a + 2, start=2, count=wide)
         )
         state[0, a + 2] = x_one
         speed[a + 2] = x_one
-        state[1, a + 2] = get(YV, a + REACH) - scale * (
+        state[1, a + 2] = get(YV, a + LEFT) - scale * (
             at(stress, a + 3, start=3, count=wide) - at(stress, a + 3, start=1, count=wide)
         )
-        state[2, a + 2] = get(ZV, a + REACH) - scale * (up(centre) - down(centre))
+        state[2, a + 2] = get(ZV, a + LEFT) - scale * (up(centre) - down(centre))
         if 0 <= a < nx:
             energy_one[a, 0:wide] = energy
 
@@ -257,12 +332,6 @@
         copy.wait()
 
 
-def shifted(value, side):
-    axis, step = ("gx", side[0]) if side[0] else ("gy", side[1])
-    count = lax.axis_size(axis)
-    return lax.ppermute(value, axis, [((i + step) % count, i) for i in range(count)])
-
-
 def body(density0, energy0, x_velocity, y_velocity, z_velocity, time_increment):
     nx, ny, nz = density0.shape
     fields = (density0, energy0, x_velocity, y_velocity, z_velocity)
@@ -277,35 +346,37 @@
     def limit(mebibytes):
         return pltpu.CompilerParams(vmem_limit_bytes=mebibytes * 1024 * 1024)
 
+    x_edge, y_edge, corner = array(x_edge_rows(ny)), array(y_layers(nx)[1]), array(2 * corner_layers()[2])
     own, *edges = pl.pallas_call(
         functools.partial(pack_kernel, nx, ny),
-        out_shape=[array(5, nx, ny)] + [array(segments(side, nx, ny)[1]) for side in SIDES],
+        out_shape=[array(5, nx, ny), x_edge, x_edge, y_edge, y_edge],
         in_specs=[HBM] * 5,
-        out_specs=[VMEM] * (1 + len(SIDES)),
-        scratch_shapes=[pltpu.SemaphoreType.DMA((5,))],
+        out_specs=[VMEM] * 5,
+        scratch_shapes=[scratch(2, ny + 20), pltpu.SemaphoreType.DMA((5,))],
         compiler_params=limit(4),
         name="pack",
     )(*[pltpu.with_memory_space_constraint(field, pltpu.HBM) for field in fields])
-    edges = [shifted(edge, side) for edge, side in zip(edges, SIDES)]
+    x_edges = [along_x(edge, side) for edge, side in zip(edges[:2], SIDES)]
+    y_edges = [along_y(edge, link) for edge, link in zip(edges[2:], LINKS)]
     corners = pl.pallas_call(
-        functools.partial(corner_kernel, nx, ny),
-        out_shape=[array(corner_segments(1, nx, ny)[1])] * 2,
+        functools.partial(corner_kernel, ny),
+        out_shape=[corner] * 2,
         in_specs=[VMEM] * 2,
         out_specs=[VMEM] * 2,
         compiler_params=limit(4),
         name="corners",
-    )(edges[0], edges[1])
-    corners = [shifted(corner, (0, side_y)) for corner, side_y in zip(corners, (-1, 1))]
-    count = lax.axis_size(("gx", "gy"))
+    )(*x_edges)
+    corners = [along_y(corner, link) for corner, link in zip(corners, LINKS)]
     increment = time_increment.reshape(1)
     passed = [array(2, nx + 4, wide), array(nx + 4, wide), array(nx, wide + 8), array(nx, wide), array(3, nx, ny)]
     *passed, smallest = pl.pallas_call(
         functools.partial(step_kernel, nx, ny),
-        out_shape=passed + [array(count)],
+        out_shape=passed + [array(lax.axis_size(("gx", "gy")))],
         in_specs=[SMEM] + [VMEM] * 7,
         out_specs=[VMEM] * 6,
         scratch_shapes=[
-            scratch(5, nx + 8, ny + 20),
+            scratch(5, nx + 6, ny + 20),
+            scratch(2, EDGE_KINDS + 1, ny + 20),
             scratch(nx + 6, tall),
             scratch(nx + 4, tall),
             scratch(nx + 4, tall),
@@ -316,7 +387,7 @@
         ],
         compiler_params=limit(12),
         name="step",
-    )(increment, own, *edges, *corners)
+    )(increment, own, *x_edges, *y_edges, *corners)
     outs = pl.pallas_call(
         functools.partial(carry_kernel, nx, ny),
         out_shape=[array(nx, ny)] * 5,

time: 30.3 us -> 30 us (0.990)
  starting transfers between devices: 15 us -> 14.6 us
where the time goes in v12:
time: 30 us; the launch traced here: 29.8 us
  starting transfers between devices  14.6 us (49%)
  waiting for transfers between devices  7.9 us (26%)
  Pallas kernels  5.27 us (18%)
  between operations  1.34 us (4%)
  other arithmetic  0.63 us (2%)
    ppermute x2, starting transfers between devices, along_x(): lax.ppermute(value, 'gx', [((i + side) % count, i) for i in range(count)])  6.12 us
    all_to_all x1, starting transfers between devices, body(): lax.all_to_all(smallest, ('gx', 'gy'), 0, 0, tiled=True)  5.13 us
    all_to_all x1, waiting for transfers between devices, body(): lax.all_to_all(smallest, ('gx', 'gy'), 0, 0, tiled=True)  5.1 us
    ppermute x4, starting transfers between devices, along_y(): return lax.ppermute(value, 'gy', list(enumerate(partners)))  3.37 us
    pallas_call x1, Pallas kernels, body(): pl.pallas_call(functools.partial(step_kernel, nx, ny), out_shape=passed +...  2.04 us
    pallas_call x1, Pallas kernels, body(): pl.pallas_call(functools.partial(carry_kernel, nx, ny), out_shape=[array(...  2.03 us
    ppermute x4, waiting for transfers between devices, along_y(): return lax.ppermute(value, 'gy', list(enumerate(partners)))  1.54 us
    ppermute x2, waiting for transfers between devices, along_x(): lax.ppermute(value, 'gx', [((i + side) % count, i) for i in range(count)])  1.25 us
  transfers between devices with their start and end apart: 7, of which 4 were waited for; matrix products, arithmetic and copies ran while one was open for 0% of the time, Pallas kernels for 7%

profile of v12, /device:TPU:0, one launch (start us, length us, event | category | flops | bytes accessed | tf_op | source)
XLA Modules:
  0.0 29.8 jit_solution(17241794641313202000)
XLA Ops:
  0.6 1.2 %pack.1 = (f32[5,12,12,128]{3,2,1,0:T(8,128)S(1)}, f32[152,128]{1,0:T(8,128)S(1)}, f32[152,128]{1,0:T(8,128)S(1)}, f32[192,128]{1,0:T(8,128)S(1)}, f32[192,128]{1,0:T(8,128)S(1)}) custom-call(f32[12,12,128]{2,1,0:T(8,128)} %refs_0_.1, f32[12,12,128]{2,1,0:T(8,128)} %refs_1_.1, f32[12,12,128]{2,1,0:T(8,128)} %refs_2_.1, f32[12,12,128]{2,1,0:T(8,128)} %refs_3_.1, ...), custom_call_target="tpu_custom_call" | custom-call | tf_op jit(solution)/shard_map/pack/pallas_call | solution.py:350
  1.8 3.0 %collective-permute-start = (f32[152,128]{1,0:T(8,128)S(1)}, f32[152,128]{1,0:T(8,128)S(1)}, u32[]{:S(2)}, u32[]{:S(2)}) collective-permute-start(f32[152,128]{1,0:T(8,128)S(1)} %get-tuple-element.25), channel_id=1, source_target_pairs={{28,0},{0,4},{4,8},{8,12},{12,16},{16,20},{20,24},{24,28},{29,1},{... | collective-permute-start | bytes 233480 | tf_op jit(solution)/shard_map/ppermute | solution.py:62
  4.8 3.1 %collective-permute-start.1 = (f32[152,128]{1,0:T(8,128)S(1)}, f32[152,128]{1,0:T(8,128)S(1)}, u32[]{:S(2)}, u32[]{:S(2)}) collective-permute-start(f32[152,128]{1,0:T(8,128)S(1)} %get-tuple-element.26), channel_id=1, source_target_pairs={{4,0},{8,4},{12,8},{16,12},{20,16},{24,20},{28,24},{0,28},{5,1},{9... | collective-permute-start | bytes 233480 | tf_op jit(solution)/shard_map/ppermute | solution.py:62
  7.9 0.7 %collective-permute-start.2 = (f32[192,128]{1,0:T(8,128)S(1)}, f32[192,128]{1,0:T(8,128)S(1)}, u32[]{:S(2)}, u32[]{:S(2)}) collective-permute-start(f32[192,128]{1,0:T(8,128)S(1)} %get-tuple-element.27), channel_id=1, source_target_pairs={{0,3},{1,2},{2,1},{3,0},{4,7},{5,6},{6,5},{7,4},{8,11},{9,10},{10,... | collective-permute-start | bytes 294920 | tf_op jit(solution)/shard_map/ppermute | solution.py:68
  8.6 1.1 %collective-permute-start.3 = (f32[192,128]{1,0:T(8,128)S(1)}, f32[192,128]{1,0:T(8,128)S(1)}, u32[]{:S(2)}, u32[]{:S(2)}) collective-permute-start(f32[192,128]{1,0:T(8,128)S(1)} %get-tuple-element.28), channel_id=1, source_target_pairs={{0,1},{1,0},{2,3},{3,2},{4,5},{5,4},{6,7},{7,6},{8,9},{9,8},{10,11... | collective-permute-start | bytes 294920 | tf_op jit(solution)/shard_map/ppermute | solution.py:68
  9.7 0.7 %collective-permute-done.refs_0_.refs_1_ = f32[152,128]{1,0:T(8,128)S(1)} collective-permute-done((f32[152,128]{1,0:T(8,128)S(1)}, f32[152,128]{1,0:T(8,128)S(1)}, u32[]{:S(2)}, u32[]{:S(2)}) %collective-permute-start) | collective-permute-done | bytes 77856 | tf_op jit(solution)/shard_map/ppermute | solution.py:62
  10.3 0.6 %collective-permute-done.1.refs_1_.refs_2_ = f32[152,128]{1,0:T(8,128)S(1)} collective-permute-done((f32[152,128]{1,0:T(8,128)S(1)}, f32[152,128]{1,0:T(8,128)S(1)}, u32[]{:S(2)}, u32[]{:S(2)}) %collective-permute-start.1) | collective-permute-done | bytes 77856 | tf_op jit(solution)/shard_map/ppermute | solution.py:62
  10.9 0.1 collective-permute-start.4
  11.0 1.6 %collective-permute-start.5 = (f32[80,128]{1,0:T(8,128)S(1)}, f32[80,128]{1,0:T(8,128)S(1)}, u32[]{:S(2)}, u32[]{:S(2)}) collective-permute-start(f32[80,128]{1,0:T(8,128)S(1)} %get-tuple-element.30), channel_id=1, source_target_pairs={{0,1},{1,0},{2,3},{3,2},{4,5},{5,4},{6,7},{7,6},{8,9},{9,8},{10,11... | collective-permute-start | bytes 122888 | tf_op jit(solution)/shard_map/ppermute | solution.py:68
  13.3 0.0 collective-permute-done.2.refs_3_
  13.3 0.0 collective-permute-done.3.refs_4_
  13.3 1.5 %collective-permute-done.4.refs_5_ = f32[80,128]{1,0:T(8,128)S(1)} collective-permute-done((f32[80,128]{1,0:T(8,128)S(1)}, f32[80,128]{1,0:T(8,128)S(1)}, u32[]{:S(2)}, u32[]{:S(2)}) %collective-permute-start.4) | collective-permute-done | bytes 40992 | tf_op jit(solution)/shard_map/ppermute | solution.py:68
  14.8 0.0 collective-permute-done.5.refs_6_
  14.8 2.0 %step.1 = (f32[2,16,16,128]{3,2,1,0:T(8,128)S(1)}, f32[16,16,128]{2,1,0:T(8,128)S(1)}, f32[12,24,128]{2,1,0:T(8,128)S(1)}, f32[12,16,128]{2,1,0:T(8,128)S(1)}, f...) custom-call(f32[1]{0:T(128)} %bitcast.4.dt_ref, f32[5,12,12,128]{3,2,1,0:T(8,128)S(1)} %get-tuple-element.24.refs_0_, ...), custom_call_target="tpu_custom_call" | custom-call | tf_op jit(solution)/shard_map/step/pallas_call | solution.py:372
  16.9 5.1 %all-to-all-start = ((f32[32,1,128]{2,1,0:T(1,128)}), f32[32,1,128]{2,1,0:T(1,128)S(1)}, u32[]{:S(2)}, u32[]{:S(2)}) async-start(f32[32,1,128]{2,1,0:T(1,128)} %bitcast.2), calls=%async_computation | async-start | bytes 32768 | tf_op jit(solution)/shard_map/all_to_all | solution.py:405
  22.0 2.0 %carry.1 = (f32[12,12,128]{2,1,0:T(8,128)}, f32[12,12,128]{2,1,0:T(8,128)}, f32[12,12,128]{2,1,0:T(8,128)}, f32[12,12,128]{2,1,0:T(8,128)}, f32[12,12,128]{2,1,0:T(8,128)}) custom-call(f32[1]{0:T(128)} %bitcast.5.dt_ref, f32[2,16,16,128]{3,2,1,0:T(8,128)S(1)} %get-tuple-element.31.refs_0_, f32[16,16,128]{2,1,0:T(8,128)S(1)} %get-tuple-element.32.refs_1_, ...), custom_call_target="tpu_custom_call" | custom-call | flops 10000000 | bytes 4000000 | tf_op jit(solution)/shard_map/carry/pallas_call | solution.py:391
  24.0 5.1 %all-to-all-done = f32[32,1,128]{2,1,0:T(1,128)S(1)} async-done(((f32[32,1,128]{2,1,0:T(1,128)}), f32[32,1,128]{2,1,0:T(1,128)S(1)}, u32[]{:S(2)}, u32[]{:S(2)}) %all-to-all-start) | async-done | bytes 16416 | tf_op jit(solution)/shard_map/all_to_all | solution.py:405
  29.1 0.6 %reduce_min.9 = f32[]{:T(128)} reduce(f32[32,1,128]{2,1,0:T(1,128)S(1)} %all-to-all-done, f32[]{:T(128)} %constant.0.clone.1), dimensions={0,1,2}, to_apply=%region_0.0 | reduce | flops 4095 | bytes 16392 | tf_op jit(solution)/shard_map/reduce_min | solution.py:405
  (1 shorter events, 0.0 us)
Async XLA Ops:
  1.8 8.5 %collective-permute-start = (f32[152,128]{1,0:T(8,128)S(1)}, f32[152,128]{1,0:T(8,128)S(1)}, u32[]{:S(2)}, u32[]{:S(2)}) collective-permute-start(f32[152,128]{1,0:T(8,128)S(1)} %get-tuple-element.25), channel_id=1, source_target_pairs={{28,0},{0,4},{4,8},{8,12},{12,16},{16,20},{20,24},{24,28},{29,1},{... | collective-permute-start | bytes 233480 | tf_op jit(solution)/shard_map/ppermute | solution.py:62
  4.8 6.1 %collective-permute-start.1 = (f32[152,128]{1,0:T(8,128)S(1)}, f32[152,128]{1,0:T(8,128)S(1)}, u32[]{:S(2)}, u32[]{:S(2)}) collective-permute-start(f32[152,128]{1,0:T(8,128)S(1)} %get-tuple-element.26), channel_id=1, source_target_pairs={{4,0},{8,4},{12,8},{16,12},{20,16},{24,20},{28,24},{0,28},{5,1},{9... | collective-permute-start | bytes 233480 | tf_op jit(solution)/shard_map/ppermute | solution.py:62
  7.9 5.3 %collective-permute-start.2 = (f32[192,128]{1,0:T(8,128)S(1)}, f32[192,128]{1,0:T(8,128)S(1)}, u32[]{:S(2)}, u32[]{:S(2)}) collective-permute-start(f32[192,128]{1,0:T(8,128)S(1)} %get-tuple-element.27), channel_id=1, source_target_pairs={{0,3},{1,2},{2,1},{3,0},{4,7},{5,6},{6,5},{7,4},{8,11},{9,10},{10,... | collective-permute-start | bytes 294920 | tf_op jit(solution)/shard_map/ppermute | solution.py:68
  8.6 4.7 %collective-permute-start.3 = (f32[192,128]{1,0:T(8,128)S(1)}, f32[192,128]{1,0:T(8,128)S(1)}, u32[]{:S(2)}, u32[]{:S(2)}) collective-permute-start(f32[192,128]{1,0:T(8,128)S(1)} %get-tuple-element.28), channel_id=1, source_target_pairs={{0,1},{1,0},{2,3},{3,2},{4,5},{5,4},{6,7},{7,6},{8,9},{9,8},{10,11... | collective-permute-start | bytes 294920 | tf_op jit(solution)/shard_map/ppermute | solution.py:68
  10.9 3.9 %collective-permute-start.4 = (f32[80,128]{1,0:T(8,128)S(1)}, f32[80,128]{1,0:T(8,128)S(1)}, u32[]{:S(2)}, u32[]{:S(2)}) collective-permute-start(f32[80,128]{1,0:T(8,128)S(1)} %get-tuple-element.29), channel_id=1, source_target_pairs={{0,3},{1,2},{2,1},{3,0},{4,7},{5,6},{6,5},{7,4},{8,11},{9,10},{10,... | collective-permute-start | bytes 122888 | tf_op jit(solution)/shard_map/ppermute | solution.py:68
  11.0 3.8 %collective-permute-start.5 = (f32[80,128]{1,0:T(8,128)S(1)}, f32[80,128]{1,0:T(8,128)S(1)}, u32[]{:S(2)}, u32[]{:S(2)}) collective-permute-start(f32[80,128]{1,0:T(8,128)S(1)} %get-tuple-element.30), channel_id=1, source_target_pairs={{0,1},{1,0},{2,3},{3,2},{4,5},{5,4},{6,7},{7,6},{8,9},{9,8},{10,11... | collective-permute-start | bytes 122888 | tf_op jit(solution)/shard_map/ppermute | solution.py:68
  16.9 12.3 %all-to-all-start = ((f32[32,1,128]{2,1,0:T(1,128)}), f32[32,1,128]{2,1,0:T(1,128)S(1)}, u32[]{:S(2)}, u32[]{:S(2)}) async-start(f32[32,1,128]{2,1,0:T(1,128)} %bitcast.2), calls=%async_computation | async-start | bytes 32768 | tf_op jit(solution)/shard_map/all_to_all | solution.py:405

commit v13 on v12

--- a/solution.py
+++ b/solution.py
@@ -371,7 +371,7 @@
     passed = [array(2, nx + 4, wide), array(nx + 4, wide), array(nx, wide + 8), array(nx, wide), array(3, nx, ny)]
     *passed, smallest = pl.pallas_call(
         functools.partial(step_kernel, nx, ny),
-        out_shape=passed + [array(lax.axis_size(("gx", "gy")))],
+        out_shape=passed + [array(8)],
         in_specs=[SMEM] + [VMEM] * 7,
         out_specs=[VMEM] * 6,
         scratch_shapes=[
@@ -402,7 +402,7 @@
         cost_estimate=pl.CostEstimate(flops=10**7, bytes_accessed=4 * 10**6, transcendentals=0),
         name="carry",
     )(increment, *passed)
-    return (*outs, jnp.min(lax.all_to_all(smallest, ("gx", "gy"), 0, 0, tiled=True)))
+    return (*outs, jnp.min(lax.all_gather(smallest, ("gx", "gy"), tiled=True)))
 
 
 def solution(mesh):

time: 30 us -> 60.5 us (2.02)
  blocking collectives: 0 us -> 41.4 us
  starting transfers between devices: 14.6 us -> 9.49 us
  waiting for transfers between devices: 7.9 us -> 2.8 us
    all_gather x0 -> x1, blocking collectives: none -> 41.4 us  [body(): return (*outs, jnp.min(lax.all_gather(smallest, ('gx', 'gy'), tiled=True)))]
    all_to_all x1 -> x0, starting transfers between devices: 5.13 us -> none  [body(): lax.all_to_all(smallest, ('gx', 'gy'), 0, 0, tiled=True)]
    all_to_all x1 -> x0, waiting for transfers between devices: 5.1 us -> none  [body(): lax.all_to_all(smallest, ('gx', 'gy'), 0, 0, tiled=True)]
  transfers between devices with their start and end apart: 7 -> 6, of which waited for: 4 -> 3; matrix products, arithmetic and copies ran while one was open for 0% -> 0% of each run, Pallas kernels for 7% -> 0%
where the time goes in v13:
time: 60.5 us; the launch traced here: 60.3 us
  blocking collectives  41.4 us (68%)
  starting transfers between devices  9.49 us (16%)
  Pallas kernels  4.67 us (8%)
  waiting for transfers between devices  2.8 us (5%)
  between operations  1.33 us (2%)
  other arithmetic  0.63 us (1%)
    all_gather x1, blocking collectives, body(): return (*outs, jnp.min(lax.all_gather(smallest, ('gx', 'gy'), tiled=True)))  41.4 us
    ppermute x2, starting transfers between devices, along_x(): lax.ppermute(value, 'gx', [((i + side) % count, i) for i in range(count)])  6.12 us
    ppermute x4, starting transfers between devices, along_y(): return lax.ppermute(value, 'gy', list(enumerate(partners)))  3.37 us
    pallas_call x1, Pallas kernels, body(): pl.pallas_call(functools.partial(carry_kernel, nx, ny), out_shape=[array(...  2.03 us
    ppermute x4, waiting for transfers between devices, along_y(): return lax.ppermute(value, 'gy', list(enumerate(partners)))  1.54 us
    pallas_call x1, Pallas kernels, body(): pl.pallas_call(functools.partial(step_kernel, nx, ny), out_shape=passed +...  1.44 us
    ppermute x2, waiting for transfers between devices, along_x(): lax.ppermute(value, 'gx', [((i + side) % count, i) for i in range(count)])  1.25 us
  transfers between devices with their start and end apart: 6, of which 3 were waited for; matrix products, arithmetic and copies ran while one was open for 0% of the time, Pallas kernels for 0%

profile of v13, /device:TPU:0, one launch (start us, length us, event | category | flops | bytes accessed | tf_op | source)
XLA Modules:
  0.0 60.3 jit_solution(10518622401977113998)
XLA Ops:
  0.6 1.2 %pack.1 = (f32[5,12,12,128]{3,2,1,0:T(8,128)S(1)}, f32[152,128]{1,0:T(8,128)S(1)}, f32[152,128]{1,0:T(8,128)S(1)}, f32[192,128]{1,0:T(8,128)S(1)}, f32[192,128]{1,0:T(8,128)S(1)}) custom-call(f32[12,12,128]{2,1,0:T(8,128)} %refs_0_.1, f32[12,12,128]{2,1,0:T(8,128)} %refs_1_.1, f32[12,12,128]{2,1,0:T(8,128)} %refs_2_.1, f32[12,12,128]{2,1,0:T(8,128)} %refs_3_.1, ...), custom_call_target="tpu_custom_call" | custom-call | tf_op jit(solution)/shard_map/pack/pallas_call | solution.py:350
  1.8 3.0 %collective-permute-start = (f32[152,128]{1,0:T(8,128)S(1)}, f32[152,128]{1,0:T(8,128)S(1)}, u32[]{:S(2)}, u32[]{:S(2)}) collective-permute-start(f32[152,128]{1,0:T(8,128)S(1)} %get-tuple-element.25), channel_id=1, source_target_pairs={{28,0},{0,4},{4,8},{8,12},{12,16},{16,20},{20,24},{24,28},{29,1},{... | collective-permute-start | bytes 233480 | tf_op jit(solution)/shard_map/ppermute | solution.py:62
  4.8 3.1 %collective-permute-start.1 = (f32[152,128]{1,0:T(8,128)S(1)}, f32[152,128]{1,0:T(8,128)S(1)}, u32[]{:S(2)}, u32[]{:S(2)}) collective-permute-start(f32[152,128]{1,0:T(8,128)S(1)} %get-tuple-element.26), channel_id=1, source_target_pairs={{4,0},{8,4},{12,8},{16,12},{20,16},{24,20},{28,24},{0,28},{5,1},{9... | collective-permute-start | bytes 233480 | tf_op jit(solution)/shard_map/ppermute | solution.py:62
  7.9 0.7 %collective-permute-start.2 = (f32[192,128]{1,0:T(8,128)S(1)}, f32[192,128]{1,0:T(8,128)S(1)}, u32[]{:S(2)}, u32[]{:S(2)}) collective-permute-start(f32[192,128]{1,0:T(8,128)S(1)} %get-tuple-element.27), channel_id=1, source_target_pairs={{0,3},{1,2},{2,1},{3,0},{4,7},{5,6},{6,5},{7,4},{8,11},{9,10},{10,... | collective-permute-start | bytes 294920 | tf_op jit(solution)/shard_map/ppermute | solution.py:68
  8.6 1.1 %collective-permute-start.3 = (f32[192,128]{1,0:T(8,128)S(1)}, f32[192,128]{1,0:T(8,128)S(1)}, u32[]{:S(2)}, u32[]{:S(2)}) collective-permute-start(f32[192,128]{1,0:T(8,128)S(1)} %get-tuple-element.28), channel_id=1, source_target_pairs={{0,1},{1,0},{2,3},{3,2},{4,5},{5,4},{6,7},{7,6},{8,9},{9,8},{10,11... | collective-permute-start | bytes 294920 | tf_op jit(solution)/shard_map/ppermute | solution.py:68
  9.7 0.7 %collective-permute-done.refs_0_.refs_1_ = f32[152,128]{1,0:T(8,128)S(1)} collective-permute-done((f32[152,128]{1,0:T(8,128)S(1)}, f32[152,128]{1,0:T(8,128)S(1)}, u32[]{:S(2)}, u32[]{:S(2)}) %collective-permute-start) | collective-permute-done | bytes 77856 | tf_op jit(solution)/shard_map/ppermute | solution.py:62
  10.3 0.6 collective-permute-done.1.refs_1_.refs_2_
  10.9 0.1 collective-permute-start.4
  11.0 1.6 %collective-permute-start.5 = (f32[80,128]{1,0:T(8,128)S(1)}, f32[80,128]{1,0:T(8,128)S(1)}, u32[]{:S(2)}, u32[]{:S(2)}) collective-permute-start(f32[80,128]{1,0:T(8,128)S(1)} %get-tuple-element.30), channel_id=1, source_target_pairs={{0,1},{1,0},{2,3},{3,2},{4,5},{5,4},{6,7},{7,6},{8,9},{9,8},{10,11... | collective-permute-start | bytes 122888 | tf_op jit(solution)/shard_map/ppermute | solution.py:68
  13.3 0.0 collective-permute-done.2.refs_3_
  13.3 0.0 collective-permute-done.3.refs_4_
  13.3 1.5 %collective-permute-done.4.refs_5_ = f32[80,128]{1,0:T(8,128)S(1)} collective-permute-done((f32[80,128]{1,0:T(8,128)S(1)}, f32[80,128]{1,0:T(8,128)S(1)}, u32[]{:S(2)}, u32[]{:S(2)}) %collective-permute-start.4) | collective-permute-done | bytes 40992 | tf_op jit(solution)/shard_map/ppermute | solution.py:68
  14.8 0.0 collective-permute-done.5.refs_6_
  14.8 1.4 %step.1 = (f32[2,16,16,128]{3,2,1,0:T(8,128)S(1)}, f32[16,16,128]{2,1,0:T(8,128)S(1)}, f32[12,24,128]{2,1,0:T(8,128)S(1)}, f32[12,16,128]{2,1,0:T(8,128)S(1)}, f...) custom-call(f32[1]{0:T(128)} %bitcast.1.dt_ref, f32[5,12,12,128]{3,2,1,0:T(8,128)S(1)} %get-tuple-element.24.refs_0_, ...), custom_call_target="tpu_custom_call" | custom-call | tf_op jit(solution)/shard_map/step/pallas_call | solution.py:372
  16.3 41.4 %all_gather.3 = f32[256,128]{1,0:T(8,128)S(1)} all-gather(f32[8,128]{1,0:T(8,128)S(1)} %get-tuple-element.41), channel_id=1, replica_groups=mesh['gx'=8,'gy'=4] {'gx','gy'}, dimensions={0}, use_global_device_ids=true | all-gather | bytes 135168 | tf_op jit(solution)/shard_map/all_gather | solution.py:405
  57.7 0.6 %reduce_min.9 = f32[]{:T(128)} reduce(f32[256,128]{1,0:T(8,128)S(1)} %all_gather.3, f32[]{:T(128)} %constant.0.clone.1), dimensions={0,1}, to_apply=%region_0.0 | reduce | flops 32767 | bytes 131080 | tf_op jit(solution)/shard_map/reduce_min | solution.py:405
  58.3 2.0 %carry.1 = (f32[12,12,128]{2,1,0:T(8,128)}, f32[12,12,128]{2,1,0:T(8,128)}, f32[12,12,128]{2,1,0:T(8,128)}, f32[12,12,128]{2,1,0:T(8,128)}, f32[12,12,128]{2,1,0:T(8,128)}) custom-call(f32[1]{0:T(128)} %bitcast.2.dt_ref, f32[2,16,16,128]{3,2,1,0:T(8,128)S(1)} %get-tuple-element.31.refs_0_, f32[16,16,128]{2,1,0:T(8,128)S(1)} %get-tuple-element.32.refs_1_, ...), custom_call_target="tpu_custom_call" | custom-call | flops 10000000 | bytes 4000000 | tf_op jit(solution)/shard_map/carry/pallas_call | solution.py:391
  (1 shorter events, 0.0 us)
Async XLA Ops:
  1.8 8.5 %collective-permute-start = (f32[152,128]{1,0:T(8,128)S(1)}, f32[152,128]{1,0:T(8,128)S(1)}, u32[]{:S(2)}, u32[]{:S(2)}) collective-permute-start(f32[152,128]{1,0:T(8,128)S(1)} %get-tuple-element.25), channel_id=1, source_target_pairs={{28,0},{0,4},{4,8},{8,12},{12,16},{16,20},{20,24},{24,28},{29,1},{... | collective-permute-start | bytes 233480 | tf_op jit(solution)/shard_map/ppermute | solution.py:62
  4.8 6.1 %collective-permute-start.1 = (f32[152,128]{1,0:T(8,128)S(1)}, f32[152,128]{1,0:T(8,128)S(1)}, u32[]{:S(2)}, u32[]{:S(2)}) collective-permute-start(f32[152,128]{1,0:T(8,128)S(1)} %get-tuple-element.26), channel_id=1, source_target_pairs={{4,0},{8,4},{12,8},{16,12},{20,16},{24,20},{28,24},{0,28},{5,1},{9... | collective-permute-start | bytes 233480 | tf_op jit(solution)/shard_map/ppermute | solution.py:62
  7.9 5.3 %collective-permute-start.2 = (f32[192,128]{1,0:T(8,128)S(1)}, f32[192,128]{1,0:T(8,128)S(1)}, u32[]{:S(2)}, u32[]{:S(2)}) collective-permute-start(f32[192,128]{1,0:T(8,128)S(1)} %get-tuple-element.27), channel_id=1, source_target_pairs={{0,3},{1,2},{2,1},{3,0},{4,7},{5,6},{6,5},{7,4},{8,11},{9,10},{10,... | collective-permute-start | bytes 294920 | tf_op jit(solution)/shard_map/ppermute | solution.py:68
  8.6 4.7 %collective-permute-start.3 = (f32[192,128]{1,0:T(8,128)S(1)}, f32[192,128]{1,0:T(8,128)S(1)}, u32[]{:S(2)}, u32[]{:S(2)}) collective-permute-start(f32[192,128]{1,0:T(8,128)S(1)} %get-tuple-element.28), channel_id=1, source_target_pairs={{0,1},{1,0},{2,3},{3,2},{4,5},{5,4},{6,7},{7,6},{8,9},{9,8},{10,11... | collective-permute-start | bytes 294920 | tf_op jit(solution)/shard_map/ppermute | solution.py:68
  10.9 3.9 %collective-permute-start.4 = (f32[80,128]{1,0:T(8,128)S(1)}, f32[80,128]{1,0:T(8,128)S(1)}, u32[]{:S(2)}, u32[]{:S(2)}) collective-permute-start(f32[80,128]{1,0:T(8,128)S(1)} %get-tuple-element.29), channel_id=1, source_target_pairs={{0,3},{1,2},{2,1},{3,0},{4,7},{5,6},{6,5},{7,4},{8,11},{9,10},{10,... | collective-permute-start | bytes 122888 | tf_op jit(solution)/shard_map/ppermute | solution.py:68
  11.0 3.8 %collective-permute-start.5 = (f32[80,128]{1,0:T(8,128)S(1)}, f32[80,128]{1,0:T(8,128)S(1)}, u32[]{:S(2)}, u32[]{:S(2)}) collective-permute-start(f32[80,128]{1,0:T(8,128)S(1)} %get-tuple-element.30), channel_id=1, source_target_pairs={{0,1},{1,0},{2,3},{3,2},{4,5},{5,4},{6,7},{7,6},{8,9},{9,8},{10,11... | collective-permute-start | bytes 122888 | tf_op jit(solution)/shard_map/ppermute | solution.py:68

commit v14 on v12

--- a/solution.py
+++ b/solution.py
@@ -151,38 +151,54 @@
     return pltpu.roll(value, 1, value.ndim - 1)
 
 
-def sweep_x(state, speed, swept, fields, half):
-    for part in range(0, state.shape[2], 8):
-        rows = pl.ds(part, 8)
-        before = [state[field, 1, rows] for field in fields]
-        here = [state[field, 2, rows] for field in fields]
+def place(pieces, a):
+    for ref, first, last, number in pieces:
+        if first <= a < last:
+            return ref, a - first + number
+    raise ValueError(a)
+
+
+def read(zero, pieces, a, start, count, *field):
+    ref, number = place(pieces, a)
+    return ref[(*field, number, pl.ds(zero + start, count), slice(None))]
+
+
+def write(pieces, a, value, *field):
+    ref, number = place(pieces, a)
+    ref[(*field, number, pl.ds(0, value.shape[0]), slice(None))] = value
+
+
+def sweep_x(state, speed, swept, fields, first, last, wide, half):
+    for part in range(0, wide, 8):
+        before = [state(field, first - 1, part) for field in fields]
+        here = [state(field, first, part) for field in fields]
         steps = [h - b for h, b in zip(here, before)]
-        slopes = [limited(st, b - state[field, 0, rows]) for field, st, b in zip(fields, steps, before)]
+        slopes = [limited(st, b - state(field, first - 2, part)) for field, st, b in zip(fields, steps, before)]
         lower = None
-        for a in range(swept.shape[1] + 1):
-            factors = face_factors(speed[a + 1, rows], speed[a + 2, rows], half)
+        for a in range(first, last + 1):
+            factors = face_factors(speed(a - 1, part), speed(a, part), half)
             fluxes = []
             for k, field in enumerate(fields):
-                after = state[field, a + 3, rows]
+                after = state(field, a + 1, part)
                 step = after - here[k]
                 slope = limited(step, steps[k])
                 fluxes.append(face_flux(factors, before[k], here[k], slopes[k], slope))
                 if lower is not None:
-                    swept[field, a - 1, rows] = before[k] - (fluxes[k] - lower[k])
+                    swept[field, a - 1 - first, pl.ds(part, 8)] = before[k] - (fluxes[k] - lower[k])
                 before[k], here[k], steps[k], slopes[k] = here[k], after, step, slope
             lower = fluxes
 
 
-def sweep_y(zero, swept, work, a, fields, factors, wide):
+def sweep_y(zero, swept, work, number, fields, factors, wide):
     moved = []
     for field in fields:
-        below = swept[field, a, pl.ds(zero + 1, wide)]
-        here = swept[field, a, pl.ds(zero + 2, wide)]
-        slope = limited(here - below, below - swept[field, a, 0:wide])
-        work[0, field, a, 0:wide] = slope
-        flux = face_flux(factors, below, here, slope, work[0, field, a, pl.ds(zero + 1, wide)])
-        work[1, field, a, 0:wide] = flux
-        moved.append(here - (work[1, field, a, pl.ds(zero + 1, wide)] - flux))
+        below = swept[field, number, pl.ds(zero + 1, wide)]
+        here = swept[field, number, pl.ds(zero + 2, wide)]
+        slope = limited(here - below, below - swept[field, number, 0:wide])
+        work[0, field, number, 0:wide] = slope
+        flux = face_flux(factors, below, here, slope, work[0, field, number, pl.ds(zero + 1, wide)])
+        work[1, field, number, 0:wide] = flux
+        moved.append(here - (work[1, field, number, pl.ds(zero + 1, wide)] - flux))
     return moved
 
 
@@ -197,25 +213,110 @@
     return final
 
 
-def step_kernel(nx, ny, dt_ref, *refs):
-    own, x_edges, y_edges, corners = refs[0], refs[1:3], refs[3:5], refs[5:7]
-    passive, speed, speed_y, speed_z, flows, increment_ref = refs[7:13]
-    cells, third, stress, growth, heat, state, energy_one, swept, work = refs[13:]
-    nz = own.shape[-1]
+def spread_columns(zero, columns, tall, half, cells, stress, heat, growth):
+    for a in columns:
+        z = read(zero, cells, a, TOP - 4, tall, ZV)
+        spread = (
+            read(zero, cells, a + 1, TOP - 4, tall, XV)
+            - read(zero, cells, a - 1, TOP - 4, tall, XV)
+            + (read(zero, cells, a, TOP - 3, tall, YV) - read(zero, cells, a, TOP - 5, tall, YV))
+            + (up(z) - down(z))
+        )
+        warmth = per_mass(read(zero, cells, a, TOP - 4, tall, ENERGY), spread)
+        write(heat, a, warmth)
+        write(stress, a, read(zero, cells, a, TOP - 4, tall, DENSITY) * warmth)
+        write(growth, a, half * spread)
+
+
+def advance_columns(zero, columns, wide, half, cells, stress, heat, growth, passive, state, energies, nx):
+    for a in columns:
+        density, energy, x, y, z = [read(zero, cells, a, TOP - 2, wide, field) for field in range(5)]
+        grown = read(zero, growth, a, 2, wide)
+        centre = read(zero, stress, a, 2, wide)
+        scale = half / density
+        density_one = density / (1.0 + grown)
+        energy = energy - read(zero, heat, a, 2, wide) * grown
+        write(passive, a, density_one, 0)
+        write(passive, a, density_one * energy, 1)
+        write(state, a, x - scale * (read(zero, stress, a + 1, 2, wide) - read(zero, stress, a - 1, 2, wide)), 0)
+        write(state, a, y - scale * (read(zero, stress, a, 3, wide) - read(zero, stress, a, 1, wide)), 1)
+        write(state, a, z - scale * (up(centre) - down(centre)), 2)
+        if 0 <= a < nx:
+            write(energies, a, energy)
+
+
+def flow_columns(zero, first, last, ny, half, state, energies, swept, work, speed_y, speed_z, flows):
+    wide = ny + 4
+    sweep_x(
+        lambda field, a, part: read(zero, state, a, part, 8, field),
+        lambda a, part: read(zero, state, a, part, 8, 0),
+        swept, (0, 1, 2), first, last, wide, half,
+    )
+    peak = None
+    for a in range(first, last):
+        number = a - first
+        write(speed_y, a, swept[1, number, 0:wide])
+        below, here = [swept[1, number, pl.ds(zero + start, wide)] for start in (1, 2)]
+        moved = sweep_y(zero, swept, work, number, (0, 1, 2), face_factors(below, here, half), wide)
+        write(speed_z, a, moved[2])
+        final = sweep_z(moved, face_factors(down(moved[2]), moved[2], half))
+        for field in range(3):
+            write(flows, a, final[field][:ny], field)
+        signal = (
+            jnp.sqrt(0.56 * read(zero, energies, a, 2, wide))
+            + jnp.abs(final[0])
+            + jnp.abs(final[1])
+            + jnp.abs(final[2])
+        )
+        peak = signal if peak is None else jnp.maximum(peak, signal)
+    return peak
+
+
+def inner_kernel(nx, ny, dt_ref, *refs):
+    own, y_edges = refs[0], refs[1:3]
+    cells, stress, state, passive, energies, speed_y, speed_z, flows, peak_ref = refs[3:12]
+    heat, growth, swept, work = refs[12:]
     zero = hidden_zero()
-    dt = dt_ref[0]
-    half = 0.5 * dt
-    wide = ny + 4
-    tall = ny + 12
-
+    half = 0.5 * dt_ref[0]
     for field in range(5):
         for a in range(nx):
-            cells[field, a + LEFT, pl.ds(TOP, ny), :] = own[field, a]
+            cells[field, a, pl.ds(TOP, ny), :] = own[field, a]
+    for link, edge in zip(LINKS, y_edges):
+        low = is_low(link)
+        for field, a, rows, offset in y_layers(nx)[0]:
+            cells[field, a, pl.ds(TOP + pick(low, -rows, ny), rows), :] = edge[pl.ds(zero + offset, rows), :]
+    cells = [(cells, 0, nx, 0)]
+    stress, heat, growth = [[(ref, 1, nx - 1, 0)] for ref in (stress, heat, growth)]
+    state, passive, energies = [[(ref, 2, nx - 2, 0)] for ref in (state, passive, energies)]
+    speed_y, speed_z, flows = [[(ref, 4, nx - 4, 0)] for ref in (speed_y, speed_z, flows)]
+    spread_columns(zero, range(1, nx - 1), ny + 12, half, cells, stress, heat, growth)
+    advance_columns(
+        zero, range(2, nx - 2), ny + 4, half, cells, stress, heat, growth, passive, state, energies, nx
+    )
+    peak_ref[...] = flow_columns(
+        zero, 4, nx - 4, ny, half, state, energies, swept, work, speed_y, speed_z, flows
+    )
+
+
+def outer_pieces(ref, nx, reach, inside):
+    return [(ref, -reach, inside, 0), (ref, nx - inside, nx + reach, reach + inside)]
+
+
+def outer_kernel(nx, ny, dt_ref, *refs):
+    x_edges, corners = refs[0:2], refs[2:4]
+    cells_in, stress_in, state_in, energies_in, peak_in = refs[4:9]
+    state_out, passive_out, speed_y, speed_z, flows, increment_ref = refs[9:15]
+    beyond, third, stress_out, heat, growth, energies_out, swept, work = refs[15:]
+    nz = increment_ref.shape[-1]
+    zero = hidden_zero()
+    half = 0.5 * dt_ref[0]
+    wide, tall = ny + 4, ny + 12
+
     columns, singles, rows_of_corner = corner_layers()
     for k, (side, edge) in enumerate(zip(SIDES, x_edges)):
         for number, (field, past) in enumerate(x_layers()):
-            column = LEFT + (-past if side < 0 else nx - 1 + past)
-            cells[field, column, pl.ds(TOP, ny), :] = edge[pl.ds(zero + number * ny, ny), :]
+            column = LEFT - past if side < 0 else LEFT - 1 + past
+            beyond[field, column, pl.ds(TOP, ny), :] = edge[pl.ds(zero + number * ny, ny), :]
         offset = len(x_layers()) * ny
         third[k, EDGE_KINDS, pl.ds(TOP, ny), :] = edge[pl.ds(zero + offset, ny), :]
         offset += ny
@@ -223,109 +324,80 @@
             for kind in range(EDGE_KINDS):
                 third[k, kind, pl.ds(TOP + row, 1), :] = edge[pl.ds(zero + offset, 1), :]
                 offset += 1
-    for link, edge, corner in zip(LINKS, y_edges, corners):
+    for link, corner in zip(LINKS, corners):
         low = is_low(link)
-        for field, a, rows, offset in y_layers(nx)[0]:
-            to = pl.ds(TOP + pick(low, -rows, ny), rows)
-            cells[field, a + LEFT, to, :] = edge[pl.ds(zero + offset, rows), :]
         for k, side in enumerate(SIDES):
             base = zero + k * rows_of_corner
             for _, field, past, rows, offset in columns:
-                column = LEFT + (-past if side < 0 else nx - 1 + past)
+                column = LEFT - past if side < 0 else LEFT - 1 + past
                 to = pl.ds(TOP + pick(low, -rows, ny), rows)
-                cells[field, column, to, :] = corner[pl.ds(base + offset, rows), :]
+                beyond[field, column, to, :] = corner[pl.ds(base + offset, rows), :]
             third[k, EDGE_KINDS, pl.ds(TOP + pick(low, -2, ny + 1), 1), :] = corner[pl.ds(base + singles, 1), :]
             for kind in range(EDGE_KINDS):
                 to = pl.ds(TOP + pick(low, -1, ny), 1)
                 third[k, kind, to, :] = corner[pl.ds(base + (singles + 1 + kind), 1), :]
 
-    def at(ref, *index, start, count):
-        return ref[(*index, pl.ds(zero + start, count), slice(None))]
+    cells = [(cells_in, 0, nx, 0)] + outer_pieces(beyond, nx, LEFT, 0)
+    stress = outer_pieces(stress_out, nx, 3, 2) + [(stress_in, 2, nx - 2, 1)]
+    heat, growth = outer_pieces(heat, nx, 2, 2), outer_pieces(growth, nx, 2, 2)
+    state = outer_pieces(state_out, nx, 2, 2) + [(state_in, 2, nx - 2, 0)]
+    passive = outer_pieces(passive_out, nx, 2, 2)
+    energies = outer_pieces(energies_out, nx, 0, 2) + [(energies_in, 2, nx - 2, 0)]
+    speed_y, speed_z, flows = [outer_pieces(ref, nx, 0, 4) for ref in (speed_y, speed_z, flows)]
 
     row = lax.broadcasted_iota(jnp.int32, (tall, nz), 0) - 4
     for k, a in enumerate((-3, nx + 2)):
-        above = at(third, k, 3, start=TOP - 3, count=tall)
-        below = at(third, k, 3, start=TOP - 5, count=tall)
-        spread = at(third, k, 2, start=TOP - 4, count=tall)
+        above, below = [third[k, 3, pl.ds(zero + start, tall)] for start in (TOP - 3, TOP - 5)]
+        density, energy, spread, _, whole = [third[k, kind, pl.ds(zero + TOP - 4, tall)] for kind in range(5)]
         spread += jnp.where((row == -1) | (row == ny - 1), above, -below)
-        density, energy = [at(third, k, kind, start=TOP - 4, count=tall) for kind in range(2)]
         split = (row == -1) | (row == 0) | (row == ny - 1) | (row == ny)
-        whole = at(third, k, EDGE_KINDS, start=TOP - 4, count=tall)
-        stress[a + 3] = jnp.where(split, density * per_mass(energy, spread), whole)
-
-    for a in range(-2, nx + 2):
-        get = functools.partial(at, cells, start=TOP - 4, count=tall)
-        z = get(ZV, a + LEFT)
-        spread = (
-            get(XV, a + LEFT + 1)
-            - get(XV, a + LEFT - 1)
-            + (at(cells, YV, a + LEFT, start=TOP - 3, count=tall) - at(cells, YV, a + LEFT, start=TOP - 5, count=tall))
-            + (up(z) - down(z))
-        )
-        heat[a + 2] = per_mass(get(ENERGY, a + LEFT), spread)
-        stress[a + 3] = get(DENSITY, a + LEFT) * heat[a + 2]
-        growth[a + 2] = half * spread
-
-    for a in range(-2, nx + 2):
-        get = functools.partial(at, cells, start=TOP - 2, count=wide)
-        density = get(DENSITY, a + LEFT)
-        grown = at(growth, a + 2, start=2, count=wide)
-        centre = at(stress, a + 3, start=2, count=wide)
-        scale = half / density
-        density_one = density / (1.0 + grown)
-        energy = get(ENERGY, a + LEFT) - at(heat, a + 2, start=2, count=wide) * grown
-        passive[0, a + 2] = density_one
-        passive[1, a + 2] = density_one * energy
-        x_one = get(XV, a + LEFT) - scale * (
-            at(stress, a + 4, start=2, count=wide) - at(stress, a + 2, start=2, count=wide)
-        )
-        state[0, a + 2] = x_one
-        speed[a + 2] = x_one
-        state[1, a + 2] = get(YV, a + LEFT) - scale * (
-            at(stress, a + 3, start=3, count=wide) - at(stress, a + 3, start=1, count=wide)
-        )
-        state[2, a + 2] = get(ZV, a + LEFT) - scale * (up(centre) - down(centre))
-        if 0 <= a < nx:
-            energy_one[a, 0:wide] = energy
-
-    sweep_x(state, speed, swept, (0, 1, 2), half)
-    for a in range(nx):
-        speed_y[a, 0:wide] = swept[1, a, 0:wide]
-
-    peak = jnp.zeros((wide, nz), jnp.float32)
-    for a in range(nx):
-        below, here = at(swept, 1, a, start=1, count=wide), at(swept, 1, a, start=2, count=wide)
-        moved = sweep_y(zero, swept, work, a, (0, 1, 2), face_factors(below, here, half), wide)
-        speed_z[a] = moved[2]
-        final = sweep_z(moved, face_factors(down(moved[2]), moved[2], half))
-        for field in range(3):
-            flows[field, a] = final[field][:ny]
+        write(stress, a, jnp.where(split, density * per_mass(energy, spread), whole))
+
+    ends = (*range(-2, 2), *range(nx - 2, nx + 2))
+    spread_columns(zero, ends, tall, half, cells, stress, heat, growth)
+    advance_columns(zero, ends, wide, half, cells, stress, heat, growth, passive, state, energies, nx)
+    peak = peak_in[...]
+    for k, first in enumerate((0, nx - 4)):
         peak = jnp.maximum(
             peak,
-            jnp.sqrt(0.56 * at(energy_one, a, start=2, count=wide))
-            + jnp.abs(final[0])
-            + jnp.abs(final[1])
-            + jnp.abs(final[2]),
+            flow_columns(
+                zero, first, first + 4, ny, half, state, energies, swept.at[k], work.at[k], speed_y, speed_z, flows
+            ),
         )
-    row = lax.broadcasted_iota(jnp.int32, peak.shape, 0)
-    peak = jnp.max(jnp.where(row < ny, peak, 0.0), axis=0, keepdims=True)
+    peak = jnp.max(jnp.where(row[4 : 4 + wide] < ny, peak, 0.0), axis=0, keepdims=True)
     increment_ref[...] = jnp.broadcast_to(0.3 / peak, increment_ref.shape)
 
 
 def carry_kernel(nx, ny, dt_ref, *refs):
-    state, speed, speed_y, speed_z, flows, density_out, energy_out = refs[:7]
-    flow_outs, swept, work, written = refs[7:10], refs[10], refs[11], refs[12]
+    state_in, passive_in, speed_y_in, speed_z_in, flows_in = refs[0:5]
+    state_out, passive_out, speed_y_out, speed_z_out, flows_out = refs[5:10]
+    density_out, energy_out, flow_outs, swept, work, written = refs[10], refs[11], refs[12:15], refs[15], refs[16], refs[17]
     zero = hidden_zero()
     half = 0.5 * dt_ref[0]
     wide = ny + 4
-    copies = [pltpu.make_async_copy(flows.at[k], flow_outs[k], written.at[k]) for k in range(3)]
+    copies = []
+    for k in range(3):
+        for piece, (ref, first, last, number) in enumerate([(flows_in, 4, nx - 4, 0)] + outer_pieces(flows_out, nx, 0, 4)):
+            source = ref.at[k, pl.ds(number, last - first)]
+            copies.append(
+                pltpu.make_async_copy(source, flow_outs[k].at[pl.ds(first, last - first)], written.at[k, piece])
+            )
     for copy in copies:
         copy.start()
-    sweep_x(state, speed, swept, (0, 1), half)
+    state = outer_pieces(state_out, nx, 2, 2) + [(state_in, 2, nx - 2, 0)]
+    passive = outer_pieces(passive_out, nx, 2, 2) + [(passive_in, 2, nx - 2, 0)]
+    speed_y = outer_pieces(speed_y_out, nx, 0, 4) + [(speed_y_in, 4, nx - 4, 0)]
+    speed_z = outer_pieces(speed_z_out, nx, 0, 4) + [(speed_z_in, 4, nx - 4, 0)]
+    sweep_x(
+        lambda field, a, part: read(zero, passive, a, part, 8, field),
+        lambda a, part: read(zero, state, a, part, 8, 0),
+        swept, (0, 1), 0, nx, wide, half,
+    )
     for a in range(nx):
-        below, here = speed_y[a, pl.ds(zero + 1, wide)], speed_y[a, pl.ds(zero + 2, wide)]
+        below, here = [read(zero, speed_y, a, start, wide) for start in (1, 2)]
         moved = sweep_y(zero, swept, work, a, (0, 1), face_factors(below, here, half), wide)
-        final = sweep_z(moved, face_factors(down(speed_z[a]), speed_z[a], half))
+        along = read(zero, speed_z, a, 0, wide)
+        final = sweep_z(moved, face_factors(down(along), along, half))
         density_out[a] = final[0][:ny]
         energy_out[a] = final[1][:ny]
     for copy in copies:
@@ -368,40 +440,62 @@
     )(*x_edges)
     corners = [along_y(corner, link) for corner, link in zip(corners, LINKS)]
     increment = time_increment.reshape(1)
-    passed = [array(2, nx + 4, wide), array(nx + 4, wide), array(nx, wide + 8), array(nx, wide), array(3, nx, ny)]
-    *passed, smallest = pl.pallas_call(
-        functools.partial(step_kernel, nx, ny),
-        out_shape=passed + [array(lax.axis_size(("gx", "gy")))],
-        in_specs=[SMEM] + [VMEM] * 7,
+    passed_in = [array(3, nx - 4, wide), array(2, nx - 4, wide), array(nx - 8, wide + 8), array(nx - 8, wide), array(3, nx - 8, ny)]
+    passed_out = [array(3, 8, wide), array(2, 8, wide), array(8, wide + 8), array(8, wide), array(3, 8, ny)]
+    cells, stress, state_in, passive_in, energies, *rest_in, peak = pl.pallas_call(
+        functools.partial(inner_kernel, nx, ny),
+        out_shape=[
+            array(5, nx, ny + 20),
+            array(nx - 2, tall),
+            *passed_in[:2],
+            array(nx - 4, wide + 8),
+            *passed_in[2:],
+            array(wide),
+        ],
+        in_specs=[SMEM] + [VMEM] * 3,
+        out_specs=[VMEM] * 9,
+        scratch_shapes=[
+            scratch(nx - 2, tall),
+            scratch(nx - 2, tall),
+            scratch(3, nx - 8, wide + 8),
+            scratch(2, 3, nx - 8, wide + 8),
+        ],
+        compiler_params=limit(8),
+        cost_estimate=pl.CostEstimate(flops=5 * 10**6, bytes_accessed=2 * 10**6, transcendentals=0),
+        name="inner",
+    )(increment, own, *y_edges)
+    *outer, smallest = pl.pallas_call(
+        functools.partial(outer_kernel, nx, ny),
+        out_shape=passed_out + [array(lax.axis_size(("gx", "gy")))],
+        in_specs=[SMEM] + [VMEM] * 9,
         out_specs=[VMEM] * 6,
         scratch_shapes=[
-            scratch(5, nx + 6, ny + 20),
+            scratch(5, 2 * LEFT, ny + 20),
             scratch(2, EDGE_KINDS + 1, ny + 20),
-            scratch(nx + 6, tall),
-            scratch(nx + 4, tall),
-            scratch(nx + 4, tall),
-            scratch(3, nx + 4, wide),
-            scratch(nx, wide + 8),
-            scratch(3, nx, wide + 8),
-            scratch(2, 3, nx, wide + 8),
+            scratch(10, tall),
+            scratch(8, tall),
+            scratch(8, tall),
+            scratch(4, wide + 8),
+            scratch(2, 3, 4, wide + 8),
+            scratch(2, 2, 3, 4, wide + 8),
         ],
-        compiler_params=limit(12),
-        name="step",
-    )(increment, own, *x_edges, *y_edges, *corners)
+        compiler_params=limit(8),
+        name="outer",
+    )(increment, *x_edges, *corners, cells, stress, state_in, energies, peak)
     outs = pl.pallas_call(
         functools.partial(carry_kernel, nx, ny),
         out_shape=[array(nx, ny)] * 5,
-        in_specs=[SMEM] + [VMEM] * 5,
+        in_specs=[SMEM] + [VMEM] * 10,
         out_specs=[VMEM] * 2 + [HBM] * 3,
         scratch_shapes=[
             scratch(2, nx, wide + 8),
             scratch(2, 2, nx, wide + 8),
-            pltpu.SemaphoreType.DMA((3,)),
+            pltpu.SemaphoreType.DMA((3, 3)),
         ],
         compiler_params=limit(8),
         cost_estimate=pl.CostEstimate(flops=10**7, bytes_accessed=4 * 10**6, transcendentals=0),
         name="carry",
-    )(increment, *passed)
+    )(increment, state_in, passive_in, *rest_in, *outer)
     return (*outs, jnp.min(lax.all_to_all(smallest, ("gx", "gy"), 0, 0, tiled=True)))
 
 

time: 30 us -> 29.5 us (0.983)
  waiting for transfers between devices: 7.9 us -> 7 us
  Pallas kernels: 5.27 us -> 5.73 us
    ppermute x4, waiting for transfers between devices: 1.54 us -> 0.65 us  [along_y(): return lax.ppermute(value, 'gy', list(enumerate(partners)))]
    pallas_call x1 -> x2, Pallas kernels: 2.04 us -> 2.49 us  [the longest x1 1.6 us: body(): pl.pallas_call(functools.partial(outer_kernel, nx, ny), out_shape=passed_...]
  transfers between devices with their start and end apart: 7 -> 7, of which waited for: 4 -> 4; matrix products, arithmetic and copies ran while one was open for 0% -> 0% of each run, Pallas kernels for 7% -> 10%
where the time goes in v14:
time: 29.5 us; the launch traced here: 29.3 us
  starting transfers between devices  14.6 us (49%)
  waiting for transfers between devices  7 us (24%)
  Pallas kernels  5.73 us (19%)
  between operations  1.34 us (5%)
  other arithmetic  0.63 us (2%)
    ppermute x2, starting transfers between devices, along_x(): lax.ppermute(value, 'gx', [((i + side) % count, i) for i in range(count)])  6.12 us
    all_to_all x1, starting transfers between devices, body(): lax.all_to_all(smallest, ('gx', 'gy'), 0, 0, tiled=True)  5.13 us
    all_to_all x1, waiting for transfers between devices, body(): lax.all_to_all(smallest, ('gx', 'gy'), 0, 0, tiled=True)  5.1 us
    ppermute x4, starting transfers between devices, along_y(): return lax.ppermute(value, 'gy', list(enumerate(partners)))  3.37 us
    pallas_call x1, Pallas kernels, body(): pl.pallas_call(functools.partial(carry_kernel, nx, ny), out_shape=[array(...  2.04 us
    pallas_call x1, Pallas kernels, body(): pl.pallas_call(functools.partial(outer_kernel, nx, ny), out_shape=passed_...  1.6 us
    ppermute x2, waiting for transfers between devices, along_x(): lax.ppermute(value, 'gx', [((i + side) % count, i) for i in range(count)])  1.25 us
    pallas_call x1, Pallas kernels, body(): pl.pallas_call(functools.partial(pack_kernel, nx, ny), out_shape=[array(5...  1.18 us
  transfers between devices with their start and end apart: 7, of which 4 were waited for; matrix products, arithmetic and copies ran while one was open for 0% of the time, Pallas kernels for 10%

profile of v14, /device:TPU:0, one launch (start us, length us, event | category | flops | bytes accessed | tf_op | source)
XLA Modules:
  0.0 29.3 jit_solution(2471706298121615300)
XLA Ops:
  0.6 1.2 %pack.1 = (f32[5,12,12,128]{3,2,1,0:T(8,128)S(1)}, f32[152,128]{1,0:T(8,128)S(1)}, f32[152,128]{1,0:T(8,128)S(1)}, f32[192,128]{1,0:T(8,128)S(1)}, f32[192,128]{1,0:T(8,128)S(1)}) custom-call(f32[12,12,128]{2,1,0:T(8,128)} %refs_0_.1, f32[12,12,128]{2,1,0:T(8,128)} %refs_1_.1, f32[12,12,128]{2,1,0:T(8,128)} %refs_2_.1, f32[12,12,128]{2,1,0:T(8,128)} %refs_3_.1, ...), custom_call_target="tpu_custom_call" | custom-call | tf_op jit(solution)/shard_map/pack/pallas_call | solution.py:422
  1.8 3.0 %collective-permute-start.2 = (f32[152,128]{1,0:T(8,128)S(1)}, f32[152,128]{1,0:T(8,128)S(1)}, u32[]{:S(2)}, u32[]{:S(2)}) collective-permute-start(f32[152,128]{1,0:T(8,128)S(1)} %get-tuple-element.41), channel_id=1, source_target_pairs={{28,0},{0,4},{4,8},{8,12},{12,16},{16,20},{20,24},{24,28},{29,1},{... | collective-permute-start | bytes 233480 | tf_op jit(solution)/shard_map/ppermute | solution.py:62
  4.8 3.1 %collective-permute-start.3 = (f32[152,128]{1,0:T(8,128)S(1)}, f32[152,128]{1,0:T(8,128)S(1)}, u32[]{:S(2)}, u32[]{:S(2)}) collective-permute-start(f32[152,128]{1,0:T(8,128)S(1)} %get-tuple-element.42), channel_id=1, source_target_pairs={{4,0},{8,4},{12,8},{16,12},{20,16},{24,20},{28,24},{0,28},{5,1},{9... | collective-permute-start | bytes 233480 | tf_op jit(solution)/shard_map/ppermute | solution.py:62
  7.9 0.7 %collective-permute-start = (f32[192,128]{1,0:T(8,128)S(1)}, f32[192,128]{1,0:T(8,128)S(1)}, u32[]{:S(2)}, u32[]{:S(2)}) collective-permute-start(f32[192,128]{1,0:T(8,128)S(1)} %get-tuple-element.34), channel_id=1, source_target_pairs={{0,3},{1,2},{2,1},{3,0},{4,7},{5,6},{6,5},{7,4},{8,11},{9,10},{10,... | collective-permute-start | bytes 294920 | tf_op jit(solution)/shard_map/ppermute | solution.py:68
  8.6 1.1 %collective-permute-start.1 = (f32[192,128]{1,0:T(8,128)S(1)}, f32[192,128]{1,0:T(8,128)S(1)}, u32[]{:S(2)}, u32[]{:S(2)}) collective-permute-start(f32[192,128]{1,0:T(8,128)S(1)} %get-tuple-element.35), channel_id=1, source_target_pairs={{0,1},{1,0},{2,3},{3,2},{4,5},{5,4},{6,7},{7,6},{8,9},{9,8},{10,11... | collective-permute-start | bytes 294920 | tf_op jit(solution)/shard_map/ppermute | solution.py:68
  9.7 0.7 %collective-permute-done.2.refs_0_ = f32[152,128]{1,0:T(8,128)S(1)} collective-permute-done((f32[152,128]{1,0:T(8,128)S(1)}, f32[152,128]{1,0:T(8,128)S(1)}, u32[]{:S(2)}, u32[]{:S(2)}) %collective-permute-start.2) | collective-permute-done | bytes 77856 | tf_op jit(solution)/shard_map/ppermute | solution.py:62
  10.3 0.6 %collective-permute-done.3.refs_1_ = f32[152,128]{1,0:T(8,128)S(1)} collective-permute-done((f32[152,128]{1,0:T(8,128)S(1)}, f32[152,128]{1,0:T(8,128)S(1)}, u32[]{:S(2)}, u32[]{:S(2)}) %collective-permute-start.3) | collective-permute-done | bytes 77856 | tf_op jit(solution)/shard_map/ppermute | solution.py:62
  10.9 0.1 collective-permute-start.4
  11.0 1.6 %collective-permute-start.5 = (f32[80,128]{1,0:T(8,128)S(1)}, f32[80,128]{1,0:T(8,128)S(1)}, u32[]{:S(2)}, u32[]{:S(2)}) collective-permute-start(f32[80,128]{1,0:T(8,128)S(1)} %get-tuple-element.44), channel_id=1, source_target_pairs={{0,1},{1,0},{2,3},{3,2},{4,5},{5,4},{6,7},{7,6},{8,9},{9,8},{10,11... | collective-permute-start | bytes 122888 | tf_op jit(solution)/shard_map/ppermute | solution.py:68
  13.3 0.0 collective-permute-done.refs_1_
  13.3 0.0 collective-permute-done.1.refs_2_
  13.3 0.9 %inner.1 = (f32[5,12,32,128]{3,2,1,0:T(8,128)S(1)}, f32[10,24,128]{2,1,0:T(8,128)S(1)}, f32[3,8,16,128]{3,2,1,0:T(8,128)S(1)}, f32[2,8,16,128]{3,2,1,0:T(8,128)S...) custom-call(f32[1]{0:T(128)} %bitcast.4.dt_ref, ...), custom_call_target="tpu_custom_call" | custom-call | flops 5000000 | bytes 2000000 | tf_op jit(solution)/shard_map/inner/pallas_call | solution.py:445
  14.2 0.6 %collective-permute-done.4.refs_2_ = f32[80,128]{1,0:T(8,128)S(1)} collective-permute-done((f32[80,128]{1,0:T(8,128)S(1)}, f32[80,128]{1,0:T(8,128)S(1)}, u32[]{:S(2)}, u32[]{:S(2)}) %collective-permute-start.4) | collective-permute-done | bytes 40992 | tf_op jit(solution)/shard_map/ppermute | solution.py:68
  14.8 0.0 collective-permute-done.5.refs_3_
  14.8 1.6 %outer.1 = (f32[3,8,16,128]{3,2,1,0:T(8,128)S(1)}, f32[2,8,16,128]{3,2,1,0:T(8,128)S(1)}, f32[8,24,128]{2,1,0:T(8,128)S(1)}, f32[8,16,128]{2,1,0:T(8,128)S(1)}, ...) custom-call(f32[1]{0:T(128)} %bitcast.5.dt_ref, f32[152,128]{1,0:T(8,128)S(1)} %collective-permute-done.2.refs_0_, ...), custom_call_target="tpu_custom_call" | custom-call | tf_op jit(solution)/shard_map/outer/pallas_call | solution.py:467
  16.4 5.1 %all-to-all-start = ((f32[32,1,128]{2,1,0:T(1,128)}), f32[32,1,128]{2,1,0:T(1,128)S(1)}, u32[]{:S(2)}, u32[]{:S(2)}) async-start(f32[32,1,128]{2,1,0:T(1,128)} %bitcast.2), calls=%async_computation | async-start | bytes 32768 | tf_op jit(solution)/shard_map/all_to_all | solution.py:499
  21.6 2.0 %carry.1 = (f32[12,12,128]{2,1,0:T(8,128)}, f32[12,12,128]{2,1,0:T(8,128)}, f32[12,12,128]{2,1,0:T(8,128)}, f32[12,12,128]{2,1,0:T(8,128)}, f32[12,12,128]{2,1,0:T(8,128)}) custom-call(f32[1]{0:T(128)} %bitcast.6.dt_ref, f32[3,8,16,128]{3,2,1,0:T(8,128)S(1)} %get-tuple-element.36.refs_6_.refs_0_, f32[2,8,16,128]{3,2,1,0:T(8,128)S(1)} %get-tuple-element.37.refs_1_, ...), custom_call_target="tpu_custom_call" | custom-call | flops 10000000 | bytes 4000000 | tf_op jit(solution)/shard_map/carry/pallas_call | solution.py:485
  23.6 5.1 %all-to-all-done = f32[32,1,128]{2,1,0:T(1,128)S(1)} async-done(((f32[32,1,128]{2,1,0:T(1,128)}), f32[32,1,128]{2,1,0:T(1,128)S(1)}, u32[]{:S(2)}, u32[]{:S(2)}) %all-to-all-start) | async-done | bytes 16416 | tf_op jit(solution)/shard_map/all_to_all | solution.py:499
  28.7 0.6 %reduce_min.9 = f32[]{:T(128)} reduce(f32[32,1,128]{2,1,0:T(1,128)S(1)} %all-to-all-done, f32[]{:T(128)} %constant.0.clone.1), dimensions={0,1,2}, to_apply=%region_0.0 | reduce | flops 4095 | bytes 16392 | tf_op jit(solution)/shard_map/reduce_min | solution.py:499
  (1 shorter events, 0.0 us)
Async XLA Ops:
  1.8 8.5 %collective-permute-start.2 = (f32[152,128]{1,0:T(8,128)S(1)}, f32[152,128]{1,0:T(8,128)S(1)}, u32[]{:S(2)}, u32[]{:S(2)}) collective-permute-start(f32[152,128]{1,0:T(8,128)S(1)} %get-tuple-element.41), channel_id=1, source_target_pairs={{28,0},{0,4},{4,8},{8,12},{12,16},{16,20},{20,24},{24,28},{29,1},{... | collective-permute-start | bytes 233480 | tf_op jit(solution)/shard_map/ppermute | solution.py:62
  4.8 6.1 %collective-permute-start.3 = (f32[152,128]{1,0:T(8,128)S(1)}, f32[152,128]{1,0:T(8,128)S(1)}, u32[]{:S(2)}, u32[]{:S(2)}) collective-permute-start(f32[152,128]{1,0:T(8,128)S(1)} %get-tuple-element.42), channel_id=1, source_target_pairs={{4,0},{8,4},{12,8},{16,12},{20,16},{24,20},{28,24},{0,28},{5,1},{9... | collective-permute-start | bytes 233480 | tf_op jit(solution)/shard_map/ppermute | solution.py:62
  7.9 5.3 %collective-permute-start = (f32[192,128]{1,0:T(8,128)S(1)}, f32[192,128]{1,0:T(8,128)S(1)}, u32[]{:S(2)}, u32[]{:S(2)}) collective-permute-start(f32[192,128]{1,0:T(8,128)S(1)} %get-tuple-element.34), channel_id=1, source_target_pairs={{0,3},{1,2},{2,1},{3,0},{4,7},{5,6},{6,5},{7,4},{8,11},{9,10},{10,... | collective-permute-start | bytes 294920 | tf_op jit(solution)/shard_map/ppermute | solution.py:68
  8.6 4.7 %collective-permute-start.1 = (f32[192,128]{1,0:T(8,128)S(1)}, f32[192,128]{1,0:T(8,128)S(1)}, u32[]{:S(2)}, u32[]{:S(2)}) collective-permute-start(f32[192,128]{1,0:T(8,128)S(1)} %get-tuple-element.35), channel_id=1, source_target_pairs={{0,1},{1,0},{2,3},{3,2},{4,5},{5,4},{6,7},{7,6},{8,9},{9,8},{10,11... | collective-permute-start | bytes 294920 | tf_op jit(solution)/shard_map/ppermute | solution.py:68
  10.9 3.9 %collective-permute-start.4 = (f32[80,128]{1,0:T(8,128)S(1)}, f32[80,128]{1,0:T(8,128)S(1)}, u32[]{:S(2)}, u32[]{:S(2)}) collective-permute-start(f32[80,128]{1,0:T(8,128)S(1)} %get-tuple-element.43), channel_id=1, source_target_pairs={{0,3},{1,2},{2,1},{3,0},{4,7},{5,6},{6,5},{7,4},{8,11},{9,10},{10,... | collective-permute-start | bytes 122888 | tf_op jit(solution)/shard_map/ppermute | solution.py:68
  11.0 3.8 %collective-permute-start.5 = (f32[80,128]{1,0:T(8,128)S(1)}, f32[80,128]{1,0:T(8,128)S(1)}, u32[]{:S(2)}, u32[]{:S(2)}) collective-permute-start(f32[80,128]{1,0:T(8,128)S(1)} %get-tuple-element.44), channel_id=1, source_target_pairs={{0,1},{1,0},{2,3},{3,2},{4,5},{5,4},{6,7},{7,6},{8,9},{9,8},{10,11... | collective-permute-start | bytes 122888 | tf_op jit(solution)/shard_map/ppermute | solution.py:68
  16.4 12.3 %all-to-all-start = ((f32[32,1,128]{2,1,0:T(1,128)}), f32[32,1,128]{2,1,0:T(1,128)S(1)}, u32[]{:S(2)}, u32[]{:S(2)}) async-start(f32[32,1,128]{2,1,0:T(1,128)} %bitcast.2), calls=%async_computation | async-start | bytes 32768 | tf_op jit(solution)/shard_map/all_to_all | solution.py:499

commit v15 on v14

--- a/solution.py
+++ b/solution.py
@@ -76,40 +76,55 @@
     return 0.4 * energy + 0.5 * jnp.square(jnp.minimum(0.5 * spread, 0.0))
 
 
-def pack_kernel(nx, ny, *refs):
-    fields, own, x_edges, y_edges, padded, arrived = refs[:5], refs[5], refs[6:8], refs[8:10], refs[10], refs[11]
+def x_pack_kernel(nx, ny, *refs):
+    fields, x_edges, near, padded, arrived = refs[:5], refs[5:7], refs[7], refs[8], refs[9]
+    zero = hidden_zero()
+    copies = [
+        pltpu.make_async_copy(
+            fields[field].at[pl.ds(first, 4)], near.at[field, pl.ds(4 * k, 4)], arrived.at[field, k]
+        )
+        for field in range(5)
+        for k, first in enumerate((nx - 4, 0))
+    ]
+    for copy in copies:
+        copy.start()
+    for current in range(5):
+        for k, (side, edge) in enumerate(zip(SIDES, x_edges)):
+            copies[2 * current + k].wait()
+            for number, (field, past) in enumerate(x_layers()):
+                if field == current:
+                    edge[pl.ds(zero + number * ny, ny), :] = near[field, 4 - past if side < 0 else 3 + past]
+    for k, (side, edge) in enumerate(zip(SIDES, x_edges)):
+        a = 1 if side < 0 else 6
+        offset = len(x_layers()) * ny
+        padded[k] = jnp.zeros_like(padded[k])
+        padded[k, pl.ds(TOP, ny), :] = near[YV, a]
+        spread = near[XV, a + 1] - near[XV, a - 1]
+        spread += padded[k, pl.ds(zero + (TOP + 1), ny), :] - padded[k, pl.ds(zero + (TOP - 1), ny), :]
+        spread += up(near[ZV, a]) - down(near[ZV, a])
+        edge[pl.ds(zero + offset, ny), :] = near[DENSITY, a] * per_mass(near[ENERGY, a], spread)
+        offset += ny
+        padded[k, pl.ds(TOP, ny), :] = spread
+        for row in (0, ny - 1):
+            for value in (near[DENSITY, a, pl.ds(row, 1), :], near[ENERGY, a, pl.ds(row, 1), :],
+                          padded[k, pl.ds(TOP + row, 1), :], near[YV, a, pl.ds(row, 1), :]):
+                edge[pl.ds(zero + offset, 1), :] = value
+                offset += 1
+
+
+def y_pack_kernel(nx, ny, *refs):
+    fields, own, y_edges, arrived = refs[:5], refs[5], refs[6:8], refs[8]
     zero = hidden_zero()
     copies = [pltpu.make_async_copy(fields[field], own.at[field], arrived.at[field]) for field in range(5)]
     for copy in copies:
         copy.start()
     for current, copy in enumerate(copies):
         copy.wait()
-        for side, edge in zip(SIDES, x_edges):
-            for number, (field, past) in enumerate(x_layers()):
-                if field == current:
-                    column = nx - past if side < 0 else past - 1
-                    edge[pl.ds(zero + number * ny, ny), :] = own[field, column]
         for link, edge in zip(LINKS, y_edges):
             for field, a, rows, offset in y_layers(nx)[0]:
                 if field == current:
                     start = pick(is_low(link), 0, ny - rows)
                     edge[pl.ds(zero + offset, rows), :] = own[field, a, pl.ds(start, rows), :]
-    for k, (side, edge) in enumerate(zip(SIDES, x_edges)):
-        a = nx - 3 if side < 0 else 2
-        offset = len(x_layers()) * ny
-        padded[k] = jnp.zeros_like(padded[k])
-        padded[k, pl.ds(TOP, ny), :] = own[YV, a]
-        spread = own[XV, a + 1] - own[XV, a - 1]
-        spread += padded[k, pl.ds(zero + (TOP + 1), ny), :] - padded[k, pl.ds(zero + (TOP - 1), ny), :]
-        spread += up(own[ZV, a]) - down(own[ZV, a])
-        edge[pl.ds(zero + offset, ny), :] = own[DENSITY, a] * per_mass(own[ENERGY, a], spread)
-        offset += ny
-        padded[k, pl.ds(TOP, ny), :] = spread
-        for row in (0, ny - 1):
-            for value in (own[DENSITY, a, pl.ds(row, 1), :], own[ENERGY, a, pl.ds(row, 1), :],
-                          padded[k, pl.ds(TOP + row, 1), :], own[YV, a, pl.ds(row, 1), :]):
-                edge[pl.ds(zero + offset, 1), :] = value
-                offset += 1
 
 
 def corner_kernel(ny, *refs):
@@ -189,17 +204,25 @@
             lower = fluxes
 
 
-def sweep_y(zero, swept, work, number, fields, factors, wide):
-    moved = []
-    for field in fields:
-        below = swept[field, number, pl.ds(zero + 1, wide)]
-        here = swept[field, number, pl.ds(zero + 2, wide)]
-        slope = limited(here - below, below - swept[field, number, 0:wide])
+def sweep_y(zero, swept, work, numbers, fields, factors, wide):
+    cases = [(number, field) for number in numbers for field in fields]
+
+    def rows(number, field, start):
+        return swept[field, number, pl.ds(zero + start, wide)]
+
+    for number, field in cases:
+        below = rows(number, field, 1)
+        slope = limited(rows(number, field, 2) - below, below - rows(number, field, 0))
         work[0, field, number, 0:wide] = slope
-        flux = face_flux(factors, below, here, slope, work[0, field, number, pl.ds(zero + 1, wide)])
+    for number, field in cases:
+        slope, above = [work[0, field, number, pl.ds(zero + start, wide)] for start in (0, 1)]
+        flux = face_flux(factors[number], rows(number, field, 1), rows(number, field, 2), slope, above)
         work[1, field, number, 0:wide] = flux
-        moved.append(here - (work[1, field, number, pl.ds(zero + 1, wide)] - flux))
-    return moved
+    moved = {}
+    for number, field in cases:
+        flux, above = [work[1, field, number, pl.ds(zero + start, wide)] for start in (0, 1)]
+        moved[number, field] = rows(number, field, 2) - (above - flux)
+    return [[moved[number, field] for field in fields] for number in numbers]
 
 
 def sweep_z(moved, factors):
@@ -252,12 +275,14 @@
         lambda a, part: read(zero, state, a, part, 8, 0),
         swept, (0, 1, 2), first, last, wide, half,
     )
+    numbers = range(last - first)
+    factors = []
+    for number in numbers:
+        below, here = [swept[1, number, pl.ds(zero + start, wide)] for start in (1, 2)]
+        factors.append(face_factors(below, here, half))
+        write(speed_y, first + number, swept[1, number, 0:wide])
     peak = None
-    for a in range(first, last):
-        number = a - first
-        write(speed_y, a, swept[1, number, 0:wide])
-        below, here = [swept[1, number, pl.ds(zero + start, wide)] for start in (1, 2)]
-        moved = sweep_y(zero, swept, work, number, (0, 1, 2), face_factors(below, here, half), wide)
+    for a, moved in zip(range(first, last), sweep_y(zero, swept, work, numbers, (0, 1, 2), factors, wide)):
         write(speed_z, a, moved[2])
         final = sweep_z(moved, face_factors(down(moved[2]), moved[2], half))
         for field in range(3):
@@ -393,9 +418,8 @@
         lambda a, part: read(zero, state, a, part, 8, 0),
         swept, (0, 1), 0, nx, wide, half,
     )
-    for a in range(nx):
-        below, here = [read(zero, speed_y, a, start, wide) for start in (1, 2)]
-        moved = sweep_y(zero, swept, work, a, (0, 1), face_factors(below, here, half), wide)
+    factors = [face_factors(*[read(zero, speed_y, a, start, wide) for start in (1, 2)], half) for a in range(nx)]
+    for a, moved in enumerate(sweep_y(zero, swept, work, range(nx), (0, 1), factors, wide)):
         along = read(zero, speed_z, a, 0, wide)
         final = sweep_z(moved, face_factors(down(along), along, half))
         density_out[a] = final[0][:ny]
@@ -419,17 +443,27 @@
         return pltpu.CompilerParams(vmem_limit_bytes=mebibytes * 1024 * 1024)
 
     x_edge, y_edge, corner = array(x_edge_rows(ny)), array(y_layers(nx)[1]), array(2 * corner_layers()[2])
-    own, *edges = pl.pallas_call(
-        functools.partial(pack_kernel, nx, ny),
-        out_shape=[array(5, nx, ny), x_edge, x_edge, y_edge, y_edge],
+    placed = [pltpu.with_memory_space_constraint(field, pltpu.HBM) for field in fields]
+    x_edges = pl.pallas_call(
+        functools.partial(x_pack_kernel, nx, ny),
+        out_shape=[x_edge] * 2,
         in_specs=[HBM] * 5,
-        out_specs=[VMEM] * 5,
-        scratch_shapes=[scratch(2, ny + 20), pltpu.SemaphoreType.DMA((5,))],
+        out_specs=[VMEM] * 2,
+        scratch_shapes=[scratch(5, 8, ny), scratch(2, ny + 20), pltpu.SemaphoreType.DMA((5, 2))],
         compiler_params=limit(4),
-        name="pack",
-    )(*[pltpu.with_memory_space_constraint(field, pltpu.HBM) for field in fields])
-    x_edges = [along_x(edge, side) for edge, side in zip(edges[:2], SIDES)]
-    y_edges = [along_y(edge, link) for edge, link in zip(edges[2:], LINKS)]
+        name="x_pack",
+    )(*placed)
+    x_edges = [along_x(edge, side) for edge, side in zip(x_edges, SIDES)]
+    own, *y_edges = pl.pallas_call(
+        functools.partial(y_pack_kernel, nx, ny),
+        out_shape=[array(5, nx, ny), y_edge, y_edge],
+        in_specs=[HBM] * 5,
+        out_specs=[VMEM] * 3,
+        scratch_shapes=[pltpu.SemaphoreType.DMA((5,))],
+        compiler_params=limit(4),
+        name="y_pack",
+    )(*placed)
+    y_edges = [along_y(edge, link) for edge, link in zip(y_edges, LINKS)]
     corners = pl.pallas_call(
         functools.partial(corner_kernel, ny),
         out_shape=[corner] * 2,

time: 29.5 us -> 29.4 us (level)
  waiting for transfers between devices: 7 us -> 6.1 us
  Pallas kernels: 5.73 us -> 6.48 us
    ppermute x2, waiting for transfers between devices: 1.25 us -> 0.1 us  [along_x(): lax.ppermute(value, 'gx', [((i + side) % count, i) for i in range(count)])]
    pallas_call x1 -> x2, Pallas kernels: 1.18 us -> 2.15 us  [the longest x1 1.08 us: body(): pl.pallas_call(functools.partial(y_pack_kernel, nx, ny), out_shape=[array...]
  transfers between devices with their start and end apart: 7 -> 7, of which waited for: 4 -> 3; matrix products, arithmetic and copies ran while one was open for 0% -> 0% of each run, Pallas kernels for 10% -> 13%
where the time goes in v15:
time: 29.4 us; the launch traced here: 29.1 us
  starting transfers between devices  14.6 us (50%)
  Pallas kernels  6.48 us (22%)
  waiting for transfers between devices  6.1 us (21%)
  between operations  1.34 us (5%)
  other arithmetic  0.63 us (2%)
    ppermute x2, starting transfers between devices, along_x(): lax.ppermute(value, 'gx', [((i + side) % count, i) for i in range(count)])  6.12 us
    all_to_all x1, waiting for transfers between devices, body(): lax.all_to_all(smallest, ('gx', 'gy'), 0, 0, tiled=True)  5.16 us
    all_to_all x1, starting transfers between devices, body(): lax.all_to_all(smallest, ('gx', 'gy'), 0, 0, tiled=True)  5.03 us
    ppermute x4, starting transfers between devices, along_y(): return lax.ppermute(value, 'gy', list(enumerate(partners)))  3.44 us
    pallas_call x1, Pallas kernels, body(): pl.pallas_call(functools.partial(carry_kernel, nx, ny), out_shape=[array(...  1.98 us
    pallas_call x1, Pallas kernels, body(): pl.pallas_call(functools.partial(outer_kernel, nx, ny), out_shape=passed_...  1.51 us
    pallas_call x1, Pallas kernels, body(): pl.pallas_call(functools.partial(y_pack_kernel, nx, ny), out_shape=[array...  1.08 us
    pallas_call x1, Pallas kernels, body(): pl.pallas_call(functools.partial(x_pack_kernel, nx, ny), out_shape=[x_edg...  1.08 us
  transfers between devices with their start and end apart: 7, of which 3 were waited for; matrix products, arithmetic and copies ran while one was open for 0% of the time, Pallas kernels for 13%

profile of v15, /device:TPU:0, one launch (start us, length us, event | category | flops | bytes accessed | tf_op | source)
XLA Modules:
  0.0 29.1 jit_solution(17244101788667802575)
XLA Ops:
  0.6 1.1 %x_pack.1 = (f32[152,128]{1,0:T(8,128)S(1)}, f32[152,128]{1,0:T(8,128)S(1)}) custom-call(f32[12,12,128]{2,1,0:T(8,128)} %refs_0_.3, f32[12,12,128]{2,1,0:T(8,128)} %refs_1_.3, f32[12,12,128]{2,1,0:T(8,128)} %refs_2_.3, f32[12,12,128]{2,1,0:T(8,128)} %refs_3_.3, f32[12,12,128]{2,1,0:T(8,128)} %refs_4_.3), custom_call_target="tpu_custom_call" | custom-call | tf_op jit(solution)/shard_map/x_pack/pallas_call | solution.py:447
  1.7 3.0 %collective-permute-start.2 = (f32[152,128]{1,0:T(8,128)S(1)}, f32[152,128]{1,0:T(8,128)S(1)}, u32[]{:S(2)}, u32[]{:S(2)}) collective-permute-start(f32[152,128]{1,0:T(8,128)S(1)} %get-tuple-element.41), channel_id=1, source_target_pairs={{28,0},{0,4},{4,8},{8,12},{12,16},{16,20},{20,24},{24,28},{29,1},{... | collective-permute-start | bytes 233480 | tf_op jit(solution)/shard_map/ppermute | solution.py:62
  4.7 3.1 %collective-permute-start.3 = (f32[152,128]{1,0:T(8,128)S(1)}, f32[152,128]{1,0:T(8,128)S(1)}, u32[]{:S(2)}, u32[]{:S(2)}) collective-permute-start(f32[152,128]{1,0:T(8,128)S(1)} %get-tuple-element.42), channel_id=1, source_target_pairs={{4,0},{8,4},{12,8},{16,12},{20,16},{24,20},{28,24},{0,28},{5,1},{9... | collective-permute-start | bytes 233480 | tf_op jit(solution)/shard_map/ppermute | solution.py:62
  7.8 1.1 %y_pack.1 = (f32[5,12,12,128]{3,2,1,0:T(8,128)S(1)}, f32[192,128]{1,0:T(8,128)S(1)}, f32[192,128]{1,0:T(8,128)S(1)}) custom-call(f32[12,12,128]{2,1,0:T(8,128)} %refs_0_.3, f32[12,12,128]{2,1,0:T(8,128)} %refs_1_.3, f32[12,12,128]{2,1,0:T(8,128)} %refs_2_.3, f32[12,12,128]{2,1,0:T(8,128)} %refs_3_.3, f32[12,12,128]{2,1,0:T(8,128)} %refs_4_.3), custom_call_target="tpu_custom_call" | custom-call | tf_op jit(solution)/shard_map/y_pack/pallas_call | solution.py:457
  8.9 0.7 %collective-permute-start = (f32[192,128]{1,0:T(8,128)S(1)}, f32[192,128]{1,0:T(8,128)S(1)}, u32[]{:S(2)}, u32[]{:S(2)}) collective-permute-start(f32[192,128]{1,0:T(8,128)S(1)} %get-tuple-element.34), channel_id=1, source_target_pairs={{0,3},{1,2},{2,1},{3,0},{4,7},{5,6},{6,5},{7,4},{8,11},{9,10},{10,... | collective-permute-start | bytes 294920 | tf_op jit(solution)/shard_map/ppermute | solution.py:68
  9.6 1.1 %collective-permute-start.1 = (f32[192,128]{1,0:T(8,128)S(1)}, f32[192,128]{1,0:T(8,128)S(1)}, u32[]{:S(2)}, u32[]{:S(2)}) collective-permute-start(f32[192,128]{1,0:T(8,128)S(1)} %get-tuple-element.35), channel_id=1, source_target_pairs={{0,1},{1,0},{2,3},{3,2},{4,5},{5,4},{6,7},{7,6},{8,9},{9,8},{10,11... | collective-permute-start | bytes 294920 | tf_op jit(solution)/shard_map/ppermute | solution.py:68
  10.7 0.0 collective-permute-done.2.refs_0_
  10.7 0.1 collective-permute-done.3.refs_1_
  10.8 0.1 collective-permute-start.4
  10.9 1.6 %collective-permute-start.5 = (f32[80,128]{1,0:T(8,128)S(1)}, f32[80,128]{1,0:T(8,128)S(1)}, u32[]{:S(2)}, u32[]{:S(2)}) collective-permute-start(f32[80,128]{1,0:T(8,128)S(1)} %get-tuple-element.44), channel_id=1, source_target_pairs={{0,1},{1,0},{2,3},{3,2},{4,5},{5,4},{6,7},{7,6},{8,9},{9,8},{10,11... | collective-permute-start | bytes 122888 | tf_op jit(solution)/shard_map/ppermute | solution.py:68
  13.1 0.8 %collective-permute-done.refs_1_ = f32[192,128]{1,0:T(8,128)S(1)} collective-permute-done((f32[192,128]{1,0:T(8,128)S(1)}, f32[192,128]{1,0:T(8,128)S(1)}, u32[]{:S(2)}, u32[]{:S(2)}) %collective-permute-start) | collective-permute-done | bytes 98336 | tf_op jit(solution)/shard_map/ppermute | solution.py:68
  13.9 0.0 collective-permute-done.1.refs_2_
  13.9 0.8 %inner.1 = (f32[5,12,32,128]{3,2,1,0:T(8,128)S(1)}, f32[10,24,128]{2,1,0:T(8,128)S(1)}, f32[3,8,16,128]{3,2,1,0:T(8,128)S(1)}, f32[2,8,16,128]{3,2,1,0:T(8,128)S...) custom-call(f32[1]{0:T(128)} %bitcast.4.dt_ref, ...), custom_call_target="tpu_custom_call" | custom-call | flops 5000000 | bytes 2000000 | tf_op jit(solution)/shard_map/inner/pallas_call | solution.py:479
  14.8 0.0 collective-permute-done.4.refs_2_
  14.8 0.0 collective-permute-done.5.refs_3_
  14.8 1.5 %outer.1 = (f32[3,8,16,128]{3,2,1,0:T(8,128)S(1)}, f32[2,8,16,128]{3,2,1,0:T(8,128)S(1)}, f32[8,24,128]{2,1,0:T(8,128)S(1)}, f32[8,16,128]{2,1,0:T(8,128)S(1)}, ...) custom-call(f32[1]{0:T(128)} %bitcast.5.dt_ref, f32[152,128]{1,0:T(8,128)S(1)} %collective-permute-done.2.refs_0_, ...), custom_call_target="tpu_custom_call" | custom-call | tf_op jit(solution)/shard_map/outer/pallas_call | solution.py:501
  16.3 5.0 %all-to-all-start = ((f32[32,1,128]{2,1,0:T(1,128)}), f32[32,1,128]{2,1,0:T(1,128)S(1)}, u32[]{:S(2)}, u32[]{:S(2)}) async-start(f32[32,1,128]{2,1,0:T(1,128)} %bitcast.2), calls=%async_computation | async-start | bytes 32768 | tf_op jit(solution)/shard_map/all_to_all | solution.py:533
  21.4 2.0 %carry.1 = (f32[12,12,128]{2,1,0:T(8,128)}, f32[12,12,128]{2,1,0:T(8,128)}, f32[12,12,128]{2,1,0:T(8,128)}, f32[12,12,128]{2,1,0:T(8,128)}, f32[12,12,128]{2,1,0:T(8,128)}) custom-call(f32[1]{0:T(128)} %bitcast.6.dt_ref, f32[3,8,16,128]{3,2,1,0:T(8,128)S(1)} %get-tuple-element.36.refs_6_.refs_0_, f32[2,8,16,128]{3,2,1,0:T(8,128)S(1)} %get-tuple-element.37.refs_1_, ...), custom_call_target="tpu_custom_call" | custom-call | flops 10000000 | bytes 4000000 | tf_op jit(solution)/shard_map/carry/pallas_call | solution.py:519
  23.3 5.2 %all-to-all-done = f32[32,1,128]{2,1,0:T(1,128)S(1)} async-done(((f32[32,1,128]{2,1,0:T(1,128)}), f32[32,1,128]{2,1,0:T(1,128)S(1)}, u32[]{:S(2)}, u32[]{:S(2)}) %all-to-all-start) | async-done | bytes 16416 | tf_op jit(solution)/shard_map/all_to_all | solution.py:533
  28.5 0.6 %reduce_min.9 = f32[]{:T(128)} reduce(f32[32,1,128]{2,1,0:T(1,128)S(1)} %all-to-all-done, f32[]{:T(128)} %constant.0.clone.1), dimensions={0,1,2}, to_apply=%region_0.0 | reduce | flops 4095 | bytes 16392 | tf_op jit(solution)/shard_map/reduce_min | solution.py:533
  (1 shorter events, 0.0 us)
Async XLA Ops:
  1.7 9.0 %collective-permute-start.2 = (f32[152,128]{1,0:T(8,128)S(1)}, f32[152,128]{1,0:T(8,128)S(1)}, u32[]{:S(2)}, u32[]{:S(2)}) collective-permute-start(f32[152,128]{1,0:T(8,128)S(1)} %get-tuple-element.41), channel_id=1, source_target_pairs={{28,0},{0,4},{4,8},{8,12},{12,16},{16,20},{20,24},{24,28},{29,1},{... | collective-permute-start | bytes 233480 | tf_op jit(solution)/shard_map/ppermute | solution.py:62
  4.7 6.1 %collective-permute-start.3 = (f32[152,128]{1,0:T(8,128)S(1)}, f32[152,128]{1,0:T(8,128)S(1)}, u32[]{:S(2)}, u32[]{:S(2)}) collective-permute-start(f32[152,128]{1,0:T(8,128)S(1)} %get-tuple-element.42), channel_id=1, source_target_pairs={{4,0},{8,4},{12,8},{16,12},{20,16},{24,20},{28,24},{0,28},{5,1},{9... | collective-permute-start | bytes 233480 | tf_op jit(solution)/shard_map/ppermute | solution.py:62
  8.9 5.0 %collective-permute-start = (f32[192,128]{1,0:T(8,128)S(1)}, f32[192,128]{1,0:T(8,128)S(1)}, u32[]{:S(2)}, u32[]{:S(2)}) collective-permute-start(f32[192,128]{1,0:T(8,128)S(1)} %get-tuple-element.34), channel_id=1, source_target_pairs={{0,3},{1,2},{2,1},{3,0},{4,7},{5,6},{6,5},{7,4},{8,11},{9,10},{10,... | collective-permute-start | bytes 294920 | tf_op jit(solution)/shard_map/ppermute | solution.py:68
  9.6 4.3 %collective-permute-start.1 = (f32[192,128]{1,0:T(8,128)S(1)}, f32[192,128]{1,0:T(8,128)S(1)}, u32[]{:S(2)}, u32[]{:S(2)}) collective-permute-start(f32[192,128]{1,0:T(8,128)S(1)} %get-tuple-element.35), channel_id=1, source_target_pairs={{0,1},{1,0},{2,3},{3,2},{4,5},{5,4},{6,7},{7,6},{8,9},{9,8},{10,11... | collective-permute-start | bytes 294920 | tf_op jit(solution)/shard_map/ppermute | solution.py:68
  10.8 4.0 %collective-permute-start.4 = (f32[80,128]{1,0:T(8,128)S(1)}, f32[80,128]{1,0:T(8,128)S(1)}, u32[]{:S(2)}, u32[]{:S(2)}) collective-permute-start(f32[80,128]{1,0:T(8,128)S(1)} %get-tuple-element.43), channel_id=1, source_target_pairs={{0,3},{1,2},{2,1},{3,0},{4,7},{5,6},{6,5},{7,4},{8,11},{9,10},{10,... | collective-permute-start | bytes 122888 | tf_op jit(solution)/shard_map/ppermute | solution.py:68
  10.9 3.9 %collective-permute-start.5 = (f32[80,128]{1,0:T(8,128)S(1)}, f32[80,128]{1,0:T(8,128)S(1)}, u32[]{:S(2)}, u32[]{:S(2)}) collective-permute-start(f32[80,128]{1,0:T(8,128)S(1)} %get-tuple-element.44), channel_id=1, source_target_pairs={{0,1},{1,0},{2,3},{3,2},{4,5},{5,4},{6,7},{7,6},{8,9},{9,8},{10,11... | collective-permute-start | bytes 122888 | tf_op jit(solution)/shard_map/ppermute | solution.py:68
  16.3 12.2 %all-to-all-start = ((f32[32,1,128]{2,1,0:T(1,128)}), f32[32,1,128]{2,1,0:T(1,128)S(1)}, u32[]{:S(2)}, u32[]{:S(2)}) async-start(f32[32,1,128]{2,1,0:T(1,128)} %bitcast.2), calls=%async_computation | async-start | bytes 32768 | tf_op jit(solution)/shard_map/all_to_all | solution.py:533

commit v16 on v14

--- a/solution.py
+++ b/solution.py
@@ -76,8 +76,8 @@
     return 0.4 * energy + 0.5 * jnp.square(jnp.minimum(0.5 * spread, 0.0))
 
 
-def pack_kernel(nx, ny, *refs):
-    fields, own, x_edges, y_edges, padded, arrived = refs[:5], refs[5], refs[6:8], refs[8:10], refs[10], refs[11]
+def x_pack_kernel(nx, ny, *refs):
+    fields, own, x_edges, padded, arrived = refs[:5], refs[5], refs[6:8], refs[8], refs[9]
     zero = hidden_zero()
     copies = [pltpu.make_async_copy(fields[field], own.at[field], arrived.at[field]) for field in range(5)]
     for copy in copies:
@@ -87,13 +87,7 @@
         for side, edge in zip(SIDES, x_edges):
             for number, (field, past) in enumerate(x_layers()):
                 if field == current:
-                    column = nx - past if side < 0 else past - 1
-                    edge[pl.ds(zero + number * ny, ny), :] = own[field, column]
-        for link, edge in zip(LINKS, y_edges):
-            for field, a, rows, offset in y_layers(nx)[0]:
-                if field == current:
-                    start = pick(is_low(link), 0, ny - rows)
-                    edge[pl.ds(zero + offset, rows), :] = own[field, a, pl.ds(start, rows), :]
+                    edge[pl.ds(zero + number * ny, ny), :] = own[field, nx - past if side < 0 else past - 1]
     for k, (side, edge) in enumerate(zip(SIDES, x_edges)):
         a = nx - 3 if side < 0 else 2
         offset = len(x_layers()) * ny
@@ -110,6 +104,14 @@
                           padded[k, pl.ds(TOP + row, 1), :], own[YV, a, pl.ds(row, 1), :]):
                 edge[pl.ds(zero + offset, 1), :] = value
                 offset += 1
+
+
+def y_pack_kernel(nx, ny, own, *y_edges):
+    zero = hidden_zero()
+    for link, edge in zip(LINKS, y_edges):
+        low = is_low(link)
+        for field, a, rows, offset in y_layers(nx)[0]:
+            edge[pl.ds(zero + offset, rows), :] = own[field, a, pl.ds(pick(low, 0, ny - rows), rows), :]
 
 
 def corner_kernel(ny, *refs):
@@ -189,17 +191,25 @@
             lower = fluxes
 
 
-def sweep_y(zero, swept, work, number, fields, factors, wide):
-    moved = []
-    for field in fields:
-        below = swept[field, number, pl.ds(zero + 1, wide)]
-        here = swept[field, number, pl.ds(zero + 2, wide)]
-        slope = limited(here - below, below - swept[field, number, 0:wide])
+def sweep_y(zero, swept, work, numbers, fields, factors, wide):
+    cases = [(number, field) for number in numbers for field in fields]
+
+    def rows(number, field, start):
+        return swept[field, number, pl.ds(zero + start, wide)]
+
+    for number, field in cases:
+        below = rows(number, field, 1)
+        slope = limited(rows(number, field, 2) - below, below - rows(number, field, 0))
         work[0, field, number, 0:wide] = slope
-        flux = face_flux(factors, below, here, slope, work[0, field, number, pl.ds(zero + 1, wide)])
+    for number, field in cases:
+        slope, above = [work[0, field, number, pl.ds(zero + start, wide)] for start in (0, 1)]
+        flux = face_flux(factors[number], rows(number, field, 1), rows(number, field, 2), slope, above)
         work[1, field, number, 0:wide] = flux
-        moved.append(here - (work[1, field, number, pl.ds(zero + 1, wide)] - flux))
-    return moved
+    moved = {}
+    for number, field in cases:
+        flux, above = [work[1, field, number, pl.ds(zero + start, wide)] for start in (0, 1)]
+        moved[number, field] = rows(number, field, 2) - (above - flux)
+    return [[moved[number, field] for field in fields] for number in numbers]
 
 
 def sweep_z(moved, factors):
@@ -252,12 +262,14 @@
         lambda a, part: read(zero, state, a, part, 8, 0),
         swept, (0, 1, 2), first, last, wide, half,
     )
+    numbers = range(last - first)
+    factors = []
+    for number in numbers:
+        below, here = [swept[1, number, pl.ds(zero + start, wide)] for start in (1, 2)]
+        factors.append(face_factors(below, here, half))
+        write(speed_y, first + number, swept[1, number, 0:wide])
     peak = None
-    for a in range(first, last):
-        number = a - first
-        write(speed_y, a, swept[1, number, 0:wide])
-        below, here = [swept[1, number, pl.ds(zero + start, wide)] for start in (1, 2)]
-        moved = sweep_y(zero, swept, work, number, (0, 1, 2), face_factors(below, here, half), wide)
+    for a, moved in zip(range(first, last), sweep_y(zero, swept, work, numbers, (0, 1, 2), factors, wide)):
         write(speed_z, a, moved[2])
         final = sweep_z(moved, face_factors(down(moved[2]), moved[2], half))
         for field in range(3):
@@ -393,9 +405,8 @@
         lambda a, part: read(zero, state, a, part, 8, 0),
         swept, (0, 1), 0, nx, wide, half,
     )
-    for a in range(nx):
-        below, here = [read(zero, speed_y, a, start, wide) for start in (1, 2)]
-        moved = sweep_y(zero, swept, work, a, (0, 1), face_factors(below, here, half), wide)
+    factors = [face_factors(*[read(zero, speed_y, a, start, wide) for start in (1, 2)], half) for a in range(nx)]
+    for a, moved in enumerate(sweep_y(zero, swept, work, range(nx), (0, 1), factors, wide)):
         along = read(zero, speed_z, a, 0, wide)
         final = sweep_z(moved, face_factors(down(along), along, half))
         density_out[a] = final[0][:ny]
@@ -419,17 +430,25 @@
         return pltpu.CompilerParams(vmem_limit_bytes=mebibytes * 1024 * 1024)
 
     x_edge, y_edge, corner = array(x_edge_rows(ny)), array(y_layers(nx)[1]), array(2 * corner_layers()[2])
-    own, *edges = pl.pallas_call(
-        functools.partial(pack_kernel, nx, ny),
-        out_shape=[array(5, nx, ny), x_edge, x_edge, y_edge, y_edge],
+    own, *x_edges = pl.pallas_call(
+        functools.partial(x_pack_kernel, nx, ny),
+        out_shape=[array(5, nx, ny), x_edge, x_edge],
         in_specs=[HBM] * 5,
-        out_specs=[VMEM] * 5,
+        out_specs=[VMEM] * 3,
         scratch_shapes=[scratch(2, ny + 20), pltpu.SemaphoreType.DMA((5,))],
         compiler_params=limit(4),
-        name="pack",
+        name="x_pack",
     )(*[pltpu.with_memory_space_constraint(field, pltpu.HBM) for field in fields])
-    x_edges = [along_x(edge, side) for edge, side in zip(edges[:2], SIDES)]
-    y_edges = [along_y(edge, link) for edge, link in zip(edges[2:], LINKS)]
+    x_edges = [along_x(edge, side) for edge, side in zip(x_edges, SIDES)]
+    y_edges = pl.pallas_call(
+        functools.partial(y_pack_kernel, nx, ny),
+        out_shape=[y_edge] * 2,
+        in_specs=[VMEM],
+        out_specs=[VMEM] * 2,
+        compiler_params=limit(4),
+        name="y_pack",
+    )(own)
+    y_edges = [along_y(edge, link) for edge, link in zip(y_edges, LINKS)]
     corners = pl.pallas_call(
         functools.partial(corner_kernel, ny),
         out_shape=[corner] * 2,

time: 29.5 us -> 29.4 us (level)
    pallas_call x1 -> x2, Pallas kernels: 1.18 us -> 1.21 us  [the longest x1 1.17 us: body(): pl.pallas_call(functools.partial(x_pack_kernel, nx, ny), out_shape=[array...]
where the time goes in v16:
time: 29.4 us; the launch traced here: 29.2 us
  starting transfers between devices  14.7 us (50%)
  waiting for transfers between devices  7.01 us (24%)
  Pallas kernels  5.54 us (19%)
  between operations  1.35 us (5%)
  other arithmetic  0.63 us (2%)
    ppermute x2, starting transfers between devices, along_x(): lax.ppermute(value, 'gx', [((i + side) % count, i) for i in range(count)])  6.12 us
    all_to_all x1, waiting for transfers between devices, body(): lax.all_to_all(smallest, ('gx', 'gy'), 0, 0, tiled=True)  5.16 us
    all_to_all x1, starting transfers between devices, body(): lax.all_to_all(smallest, ('gx', 'gy'), 0, 0, tiled=True)  5.13 us
    ppermute x4, starting transfers between devices, along_y(): return lax.ppermute(value, 'gy', list(enumerate(partners)))  3.44 us
    pallas_call x1, Pallas kernels, body(): pl.pallas_call(functools.partial(carry_kernel, nx, ny), out_shape=[array(...  1.98 us
    pallas_call x1, Pallas kernels, body(): pl.pallas_call(functools.partial(outer_kernel, nx, ny), out_shape=passed_...  1.51 us
    pallas_call x1, Pallas kernels, body(): pl.pallas_call(functools.partial(x_pack_kernel, nx, ny), out_shape=[array...  1.17 us
    ppermute x2, waiting for transfers between devices, along_x(): lax.ppermute(value, 'gx', [((i + side) % count, i) for i in range(count)])  1.14 us
  transfers between devices with their start and end apart: 7, of which 4 were waited for; matrix products, arithmetic and copies ran while one was open for 0% of the time, Pallas kernels for 10%

profile of v16, /device:TPU:0, one launch (start us, length us, event | category | flops | bytes accessed | tf_op | source)
XLA Modules:
  0.0 29.2 jit_solution(4294022605657596309)
XLA Ops:
  0.6 1.2 %x_pack.1 = (f32[5,12,12,128]{3,2,1,0:T(8,128)S(1)}, f32[152,128]{1,0:T(8,128)S(1)}, f32[152,128]{1,0:T(8,128)S(1)}) custom-call(f32[12,12,128]{2,1,0:T(8,128)} %refs_0_.1, f32[12,12,128]{2,1,0:T(8,128)} %refs_1_.1, f32[12,12,128]{2,1,0:T(8,128)} %refs_2_.1, f32[12,12,128]{2,1,0:T(8,128)} %refs_3_.1, f32[12,12,128]{2,1,0:T(8,128)} %refs_4_.1), custom_call_target="tpu_custom_call" | custom-call | tf_op jit(solution)/shard_map/x_pack/pallas_call | solution.py:433
  1.8 3.0 %collective-permute-start.2 = (f32[152,128]{1,0:T(8,128)S(1)}, f32[152,128]{1,0:T(8,128)S(1)}, u32[]{:S(2)}, u32[]{:S(2)}) collective-permute-start(f32[152,128]{1,0:T(8,128)S(1)} %get-tuple-element.41), channel_id=1, source_target_pairs={{28,0},{0,4},{4,8},{8,12},{12,16},{16,20},{20,24},{24,28},{29,1},{... | collective-permute-start | bytes 233480 | tf_op jit(solution)/shard_map/ppermute | solution.py:62
  4.8 3.1 %collective-permute-start.3 = (f32[152,128]{1,0:T(8,128)S(1)}, f32[152,128]{1,0:T(8,128)S(1)}, u32[]{:S(2)}, u32[]{:S(2)}) collective-permute-start(f32[152,128]{1,0:T(8,128)S(1)} %get-tuple-element.42), channel_id=1, source_target_pairs={{4,0},{8,4},{12,8},{16,12},{20,16},{24,20},{28,24},{0,28},{5,1},{9... | collective-permute-start | bytes 233480 | tf_op jit(solution)/shard_map/ppermute | solution.py:62
  8.0 0.7 %collective-permute-start = (f32[192,128]{1,0:T(8,128)S(1)}, f32[192,128]{1,0:T(8,128)S(1)}, u32[]{:S(2)}, u32[]{:S(2)}) collective-permute-start(f32[192,128]{1,0:T(8,128)S(1)} %get-tuple-element.34), channel_id=1, source_target_pairs={{0,3},{1,2},{2,1},{3,0},{4,7},{5,6},{6,5},{7,4},{8,11},{9,10},{10,... | collective-permute-start | bytes 294920 | tf_op jit(solution)/shard_map/ppermute | solution.py:68
  8.7 1.1 %collective-permute-start.1 = (f32[192,128]{1,0:T(8,128)S(1)}, f32[192,128]{1,0:T(8,128)S(1)}, u32[]{:S(2)}, u32[]{:S(2)}) collective-permute-start(f32[192,128]{1,0:T(8,128)S(1)} %get-tuple-element.35), channel_id=1, source_target_pairs={{0,1},{1,0},{2,3},{3,2},{4,5},{5,4},{6,7},{7,6},{8,9},{9,8},{10,11... | collective-permute-start | bytes 294920 | tf_op jit(solution)/shard_map/ppermute | solution.py:68
  9.8 0.6 %collective-permute-done.2.refs_0_ = f32[152,128]{1,0:T(8,128)S(1)} collective-permute-done((f32[152,128]{1,0:T(8,128)S(1)}, f32[152,128]{1,0:T(8,128)S(1)}, u32[]{:S(2)}, u32[]{:S(2)}) %collective-permute-start.2) | collective-permute-done | bytes 77856 | tf_op jit(solution)/shard_map/ppermute | solution.py:62
  10.3 0.6 %collective-permute-done.3.refs_1_ = f32[152,128]{1,0:T(8,128)S(1)} collective-permute-done((f32[152,128]{1,0:T(8,128)S(1)}, f32[152,128]{1,0:T(8,128)S(1)}, u32[]{:S(2)}, u32[]{:S(2)}) %collective-permute-start.3) | collective-permute-done | bytes 77856 | tf_op jit(solution)/shard_map/ppermute | solution.py:62
  10.9 0.1 collective-permute-start.4
  11.0 1.6 %collective-permute-start.5 = (f32[80,128]{1,0:T(8,128)S(1)}, f32[80,128]{1,0:T(8,128)S(1)}, u32[]{:S(2)}, u32[]{:S(2)}) collective-permute-start(f32[80,128]{1,0:T(8,128)S(1)} %get-tuple-element.44), channel_id=1, source_target_pairs={{0,1},{1,0},{2,3},{3,2},{4,5},{5,4},{6,7},{7,6},{8,9},{9,8},{10,11... | collective-permute-start | bytes 122888 | tf_op jit(solution)/shard_map/ppermute | solution.py:68
  13.2 0.0 collective-permute-done.refs_1_
  13.3 0.0 collective-permute-done.1.refs_2_
  13.3 0.8 %inner.1 = (f32[5,12,32,128]{3,2,1,0:T(8,128)S(1)}, f32[10,24,128]{2,1,0:T(8,128)S(1)}, f32[3,8,16,128]{3,2,1,0:T(8,128)S(1)}, f32[2,8,16,128]{3,2,1,0:T(8,128)S...) custom-call(f32[1]{0:T(128)} %bitcast.4.dt_ref, ...), custom_call_target="tpu_custom_call" | custom-call | flops 5000000 | bytes 2000000 | tf_op jit(solution)/shard_map/inner/pallas_call | solution.py:464
  14.1 0.7 %collective-permute-done.4.refs_2_ = f32[80,128]{1,0:T(8,128)S(1)} collective-permute-done((f32[80,128]{1,0:T(8,128)S(1)}, f32[80,128]{1,0:T(8,128)S(1)}, u32[]{:S(2)}, u32[]{:S(2)}) %collective-permute-start.4) | collective-permute-done | bytes 40992 | tf_op jit(solution)/shard_map/ppermute | solution.py:68
  14.8 0.0 collective-permute-done.5.refs_3_
  14.8 1.5 %outer.1 = (f32[3,8,16,128]{3,2,1,0:T(8,128)S(1)}, f32[2,8,16,128]{3,2,1,0:T(8,128)S(1)}, f32[8,24,128]{2,1,0:T(8,128)S(1)}, f32[8,16,128]{2,1,0:T(8,128)S(1)}, ...) custom-call(f32[1]{0:T(128)} %bitcast.5.dt_ref, f32[152,128]{1,0:T(8,128)S(1)} %collective-permute-done.2.refs_0_, ...), custom_call_target="tpu_custom_call" | custom-call | tf_op jit(solution)/shard_map/outer/pallas_call | solution.py:486
  16.3 5.1 %all-to-all-start = ((f32[32,1,128]{2,1,0:T(1,128)}), f32[32,1,128]{2,1,0:T(1,128)S(1)}, u32[]{:S(2)}, u32[]{:S(2)}) async-start(f32[32,1,128]{2,1,0:T(1,128)} %bitcast.2), calls=%async_computation | async-start | bytes 32768 | tf_op jit(solution)/shard_map/all_to_all | solution.py:518
  21.5 2.0 %carry.1 = (f32[12,12,128]{2,1,0:T(8,128)}, f32[12,12,128]{2,1,0:T(8,128)}, f32[12,12,128]{2,1,0:T(8,128)}, f32[12,12,128]{2,1,0:T(8,128)}, f32[12,12,128]{2,1,0:T(8,128)}) custom-call(f32[1]{0:T(128)} %bitcast.6.dt_ref, f32[3,8,16,128]{3,2,1,0:T(8,128)S(1)} %get-tuple-element.36.refs_6_.refs_0_, f32[2,8,16,128]{3,2,1,0:T(8,128)S(1)} %get-tuple-element.37.refs_1_, ...), custom_call_target="tpu_custom_call" | custom-call | flops 10000000 | bytes 4000000 | tf_op jit(solution)/shard_map/carry/pallas_call | solution.py:504
  23.4 5.2 %all-to-all-done = f32[32,1,128]{2,1,0:T(1,128)S(1)} async-done(((f32[32,1,128]{2,1,0:T(1,128)}), f32[32,1,128]{2,1,0:T(1,128)S(1)}, u32[]{:S(2)}, u32[]{:S(2)}) %all-to-all-start) | async-done | bytes 16416 | tf_op jit(solution)/shard_map/all_to_all | solution.py:518
  28.6 0.6 %reduce_min.9 = f32[]{:T(128)} reduce(f32[32,1,128]{2,1,0:T(1,128)S(1)} %all-to-all-done, f32[]{:T(128)} %constant.0.clone.1), dimensions={0,1,2}, to_apply=%region_0.0 | reduce | flops 4095 | bytes 16392 | tf_op jit(solution)/shard_map/reduce_min | solution.py:518
  (2 shorter events, 0.1 us)
Async XLA Ops:
  1.8 8.5 %collective-permute-start.2 = (f32[152,128]{1,0:T(8,128)S(1)}, f32[152,128]{1,0:T(8,128)S(1)}, u32[]{:S(2)}, u32[]{:S(2)}) collective-permute-start(f32[152,128]{1,0:T(8,128)S(1)} %get-tuple-element.41), channel_id=1, source_target_pairs={{28,0},{0,4},{4,8},{8,12},{12,16},{16,20},{20,24},{24,28},{29,1},{... | collective-permute-start | bytes 233480 | tf_op jit(solution)/shard_map/ppermute | solution.py:62
  4.8 6.1 %collective-permute-start.3 = (f32[152,128]{1,0:T(8,128)S(1)}, f32[152,128]{1,0:T(8,128)S(1)}, u32[]{:S(2)}, u32[]{:S(2)}) collective-permute-start(f32[152,128]{1,0:T(8,128)S(1)} %get-tuple-element.42), channel_id=1, source_target_pairs={{4,0},{8,4},{12,8},{16,12},{20,16},{24,20},{28,24},{0,28},{5,1},{9... | collective-permute-start | bytes 233480 | tf_op jit(solution)/shard_map/ppermute | solution.py:62
  8.0 5.3 %collective-permute-start = (f32[192,128]{1,0:T(8,128)S(1)}, f32[192,128]{1,0:T(8,128)S(1)}, u32[]{:S(2)}, u32[]{:S(2)}) collective-permute-start(f32[192,128]{1,0:T(8,128)S(1)} %get-tuple-element.34), channel_id=1, source_target_pairs={{0,3},{1,2},{2,1},{3,0},{4,7},{5,6},{6,5},{7,4},{8,11},{9,10},{10,... | collective-permute-start | bytes 294920 | tf_op jit(solution)/shard_map/ppermute | solution.py:68
  8.7 4.6 %collective-permute-start.1 = (f32[192,128]{1,0:T(8,128)S(1)}, f32[192,128]{1,0:T(8,128)S(1)}, u32[]{:S(2)}, u32[]{:S(2)}) collective-permute-start(f32[192,128]{1,0:T(8,128)S(1)} %get-tuple-element.35), channel_id=1, source_target_pairs={{0,1},{1,0},{2,3},{3,2},{4,5},{5,4},{6,7},{7,6},{8,9},{9,8},{10,11... | collective-permute-start | bytes 294920 | tf_op jit(solution)/shard_map/ppermute | solution.py:68
  10.9 3.9 %collective-permute-start.4 = (f32[80,128]{1,0:T(8,128)S(1)}, f32[80,128]{1,0:T(8,128)S(1)}, u32[]{:S(2)}, u32[]{:S(2)}) collective-permute-start(f32[80,128]{1,0:T(8,128)S(1)} %get-tuple-element.43), channel_id=1, source_target_pairs={{0,3},{1,2},{2,1},{3,0},{4,7},{5,6},{6,5},{7,4},{8,11},{9,10},{10,... | collective-permute-start | bytes 122888 | tf_op jit(solution)/shard_map/ppermute | solution.py:68
  11.0 3.8 %collective-permute-start.5 = (f32[80,128]{1,0:T(8,128)S(1)}, f32[80,128]{1,0:T(8,128)S(1)}, u32[]{:S(2)}, u32[]{:S(2)}) collective-permute-start(f32[80,128]{1,0:T(8,128)S(1)} %get-tuple-element.44), channel_id=1, source_target_pairs={{0,1},{1,0},{2,3},{3,2},{4,5},{5,4},{6,7},{7,6},{8,9},{9,8},{10,11... | collective-permute-start | bytes 122888 | tf_op jit(solution)/shard_map/ppermute | solution.py:68
  16.3 12.3 %all-to-all-start = ((f32[32,1,128]{2,1,0:T(1,128)}), f32[32,1,128]{2,1,0:T(1,128)S(1)}, u32[]{:S(2)}, u32[]{:S(2)}) async-start(f32[32,1,128]{2,1,0:T(1,128)} %bitcast.2), calls=%async_computation | async-start | bytes 32768 | tf_op jit(solution)/shard_map/all_to_all | solution.py:518

commit v17 on v15

--- a/solution.py
+++ b/solution.py
@@ -211,16 +211,13 @@
         return swept[field, number, pl.ds(zero + start, wide)]
 
     for number, field in cases:
-        below = rows(number, field, 1)
-        slope = limited(rows(number, field, 2) - below, below - rows(number, field, 0))
-        work[0, field, number, 0:wide] = slope
-    for number, field in cases:
-        slope, above = [work[0, field, number, pl.ds(zero + start, wide)] for start in (0, 1)]
-        flux = face_flux(factors[number], rows(number, field, 1), rows(number, field, 2), slope, above)
-        work[1, field, number, 0:wide] = flux
+        start = [rows(number, field, first) for first in range(4)]
+        steps = [after - before for before, after in zip(start, start[1:])]
+        slopes = [limited(after, before) for before, after in zip(steps, steps[1:])]
+        work[field, number, 0:wide] = face_flux(factors[number], start[1], start[2], *slopes)
     moved = {}
     for number, field in cases:
-        flux, above = [work[1, field, number, pl.ds(zero + start, wide)] for start in (0, 1)]
+        flux, above = [work[field, number, pl.ds(zero + start, wide)] for start in (0, 1)]
         moved[number, field] = rows(number, field, 2) - (above - flux)
     return [[moved[number, field] for field in fields] for number in numbers]
 
@@ -228,10 +225,10 @@
 def sweep_z(moved, factors):
     final = []
     for value in moved:
-        below = down(value)
+        below, above = down(value), up(value)
         step = value - below
-        slope = limited(up(step), step)
-        flux = face_flux(factors, below, value, down(slope), slope)
+        slopes = limited(step, below - pltpu.roll(value, 2, 1)), limited(above - value, step)
+        flux = face_flux(factors, below, value, *slopes)
         final.append(value - (up(flux) - flux))
     return final
 
@@ -331,7 +328,8 @@
     x_edges, corners = refs[0:2], refs[2:4]
     cells_in, stress_in, state_in, energies_in, peak_in = refs[4:9]
     state_out, passive_out, speed_y, speed_z, flows, increment_ref = refs[9:15]
-    beyond, third, stress_out, heat, growth, energies_out, swept, work = refs[15:]
+    beyond, third, stress_out, heat, growth, energies_out = refs[15:21]
+    swept, work = refs[21:23], refs[23:25]
     nz = increment_ref.shape[-1]
     zero = hidden_zero()
     half = 0.5 * dt_ref[0]
@@ -386,7 +384,7 @@
         peak = jnp.maximum(
             peak,
             flow_columns(
-                zero, first, first + 4, ny, half, state, energies, swept.at[k], work.at[k], speed_y, speed_z, flows
+                zero, first, first + 4, ny, half, state, energies, swept[k], work[k], speed_y, speed_z, flows
             ),
         )
     peak = jnp.max(jnp.where(row[4 : 4 + wide] < ny, peak, 0.0), axis=0, keepdims=True)
@@ -492,7 +490,7 @@
             scratch(nx - 2, tall),
             scratch(nx - 2, tall),
             scratch(3, nx - 8, wide + 8),
-            scratch(2, 3, nx - 8, wide + 8),
+            scratch(3, nx - 8, wide + 8),
         ],
         compiler_params=limit(8),
         cost_estimate=pl.CostEstimate(flops=5 * 10**6, bytes_accessed=2 * 10**6, transcendentals=0),
@@ -510,8 +508,10 @@
             scratch(8, tall),
             scratch(8, tall),
             scratch(4, wide + 8),
-            scratch(2, 3, 4, wide + 8),
-            scratch(2, 2, 3, 4, wide + 8),
+            scratch(3, 4, wide + 8),
+            scratch(3, 4, wide + 8),
+            scratch(3, 4, wide + 8),
+            scratch(3, 4, wide + 8),
         ],
         compiler_params=limit(8),
         name="outer",
@@ -523,7 +523,7 @@
         out_specs=[VMEM] * 2 + [HBM] * 3,
         scratch_shapes=[
             scratch(2, nx, wide + 8),
-            scratch(2, 2, nx, wide + 8),
+            scratch(2, nx, wide + 8),
             pltpu.SemaphoreType.DMA((3, 3)),
         ],
         compiler_params=limit(8),

time: 29.4 us -> 29.3 us (level)
  transfers between devices with their start and end apart: 7 -> 7, of which waited for: 3 -> 4; matrix products, arithmetic and copies ran while one was open for 0% -> 0% of each run, Pallas kernels for 13% -> 14%
where the time goes in v17:
time: 29.3 us; the launch traced here: 29 us
  starting transfers between devices  14.6 us (50%)
  Pallas kernels  6.48 us (22%)
  waiting for transfers between devices  5.97 us (20%)
  between operations  1.34 us (5%)
  other arithmetic  0.63 us (2%)
    ppermute x2, starting transfers between devices, along_x(): lax.ppermute(value, 'gx', [((i + side) % count, i) for i in range(count)])  6.12 us
    all_to_all x1, starting transfers between devices, body(): lax.all_to_all(smallest, ('gx', 'gy'), 0, 0, tiled=True)  5.03 us
    all_to_all x1, waiting for transfers between devices, body(): lax.all_to_all(smallest, ('gx', 'gy'), 0, 0, tiled=True)  4.92 us
    ppermute x4, starting transfers between devices, along_y(): return lax.ppermute(value, 'gy', list(enumerate(partners)))  3.44 us
    pallas_call x1, Pallas kernels, body(): pl.pallas_call(functools.partial(carry_kernel, nx, ny), out_shape=[array(...  2.21 us
    pallas_call x1, Pallas kernels, body(): pl.pallas_call(functools.partial(outer_kernel, nx, ny), out_shape=passed_...  1.38 us
    pallas_call x1, Pallas kernels, body(): pl.pallas_call(functools.partial(y_pack_kernel, nx, ny), out_shape=[array...  1.08 us
    pallas_call x1, Pallas kernels, body(): pl.pallas_call(functools.partial(x_pack_kernel, nx, ny), out_shape=[x_edg...  1.08 us
  transfers between devices with their start and end apart: 7, of which 4 were waited for; matrix products, arithmetic and copies ran while one was open for 0% of the time, Pallas kernels for 14%

profile of v17, /device:TPU:0, one launch (start us, length us, event | category | flops | bytes accessed | tf_op | source)
XLA Modules:
  0.0 29.0 jit_solution(6025201290327732206)
XLA Ops:
  0.6 1.1 %x_pack.1 = (f32[152,128]{1,0:T(8,128)S(1)}, f32[152,128]{1,0:T(8,128)S(1)}) custom-call(f32[12,12,128]{2,1,0:T(8,128)} %refs_0_.3, f32[12,12,128]{2,1,0:T(8,128)} %refs_1_.3, f32[12,12,128]{2,1,0:T(8,128)} %refs_2_.3, f32[12,12,128]{2,1,0:T(8,128)} %refs_3_.3, f32[12,12,128]{2,1,0:T(8,128)} %refs_4_.3), custom_call_target="tpu_custom_call" | custom-call | tf_op jit(solution)/shard_map/x_pack/pallas_call | solution.py:445
  1.7 3.0 %collective-permute-start.2 = (f32[152,128]{1,0:T(8,128)S(1)}, f32[152,128]{1,0:T(8,128)S(1)}, u32[]{:S(2)}, u32[]{:S(2)}) collective-permute-start(f32[152,128]{1,0:T(8,128)S(1)} %get-tuple-element.41), channel_id=1, source_target_pairs={{28,0},{0,4},{4,8},{8,12},{12,16},{16,20},{20,24},{24,28},{29,1},{... | collective-permute-start | bytes 233480 | tf_op jit(solution)/shard_map/ppermute | solution.py:62
  4.7 3.1 %collective-permute-start.3 = (f32[152,128]{1,0:T(8,128)S(1)}, f32[152,128]{1,0:T(8,128)S(1)}, u32[]{:S(2)}, u32[]{:S(2)}) collective-permute-start(f32[152,128]{1,0:T(8,128)S(1)} %get-tuple-element.42), channel_id=1, source_target_pairs={{4,0},{8,4},{12,8},{16,12},{20,16},{24,20},{28,24},{0,28},{5,1},{9... | collective-permute-start | bytes 233480 | tf_op jit(solution)/shard_map/ppermute | solution.py:62
  7.8 1.1 %y_pack.1 = (f32[5,12,12,128]{3,2,1,0:T(8,128)S(1)}, f32[192,128]{1,0:T(8,128)S(1)}, f32[192,128]{1,0:T(8,128)S(1)}) custom-call(f32[12,12,128]{2,1,0:T(8,128)} %refs_0_.3, f32[12,12,128]{2,1,0:T(8,128)} %refs_1_.3, f32[12,12,128]{2,1,0:T(8,128)} %refs_2_.3, f32[12,12,128]{2,1,0:T(8,128)} %refs_3_.3, f32[12,12,128]{2,1,0:T(8,128)} %refs_4_.3), custom_call_target="tpu_custom_call" | custom-call | tf_op jit(solution)/shard_map/y_pack/pallas_call | solution.py:455
  8.9 0.7 %collective-permute-start = (f32[192,128]{1,0:T(8,128)S(1)}, f32[192,128]{1,0:T(8,128)S(1)}, u32[]{:S(2)}, u32[]{:S(2)}) collective-permute-start(f32[192,128]{1,0:T(8,128)S(1)} %get-tuple-element.34), channel_id=1, source_target_pairs={{0,3},{1,2},{2,1},{3,0},{4,7},{5,6},{6,5},{7,4},{8,11},{9,10},{10,... | collective-permute-start | bytes 294920 | tf_op jit(solution)/shard_map/ppermute | solution.py:68
  9.6 1.1 %collective-permute-start.1 = (f32[192,128]{1,0:T(8,128)S(1)}, f32[192,128]{1,0:T(8,128)S(1)}, u32[]{:S(2)}, u32[]{:S(2)}) collective-permute-start(f32[192,128]{1,0:T(8,128)S(1)} %get-tuple-element.35), channel_id=1, source_target_pairs={{0,1},{1,0},{2,3},{3,2},{4,5},{5,4},{6,7},{7,6},{8,9},{9,8},{10,11... | collective-permute-start | bytes 294920 | tf_op jit(solution)/shard_map/ppermute | solution.py:68
  10.7 0.0 collective-permute-done.2.refs_0_
  10.7 0.1 collective-permute-done.3.refs_1_
  10.8 0.1 collective-permute-start.4
  10.9 1.6 %collective-permute-start.5 = (f32[80,128]{1,0:T(8,128)S(1)}, f32[80,128]{1,0:T(8,128)S(1)}, u32[]{:S(2)}, u32[]{:S(2)}) collective-permute-start(f32[80,128]{1,0:T(8,128)S(1)} %get-tuple-element.44), channel_id=1, source_target_pairs={{0,1},{1,0},{2,3},{3,2},{4,5},{5,4},{6,7},{7,6},{8,9},{9,8},{10,11... | collective-permute-start | bytes 122888 | tf_op jit(solution)/shard_map/ppermute | solution.py:68
  13.1 0.8 %collective-permute-done.refs_1_ = f32[192,128]{1,0:T(8,128)S(1)} collective-permute-done((f32[192,128]{1,0:T(8,128)S(1)}, f32[192,128]{1,0:T(8,128)S(1)}, u32[]{:S(2)}, u32[]{:S(2)}) %collective-permute-start) | collective-permute-done | bytes 98336 | tf_op jit(solution)/shard_map/ppermute | solution.py:68
  13.9 0.0 collective-permute-done.1.refs_2_
  13.9 0.7 %inner.1 = (f32[5,12,32,128]{3,2,1,0:T(8,128)S(1)}, f32[10,24,128]{2,1,0:T(8,128)S(1)}, f32[3,8,16,128]{3,2,1,0:T(8,128)S(1)}, f32[2,8,16,128]{3,2,1,0:T(8,128)S...) custom-call(f32[1]{0:T(128)} %bitcast.4.dt_ref, ...), custom_call_target="tpu_custom_call" | custom-call | flops 5000000 | bytes 2000000 | tf_op jit(solution)/shard_map/inner/pallas_call | solution.py:477
  14.7 0.2 collective-permute-done.4.refs_2_
  14.8 0.0 collective-permute-done.5.refs_3_
  14.8 1.4 %outer.1 = (f32[3,8,16,128]{3,2,1,0:T(8,128)S(1)}, f32[2,8,16,128]{3,2,1,0:T(8,128)S(1)}, f32[8,24,128]{2,1,0:T(8,128)S(1)}, f32[8,16,128]{2,1,0:T(8,128)S(1)}, ...) custom-call(f32[1]{0:T(128)} %bitcast.5.dt_ref, f32[152,128]{1,0:T(8,128)S(1)} %collective-permute-done.2.refs_0_, ...), custom_call_target="tpu_custom_call" | custom-call | tf_op jit(solution)/shard_map/outer/pallas_call | solution.py:499
  16.2 5.0 %all-to-all-start = ((f32[32,1,128]{2,1,0:T(1,128)}), f32[32,1,128]{2,1,0:T(1,128)S(1)}, u32[]{:S(2)}, u32[]{:S(2)}) async-start(f32[32,1,128]{2,1,0:T(1,128)} %bitcast.2), calls=%async_computation | async-start | bytes 32768 | tf_op jit(solution)/shard_map/all_to_all | solution.py:533
  21.2 2.2 %carry.1 = (f32[12,12,128]{2,1,0:T(8,128)}, f32[12,12,128]{2,1,0:T(8,128)}, f32[12,12,128]{2,1,0:T(8,128)}, f32[12,12,128]{2,1,0:T(8,128)}, f32[12,12,128]{2,1,0:T(8,128)}) custom-call(f32[1]{0:T(128)} %bitcast.6.dt_ref, f32[3,8,16,128]{3,2,1,0:T(8,128)S(1)} %get-tuple-element.36.refs_6_.refs_0_, f32[2,8,16,128]{3,2,1,0:T(8,128)S(1)} %get-tuple-element.37.refs_1_, ...), custom_call_target="tpu_custom_call" | custom-call | flops 10000000 | bytes 4000000 | tf_op jit(solution)/shard_map/carry/pallas_call | solution.py:519
  23.5 4.9 %all-to-all-done = f32[32,1,128]{2,1,0:T(1,128)S(1)} async-done(((f32[32,1,128]{2,1,0:T(1,128)}), f32[32,1,128]{2,1,0:T(1,128)S(1)}, u32[]{:S(2)}, u32[]{:S(2)}) %all-to-all-start) | async-done | bytes 16416 | tf_op jit(solution)/shard_map/all_to_all | solution.py:533
  28.4 0.6 %reduce_min.9 = f32[]{:T(128)} reduce(f32[32,1,128]{2,1,0:T(1,128)S(1)} %all-to-all-done, f32[]{:T(128)} %constant.0.clone.1), dimensions={0,1,2}, to_apply=%region_0.0 | reduce | flops 4095 | bytes 16392 | tf_op jit(solution)/shard_map/reduce_min | solution.py:533
  (1 shorter events, 0.0 us)
Async XLA Ops:
  1.7 9.0 %collective-permute-start.2 = (f32[152,128]{1,0:T(8,128)S(1)}, f32[152,128]{1,0:T(8,128)S(1)}, u32[]{:S(2)}, u32[]{:S(2)}) collective-permute-start(f32[152,128]{1,0:T(8,128)S(1)} %get-tuple-element.41), channel_id=1, source_target_pairs={{28,0},{0,4},{4,8},{8,12},{12,16},{16,20},{20,24},{24,28},{29,1},{... | collective-permute-start | bytes 233480 | tf_op jit(solution)/shard_map/ppermute | solution.py:62
  4.7 6.1 %collective-permute-start.3 = (f32[152,128]{1,0:T(8,128)S(1)}, f32[152,128]{1,0:T(8,128)S(1)}, u32[]{:S(2)}, u32[]{:S(2)}) collective-permute-start(f32[152,128]{1,0:T(8,128)S(1)} %get-tuple-element.42), channel_id=1, source_target_pairs={{4,0},{8,4},{12,8},{16,12},{20,16},{24,20},{28,24},{0,28},{5,1},{9... | collective-permute-start | bytes 233480 | tf_op jit(solution)/shard_map/ppermute | solution.py:62
  8.9 5.0 %collective-permute-start = (f32[192,128]{1,0:T(8,128)S(1)}, f32[192,128]{1,0:T(8,128)S(1)}, u32[]{:S(2)}, u32[]{:S(2)}) collective-permute-start(f32[192,128]{1,0:T(8,128)S(1)} %get-tuple-element.34), channel_id=1, source_target_pairs={{0,3},{1,2},{2,1},{3,0},{4,7},{5,6},{6,5},{7,4},{8,11},{9,10},{10,... | collective-permute-start | bytes 294920 | tf_op jit(solution)/shard_map/ppermute | solution.py:68
  9.6 4.3 %collective-permute-start.1 = (f32[192,128]{1,0:T(8,128)S(1)}, f32[192,128]{1,0:T(8,128)S(1)}, u32[]{:S(2)}, u32[]{:S(2)}) collective-permute-start(f32[192,128]{1,0:T(8,128)S(1)} %get-tuple-element.35), channel_id=1, source_target_pairs={{0,1},{1,0},{2,3},{3,2},{4,5},{5,4},{6,7},{7,6},{8,9},{9,8},{10,11... | collective-permute-start | bytes 294920 | tf_op jit(solution)/shard_map/ppermute | solution.py:68
  10.8 4.0 %collective-permute-start.4 = (f32[80,128]{1,0:T(8,128)S(1)}, f32[80,128]{1,0:T(8,128)S(1)}, u32[]{:S(2)}, u32[]{:S(2)}) collective-permute-start(f32[80,128]{1,0:T(8,128)S(1)} %get-tuple-element.43), channel_id=1, source_target_pairs={{0,3},{1,2},{2,1},{3,0},{4,7},{5,6},{6,5},{7,4},{8,11},{9,10},{10,... | collective-permute-start | bytes 122888 | tf_op jit(solution)/shard_map/ppermute | solution.py:68
  10.9 3.9 %collective-permute-start.5 = (f32[80,128]{1,0:T(8,128)S(1)}, f32[80,128]{1,0:T(8,128)S(1)}, u32[]{:S(2)}, u32[]{:S(2)}) collective-permute-start(f32[80,128]{1,0:T(8,128)S(1)} %get-tuple-element.44), channel_id=1, source_target_pairs={{0,1},{1,0},{2,3},{3,2},{4,5},{5,4},{6,7},{7,6},{8,9},{9,8},{10,11... | collective-permute-start | bytes 122888 | tf_op jit(solution)/shard_map/ppermute | solution.py:68
  16.2 12.2 %all-to-all-start = ((f32[32,1,128]{2,1,0:T(1,128)}), f32[32,1,128]{2,1,0:T(1,128)S(1)}, u32[]{:S(2)}, u32[]{:S(2)}) async-start(f32[32,1,128]{2,1,0:T(1,128)} %bitcast.2), calls=%async_computation | async-start | bytes 32768 | tf_op jit(solution)/shard_map/all_to_all | solution.py:533

commit v18 on v17

--- a/solution.py
+++ b/solution.py
@@ -37,7 +37,7 @@
         for field in range(5):
             found.append((field, a, ghost_rows(field), offset))
             offset += ghost_rows(field)
-    return found, -(-offset // 8) * 8
+    return found, (offset // 8 + 2) * 8
 
 
 def corner_layers():
@@ -70,6 +70,10 @@
 
 def hidden_zero():
     return lax.shift_right_logical(lax.axis_index("gx"), 20)
+
+
+def span(zero, start, count, total):
+    return pl.ds(start if start + -(-count // 8) * 8 > total else zero + start, count)
 
 
 def per_mass(energy, spread):
@@ -108,14 +112,17 @@
         for row in (0, ny - 1):
             for value in (near[DENSITY, a, pl.ds(row, 1), :], near[ENERGY, a, pl.ds(row, 1), :],
                           padded[k, pl.ds(TOP + row, 1), :], near[YV, a, pl.ds(row, 1), :]):
-                edge[pl.ds(zero + offset, 1), :] = value
+                edge[pl.ds(offset, 1), :] = value
                 offset += 1
 
 
 def y_pack_kernel(nx, ny, *refs):
     fields, own, y_edges, arrived = refs[:5], refs[5], refs[6:8], refs[8]
     zero = hidden_zero()
-    copies = [pltpu.make_async_copy(fields[field], own.at[field], arrived.at[field]) for field in range(5)]
+    copies = [
+        pltpu.make_async_copy(fields[field], own.at[field, pl.ds(0, nx), pl.ds(0, ny), :], arrived.at[field])
+        for field in range(5)
+    ]
     for copy in copies:
         copy.start()
     for current, copy in enumerate(copies):
@@ -134,13 +141,15 @@
     for link, out in zip(LINKS, outs):
         low = is_low(link)
         for k, edge in enumerate(x_edges):
-            base = zero + k * rows_of_corner
+            base, total = k * rows_of_corner, out.shape[0]
             for number, _, _, rows, offset in columns:
-                out[pl.ds(base + offset, rows), :] = edge[pl.ds(number * ny + pick(low, 0, ny - rows), rows), :]
+                out[span(zero, base + offset, rows, total), :] = edge[pl.ds(number * ny + pick(low, 0, ny - rows), rows), :]
             number = len(x_layers())
-            out[pl.ds(base + singles, 1), :] = edge[pl.ds(number * ny + pick(low, 1, ny - 2), 1), :]
-            first = (number + 1) * ny + pick(low, 0, EDGE_KINDS)
-            out[pl.ds(base + (singles + 1), EDGE_KINDS), :] = edge[pl.ds(first, EDGE_KINDS), :]
+            out[span(zero, base + singles, 1, total), :] = edge[pl.ds(number * ny + pick(low, 1, ny - 2), 1), :]
+            first, last = [
+                edge[pl.ds((number + 1) * ny + k * EDGE_KINDS, EDGE_KINDS), :] for k in range(2)
+            ]
+            out[span(zero, base + singles + 1, EDGE_KINDS, total), :] = jnp.where(low == 1, first, last)
 
 
 def limited(above, below):
@@ -302,7 +311,7 @@
     half = 0.5 * dt_ref[0]
     for field in range(5):
         for a in range(nx):
-            cells[field, a, pl.ds(TOP, ny), :] = own[field, a]
+            cells[field, a, pl.ds(TOP, ny), :] = own[field, a, pl.ds(0, ny), :]
     for link, edge in zip(LINKS, y_edges):
         low = is_low(link)
         for field, a, rows, offset in y_layers(nx)[0]:
@@ -345,20 +354,21 @@
         offset += ny
         for row in (0, ny - 1):
             for kind in range(EDGE_KINDS):
-                third[k, kind, pl.ds(TOP + row, 1), :] = edge[pl.ds(zero + offset, 1), :]
+                third[k, kind, pl.ds(TOP + row, 1), :] = edge[pl.ds(offset, 1), :]
                 offset += 1
     for link, corner in zip(LINKS, corners):
         low = is_low(link)
         for k, side in enumerate(SIDES):
-            base = zero + k * rows_of_corner
+            base, total = k * rows_of_corner, corner.shape[0]
             for _, field, past, rows, offset in columns:
                 column = LEFT - past if side < 0 else LEFT - 1 + past
                 to = pl.ds(TOP + pick(low, -rows, ny), rows)
-                beyond[field, column, to, :] = corner[pl.ds(base + offset, rows), :]
-            third[k, EDGE_KINDS, pl.ds(TOP + pick(low, -2, ny + 1), 1), :] = corner[pl.ds(base + singles, 1), :]
+                beyond[field, column, to, :] = corner[span(zero, base + offset, rows, total), :]
+            to = pl.ds(TOP + pick(low, -2, ny + 1), 1)
+            third[k, EDGE_KINDS, to, :] = corner[span(zero, base + singles, 1, total), :]
             for kind in range(EDGE_KINDS):
                 to = pl.ds(TOP + pick(low, -1, ny), 1)
-                third[k, kind, to, :] = corner[pl.ds(base + (singles + 1 + kind), 1), :]
+                third[k, kind, to, :] = corner[span(zero, base + singles + 1 + kind, 1, total), :]
 
     cells = [(cells_in, 0, nx, 0)] + outer_pieces(beyond, nx, LEFT, 0)
     stress = outer_pieces(stress_out, nx, 3, 2) + [(stress_in, 2, nx - 2, 1)]
@@ -454,7 +464,7 @@
     x_edges = [along_x(edge, side) for edge, side in zip(x_edges, SIDES)]
     own, *y_edges = pl.pallas_call(
         functools.partial(y_pack_kernel, nx, ny),
-        out_shape=[array(5, nx, ny), y_edge, y_edge],
+        out_shape=[array(5, nx, ny + 12), y_edge, y_edge],
         in_specs=[HBM] * 5,
         out_specs=[VMEM] * 3,
         scratch_shapes=[pltpu.SemaphoreType.DMA((5,))],

time: 29.3 us -> 29.3 us (level)
  no operation moved by 1% of the time
where the time goes in v18:
time: 29.3 us; the launch traced here: 29 us
  starting transfers between devices  14.4 us (49%)
  Pallas kernels  6.47 us (22%)
  waiting for transfers between devices  6.15 us (21%)
  between operations  1.34 us (5%)
  other arithmetic  0.63 us (2%)
    ppermute x2, starting transfers between devices, along_x(): lax.ppermute(value, 'gx', [((i + side) % count, i) for i in range(count)])  6.12 us
    all_to_all x1, waiting for transfers between devices, body(): lax.all_to_all(smallest, ('gx', 'gy'), 0, 0, tiled=True)  4.93 us
    all_to_all x1, starting transfers between devices, body(): lax.all_to_all(smallest, ('gx', 'gy'), 0, 0, tiled=True)  4.85 us
    ppermute x4, starting transfers between devices, along_y(): return lax.ppermute(value, 'gy', list(enumerate(partners)))  3.44 us
    pallas_call x1, Pallas kernels, body(): pl.pallas_call(functools.partial(carry_kernel, nx, ny), out_shape=[array(...  2.21 us
    pallas_call x1, Pallas kernels, body(): pl.pallas_call(functools.partial(outer_kernel, nx, ny), out_shape=passed_...  1.38 us
    ppermute x4, waiting for transfers between devices, along_y(): return lax.ppermute(value, 'gy', list(enumerate(partners)))  1.12 us
    pallas_call x1, Pallas kernels, body(): pl.pallas_call(functools.partial(y_pack_kernel, nx, ny), out_shape=[array...  1.08 us
  transfers between devices with their start and end apart: 7, of which 4 were waited for; matrix products, arithmetic and copies ran while one was open for 0% of the time, Pallas kernels for 14%

profile of v18, /device:TPU:0, one launch (start us, length us, event | category | flops | bytes accessed | tf_op | source)
XLA Modules:
  0.0 29.0 jit_solution(9612889815109002814)
XLA Ops:
  0.6 1.1 %x_pack.1 = (f32[152,128]{1,0:T(8,128)S(1)}, f32[152,128]{1,0:T(8,128)S(1)}) custom-call(f32[12,12,128]{2,1,0:T(8,128)} %refs_0_.3, f32[12,12,128]{2,1,0:T(8,128)} %refs_1_.3, f32[12,12,128]{2,1,0:T(8,128)} %refs_2_.3, f32[12,12,128]{2,1,0:T(8,128)} %refs_3_.3, f32[12,12,128]{2,1,0:T(8,128)} %refs_4_.3), custom_call_target="tpu_custom_call" | custom-call | tf_op jit(solution)/shard_map/x_pack/pallas_call | solution.py:455
  1.7 3.0 %collective-permute-start.2 = (f32[152,128]{1,0:T(8,128)S(1)}, f32[152,128]{1,0:T(8,128)S(1)}, u32[]{:S(2)}, u32[]{:S(2)}) collective-permute-start(f32[152,128]{1,0:T(8,128)S(1)} %get-tuple-element.41), channel_id=1, source_target_pairs={{28,0},{0,4},{4,8},{8,12},{12,16},{16,20},{20,24},{24,28},{29,1},{... | collective-permute-start | bytes 233480 | tf_op jit(solution)/shard_map/ppermute | solution.py:62
  4.7 3.1 %collective-permute-start.3 = (f32[152,128]{1,0:T(8,128)S(1)}, f32[152,128]{1,0:T(8,128)S(1)}, u32[]{:S(2)}, u32[]{:S(2)}) collective-permute-start(f32[152,128]{1,0:T(8,128)S(1)} %get-tuple-element.42), channel_id=1, source_target_pairs={{4,0},{8,4},{12,8},{16,12},{20,16},{24,20},{28,24},{0,28},{5,1},{9... | collective-permute-start | bytes 233480 | tf_op jit(solution)/shard_map/ppermute | solution.py:62
  7.8 1.1 %y_pack.1 = (f32[5,12,24,128]{3,2,1,0:T(8,128)S(1)}, f32[208,128]{1,0:T(8,128)S(1)}, f32[208,128]{1,0:T(8,128)S(1)}) custom-call(f32[12,12,128]{2,1,0:T(8,128)} %refs_0_.3, f32[12,12,128]{2,1,0:T(8,128)} %refs_1_.3, f32[12,12,128]{2,1,0:T(8,128)} %refs_2_.3, f32[12,12,128]{2,1,0:T(8,128)} %refs_3_.3, f32[12,12,128]{2,1,0:T(8,128)} %refs_4_.3), custom_call_target="tpu_custom_call" | custom-call | tf_op jit(solution)/shard_map/y_pack/pallas_call | solution.py:465
  8.9 0.7 %collective-permute-start = (f32[208,128]{1,0:T(8,128)S(1)}, f32[208,128]{1,0:T(8,128)S(1)}, u32[]{:S(2)}, u32[]{:S(2)}) collective-permute-start(f32[208,128]{1,0:T(8,128)S(1)} %get-tuple-element.34), channel_id=1, source_target_pairs={{0,3},{1,2},{2,1},{3,0},{4,7},{5,6},{6,5},{7,4},{8,11},{9,10},{10,... | collective-permute-start | bytes 319496 | tf_op jit(solution)/shard_map/ppermute | solution.py:68
  9.6 1.1 %collective-permute-start.1 = (f32[208,128]{1,0:T(8,128)S(1)}, f32[208,128]{1,0:T(8,128)S(1)}, u32[]{:S(2)}, u32[]{:S(2)}) collective-permute-start(f32[208,128]{1,0:T(8,128)S(1)} %get-tuple-element.35), channel_id=1, source_target_pairs={{0,1},{1,0},{2,3},{3,2},{4,5},{5,4},{6,7},{7,6},{8,9},{9,8},{10,11... | collective-permute-start | bytes 319496 | tf_op jit(solution)/shard_map/ppermute | solution.py:68
  10.7 0.0 collective-permute-done.2.refs_0_
  10.7 0.1 collective-permute-done.3.refs_1_
  10.8 0.1 collective-permute-start.4
  10.9 1.6 %collective-permute-start.5 = (f32[80,128]{1,0:T(8,128)S(1)}, f32[80,128]{1,0:T(8,128)S(1)}, u32[]{:S(2)}, u32[]{:S(2)}) collective-permute-start(f32[80,128]{1,0:T(8,128)S(1)} %get-tuple-element.44), channel_id=1, source_target_pairs={{0,1},{1,0},{2,3},{3,2},{4,5},{5,4},{6,7},{7,6},{8,9},{9,8},{10,11... | collective-permute-start | bytes 122888 | tf_op jit(solution)/shard_map/ppermute | solution.py:68
  13.1 1.0 %collective-permute-done.refs_1_ = f32[208,128]{1,0:T(8,128)S(1)} collective-permute-done((f32[208,128]{1,0:T(8,128)S(1)}, f32[208,128]{1,0:T(8,128)S(1)}, u32[]{:S(2)}, u32[]{:S(2)}) %collective-permute-start) | collective-permute-done | bytes 106528 | tf_op jit(solution)/shard_map/ppermute | solution.py:68
  14.1 0.0 collective-permute-done.1.refs_2_
  14.1 0.7 %inner.1 = (f32[5,12,32,128]{3,2,1,0:T(8,128)S(1)}, f32[10,24,128]{2,1,0:T(8,128)S(1)}, f32[3,8,16,128]{3,2,1,0:T(8,128)S(1)}, f32[2,8,16,128]{3,2,1,0:T(8,128)S...) custom-call(f32[1]{0:T(128)} %bitcast.4.dt_ref, ...), custom_call_target="tpu_custom_call" | custom-call | flops 5000000 | bytes 2000000 | tf_op jit(solution)/shard_map/inner/pallas_call | solution.py:487
  14.8 0.2 collective-permute-done.4.refs_2_
  15.0 0.0 collective-permute-done.5.refs_3_
  15.0 1.4 %outer.1 = (f32[3,8,16,128]{3,2,1,0:T(8,128)S(1)}, f32[2,8,16,128]{3,2,1,0:T(8,128)S(1)}, f32[8,24,128]{2,1,0:T(8,128)S(1)}, f32[8,16,128]{2,1,0:T(8,128)S(1)}, ...) custom-call(f32[1]{0:T(128)} %bitcast.5.dt_ref, f32[152,128]{1,0:T(8,128)S(1)} %collective-permute-done.2.refs_0_, ...), custom_call_target="tpu_custom_call" | custom-call | tf_op jit(solution)/shard_map/outer/pallas_call | solution.py:509
  16.4 4.9 %all-to-all-start = ((f32[32,1,128]{2,1,0:T(1,128)}), f32[32,1,128]{2,1,0:T(1,128)S(1)}, u32[]{:S(2)}, u32[]{:S(2)}) async-start(f32[32,1,128]{2,1,0:T(1,128)} %bitcast.2), calls=%async_computation | async-start | bytes 32768 | tf_op jit(solution)/shard_map/all_to_all | solution.py:543
  21.2 2.2 %carry.1 = (f32[12,12,128]{2,1,0:T(8,128)}, f32[12,12,128]{2,1,0:T(8,128)}, f32[12,12,128]{2,1,0:T(8,128)}, f32[12,12,128]{2,1,0:T(8,128)}, f32[12,12,128]{2,1,0:T(8,128)}) custom-call(f32[1]{0:T(128)} %bitcast.6.dt_ref, f32[3,8,16,128]{3,2,1,0:T(8,128)S(1)} %get-tuple-element.36.refs_6_.refs_0_, f32[2,8,16,128]{3,2,1,0:T(8,128)S(1)} %get-tuple-element.37.refs_1_, ...), custom_call_target="tpu_custom_call" | custom-call | flops 10000000 | bytes 4000000 | tf_op jit(solution)/shard_map/carry/pallas_call | solution.py:529
  23.4 4.9 %all-to-all-done = f32[32,1,128]{2,1,0:T(1,128)S(1)} async-done(((f32[32,1,128]{2,1,0:T(1,128)}), f32[32,1,128]{2,1,0:T(1,128)S(1)}, u32[]{:S(2)}, u32[]{:S(2)}) %all-to-all-start) | async-done | bytes 16416 | tf_op jit(solution)/shard_map/all_to_all | solution.py:543
  28.4 0.6 %reduce_min.9 = f32[]{:T(128)} reduce(f32[32,1,128]{2,1,0:T(1,128)S(1)} %all-to-all-done, f32[]{:T(128)} %constant.0.clone.1), dimensions={0,1,2}, to_apply=%region_0.0 | reduce | flops 4095 | bytes 16392 | tf_op jit(solution)/shard_map/reduce_min | solution.py:543
  (1 shorter events, 0.0 us)
Async XLA Ops:
  1.7 9.0 %collective-permute-start.2 = (f32[152,128]{1,0:T(8,128)S(1)}, f32[152,128]{1,0:T(8,128)S(1)}, u32[]{:S(2)}, u32[]{:S(2)}) collective-permute-start(f32[152,128]{1,0:T(8,128)S(1)} %get-tuple-element.41), channel_id=1, source_target_pairs={{28,0},{0,4},{4,8},{8,12},{12,16},{16,20},{20,24},{24,28},{29,1},{... | collective-permute-start | bytes 233480 | tf_op jit(solution)/shard_map/ppermute | solution.py:62
  4.7 6.1 %collective-permute-start.3 = (f32[152,128]{1,0:T(8,128)S(1)}, f32[152,128]{1,0:T(8,128)S(1)}, u32[]{:S(2)}, u32[]{:S(2)}) collective-permute-start(f32[152,128]{1,0:T(8,128)S(1)} %get-tuple-element.42), channel_id=1, source_target_pairs={{4,0},{8,4},{12,8},{16,12},{20,16},{24,20},{28,24},{0,28},{5,1},{9... | collective-permute-start | bytes 233480 | tf_op jit(solution)/shard_map/ppermute | solution.py:62
  8.9 5.2 %collective-permute-start = (f32[208,128]{1,0:T(8,128)S(1)}, f32[208,128]{1,0:T(8,128)S(1)}, u32[]{:S(2)}, u32[]{:S(2)}) collective-permute-start(f32[208,128]{1,0:T(8,128)S(1)} %get-tuple-element.34), channel_id=1, source_target_pairs={{0,3},{1,2},{2,1},{3,0},{4,7},{5,6},{6,5},{7,4},{8,11},{9,10},{10,... | collective-permute-start | bytes 319496 | tf_op jit(solution)/shard_map/ppermute | solution.py:68
  9.6 4.5 %collective-permute-start.1 = (f32[208,128]{1,0:T(8,128)S(1)}, f32[208,128]{1,0:T(8,128)S(1)}, u32[]{:S(2)}, u32[]{:S(2)}) collective-permute-start(f32[208,128]{1,0:T(8,128)S(1)} %get-tuple-element.35), channel_id=1, source_target_pairs={{0,1},{1,0},{2,3},{3,2},{4,5},{5,4},{6,7},{7,6},{8,9},{9,8},{10,11... | collective-permute-start | bytes 319496 | tf_op jit(solution)/shard_map/ppermute | solution.py:68
  10.8 4.2 %collective-permute-start.4 = (f32[80,128]{1,0:T(8,128)S(1)}, f32[80,128]{1,0:T(8,128)S(1)}, u32[]{:S(2)}, u32[]{:S(2)}) collective-permute-start(f32[80,128]{1,0:T(8,128)S(1)} %get-tuple-element.43), channel_id=1, source_target_pairs={{0,3},{1,2},{2,1},{3,0},{4,7},{5,6},{6,5},{7,4},{8,11},{9,10},{10,... | collective-permute-start | bytes 122888 | tf_op jit(solution)/shard_map/ppermute | solution.py:68
  10.9 4.1 %collective-permute-start.5 = (f32[80,128]{1,0:T(8,128)S(1)}, f32[80,128]{1,0:T(8,128)S(1)}, u32[]{:S(2)}, u32[]{:S(2)}) collective-permute-start(f32[80,128]{1,0:T(8,128)S(1)} %get-tuple-element.44), channel_id=1, source_target_pairs={{0,1},{1,0},{2,3},{3,2},{4,5},{5,4},{6,7},{7,6},{8,9},{9,8},{10,11... | collective-permute-start | bytes 122888 | tf_op jit(solution)/shard_map/ppermute | solution.py:68
  16.4 12.0 %all-to-all-start = ((f32[32,1,128]{2,1,0:T(1,128)}), f32[32,1,128]{2,1,0:T(1,128)S(1)}, u32[]{:S(2)}, u32[]{:S(2)}) async-start(f32[32,1,128]{2,1,0:T(1,128)} %bitcast.2), calls=%async_computation | async-start | bytes 32768 | tf_op jit(solution)/shard_map/all_to_all | solution.py:543

commit v19 on v18

--- a/solution.py
+++ b/solution.py
@@ -83,35 +83,40 @@
 def x_pack_kernel(nx, ny, *refs):
     fields, x_edges, near, padded, arrived = refs[:5], refs[5:7], refs[7], refs[8], refs[9]
     zero = hidden_zero()
-    copies = [
-        pltpu.make_async_copy(
+    order = (ZV, YV, XV, ENERGY, DENSITY)
+    copies = {
+        (field, k): pltpu.make_async_copy(
             fields[field].at[pl.ds(first, 4)], near.at[field, pl.ds(4 * k, 4)], arrived.at[field, k]
         )
-        for field in range(5)
+        for field in order
         for k, first in enumerate((nx - 4, 0))
-    ]
-    for copy in copies:
+    }
+    for copy in copies.values():
         copy.start()
-    for current in range(5):
+    thirds = (1, 6)
+    for current in order:
         for k, (side, edge) in enumerate(zip(SIDES, x_edges)):
-            copies[2 * current + k].wait()
+            copies[current, k].wait()
+            if current == ZV:
+                padded[k] = jnp.zeros_like(padded[k])
+                padded[2 + k, pl.ds(TOP, ny), :] = up(near[ZV, thirds[k]]) - down(near[ZV, thirds[k]])
+            if current == YV:
+                padded[k, pl.ds(TOP, ny), :] = near[YV, thirds[k]]
             for number, (field, past) in enumerate(x_layers()):
                 if field == current:
                     edge[pl.ds(zero + number * ny, ny), :] = near[field, 4 - past if side < 0 else 3 + past]
-    for k, (side, edge) in enumerate(zip(SIDES, x_edges)):
-        a = 1 if side < 0 else 6
+    for k, edge in enumerate(x_edges):
+        a = thirds[k]
         offset = len(x_layers()) * ny
-        padded[k] = jnp.zeros_like(padded[k])
-        padded[k, pl.ds(TOP, ny), :] = near[YV, a]
         spread = near[XV, a + 1] - near[XV, a - 1]
         spread += padded[k, pl.ds(zero + (TOP + 1), ny), :] - padded[k, pl.ds(zero + (TOP - 1), ny), :]
-        spread += up(near[ZV, a]) - down(near[ZV, a])
+        spread += padded[2 + k, pl.ds(TOP, ny), :]
         edge[pl.ds(zero + offset, ny), :] = near[DENSITY, a] * per_mass(near[ENERGY, a], spread)
         offset += ny
-        padded[k, pl.ds(TOP, ny), :] = spread
+        padded[2 + k, pl.ds(TOP, ny), :] = spread
         for row in (0, ny - 1):
             for value in (near[DENSITY, a, pl.ds(row, 1), :], near[ENERGY, a, pl.ds(row, 1), :],
-                          padded[k, pl.ds(TOP + row, 1), :], near[YV, a, pl.ds(row, 1), :]):
+                          padded[2 + k, pl.ds(TOP + row, 1), :], near[YV, a, pl.ds(row, 1), :]):
                 edge[pl.ds(offset, 1), :] = value
                 offset += 1
 
@@ -457,7 +462,7 @@
         out_shape=[x_edge] * 2,
         in_specs=[HBM] * 5,
         out_specs=[VMEM] * 2,
-        scratch_shapes=[scratch(5, 8, ny), scratch(2, ny + 20), pltpu.SemaphoreType.DMA((5, 2))],
+        scratch_shapes=[scratch(5, 8, ny), scratch(4, ny + 20), pltpu.SemaphoreType.DMA((5, 2))],
         compiler_params=limit(4),
         name="x_pack",
     )(*placed)

time: 29.3 us -> 29.2 us (level)
  no operation moved by 1% of the time
where the time goes in v19:
time: 29.2 us; the launch traced here: 29 us
  starting transfers between devices  14.4 us (49%)
  Pallas kernels  6.42 us (22%)
  waiting for transfers between devices  6.15 us (21%)
  between operations  1.34 us (5%)
  other arithmetic  0.63 us (2%)
    ppermute x2, starting transfers between devices, along_x(): lax.ppermute(value, 'gx', [((i + side) % count, i) for i in range(count)])  6.12 us
    all_to_all x1, waiting for transfers between devices, body(): lax.all_to_all(smallest, ('gx', 'gy'), 0, 0, tiled=True)  4.93 us
    all_to_all x1, starting transfers between devices, body(): lax.all_to_all(smallest, ('gx', 'gy'), 0, 0, tiled=True)  4.85 us
    ppermute x4, starting transfers between devices, along_y(): return lax.ppermute(value, 'gy', list(enumerate(partners)))  3.44 us
    pallas_call x1, Pallas kernels, body(): pl.pallas_call(functools.partial(carry_kernel, nx, ny), out_shape=[array(...  2.21 us
    pallas_call x1, Pallas kernels, body(): pl.pallas_call(functools.partial(outer_kernel, nx, ny), out_shape=passed_...  1.38 us
    ppermute x4, waiting for transfers between devices, along_y(): return lax.ppermute(value, 'gy', list(enumerate(partners)))  1.12 us
    pallas_call x1, Pallas kernels, body(): pl.pallas_call(functools.partial(y_pack_kernel, nx, ny), out_shape=[array...  1.08 us
  transfers between devices with their start and end apart: 7, of which 4 were waited for; matrix products, arithmetic and copies ran while one was open for 0% of the time, Pallas kernels for 14%

profile of v19, /device:TPU:0, one launch (start us, length us, event | category | flops | bytes accessed | tf_op | source)
XLA Modules:
  0.0 29.0 jit_solution(10014316393481592590)
XLA Ops:
  0.6 1.0 %x_pack.1 = (f32[152,128]{1,0:T(8,128)S(1)}, f32[152,128]{1,0:T(8,128)S(1)}) custom-call(f32[12,12,128]{2,1,0:T(8,128)} %refs_0_.3, f32[12,12,128]{2,1,0:T(8,128)} %refs_1_.3, f32[12,12,128]{2,1,0:T(8,128)} %refs_2_.3, f32[12,12,128]{2,1,0:T(8,128)} %refs_3_.3, f32[12,12,128]{2,1,0:T(8,128)} %refs_4_.3), custom_call_target="tpu_custom_call" | custom-call | tf_op jit(solution)/shard_map/x_pack/pallas_call | solution.py:460
  1.7 3.0 %collective-permute-start.2 = (f32[152,128]{1,0:T(8,128)S(1)}, f32[152,128]{1,0:T(8,128)S(1)}, u32[]{:S(2)}, u32[]{:S(2)}) collective-permute-start(f32[152,128]{1,0:T(8,128)S(1)} %get-tuple-element.41), channel_id=1, source_target_pairs={{28,0},{0,4},{4,8},{8,12},{12,16},{16,20},{20,24},{24,28},{29,1},{... | collective-permute-start | bytes 233480 | tf_op jit(solution)/shard_map/ppermute | solution.py:62
  4.7 3.1 %collective-permute-start.3 = (f32[152,128]{1,0:T(8,128)S(1)}, f32[152,128]{1,0:T(8,128)S(1)}, u32[]{:S(2)}, u32[]{:S(2)}) collective-permute-start(f32[152,128]{1,0:T(8,128)S(1)} %get-tuple-element.42), channel_id=1, source_target_pairs={{4,0},{8,4},{12,8},{16,12},{20,16},{24,20},{28,24},{0,28},{5,1},{9... | collective-permute-start | bytes 233480 | tf_op jit(solution)/shard_map/ppermute | solution.py:62
  7.8 1.1 %y_pack.1 = (f32[5,12,24,128]{3,2,1,0:T(8,128)S(1)}, f32[208,128]{1,0:T(8,128)S(1)}, f32[208,128]{1,0:T(8,128)S(1)}) custom-call(f32[12,12,128]{2,1,0:T(8,128)} %refs_0_.3, f32[12,12,128]{2,1,0:T(8,128)} %refs_1_.3, f32[12,12,128]{2,1,0:T(8,128)} %refs_2_.3, f32[12,12,128]{2,1,0:T(8,128)} %refs_3_.3, f32[12,12,128]{2,1,0:T(8,128)} %refs_4_.3), custom_call_target="tpu_custom_call" | custom-call | tf_op jit(solution)/shard_map/y_pack/pallas_call | solution.py:470
  8.9 0.7 %collective-permute-start = (f32[208,128]{1,0:T(8,128)S(1)}, f32[208,128]{1,0:T(8,128)S(1)}, u32[]{:S(2)}, u32[]{:S(2)}) collective-permute-start(f32[208,128]{1,0:T(8,128)S(1)} %get-tuple-element.34), channel_id=1, source_target_pairs={{0,3},{1,2},{2,1},{3,0},{4,7},{5,6},{6,5},{7,4},{8,11},{9,10},{10,... | collective-permute-start | bytes 319496 | tf_op jit(solution)/shard_map/ppermute | solution.py:68
  9.6 1.1 %collective-permute-start.1 = (f32[208,128]{1,0:T(8,128)S(1)}, f32[208,128]{1,0:T(8,128)S(1)}, u32[]{:S(2)}, u32[]{:S(2)}) collective-permute-start(f32[208,128]{1,0:T(8,128)S(1)} %get-tuple-element.35), channel_id=1, source_target_pairs={{0,1},{1,0},{2,3},{3,2},{4,5},{5,4},{6,7},{7,6},{8,9},{9,8},{10,11... | collective-permute-start | bytes 319496 | tf_op jit(solution)/shard_map/ppermute | solution.py:68
  10.6 0.0 collective-permute-done.2.refs_0_
  10.6 0.1 collective-permute-done.3.refs_1_
  10.8 0.1 collective-permute-start.4
  10.9 1.6 %collective-permute-start.5 = (f32[80,128]{1,0:T(8,128)S(1)}, f32[80,128]{1,0:T(8,128)S(1)}, u32[]{:S(2)}, u32[]{:S(2)}) collective-permute-start(f32[80,128]{1,0:T(8,128)S(1)} %get-tuple-element.44), channel_id=1, source_target_pairs={{0,1},{1,0},{2,3},{3,2},{4,5},{5,4},{6,7},{7,6},{8,9},{9,8},{10,11... | collective-permute-start | bytes 122888 | tf_op jit(solution)/shard_map/ppermute | solution.py:68
  13.1 1.0 %collective-permute-done.refs_1_ = f32[208,128]{1,0:T(8,128)S(1)} collective-permute-done((f32[208,128]{1,0:T(8,128)S(1)}, f32[208,128]{1,0:T(8,128)S(1)}, u32[]{:S(2)}, u32[]{:S(2)}) %collective-permute-start) | collective-permute-done | bytes 106528 | tf_op jit(solution)/shard_map/ppermute | solution.py:68
  14.1 0.0 collective-permute-done.1.refs_2_
  14.1 0.7 %inner.1 = (f32[5,12,32,128]{3,2,1,0:T(8,128)S(1)}, f32[10,24,128]{2,1,0:T(8,128)S(1)}, f32[3,8,16,128]{3,2,1,0:T(8,128)S(1)}, f32[2,8,16,128]{3,2,1,0:T(8,128)S...) custom-call(f32[1]{0:T(128)} %bitcast.4.dt_ref, ...), custom_call_target="tpu_custom_call" | custom-call | flops 5000000 | bytes 2000000 | tf_op jit(solution)/shard_map/inner/pallas_call | solution.py:492
  14.8 0.2 collective-permute-done.4.refs_2_
  14.9 0.0 collective-permute-done.5.refs_3_
  14.9 1.4 %outer.1 = (f32[3,8,16,128]{3,2,1,0:T(8,128)S(1)}, f32[2,8,16,128]{3,2,1,0:T(8,128)S(1)}, f32[8,24,128]{2,1,0:T(8,128)S(1)}, f32[8,16,128]{2,1,0:T(8,128)S(1)}, ...) custom-call(f32[1]{0:T(128)} %bitcast.5.dt_ref, f32[152,128]{1,0:T(8,128)S(1)} %collective-permute-done.2.refs_0_, ...), custom_call_target="tpu_custom_call" | custom-call | tf_op jit(solution)/shard_map/outer/pallas_call | solution.py:514
  16.3 4.9 %all-to-all-start = ((f32[32,1,128]{2,1,0:T(1,128)}), f32[32,1,128]{2,1,0:T(1,128)S(1)}, u32[]{:S(2)}, u32[]{:S(2)}) async-start(f32[32,1,128]{2,1,0:T(1,128)} %bitcast.2), calls=%async_computation | async-start | bytes 32768 | tf_op jit(solution)/shard_map/all_to_all | solution.py:548
  21.2 2.2 %carry.1 = (f32[12,12,128]{2,1,0:T(8,128)}, f32[12,12,128]{2,1,0:T(8,128)}, f32[12,12,128]{2,1,0:T(8,128)}, f32[12,12,128]{2,1,0:T(8,128)}, f32[12,12,128]{2,1,0:T(8,128)}) custom-call(f32[1]{0:T(128)} %bitcast.6.dt_ref, f32[3,8,16,128]{3,2,1,0:T(8,128)S(1)} %get-tuple-element.36.refs_6_.refs_0_, f32[2,8,16,128]{3,2,1,0:T(8,128)S(1)} %get-tuple-element.37.refs_1_, ...), custom_call_target="tpu_custom_call" | custom-call | flops 10000000 | bytes 4000000 | tf_op jit(solution)/shard_map/carry/pallas_call | solution.py:534
  23.4 4.9 %all-to-all-done = f32[32,1,128]{2,1,0:T(1,128)S(1)} async-done(((f32[32,1,128]{2,1,0:T(1,128)}), f32[32,1,128]{2,1,0:T(1,128)S(1)}, u32[]{:S(2)}, u32[]{:S(2)}) %all-to-all-start) | async-done | bytes 16416 | tf_op jit(solution)/shard_map/all_to_all | solution.py:548
  28.3 0.6 %reduce_min.9 = f32[]{:T(128)} reduce(f32[32,1,128]{2,1,0:T(1,128)S(1)} %all-to-all-done, f32[]{:T(128)} %constant.0.clone.1), dimensions={0,1,2}, to_apply=%region_0.0 | reduce | flops 4095 | bytes 16392 | tf_op jit(solution)/shard_map/reduce_min | solution.py:548
  (1 shorter events, 0.0 us)
Async XLA Ops:
  1.7 9.0 %collective-permute-start.2 = (f32[152,128]{1,0:T(8,128)S(1)}, f32[152,128]{1,0:T(8,128)S(1)}, u32[]{:S(2)}, u32[]{:S(2)}) collective-permute-start(f32[152,128]{1,0:T(8,128)S(1)} %get-tuple-element.41), channel_id=1, source_target_pairs={{28,0},{0,4},{4,8},{8,12},{12,16},{16,20},{20,24},{24,28},{29,1},{... | collective-permute-start | bytes 233480 | tf_op jit(solution)/shard_map/ppermute | solution.py:62
  4.7 6.1 %collective-permute-start.3 = (f32[152,128]{1,0:T(8,128)S(1)}, f32[152,128]{1,0:T(8,128)S(1)}, u32[]{:S(2)}, u32[]{:S(2)}) collective-permute-start(f32[152,128]{1,0:T(8,128)S(1)} %get-tuple-element.42), channel_id=1, source_target_pairs={{4,0},{8,4},{12,8},{16,12},{20,16},{24,20},{28,24},{0,28},{5,1},{9... | collective-permute-start | bytes 233480 | tf_op jit(solution)/shard_map/ppermute | solution.py:62
  8.9 5.2 %collective-permute-start = (f32[208,128]{1,0:T(8,128)S(1)}, f32[208,128]{1,0:T(8,128)S(1)}, u32[]{:S(2)}, u32[]{:S(2)}) collective-permute-start(f32[208,128]{1,0:T(8,128)S(1)} %get-tuple-element.34), channel_id=1, source_target_pairs={{0,3},{1,2},{2,1},{3,0},{4,7},{5,6},{6,5},{7,4},{8,11},{9,10},{10,... | collective-permute-start | bytes 319496 | tf_op jit(solution)/shard_map/ppermute | solution.py:68
  9.6 4.5 %collective-permute-start.1 = (f32[208,128]{1,0:T(8,128)S(1)}, f32[208,128]{1,0:T(8,128)S(1)}, u32[]{:S(2)}, u32[]{:S(2)}) collective-permute-start(f32[208,128]{1,0:T(8,128)S(1)} %get-tuple-element.35), channel_id=1, source_target_pairs={{0,1},{1,0},{2,3},{3,2},{4,5},{5,4},{6,7},{7,6},{8,9},{9,8},{10,11... | collective-permute-start | bytes 319496 | tf_op jit(solution)/shard_map/ppermute | solution.py:68
  10.8 4.2 %collective-permute-start.4 = (f32[80,128]{1,0:T(8,128)S(1)}, f32[80,128]{1,0:T(8,128)S(1)}, u32[]{:S(2)}, u32[]{:S(2)}) collective-permute-start(f32[80,128]{1,0:T(8,128)S(1)} %get-tuple-element.43), channel_id=1, source_target_pairs={{0,3},{1,2},{2,1},{3,0},{4,7},{5,6},{6,5},{7,4},{8,11},{9,10},{10,... | collective-permute-start | bytes 122888 | tf_op jit(solution)/shard_map/ppermute | solution.py:68
  10.9 4.1 %collective-permute-start.5 = (f32[80,128]{1,0:T(8,128)S(1)}, f32[80,128]{1,0:T(8,128)S(1)}, u32[]{:S(2)}, u32[]{:S(2)}) collective-permute-start(f32[80,128]{1,0:T(8,128)S(1)} %get-tuple-element.44), channel_id=1, source_target_pairs={{0,1},{1,0},{2,3},{3,2},{4,5},{5,4},{6,7},{7,6},{8,9},{9,8},{10,11... | collective-permute-start | bytes 122888 | tf_op jit(solution)/shard_map/ppermute | solution.py:68
  16.3 12.0 %all-to-all-start = ((f32[32,1,128]{2,1,0:T(1,128)}), f32[32,1,128]{2,1,0:T(1,128)S(1)}, u32[]{:S(2)}, u32[]{:S(2)}) async-start(f32[32,1,128]{2,1,0:T(1,128)} %bitcast.2), calls=%async_computation | async-start | bytes 32768 | tf_op jit(solution)/shard_map/all_to_all | solution.py:548

commit v20 on v19

--- a/solution.py
+++ b/solution.py
@@ -218,22 +218,23 @@
             lower = fluxes
 
 
-def sweep_y(zero, swept, work, numbers, fields, factors, wide):
-    cases = [(number, field) for number in numbers for field in fields]
-
-    def rows(number, field, start):
+def sweep_y(zero, columns, fields, wide):
+    def rows(swept, number, field, start):
         return swept[field, number, pl.ds(zero + start, wide)]
 
-    for number, field in cases:
-        start = [rows(number, field, first) for first in range(4)]
-        steps = [after - before for before, after in zip(start, start[1:])]
-        slopes = [limited(after, before) for before, after in zip(steps, steps[1:])]
-        work[field, number, 0:wide] = face_flux(factors[number], start[1], start[2], *slopes)
-    moved = {}
-    for number, field in cases:
-        flux, above = [work[field, number, pl.ds(zero + start, wide)] for start in (0, 1)]
-        moved[number, field] = rows(number, field, 2) - (above - flux)
-    return [[moved[number, field] for field in fields] for number in numbers]
+    for swept, work, number, factors in columns:
+        for field in fields:
+            start = [rows(swept, number, field, first) for first in range(4)]
+            steps = [after - before for before, after in zip(start, start[1:])]
+            slopes = [limited(after, before) for before, after in zip(steps, steps[1:])]
+            work[field, number, 0:wide] = face_flux(factors, start[1], start[2], *slopes)
+    moved = []
+    for swept, work, number, _ in columns:
+        moved.append([])
+        for field in fields:
+            flux, above = [work[field, number, pl.ds(zero + start, wide)] for start in (0, 1)]
+            moved[-1].append(rows(swept, number, field, 2) - (above - flux))
+    return moved
 
 
 def sweep_z(moved, factors):
@@ -262,7 +263,7 @@
         write(growth, a, half * spread)
 
 
-def advance_columns(zero, columns, wide, half, cells, stress, heat, growth, passive, state, energies, nx):
+def advance_columns(zero, columns, wide, half, cells, stress, heat, growth, passive, state, roots, nx):
     for a in columns:
         density, energy, x, y, z = [read(zero, cells, a, TOP - 2, wide, field) for field in range(5)]
         grown = read(zero, growth, a, 2, wide)
@@ -276,41 +277,38 @@
         write(state, a, y - scale * (read(zero, stress, a, 3, wide) - read(zero, stress, a, 1, wide)), 1)
         write(state, a, z - scale * (up(centre) - down(centre)), 2)
         if 0 <= a < nx:
-            write(energies, a, energy)
-
-
-def flow_columns(zero, first, last, ny, half, state, energies, swept, work, speed_y, speed_z, flows):
+            write(roots, a, jnp.sqrt(0.56 * energy))
+
+
+def flow_columns(zero, groups, ny, half, state, roots, speed_y, speed_z, flows):
     wide = ny + 4
-    sweep_x(
-        lambda field, a, part: read(zero, state, a, part, 8, field),
-        lambda a, part: read(zero, state, a, part, 8, 0),
-        swept, (0, 1, 2), first, last, wide, half,
-    )
-    numbers = range(last - first)
-    factors = []
-    for number in numbers:
-        below, here = [swept[1, number, pl.ds(zero + start, wide)] for start in (1, 2)]
-        factors.append(face_factors(below, here, half))
-        write(speed_y, first + number, swept[1, number, 0:wide])
+    columns, names = [], []
+    for first, last, swept, work in groups:
+        sweep_x(
+            lambda field, a, part: read(zero, state, a, part, 8, field),
+            lambda a, part: read(zero, state, a, part, 8, 0),
+            swept, (0, 1, 2), first, last, wide, half,
+        )
+    for first, last, swept, work in groups:
+        for a in range(first, last):
+            below, here = [swept[1, a - first, pl.ds(zero + start, wide)] for start in (1, 2)]
+            columns.append((swept, work, a - first, face_factors(below, here, half)))
+            names.append(a)
+            write(speed_y, a, swept[1, a - first, 0:wide])
     peak = None
-    for a, moved in zip(range(first, last), sweep_y(zero, swept, work, numbers, (0, 1, 2), factors, wide)):
+    for a, moved in zip(names, sweep_y(zero, columns, (0, 1, 2), wide)):
         write(speed_z, a, moved[2])
         final = sweep_z(moved, face_factors(down(moved[2]), moved[2], half))
         for field in range(3):
             write(flows, a, final[field][:ny], field)
-        signal = (
-            jnp.sqrt(0.56 * read(zero, energies, a, 2, wide))
-            + jnp.abs(final[0])
-            + jnp.abs(final[1])
-            + jnp.abs(final[2])
-        )
+        signal = read(zero, roots, a, 2, wide) + jnp.abs(final[0]) + jnp.abs(final[1]) + jnp.abs(final[2])
         peak = signal if peak is None else jnp.maximum(peak, signal)
     return peak
 
 
 def inner_kernel(nx, ny, dt_ref, *refs):
     own, y_edges = refs[0], refs[1:3]
-    cells, stress, state, passive, energies, speed_y, speed_z, flows, peak_ref = refs[3:12]
+    cells, stress, state, passive, roots, speed_y, speed_z, flows, peak_ref = refs[3:12]
     heat, growth, swept, work = refs[12:]
     zero = hidden_zero()
     half = 0.5 * dt_ref[0]
@@ -323,14 +321,14 @@
             cells[field, a, pl.ds(TOP + pick(low, -rows, ny), rows), :] = edge[pl.ds(zero + offset, rows), :]
     cells = [(cells, 0, nx, 0)]
     stress, heat, growth = [[(ref, 1, nx - 1, 0)] for ref in (stress, heat, growth)]
-    state, passive, energies = [[(ref, 2, nx - 2, 0)] for ref in (state, passive, energies)]
+    state, passive, roots = [[(ref, 2, nx - 2, 0)] for ref in (state, passive, roots)]
     speed_y, speed_z, flows = [[(ref, 4, nx - 4, 0)] for ref in (speed_y, speed_z, flows)]
     spread_columns(zero, range(1, nx - 1), ny + 12, half, cells, stress, heat, growth)
     advance_columns(
-        zero, range(2, nx - 2), ny + 4, half, cells, stress, heat, growth, passive, state, energies, nx
+        zero, range(2, nx - 2), ny + 4, half, cells, stress, heat, growth, passive, state, roots, nx
     )
     peak_ref[...] = flow_columns(
-        zero, 4, nx - 4, ny, half, state, energies, swept, work, speed_y, speed_z, flows
+        zero, [(4, nx - 4, swept, work)], ny, half, state, roots, speed_y, speed_z, flows
     )
 
 
@@ -340,9 +338,9 @@
 
 def outer_kernel(nx, ny, dt_ref, *refs):
     x_edges, corners = refs[0:2], refs[2:4]
-    cells_in, stress_in, state_in, energies_in, peak_in = refs[4:9]
+    cells_in, stress_in, state_in, roots_in, peak_in = refs[4:9]
     state_out, passive_out, speed_y, speed_z, flows, increment_ref = refs[9:15]
-    beyond, third, stress_out, heat, growth, energies_out = refs[15:21]
+    beyond, third, stress_out, heat, growth, roots_out = refs[15:21]
     swept, work = refs[21:23], refs[23:25]
     nz = increment_ref.shape[-1]
     zero = hidden_zero()
@@ -380,7 +378,7 @@
     heat, growth = outer_pieces(heat, nx, 2, 2), outer_pieces(growth, nx, 2, 2)
     state = outer_pieces(state_out, nx, 2, 2) + [(state_in, 2, nx - 2, 0)]
     passive = outer_pieces(passive_out, nx, 2, 2)
-    energies = outer_pieces(energies_out, nx, 0, 2) + [(energies_in, 2, nx - 2, 0)]
+    roots = outer_pieces(roots_out, nx, 0, 2) + [(roots_in, 2, nx - 2, 0)]
     speed_y, speed_z, flows = [outer_pieces(ref, nx, 0, 4) for ref in (speed_y, speed_z, flows)]
 
     row = lax.broadcasted_iota(jnp.int32, (tall, nz), 0) - 4
@@ -393,15 +391,10 @@
 
     ends = (*range(-2, 2), *range(nx - 2, nx + 2))
     spread_columns(zero, ends, tall, half, cells, stress, heat, growth)
-    advance_columns(zero, ends, wide, half, cells, stress, heat, growth, passive, state, energies, nx)
-    peak = peak_in[...]
-    for k, first in enumerate((0, nx - 4)):
-        peak = jnp.maximum(
-            peak,
-            flow_columns(
-                zero, first, first + 4, ny, half, state, energies, swept[k], work[k], speed_y, speed_z, flows
-            ),
-        )
+    advance_columns(zero, ends, wide, half, cells, stress, heat, growth, passive, state, roots, nx)
+    groups = [(first, first + 4, swept[k], work[k]) for k, first in enumerate((0, nx - 4))]
+    peak = flow_columns(zero, groups, ny, half, state, roots, speed_y, speed_z, flows)
+    peak = jnp.maximum(peak, peak_in[...])
     peak = jnp.max(jnp.where(row[4 : 4 + wide] < ny, peak, 0.0), axis=0, keepdims=True)
     increment_ref[...] = jnp.broadcast_to(0.3 / peak, increment_ref.shape)
 
@@ -432,7 +425,8 @@
         swept, (0, 1), 0, nx, wide, half,
     )
     factors = [face_factors(*[read(zero, speed_y, a, start, wide) for start in (1, 2)], half) for a in range(nx)]
-    for a, moved in enumerate(sweep_y(zero, swept, work, range(nx), (0, 1), factors, wide)):
+    columns = [(swept, work, a, factors[a]) for a in range(nx)]
+    for a, moved in enumerate(sweep_y(zero, columns, (0, 1), wide)):
         along = read(zero, speed_z, a, 0, wide)
         final = sweep_z(moved, face_factors(down(along), along, half))
         density_out[a] = final[0][:ny]
@@ -489,7 +483,7 @@
     increment = time_increment.reshape(1)
     passed_in = [array(3, nx - 4, wide), array(2, nx - 4, wide), array(nx - 8, wide + 8), array(nx - 8, wide), array(3, nx - 8, ny)]
     passed_out = [array(3, 8, wide), array(2, 8, wide), array(8, wide + 8), array(8, wide), array(3, 8, ny)]
-    cells, stress, state_in, passive_in, energies, *rest_in, peak = pl.pallas_call(
+    cells, stress, state_in, passive_in, roots, *rest_in, peak = pl.pallas_call(
         functools.partial(inner_kernel, nx, ny),
         out_shape=[
             array(5, nx, ny + 20),
@@ -530,7 +524,7 @@
         ],
         compiler_params=limit(8),
         name="outer",
-    )(increment, *x_edges, *corners, cells, stress, state_in, energies, peak)
+    )(increment, *x_edges, *corners, cells, stress, state_in, roots, peak)
     outs = pl.pallas_call(
         functools.partial(carry_kernel, nx, ny),
         out_shape=[array(nx, ny)] * 5,

time: 29.2 us -> 29.2 us (level)
  no operation moved by 1% of the time
where the time goes in v20:
time: 29.2 us; the launch traced here: 29 us
  starting transfers between devices  14.4 us (49%)
  Pallas kernels  6.42 us (22%)
  waiting for transfers between devices  6.15 us (21%)
  between operations  1.34 us (5%)
  other arithmetic  0.63 us (2%)
    ppermute x2, starting transfers between devices, along_x(): lax.ppermute(value, 'gx', [((i + side) % count, i) for i in range(count)])  6.12 us
    all_to_all x1, waiting for transfers between devices, body(): lax.all_to_all(smallest, ('gx', 'gy'), 0, 0, tiled=True)  4.93 us
    all_to_all x1, starting transfers between devices, body(): lax.all_to_all(smallest, ('gx', 'gy'), 0, 0, tiled=True)  4.85 us
    ppermute x4, starting transfers between devices, along_y(): return lax.ppermute(value, 'gy', list(enumerate(partners)))  3.44 us
    pallas_call x1, Pallas kernels, body(): pl.pallas_call(functools.partial(carry_kernel, nx, ny), out_shape=[array(...  2.21 us
    pallas_call x1, Pallas kernels, body(): pl.pallas_call(functools.partial(outer_kernel, nx, ny), out_shape=passed_...  1.38 us
    ppermute x4, waiting for transfers between devices, along_y(): return lax.ppermute(value, 'gy', list(enumerate(partners)))  1.12 us
    pallas_call x1, Pallas kernels, body(): pl.pallas_call(functools.partial(y_pack_kernel, nx, ny), out_shape=[array...  1.08 us
  transfers between devices with their start and end apart: 7, of which 4 were waited for; matrix products, arithmetic and copies ran while one was open for 0% of the time, Pallas kernels for 14%

profile of v20, /device:TPU:0, one launch (start us, length us, event | category | flops | bytes accessed | tf_op | source)
XLA Modules:
  0.0 29.0 jit_solution(14582452700129928959)
XLA Ops:
  0.6 1.0 %x_pack.1 = (f32[152,128]{1,0:T(8,128)S(1)}, f32[152,128]{1,0:T(8,128)S(1)}) custom-call(f32[12,12,128]{2,1,0:T(8,128)} %refs_0_.3, f32[12,12,128]{2,1,0:T(8,128)} %refs_1_.3, f32[12,12,128]{2,1,0:T(8,128)} %refs_2_.3, f32[12,12,128]{2,1,0:T(8,128)} %refs_3_.3, f32[12,12,128]{2,1,0:T(8,128)} %refs_4_.3), custom_call_target="tpu_custom_call" | custom-call | tf_op jit(solution)/shard_map/x_pack/pallas_call | solution.py:454
  1.7 3.0 %collective-permute-start.2 = (f32[152,128]{1,0:T(8,128)S(1)}, f32[152,128]{1,0:T(8,128)S(1)}, u32[]{:S(2)}, u32[]{:S(2)}) collective-permute-start(f32[152,128]{1,0:T(8,128)S(1)} %get-tuple-element.41), channel_id=1, source_target_pairs={{28,0},{0,4},{4,8},{8,12},{12,16},{16,20},{20,24},{24,28},{29,1},{... | collective-permute-start | bytes 233480 | tf_op jit(solution)/shard_map/ppermute | solution.py:62
  4.7 3.1 %collective-permute-start.3 = (f32[152,128]{1,0:T(8,128)S(1)}, f32[152,128]{1,0:T(8,128)S(1)}, u32[]{:S(2)}, u32[]{:S(2)}) collective-permute-start(f32[152,128]{1,0:T(8,128)S(1)} %get-tuple-element.42), channel_id=1, source_target_pairs={{4,0},{8,4},{12,8},{16,12},{20,16},{24,20},{28,24},{0,28},{5,1},{9... | collective-permute-start | bytes 233480 | tf_op jit(solution)/shard_map/ppermute | solution.py:62
  7.8 1.1 %y_pack.1 = (f32[5,12,24,128]{3,2,1,0:T(8,128)S(1)}, f32[208,128]{1,0:T(8,128)S(1)}, f32[208,128]{1,0:T(8,128)S(1)}) custom-call(f32[12,12,128]{2,1,0:T(8,128)} %refs_0_.3, f32[12,12,128]{2,1,0:T(8,128)} %refs_1_.3, f32[12,12,128]{2,1,0:T(8,128)} %refs_2_.3, f32[12,12,128]{2,1,0:T(8,128)} %refs_3_.3, f32[12,12,128]{2,1,0:T(8,128)} %refs_4_.3), custom_call_target="tpu_custom_call" | custom-call | tf_op jit(solution)/shard_map/y_pack/pallas_call | solution.py:464
  8.9 0.7 %collective-permute-start = (f32[208,128]{1,0:T(8,128)S(1)}, f32[208,128]{1,0:T(8,128)S(1)}, u32[]{:S(2)}, u32[]{:S(2)}) collective-permute-start(f32[208,128]{1,0:T(8,128)S(1)} %get-tuple-element.34), channel_id=1, source_target_pairs={{0,3},{1,2},{2,1},{3,0},{4,7},{5,6},{6,5},{7,4},{8,11},{9,10},{10,... | collective-permute-start | bytes 319496 | tf_op jit(solution)/shard_map/ppermute | solution.py:68
  9.6 1.1 %collective-permute-start.1 = (f32[208,128]{1,0:T(8,128)S(1)}, f32[208,128]{1,0:T(8,128)S(1)}, u32[]{:S(2)}, u32[]{:S(2)}) collective-permute-start(f32[208,128]{1,0:T(8,128)S(1)} %get-tuple-element.35), channel_id=1, source_target_pairs={{0,1},{1,0},{2,3},{3,2},{4,5},{5,4},{6,7},{7,6},{8,9},{9,8},{10,11... | collective-permute-start | bytes 319496 | tf_op jit(solution)/shard_map/ppermute | solution.py:68
  10.6 0.0 collective-permute-done.2.refs_0_
  10.6 0.1 collective-permute-done.3.refs_1_
  10.8 0.1 collective-permute-start.4
  10.9 1.6 %collective-permute-start.5 = (f32[80,128]{1,0:T(8,128)S(1)}, f32[80,128]{1,0:T(8,128)S(1)}, u32[]{:S(2)}, u32[]{:S(2)}) collective-permute-start(f32[80,128]{1,0:T(8,128)S(1)} %get-tuple-element.44), channel_id=1, source_target_pairs={{0,1},{1,0},{2,3},{3,2},{4,5},{5,4},{6,7},{7,6},{8,9},{9,8},{10,11... | collective-permute-start | bytes 122888 | tf_op jit(solution)/shard_map/ppermute | solution.py:68
  13.1 1.0 %collective-permute-done.refs_1_ = f32[208,128]{1,0:T(8,128)S(1)} collective-permute-done((f32[208,128]{1,0:T(8,128)S(1)}, f32[208,128]{1,0:T(8,128)S(1)}, u32[]{:S(2)}, u32[]{:S(2)}) %collective-permute-start) | collective-permute-done | bytes 106528 | tf_op jit(solution)/shard_map/ppermute | solution.py:68
  14.1 0.0 collective-permute-done.1.refs_2_
  14.1 0.7 %inner.1 = (f32[5,12,32,128]{3,2,1,0:T(8,128)S(1)}, f32[10,24,128]{2,1,0:T(8,128)S(1)}, f32[3,8,16,128]{3,2,1,0:T(8,128)S(1)}, f32[2,8,16,128]{3,2,1,0:T(8,128)S...) custom-call(f32[1]{0:T(128)} %bitcast.4.dt_ref, ...), custom_call_target="tpu_custom_call" | custom-call | flops 5000000 | bytes 2000000 | tf_op jit(solution)/shard_map/inner/pallas_call | solution.py:486
  14.8 0.2 collective-permute-done.4.refs_2_
  14.9 0.0 collective-permute-done.5.refs_3_
  14.9 1.4 %outer.1 = (f32[3,8,16,128]{3,2,1,0:T(8,128)S(1)}, f32[2,8,16,128]{3,2,1,0:T(8,128)S(1)}, f32[8,24,128]{2,1,0:T(8,128)S(1)}, f32[8,16,128]{2,1,0:T(8,128)S(1)}, ...) custom-call(f32[1]{0:T(128)} %bitcast.5.dt_ref, f32[152,128]{1,0:T(8,128)S(1)} %collective-permute-done.2.refs_0_, ...), custom_call_target="tpu_custom_call" | custom-call | tf_op jit(solution)/shard_map/outer/pallas_call | solution.py:508
  16.3 4.9 %all-to-all-start = ((f32[32,1,128]{2,1,0:T(1,128)}), f32[32,1,128]{2,1,0:T(1,128)S(1)}, u32[]{:S(2)}, u32[]{:S(2)}) async-start(f32[32,1,128]{2,1,0:T(1,128)} %bitcast.2), calls=%async_computation | async-start | bytes 32768 | tf_op jit(solution)/shard_map/all_to_all | solution.py:542
  21.2 2.2 %carry.1 = (f32[12,12,128]{2,1,0:T(8,128)}, f32[12,12,128]{2,1,0:T(8,128)}, f32[12,12,128]{2,1,0:T(8,128)}, f32[12,12,128]{2,1,0:T(8,128)}, f32[12,12,128]{2,1,0:T(8,128)}) custom-call(f32[1]{0:T(128)} %bitcast.6.dt_ref, f32[3,8,16,128]{3,2,1,0:T(8,128)S(1)} %get-tuple-element.36.refs_6_.refs_0_, f32[2,8,16,128]{3,2,1,0:T(8,128)S(1)} %get-tuple-element.37.refs_1_, ...), custom_call_target="tpu_custom_call" | custom-call | flops 10000000 | bytes 4000000 | tf_op jit(solution)/shard_map/carry/pallas_call | solution.py:528
  23.4 4.9 %all-to-all-done = f32[32,1,128]{2,1,0:T(1,128)S(1)} async-done(((f32[32,1,128]{2,1,0:T(1,128)}), f32[32,1,128]{2,1,0:T(1,128)S(1)}, u32[]{:S(2)}, u32[]{:S(2)}) %all-to-all-start) | async-done | bytes 16416 | tf_op jit(solution)/shard_map/all_to_all | solution.py:542
  28.3 0.6 %reduce_min.9 = f32[]{:T(128)} reduce(f32[32,1,128]{2,1,0:T(1,128)S(1)} %all-to-all-done, f32[]{:T(128)} %constant.0.clone.1), dimensions={0,1,2}, to_apply=%region_0.0 | reduce | flops 4095 | bytes 16392 | tf_op jit(solution)/shard_map/reduce_min | solution.py:542
  (1 shorter events, 0.0 us)
Async XLA Ops:
  1.7 9.0 %collective-permute-start.2 = (f32[152,128]{1,0:T(8,128)S(1)}, f32[152,128]{1,0:T(8,128)S(1)}, u32[]{:S(2)}, u32[]{:S(2)}) collective-permute-start(f32[152,128]{1,0:T(8,128)S(1)} %get-tuple-element.41), channel_id=1, source_target_pairs={{28,0},{0,4},{4,8},{8,12},{12,16},{16,20},{20,24},{24,28},{29,1},{... | collective-permute-start | bytes 233480 | tf_op jit(solution)/shard_map/ppermute | solution.py:62
  4.7 6.1 %collective-permute-start.3 = (f32[152,128]{1,0:T(8,128)S(1)}, f32[152,128]{1,0:T(8,128)S(1)}, u32[]{:S(2)}, u32[]{:S(2)}) collective-permute-start(f32[152,128]{1,0:T(8,128)S(1)} %get-tuple-element.42), channel_id=1, source_target_pairs={{4,0},{8,4},{12,8},{16,12},{20,16},{24,20},{28,24},{0,28},{5,1},{9... | collective-permute-start | bytes 233480 | tf_op jit(solution)/shard_map/ppermute | solution.py:62
  8.9 5.2 %collective-permute-start = (f32[208,128]{1,0:T(8,128)S(1)}, f32[208,128]{1,0:T(8,128)S(1)}, u32[]{:S(2)}, u32[]{:S(2)}) collective-permute-start(f32[208,128]{1,0:T(8,128)S(1)} %get-tuple-element.34), channel_id=1, source_target_pairs={{0,3},{1,2},{2,1},{3,0},{4,7},{5,6},{6,5},{7,4},{8,11},{9,10},{10,... | collective-permute-start | bytes 319496 | tf_op jit(solution)/shard_map/ppermute | solution.py:68
  9.6 4.5 %collective-permute-start.1 = (f32[208,128]{1,0:T(8,128)S(1)}, f32[208,128]{1,0:T(8,128)S(1)}, u32[]{:S(2)}, u32[]{:S(2)}) collective-permute-start(f32[208,128]{1,0:T(8,128)S(1)} %get-tuple-element.35), channel_id=1, source_target_pairs={{0,1},{1,0},{2,3},{3,2},{4,5},{5,4},{6,7},{7,6},{8,9},{9,8},{10,11... | collective-permute-start | bytes 319496 | tf_op jit(solution)/shard_map/ppermute | solution.py:68
  10.8 4.2 %collective-permute-start.4 = (f32[80,128]{1,0:T(8,128)S(1)}, f32[80,128]{1,0:T(8,128)S(1)}, u32[]{:S(2)}, u32[]{:S(2)}) collective-permute-start(f32[80,128]{1,0:T(8,128)S(1)} %get-tuple-element.43), channel_id=1, source_target_pairs={{0,3},{1,2},{2,1},{3,0},{4,7},{5,6},{6,5},{7,4},{8,11},{9,10},{10,... | collective-permute-start | bytes 122888 | tf_op jit(solution)/shard_map/ppermute | solution.py:68
  10.9 4.1 %collective-permute-start.5 = (f32[80,128]{1,0:T(8,128)S(1)}, f32[80,128]{1,0:T(8,128)S(1)}, u32[]{:S(2)}, u32[]{:S(2)}) collective-permute-start(f32[80,128]{1,0:T(8,128)S(1)} %get-tuple-element.44), channel_id=1, source_target_pairs={{0,1},{1,0},{2,3},{3,2},{4,5},{5,4},{6,7},{7,6},{8,9},{9,8},{10,11... | collective-permute-start | bytes 122888 | tf_op jit(solution)/shard_map/ppermute | solution.py:68
  16.3 12.0 %all-to-all-start = ((f32[32,1,128]{2,1,0:T(1,128)}), f32[32,1,128]{2,1,0:T(1,128)S(1)}, u32[]{:S(2)}, u32[]{:S(2)}) async-start(f32[32,1,128]{2,1,0:T(1,128)} %bitcast.2), calls=%async_computation | async-start | bytes 32768 | tf_op jit(solution)/shard_map/all_to_all | solution.py:542

commit v21 on v19

--- a/solution.py
+++ b/solution.py
@@ -84,13 +84,13 @@
     fields, x_edges, near, padded, arrived = refs[:5], refs[5:7], refs[7], refs[8], refs[9]
     zero = hidden_zero()
     order = (ZV, YV, XV, ENERGY, DENSITY)
-    copies = {
-        (field, k): pltpu.make_async_copy(
-            fields[field].at[pl.ds(first, 4)], near.at[field, pl.ds(4 * k, 4)], arrived.at[field, k]
-        )
-        for field in order
-        for k, first in enumerate((nx - 4, 0))
-    }
+    copies = {}
+    for field in order:
+        width = 4 if field == XV else 3
+        for k, (first, place_at) in enumerate(((nx - width, 4 - width), (0, 4))):
+            copies[field, k] = pltpu.make_async_copy(
+                fields[field].at[pl.ds(first, width)], near.at[field, pl.ds(place_at, width)], arrived.at[field, k]
+            )
     for copy in copies.values():
         copy.start()
     thirds = (1, 6)

time: 29.2 us -> 29.2 us (level)
  no operation moved by 1% of the time
where the time goes in v21:
time: 29.2 us; the launch traced here: 28.9 us
  starting transfers between devices  14.4 us (49%)
  Pallas kernels  6.41 us (22%)
  waiting for transfers between devices  6.15 us (21%)
  between operations  1.34 us (5%)
  other arithmetic  0.63 us (2%)
    ppermute x2, starting transfers between devices, along_x(): lax.ppermute(value, 'gx', [((i + side) % count, i) for i in range(count)])  6.12 us
    all_to_all x1, waiting for transfers between devices, body(): lax.all_to_all(smallest, ('gx', 'gy'), 0, 0, tiled=True)  4.93 us
    all_to_all x1, starting transfers between devices, body(): lax.all_to_all(smallest, ('gx', 'gy'), 0, 0, tiled=True)  4.85 us
    ppermute x4, starting transfers between devices, along_y(): return lax.ppermute(value, 'gy', list(enumerate(partners)))  3.44 us
    pallas_call x1, Pallas kernels, body(): pl.pallas_call(functools.partial(carry_kernel, nx, ny), out_shape=[array(...  2.21 us
    pallas_call x1, Pallas kernels, body(): pl.pallas_call(functools.partial(outer_kernel, nx, ny), out_shape=passed_...  1.38 us
    ppermute x4, waiting for transfers between devices, along_y(): return lax.ppermute(value, 'gy', list(enumerate(partners)))  1.12 us
    pallas_call x1, Pallas kernels, body(): pl.pallas_call(functools.partial(y_pack_kernel, nx, ny), out_shape=[array...  1.08 us
  transfers between devices with their start and end apart: 7, of which 4 were waited for; matrix products, arithmetic and copies ran while one was open for 0% of the time, Pallas kernels for 14%

profile of v21, /device:TPU:0, one launch (start us, length us, event | category | flops | bytes accessed | tf_op | source)
XLA Modules:
  0.0 28.9 jit_solution(18071082379739664074)
XLA Ops:
  0.6 1.0 %x_pack.1 = (f32[152,128]{1,0:T(8,128)S(1)}, f32[152,128]{1,0:T(8,128)S(1)}) custom-call(f32[12,12,128]{2,1,0:T(8,128)} %refs_0_.3, f32[12,12,128]{2,1,0:T(8,128)} %refs_1_.3, f32[12,12,128]{2,1,0:T(8,128)} %refs_2_.3, f32[12,12,128]{2,1,0:T(8,128)} %refs_3_.3, f32[12,12,128]{2,1,0:T(8,128)} %refs_4_.3), custom_call_target="tpu_custom_call" | custom-call | tf_op jit(solution)/shard_map/x_pack/pallas_call | solution.py:460
  1.6 3.0 %collective-permute-start.2 = (f32[152,128]{1,0:T(8,128)S(1)}, f32[152,128]{1,0:T(8,128)S(1)}, u32[]{:S(2)}, u32[]{:S(2)}) collective-permute-start(f32[152,128]{1,0:T(8,128)S(1)} %get-tuple-element.41), channel_id=1, source_target_pairs={{28,0},{0,4},{4,8},{8,12},{12,16},{16,20},{20,24},{24,28},{29,1},{... | collective-permute-start | bytes 233480 | tf_op jit(solution)/shard_map/ppermute | solution.py:62
  4.7 3.1 %collective-permute-start.3 = (f32[152,128]{1,0:T(8,128)S(1)}, f32[152,128]{1,0:T(8,128)S(1)}, u32[]{:S(2)}, u32[]{:S(2)}) collective-permute-start(f32[152,128]{1,0:T(8,128)S(1)} %get-tuple-element.42), channel_id=1, source_target_pairs={{4,0},{8,4},{12,8},{16,12},{20,16},{24,20},{28,24},{0,28},{5,1},{9... | collective-permute-start | bytes 233480 | tf_op jit(solution)/shard_map/ppermute | solution.py:62
  7.8 1.1 %y_pack.1 = (f32[5,12,24,128]{3,2,1,0:T(8,128)S(1)}, f32[208,128]{1,0:T(8,128)S(1)}, f32[208,128]{1,0:T(8,128)S(1)}) custom-call(f32[12,12,128]{2,1,0:T(8,128)} %refs_0_.3, f32[12,12,128]{2,1,0:T(8,128)} %refs_1_.3, f32[12,12,128]{2,1,0:T(8,128)} %refs_2_.3, f32[12,12,128]{2,1,0:T(8,128)} %refs_3_.3, f32[12,12,128]{2,1,0:T(8,128)} %refs_4_.3), custom_call_target="tpu_custom_call" | custom-call | tf_op jit(solution)/shard_map/y_pack/pallas_call | solution.py:470
  8.9 0.7 %collective-permute-start = (f32[208,128]{1,0:T(8,128)S(1)}, f32[208,128]{1,0:T(8,128)S(1)}, u32[]{:S(2)}, u32[]{:S(2)}) collective-permute-start(f32[208,128]{1,0:T(8,128)S(1)} %get-tuple-element.34), channel_id=1, source_target_pairs={{0,3},{1,2},{2,1},{3,0},{4,7},{5,6},{6,5},{7,4},{8,11},{9,10},{10,... | collective-permute-start | bytes 319496 | tf_op jit(solution)/shard_map/ppermute | solution.py:68
  9.6 1.1 %collective-permute-start.1 = (f32[208,128]{1,0:T(8,128)S(1)}, f32[208,128]{1,0:T(8,128)S(1)}, u32[]{:S(2)}, u32[]{:S(2)}) collective-permute-start(f32[208,128]{1,0:T(8,128)S(1)} %get-tuple-element.35), channel_id=1, source_target_pairs={{0,1},{1,0},{2,3},{3,2},{4,5},{5,4},{6,7},{7,6},{8,9},{9,8},{10,11... | collective-permute-start | bytes 319496 | tf_op jit(solution)/shard_map/ppermute | solution.py:68
  10.6 0.0 collective-permute-done.2.refs_0_
  10.6 0.1 collective-permute-done.3.refs_1_
  10.8 0.1 collective-permute-start.4
  10.8 1.6 %collective-permute-start.5 = (f32[80,128]{1,0:T(8,128)S(1)}, f32[80,128]{1,0:T(8,128)S(1)}, u32[]{:S(2)}, u32[]{:S(2)}) collective-permute-start(f32[80,128]{1,0:T(8,128)S(1)} %get-tuple-element.44), channel_id=1, source_target_pairs={{0,1},{1,0},{2,3},{3,2},{4,5},{5,4},{6,7},{7,6},{8,9},{9,8},{10,11... | collective-permute-start | bytes 122888 | tf_op jit(solution)/shard_map/ppermute | solution.py:68
  13.1 1.0 %collective-permute-done.refs_1_ = f32[208,128]{1,0:T(8,128)S(1)} collective-permute-done((f32[208,128]{1,0:T(8,128)S(1)}, f32[208,128]{1,0:T(8,128)S(1)}, u32[]{:S(2)}, u32[]{:S(2)}) %collective-permute-start) | collective-permute-done | bytes 106528 | tf_op jit(solution)/shard_map/ppermute | solution.py:68
  14.0 0.0 collective-permute-done.1.refs_2_
  14.0 0.7 %inner.1 = (f32[5,12,32,128]{3,2,1,0:T(8,128)S(1)}, f32[10,24,128]{2,1,0:T(8,128)S(1)}, f32[3,8,16,128]{3,2,1,0:T(8,128)S(1)}, f32[2,8,16,128]{3,2,1,0:T(8,128)S...) custom-call(f32[1]{0:T(128)} %bitcast.4.dt_ref, ...), custom_call_target="tpu_custom_call" | custom-call | flops 5000000 | bytes 2000000 | tf_op jit(solution)/shard_map/inner/pallas_call | solution.py:492
  14.8 0.2 collective-permute-done.4.refs_2_
  14.9 0.0 collective-permute-done.5.refs_3_
  14.9 1.4 %outer.1 = (f32[3,8,16,128]{3,2,1,0:T(8,128)S(1)}, f32[2,8,16,128]{3,2,1,0:T(8,128)S(1)}, f32[8,24,128]{2,1,0:T(8,128)S(1)}, f32[8,16,128]{2,1,0:T(8,128)S(1)}, ...) custom-call(f32[1]{0:T(128)} %bitcast.5.dt_ref, f32[152,128]{1,0:T(8,128)S(1)} %collective-permute-done.2.refs_0_, ...), custom_call_target="tpu_custom_call" | custom-call | tf_op jit(solution)/shard_map/outer/pallas_call | solution.py:514
  16.3 4.9 %all-to-all-start = ((f32[32,1,128]{2,1,0:T(1,128)}), f32[32,1,128]{2,1,0:T(1,128)S(1)}, u32[]{:S(2)}, u32[]{:S(2)}) async-start(f32[32,1,128]{2,1,0:T(1,128)} %bitcast.2), calls=%async_computation | async-start | bytes 32768 | tf_op jit(solution)/shard_map/all_to_all | solution.py:548
  21.2 2.2 %carry.1 = (f32[12,12,128]{2,1,0:T(8,128)}, f32[12,12,128]{2,1,0:T(8,128)}, f32[12,12,128]{2,1,0:T(8,128)}, f32[12,12,128]{2,1,0:T(8,128)}, f32[12,12,128]{2,1,0:T(8,128)}) custom-call(f32[1]{0:T(128)} %bitcast.6.dt_ref, f32[3,8,16,128]{3,2,1,0:T(8,128)S(1)} %get-tuple-element.36.refs_6_.refs_0_, f32[2,8,16,128]{3,2,1,0:T(8,128)S(1)} %get-tuple-element.37.refs_1_, ...), custom_call_target="tpu_custom_call" | custom-call | flops 10000000 | bytes 4000000 | tf_op jit(solution)/shard_map/carry/pallas_call | solution.py:534
  23.4 4.9 %all-to-all-done = f32[32,1,128]{2,1,0:T(1,128)S(1)} async-done(((f32[32,1,128]{2,1,0:T(1,128)}), f32[32,1,128]{2,1,0:T(1,128)S(1)}, u32[]{:S(2)}, u32[]{:S(2)}) %all-to-all-start) | async-done | bytes 16416 | tf_op jit(solution)/shard_map/all_to_all | solution.py:548
  28.3 0.6 %reduce_min.9 = f32[]{:T(128)} reduce(f32[32,1,128]{2,1,0:T(1,128)S(1)} %all-to-all-done, f32[]{:T(128)} %constant.0.clone.1), dimensions={0,1,2}, to_apply=%region_0.0 | reduce | flops 4095 | bytes 16392 | tf_op jit(solution)/shard_map/reduce_min | solution.py:548
  (1 shorter events, 0.0 us)
Async XLA Ops:
  1.6 9.0 %collective-permute-start.2 = (f32[152,128]{1,0:T(8,128)S(1)}, f32[152,128]{1,0:T(8,128)S(1)}, u32[]{:S(2)}, u32[]{:S(2)}) collective-permute-start(f32[152,128]{1,0:T(8,128)S(1)} %get-tuple-element.41), channel_id=1, source_target_pairs={{28,0},{0,4},{4,8},{8,12},{12,16},{16,20},{20,24},{24,28},{29,1},{... | collective-permute-start | bytes 233480 | tf_op jit(solution)/shard_map/ppermute | solution.py:62
  4.7 6.1 %collective-permute-start.3 = (f32[152,128]{1,0:T(8,128)S(1)}, f32[152,128]{1,0:T(8,128)S(1)}, u32[]{:S(2)}, u32[]{:S(2)}) collective-permute-start(f32[152,128]{1,0:T(8,128)S(1)} %get-tuple-element.42), channel_id=1, source_target_pairs={{4,0},{8,4},{12,8},{16,12},{20,16},{24,20},{28,24},{0,28},{5,1},{9... | collective-permute-start | bytes 233480 | tf_op jit(solution)/shard_map/ppermute | solution.py:62
  8.9 5.2 %collective-permute-start = (f32[208,128]{1,0:T(8,128)S(1)}, f32[208,128]{1,0:T(8,128)S(1)}, u32[]{:S(2)}, u32[]{:S(2)}) collective-permute-start(f32[208,128]{1,0:T(8,128)S(1)} %get-tuple-element.34), channel_id=1, source_target_pairs={{0,3},{1,2},{2,1},{3,0},{4,7},{5,6},{6,5},{7,4},{8,11},{9,10},{10,... | collective-permute-start | bytes 319496 | tf_op jit(solution)/shard_map/ppermute | solution.py:68
  9.6 4.5 %collective-permute-start.1 = (f32[208,128]{1,0:T(8,128)S(1)}, f32[208,128]{1,0:T(8,128)S(1)}, u32[]{:S(2)}, u32[]{:S(2)}) collective-permute-start(f32[208,128]{1,0:T(8,128)S(1)} %get-tuple-element.35), channel_id=1, source_target_pairs={{0,1},{1,0},{2,3},{3,2},{4,5},{5,4},{6,7},{7,6},{8,9},{9,8},{10,11... | collective-permute-start | bytes 319496 | tf_op jit(solution)/shard_map/ppermute | solution.py:68
  10.8 4.2 %collective-permute-start.4 = (f32[80,128]{1,0:T(8,128)S(1)}, f32[80,128]{1,0:T(8,128)S(1)}, u32[]{:S(2)}, u32[]{:S(2)}) collective-permute-start(f32[80,128]{1,0:T(8,128)S(1)} %get-tuple-element.43), channel_id=1, source_target_pairs={{0,3},{1,2},{2,1},{3,0},{4,7},{5,6},{6,5},{7,4},{8,11},{9,10},{10,... | collective-permute-start | bytes 122888 | tf_op jit(solution)/shard_map/ppermute | solution.py:68
  10.8 4.1 %collective-permute-start.5 = (f32[80,128]{1,0:T(8,128)S(1)}, f32[80,128]{1,0:T(8,128)S(1)}, u32[]{:S(2)}, u32[]{:S(2)}) collective-permute-start(f32[80,128]{1,0:T(8,128)S(1)} %get-tuple-element.44), channel_id=1, source_target_pairs={{0,1},{1,0},{2,3},{3,2},{4,5},{5,4},{6,7},{7,6},{8,9},{9,8},{10,11... | collective-permute-start | bytes 122888 | tf_op jit(solution)/shard_map/ppermute | solution.py:68
  16.3 12.0 %all-to-all-start = ((f32[32,1,128]{2,1,0:T(1,128)}), f32[32,1,128]{2,1,0:T(1,128)S(1)}, u32[]{:S(2)}, u32[]{:S(2)}) async-start(f32[32,1,128]{2,1,0:T(1,128)} %bitcast.2), calls=%async_computation | async-start | bytes 32768 | tf_op jit(solution)/shard_map/all_to_all | solution.py:548

commit v22 on v21

--- a/solution.py
+++ b/solution.py
@@ -94,26 +94,30 @@
     for copy in copies.values():
         copy.start()
     thirds = (1, 6)
+    for k in range(2):
+        padded[k] = jnp.zeros_like(padded[k])
     for current in order:
         for k, (side, edge) in enumerate(zip(SIDES, x_edges)):
             copies[current, k].wait()
             if current == ZV:
-                padded[k] = jnp.zeros_like(padded[k])
                 padded[2 + k, pl.ds(TOP, ny), :] = up(near[ZV, thirds[k]]) - down(near[ZV, thirds[k]])
             if current == YV:
                 padded[k, pl.ds(TOP, ny), :] = near[YV, thirds[k]]
+            if current == ENERGY:
+                a = thirds[k]
+                spread = near[XV, a + 1] - near[XV, a - 1]
+                spread += padded[k, pl.ds(zero + (TOP + 1), ny), :] - padded[k, pl.ds(zero + (TOP - 1), ny), :]
+                spread += padded[2 + k, pl.ds(TOP, ny), :]
+                padded[2 + k, pl.ds(TOP, ny), :] = spread
+                padded[4 + k, pl.ds(TOP, ny), :] = per_mass(near[ENERGY, a], spread)
             for number, (field, past) in enumerate(x_layers()):
                 if field == current:
                     edge[pl.ds(zero + number * ny, ny), :] = near[field, 4 - past if side < 0 else 3 + past]
     for k, edge in enumerate(x_edges):
         a = thirds[k]
         offset = len(x_layers()) * ny
-        spread = near[XV, a + 1] - near[XV, a - 1]
-        spread += padded[k, pl.ds(zero + (TOP + 1), ny), :] - padded[k, pl.ds(zero + (TOP - 1), ny), :]
-        spread += padded[2 + k, pl.ds(TOP, ny), :]
-        edge[pl.ds(zero + offset, ny), :] = near[DENSITY, a] * per_mass(near[ENERGY, a], spread)
+        edge[pl.ds(zero + offset, ny), :] = near[DENSITY, a] * padded[4 + k, pl.ds(TOP, ny), :]
         offset += ny
-        padded[2 + k, pl.ds(TOP, ny), :] = spread
         for row in (0, ny - 1):
             for value in (near[DENSITY, a, pl.ds(row, 1), :], near[ENERGY, a, pl.ds(row, 1), :],
                           padded[2 + k, pl.ds(TOP + row, 1), :], near[YV, a, pl.ds(row, 1), :]):
@@ -462,7 +466,7 @@
         out_shape=[x_edge] * 2,
         in_specs=[HBM] * 5,
         out_specs=[VMEM] * 2,
-        scratch_shapes=[scratch(5, 8, ny), scratch(4, ny + 20), pltpu.SemaphoreType.DMA((5, 2))],
+        scratch_shapes=[scratch(5, 8, ny), scratch(6, ny + 20), pltpu.SemaphoreType.DMA((5, 2))],
         compiler_params=limit(4),
         name="x_pack",
     )(*placed)

time: 29.2 us -> 29.2 us (level)
  no operation moved by 1% of the time
where the time goes in v22:
time: 29.2 us; the launch traced here: 28.9 us
  starting transfers between devices  14.4 us (49%)
  Pallas kernels  6.41 us (22%)
  waiting for transfers between devices  6.15 us (21%)
  between operations  1.34 us (5%)
  other arithmetic  0.63 us (2%)
    ppermute x2, starting transfers between devices, along_x(): lax.ppermute(value, 'gx', [((i + side) % count, i) for i in range(count)])  6.12 us
    all_to_all x1, waiting for transfers between devices, body(): lax.all_to_all(smallest, ('gx', 'gy'), 0, 0, tiled=True)  4.93 us
    all_to_all x1, starting transfers between devices, body(): lax.all_to_all(smallest, ('gx', 'gy'), 0, 0, tiled=True)  4.85 us
    ppermute x4, starting transfers between devices, along_y(): return lax.ppermute(value, 'gy', list(enumerate(partners)))  3.44 us
    pallas_call x1, Pallas kernels, body(): pl.pallas_call(functools.partial(carry_kernel, nx, ny), out_shape=[array(...  2.21 us
    pallas_call x1, Pallas kernels, body(): pl.pallas_call(functools.partial(outer_kernel, nx, ny), out_shape=passed_...  1.38 us
    ppermute x4, waiting for transfers between devices, along_y(): return lax.ppermute(value, 'gy', list(enumerate(partners)))  1.12 us
    pallas_call x1, Pallas kernels, body(): pl.pallas_call(functools.partial(y_pack_kernel, nx, ny), out_shape=[array...  1.08 us
  transfers between devices with their start and end apart: 7, of which 4 were waited for; matrix products, arithmetic and copies ran while one was open for 0% of the time, Pallas kernels for 14%

profile of v22, /device:TPU:0, one launch (start us, length us, event | category | flops | bytes accessed | tf_op | source)
XLA Modules:
  0.0 28.9 jit_solution(13830084013901969163)
XLA Ops:
  0.6 1.0 %x_pack.1 = (f32[152,128]{1,0:T(8,128)S(1)}, f32[152,128]{1,0:T(8,128)S(1)}) custom-call(f32[12,12,128]{2,1,0:T(8,128)} %refs_0_.3, f32[12,12,128]{2,1,0:T(8,128)} %refs_1_.3, f32[12,12,128]{2,1,0:T(8,128)} %refs_2_.3, f32[12,12,128]{2,1,0:T(8,128)} %refs_3_.3, f32[12,12,128]{2,1,0:T(8,128)} %refs_4_.3), custom_call_target="tpu_custom_call" | custom-call | tf_op jit(solution)/shard_map/x_pack/pallas_call | solution.py:464
  1.7 3.0 %collective-permute-start.2 = (f32[152,128]{1,0:T(8,128)S(1)}, f32[152,128]{1,0:T(8,128)S(1)}, u32[]{:S(2)}, u32[]{:S(2)}) collective-permute-start(f32[152,128]{1,0:T(8,128)S(1)} %get-tuple-element.41), channel_id=1, source_target_pairs={{28,0},{0,4},{4,8},{8,12},{12,16},{16,20},{20,24},{24,28},{29,1},{... | collective-permute-start | bytes 233480 | tf_op jit(solution)/shard_map/ppermute | solution.py:62
  4.7 3.1 %collective-permute-start.3 = (f32[152,128]{1,0:T(8,128)S(1)}, f32[152,128]{1,0:T(8,128)S(1)}, u32[]{:S(2)}, u32[]{:S(2)}) collective-permute-start(f32[152,128]{1,0:T(8,128)S(1)} %get-tuple-element.42), channel_id=1, source_target_pairs={{4,0},{8,4},{12,8},{16,12},{20,16},{24,20},{28,24},{0,28},{5,1},{9... | collective-permute-start | bytes 233480 | tf_op jit(solution)/shard_map/ppermute | solution.py:62
  7.8 1.1 %y_pack.1 = (f32[5,12,24,128]{3,2,1,0:T(8,128)S(1)}, f32[208,128]{1,0:T(8,128)S(1)}, f32[208,128]{1,0:T(8,128)S(1)}) custom-call(f32[12,12,128]{2,1,0:T(8,128)} %refs_0_.3, f32[12,12,128]{2,1,0:T(8,128)} %refs_1_.3, f32[12,12,128]{2,1,0:T(8,128)} %refs_2_.3, f32[12,12,128]{2,1,0:T(8,128)} %refs_3_.3, f32[12,12,128]{2,1,0:T(8,128)} %refs_4_.3), custom_call_target="tpu_custom_call" | custom-call | tf_op jit(solution)/shard_map/y_pack/pallas_call | solution.py:474
  8.9 0.7 %collective-permute-start = (f32[208,128]{1,0:T(8,128)S(1)}, f32[208,128]{1,0:T(8,128)S(1)}, u32[]{:S(2)}, u32[]{:S(2)}) collective-permute-start(f32[208,128]{1,0:T(8,128)S(1)} %get-tuple-element.34), channel_id=1, source_target_pairs={{0,3},{1,2},{2,1},{3,0},{4,7},{5,6},{6,5},{7,4},{8,11},{9,10},{10,... | collective-permute-start | bytes 319496 | tf_op jit(solution)/shard_map/ppermute | solution.py:68
  9.6 1.1 %collective-permute-start.1 = (f32[208,128]{1,0:T(8,128)S(1)}, f32[208,128]{1,0:T(8,128)S(1)}, u32[]{:S(2)}, u32[]{:S(2)}) collective-permute-start(f32[208,128]{1,0:T(8,128)S(1)} %get-tuple-element.35), channel_id=1, source_target_pairs={{0,1},{1,0},{2,3},{3,2},{4,5},{5,4},{6,7},{7,6},{8,9},{9,8},{10,11... | collective-permute-start | bytes 319496 | tf_op jit(solution)/shard_map/ppermute | solution.py:68
  10.6 0.0 collective-permute-done.2.refs_0_
  10.6 0.1 collective-permute-done.3.refs_1_
  10.8 0.1 collective-permute-start.4
  10.8 1.6 %collective-permute-start.5 = (f32[80,128]{1,0:T(8,128)S(1)}, f32[80,128]{1,0:T(8,128)S(1)}, u32[]{:S(2)}, u32[]{:S(2)}) collective-permute-start(f32[80,128]{1,0:T(8,128)S(1)} %get-tuple-element.44), channel_id=1, source_target_pairs={{0,1},{1,0},{2,3},{3,2},{4,5},{5,4},{6,7},{7,6},{8,9},{9,8},{10,11... | collective-permute-start | bytes 122888 | tf_op jit(solution)/shard_map/ppermute | solution.py:68
  13.1 1.0 %collective-permute-done.refs_1_ = f32[208,128]{1,0:T(8,128)S(1)} collective-permute-done((f32[208,128]{1,0:T(8,128)S(1)}, f32[208,128]{1,0:T(8,128)S(1)}, u32[]{:S(2)}, u32[]{:S(2)}) %collective-permute-start) | collective-permute-done | bytes 106528 | tf_op jit(solution)/shard_map/ppermute | solution.py:68
  14.0 0.0 collective-permute-done.1.refs_2_
  14.1 0.7 %inner.1 = (f32[5,12,32,128]{3,2,1,0:T(8,128)S(1)}, f32[10,24,128]{2,1,0:T(8,128)S(1)}, f32[3,8,16,128]{3,2,1,0:T(8,128)S(1)}, f32[2,8,16,128]{3,2,1,0:T(8,128)S...) custom-call(f32[1]{0:T(128)} %bitcast.4.dt_ref, ...), custom_call_target="tpu_custom_call" | custom-call | flops 5000000 | bytes 2000000 | tf_op jit(solution)/shard_map/inner/pallas_call | solution.py:496
  14.8 0.2 collective-permute-done.4.refs_2_
  14.9 0.0 collective-permute-done.5.refs_3_
  14.9 1.4 %outer.1 = (f32[3,8,16,128]{3,2,1,0:T(8,128)S(1)}, f32[2,8,16,128]{3,2,1,0:T(8,128)S(1)}, f32[8,24,128]{2,1,0:T(8,128)S(1)}, f32[8,16,128]{2,1,0:T(8,128)S(1)}, ...) custom-call(f32[1]{0:T(128)} %bitcast.5.dt_ref, f32[152,128]{1,0:T(8,128)S(1)} %collective-permute-done.2.refs_0_, ...), custom_call_target="tpu_custom_call" | custom-call | tf_op jit(solution)/shard_map/outer/pallas_call | solution.py:518
  16.3 4.9 %all-to-all-start = ((f32[32,1,128]{2,1,0:T(1,128)}), f32[32,1,128]{2,1,0:T(1,128)S(1)}, u32[]{:S(2)}, u32[]{:S(2)}) async-start(f32[32,1,128]{2,1,0:T(1,128)} %bitcast.2), calls=%async_computation | async-start | bytes 32768 | tf_op jit(solution)/shard_map/all_to_all | solution.py:552
  21.2 2.2 %carry.1 = (f32[12,12,128]{2,1,0:T(8,128)}, f32[12,12,128]{2,1,0:T(8,128)}, f32[12,12,128]{2,1,0:T(8,128)}, f32[12,12,128]{2,1,0:T(8,128)}, f32[12,12,128]{2,1,0:T(8,128)}) custom-call(f32[1]{0:T(128)} %bitcast.6.dt_ref, f32[3,8,16,128]{3,2,1,0:T(8,128)S(1)} %get-tuple-element.36.refs_6_.refs_0_, f32[2,8,16,128]{3,2,1,0:T(8,128)S(1)} %get-tuple-element.37.refs_1_, ...), custom_call_target="tpu_custom_call" | custom-call | flops 10000000 | bytes 4000000 | tf_op jit(solution)/shard_map/carry/pallas_call | solution.py:538
  23.4 4.9 %all-to-all-done = f32[32,1,128]{2,1,0:T(1,128)S(1)} async-done(((f32[32,1,128]{2,1,0:T(1,128)}), f32[32,1,128]{2,1,0:T(1,128)S(1)}, u32[]{:S(2)}, u32[]{:S(2)}) %all-to-all-start) | async-done | bytes 16416 | tf_op jit(solution)/shard_map/all_to_all | solution.py:552
  28.3 0.6 %reduce_min.9 = f32[]{:T(128)} reduce(f32[32,1,128]{2,1,0:T(1,128)S(1)} %all-to-all-done, f32[]{:T(128)} %constant.0.clone.1), dimensions={0,1,2}, to_apply=%region_0.0 | reduce | flops 4095 | bytes 16392 | tf_op jit(solution)/shard_map/reduce_min | solution.py:552
  (1 shorter events, 0.0 us)
Async XLA Ops:
  1.7 9.0 %collective-permute-start.2 = (f32[152,128]{1,0:T(8,128)S(1)}, f32[152,128]{1,0:T(8,128)S(1)}, u32[]{:S(2)}, u32[]{:S(2)}) collective-permute-start(f32[152,128]{1,0:T(8,128)S(1)} %get-tuple-element.41), channel_id=1, source_target_pairs={{28,0},{0,4},{4,8},{8,12},{12,16},{16,20},{20,24},{24,28},{29,1},{... | collective-permute-start | bytes 233480 | tf_op jit(solution)/shard_map/ppermute | solution.py:62
  4.7 6.1 %collective-permute-start.3 = (f32[152,128]{1,0:T(8,128)S(1)}, f32[152,128]{1,0:T(8,128)S(1)}, u32[]{:S(2)}, u32[]{:S(2)}) collective-permute-start(f32[152,128]{1,0:T(8,128)S(1)} %get-tuple-element.42), channel_id=1, source_target_pairs={{4,0},{8,4},{12,8},{16,12},{20,16},{24,20},{28,24},{0,28},{5,1},{9... | collective-permute-start | bytes 233480 | tf_op jit(solution)/shard_map/ppermute | solution.py:62
  8.9 5.2 %collective-permute-start = (f32[208,128]{1,0:T(8,128)S(1)}, f32[208,128]{1,0:T(8,128)S(1)}, u32[]{:S(2)}, u32[]{:S(2)}) collective-permute-start(f32[208,128]{1,0:T(8,128)S(1)} %get-tuple-element.34), channel_id=1, source_target_pairs={{0,3},{1,2},{2,1},{3,0},{4,7},{5,6},{6,5},{7,4},{8,11},{9,10},{10,... | collective-permute-start | bytes 319496 | tf_op jit(solution)/shard_map/ppermute | solution.py:68
  9.6 4.5 %collective-permute-start.1 = (f32[208,128]{1,0:T(8,128)S(1)}, f32[208,128]{1,0:T(8,128)S(1)}, u32[]{:S(2)}, u32[]{:S(2)}) collective-permute-start(f32[208,128]{1,0:T(8,128)S(1)} %get-tuple-element.35), channel_id=1, source_target_pairs={{0,1},{1,0},{2,3},{3,2},{4,5},{5,4},{6,7},{7,6},{8,9},{9,8},{10,11... | collective-permute-start | bytes 319496 | tf_op jit(solution)/shard_map/ppermute | solution.py:68
  10.8 4.2 %collective-permute-start.4 = (f32[80,128]{1,0:T(8,128)S(1)}, f32[80,128]{1,0:T(8,128)S(1)}, u32[]{:S(2)}, u32[]{:S(2)}) collective-permute-start(f32[80,128]{1,0:T(8,128)S(1)} %get-tuple-element.43), channel_id=1, source_target_pairs={{0,3},{1,2},{2,1},{3,0},{4,7},{5,6},{6,5},{7,4},{8,11},{9,10},{10,... | collective-permute-start | bytes 122888 | tf_op jit(solution)/shard_map/ppermute | solution.py:68
  10.8 4.1 %collective-permute-start.5 = (f32[80,128]{1,0:T(8,128)S(1)}, f32[80,128]{1,0:T(8,128)S(1)}, u32[]{:S(2)}, u32[]{:S(2)}) collective-permute-start(f32[80,128]{1,0:T(8,128)S(1)} %get-tuple-element.44), channel_id=1, source_target_pairs={{0,1},{1,0},{2,3},{3,2},{4,5},{5,4},{6,7},{7,6},{8,9},{9,8},{10,11... | collective-permute-start | bytes 122888 | tf_op jit(solution)/shard_map/ppermute | solution.py:68
  16.3 12.0 %all-to-all-start = ((f32[32,1,128]{2,1,0:T(1,128)}), f32[32,1,128]{2,1,0:T(1,128)S(1)}, u32[]{:S(2)}, u32[]{:S(2)}) async-start(f32[32,1,128]{2,1,0:T(1,128)} %bitcast.2), calls=%async_computation | async-start | bytes 32768 | tf_op jit(solution)/shard_map/all_to_all | solution.py:552

commit v23 on v21

--- a/solution.py
+++ b/solution.py
@@ -262,7 +262,7 @@
         write(growth, a, half * spread)
 
 
-def advance_columns(zero, columns, wide, half, cells, stress, heat, growth, passive, state, energies, nx):
+def advance_columns(zero, columns, wide, half, cells, stress, heat, growth, passive, state, roots, nx):
     for a in columns:
         density, energy, x, y, z = [read(zero, cells, a, TOP - 2, wide, field) for field in range(5)]
         grown = read(zero, growth, a, 2, wide)
@@ -276,10 +276,10 @@
         write(state, a, y - scale * (read(zero, stress, a, 3, wide) - read(zero, stress, a, 1, wide)), 1)
         write(state, a, z - scale * (up(centre) - down(centre)), 2)
         if 0 <= a < nx:
-            write(energies, a, energy)
-
-
-def flow_columns(zero, first, last, ny, half, state, energies, swept, work, speed_y, speed_z, flows):
+            write(roots, a, jnp.sqrt(0.56 * energy))
+
+
+def flow_columns(zero, first, last, ny, half, state, roots, swept, work, speed_y, speed_z, flows):
     wide = ny + 4
     sweep_x(
         lambda field, a, part: read(zero, state, a, part, 8, field),
@@ -299,7 +299,7 @@
         for field in range(3):
             write(flows, a, final[field][:ny], field)
         signal = (
-            jnp.sqrt(0.56 * read(zero, energies, a, 2, wide))
+            read(zero, roots, a, 2, wide)
             + jnp.abs(final[0])
             + jnp.abs(final[1])
             + jnp.abs(final[2])
@@ -310,7 +310,7 @@
 
 def inner_kernel(nx, ny, dt_ref, *refs):
     own, y_edges = refs[0], refs[1:3]
-    cells, stress, state, passive, energies, speed_y, speed_z, flows, peak_ref = refs[3:12]
+    cells, stress, state, passive, roots, speed_y, speed_z, flows, peak_ref = refs[3:12]
     heat, growth, swept, work = refs[12:]
     zero = hidden_zero()
     half = 0.5 * dt_ref[0]
@@ -323,14 +323,14 @@
             cells[field, a, pl.ds(TOP + pick(low, -rows, ny), rows), :] = edge[pl.ds(zero + offset, rows), :]
     cells = [(cells, 0, nx, 0)]
     stress, heat, growth = [[(ref, 1, nx - 1, 0)] for ref in (stress, heat, growth)]
-    state, passive, energies = [[(ref, 2, nx - 2, 0)] for ref in (state, passive, energies)]
+    state, passive, roots = [[(ref, 2, nx - 2, 0)] for ref in (state, passive, roots)]
     speed_y, speed_z, flows = [[(ref, 4, nx - 4, 0)] for ref in (speed_y, speed_z, flows)]
     spread_columns(zero, range(1, nx - 1), ny + 12, half, cells, stress, heat, growth)
     advance_columns(
-        zero, range(2, nx - 2), ny + 4, half, cells, stress, heat, growth, passive, state, energies, nx
+        zero, range(2, nx - 2), ny + 4, half, cells, stress, heat, growth, passive, state, roots, nx
     )
     peak_ref[...] = flow_columns(
-        zero, 4, nx - 4, ny, half, state, energies, swept, work, speed_y, speed_z, flows
+        zero, 4, nx - 4, ny, half, state, roots, swept, work, speed_y, speed_z, flows
     )
 
 
@@ -340,9 +340,9 @@
 
 def outer_kernel(nx, ny, dt_ref, *refs):
     x_edges, corners = refs[0:2], refs[2:4]
-    cells_in, stress_in, state_in, energies_in, peak_in = refs[4:9]
+    cells_in, stress_in, state_in, roots_in, peak_in = refs[4:9]
     state_out, passive_out, speed_y, speed_z, flows, increment_ref = refs[9:15]
-    beyond, third, stress_out, heat, growth, energies_out = refs[15:21]
+    beyond, third, stress_out, heat, growth, roots_out = refs[15:21]
     swept, work = refs[21:23], refs[23:25]
     nz = increment_ref.shape[-1]
     zero = hidden_zero()
@@ -380,7 +380,7 @@
     heat, growth = outer_pieces(heat, nx, 2, 2), outer_pieces(growth, nx, 2, 2)
     state = outer_pieces(state_out, nx, 2, 2) + [(state_in, 2, nx - 2, 0)]
     passive = outer_pieces(passive_out, nx, 2, 2)
-    energies = outer_pieces(energies_out, nx, 0, 2) + [(energies_in, 2, nx - 2, 0)]
+    roots = outer_pieces(roots_out, nx, 0, 2) + [(roots_in, 2, nx - 2, 0)]
     speed_y, speed_z, flows = [outer_pieces(ref, nx, 0, 4) for ref in (speed_y, speed_z, flows)]
 
     row = lax.broadcasted_iota(jnp.int32, (tall, nz), 0) - 4
@@ -393,13 +393,13 @@
 
     ends = (*range(-2, 2), *range(nx - 2, nx + 2))
     spread_columns(zero, ends, tall, half, cells, stress, heat, growth)
-    advance_columns(zero, ends, wide, half, cells, stress, heat, growth, passive, state, energies, nx)
+    advance_columns(zero, ends, wide, half, cells, stress, heat, growth, passive, state, roots, nx)
     peak = peak_in[...]
     for k, first in enumerate((0, nx - 4)):
         peak = jnp.maximum(
             peak,
             flow_columns(
-                zero, first, first + 4, ny, half, state, energies, swept[k], work[k], speed_y, speed_z, flows
+                zero, first, first + 4, ny, half, state, roots, swept[k], work[k], speed_y, speed_z, flows
             ),
         )
     peak = jnp.max(jnp.where(row[4 : 4 + wide] < ny, peak, 0.0), axis=0, keepdims=True)
@@ -489,7 +489,7 @@
     increment = time_increment.reshape(1)
     passed_in = [array(3, nx - 4, wide), array(2, nx - 4, wide), array(nx - 8, wide + 8), array(nx - 8, wide), array(3, nx - 8, ny)]
     passed_out = [array(3, 8, wide), array(2, 8, wide), array(8, wide + 8), array(8, wide), array(3, 8, ny)]
-    cells, stress, state_in, passive_in, energies, *rest_in, peak = pl.pallas_call(
+    cells, stress, state_in, passive_in, roots, *rest_in, peak = pl.pallas_call(
         functools.partial(inner_kernel, nx, ny),
         out_shape=[
             array(5, nx, ny + 20),
@@ -530,7 +530,7 @@
         ],
         compiler_params=limit(8),
         name="outer",
-    )(increment, *x_edges, *corners, cells, stress, state_in, energies, peak)
+    )(increment, *x_edges, *corners, cells, stress, state_in, roots, peak)
     outs = pl.pallas_call(
         functools.partial(carry_kernel, nx, ny),
         out_shape=[array(nx, ny)] * 5,

time: 29.2 us -> 29.2 us (level)
  no operation moved by 1% of the time
where the time goes in v23:
time: 29.2 us; the launch traced here: 28.9 us
  starting transfers between devices  14.4 us (49%)
  Pallas kernels  6.41 us (22%)
  waiting for transfers between devices  6.15 us (21%)
  between operations  1.34 us (5%)
  other arithmetic  0.63 us (2%)
    ppermute x2, starting transfers between devices, along_x(): lax.ppermute(value, 'gx', [((i + side) % count, i) for i in range(count)])  6.12 us
    all_to_all x1, waiting for transfers between devices, body(): lax.all_to_all(smallest, ('gx', 'gy'), 0, 0, tiled=True)  4.93 us
    all_to_all x1, starting transfers between devices, body(): lax.all_to_all(smallest, ('gx', 'gy'), 0, 0, tiled=True)  4.85 us
    ppermute x4, starting transfers between devices, along_y(): return lax.ppermute(value, 'gy', list(enumerate(partners)))  3.44 us
    pallas_call x1, Pallas kernels, body(): pl.pallas_call(functools.partial(carry_kernel, nx, ny), out_shape=[array(...  2.21 us
    pallas_call x1, Pallas kernels, body(): pl.pallas_call(functools.partial(outer_kernel, nx, ny), out_shape=passed_...  1.37 us
    ppermute x4, waiting for transfers between devices, along_y(): return lax.ppermute(value, 'gy', list(enumerate(partners)))  1.12 us
    pallas_call x1, Pallas kernels, body(): pl.pallas_call(functools.partial(y_pack_kernel, nx, ny), out_shape=[array...  1.08 us
  transfers between devices with their start and end apart: 7, of which 4 were waited for; matrix products, arithmetic and copies ran while one was open for 0% of the time, Pallas kernels for 14%

profile of v23, /device:TPU:0, one launch (start us, length us, event | category | flops | bytes accessed | tf_op | source)
XLA Modules:
  0.0 28.9 jit_solution(11937140801874998716)
XLA Ops:
  0.6 1.0 %x_pack.1 = (f32[152,128]{1,0:T(8,128)S(1)}, f32[152,128]{1,0:T(8,128)S(1)}) custom-call(f32[12,12,128]{2,1,0:T(8,128)} %refs_0_.3, f32[12,12,128]{2,1,0:T(8,128)} %refs_1_.3, f32[12,12,128]{2,1,0:T(8,128)} %refs_2_.3, f32[12,12,128]{2,1,0:T(8,128)} %refs_3_.3, f32[12,12,128]{2,1,0:T(8,128)} %refs_4_.3), custom_call_target="tpu_custom_call" | custom-call | tf_op jit(solution)/shard_map/x_pack/pallas_call | solution.py:460
  1.6 3.0 %collective-permute-start.2 = (f32[152,128]{1,0:T(8,128)S(1)}, f32[152,128]{1,0:T(8,128)S(1)}, u32[]{:S(2)}, u32[]{:S(2)}) collective-permute-start(f32[152,128]{1,0:T(8,128)S(1)} %get-tuple-element.41), channel_id=1, source_target_pairs={{28,0},{0,4},{4,8},{8,12},{12,16},{16,20},{20,24},{24,28},{29,1},{... | collective-permute-start | bytes 233480 | tf_op jit(solution)/shard_map/ppermute | solution.py:62
  4.7 3.1 %collective-permute-start.3 = (f32[152,128]{1,0:T(8,128)S(1)}, f32[152,128]{1,0:T(8,128)S(1)}, u32[]{:S(2)}, u32[]{:S(2)}) collective-permute-start(f32[152,128]{1,0:T(8,128)S(1)} %get-tuple-element.42), channel_id=1, source_target_pairs={{4,0},{8,4},{12,8},{16,12},{20,16},{24,20},{28,24},{0,28},{5,1},{9... | collective-permute-start | bytes 233480 | tf_op jit(solution)/shard_map/ppermute | solution.py:62
  7.8 1.1 %y_pack.1 = (f32[5,12,24,128]{3,2,1,0:T(8,128)S(1)}, f32[208,128]{1,0:T(8,128)S(1)}, f32[208,128]{1,0:T(8,128)S(1)}) custom-call(f32[12,12,128]{2,1,0:T(8,128)} %refs_0_.3, f32[12,12,128]{2,1,0:T(8,128)} %refs_1_.3, f32[12,12,128]{2,1,0:T(8,128)} %refs_2_.3, f32[12,12,128]{2,1,0:T(8,128)} %refs_3_.3, f32[12,12,128]{2,1,0:T(8,128)} %refs_4_.3), custom_call_target="tpu_custom_call" | custom-call | tf_op jit(solution)/shard_map/y_pack/pallas_call | solution.py:470
  8.9 0.7 %collective-permute-start = (f32[208,128]{1,0:T(8,128)S(1)}, f32[208,128]{1,0:T(8,128)S(1)}, u32[]{:S(2)}, u32[]{:S(2)}) collective-permute-start(f32[208,128]{1,0:T(8,128)S(1)} %get-tuple-element.34), channel_id=1, source_target_pairs={{0,3},{1,2},{2,1},{3,0},{4,7},{5,6},{6,5},{7,4},{8,11},{9,10},{10,... | collective-permute-start | bytes 319496 | tf_op jit(solution)/shard_map/ppermute | solution.py:68
  9.6 1.1 %collective-permute-start.1 = (f32[208,128]{1,0:T(8,128)S(1)}, f32[208,128]{1,0:T(8,128)S(1)}, u32[]{:S(2)}, u32[]{:S(2)}) collective-permute-start(f32[208,128]{1,0:T(8,128)S(1)} %get-tuple-element.35), channel_id=1, source_target_pairs={{0,1},{1,0},{2,3},{3,2},{4,5},{5,4},{6,7},{7,6},{8,9},{9,8},{10,11... | collective-permute-start | bytes 319496 | tf_op jit(solution)/shard_map/ppermute | solution.py:68
  10.6 0.0 collective-permute-done.2.refs_0_
  10.6 0.1 collective-permute-done.3.refs_1_
  10.8 0.1 collective-permute-start.4
  10.8 1.6 %collective-permute-start.5 = (f32[80,128]{1,0:T(8,128)S(1)}, f32[80,128]{1,0:T(8,128)S(1)}, u32[]{:S(2)}, u32[]{:S(2)}) collective-permute-start(f32[80,128]{1,0:T(8,128)S(1)} %get-tuple-element.44), channel_id=1, source_target_pairs={{0,1},{1,0},{2,3},{3,2},{4,5},{5,4},{6,7},{7,6},{8,9},{9,8},{10,11... | collective-permute-start | bytes 122888 | tf_op jit(solution)/shard_map/ppermute | solution.py:68
  13.1 1.0 %collective-permute-done.refs_1_ = f32[208,128]{1,0:T(8,128)S(1)} collective-permute-done((f32[208,128]{1,0:T(8,128)S(1)}, f32[208,128]{1,0:T(8,128)S(1)}, u32[]{:S(2)}, u32[]{:S(2)}) %collective-permute-start) | collective-permute-done | bytes 106528 | tf_op jit(solution)/shard_map/ppermute | solution.py:68
  14.0 0.0 collective-permute-done.1.refs_2_
  14.0 0.7 %inner.1 = (f32[5,12,32,128]{3,2,1,0:T(8,128)S(1)}, f32[10,24,128]{2,1,0:T(8,128)S(1)}, f32[3,8,16,128]{3,2,1,0:T(8,128)S(1)}, f32[2,8,16,128]{3,2,1,0:T(8,128)S...) custom-call(f32[1]{0:T(128)} %bitcast.4.dt_ref, ...), custom_call_target="tpu_custom_call" | custom-call | flops 5000000 | bytes 2000000 | tf_op jit(solution)/shard_map/inner/pallas_call | solution.py:492
  14.8 0.2 collective-permute-done.4.refs_2_
  14.9 0.0 collective-permute-done.5.refs_3_
  14.9 1.4 %outer.1 = (f32[3,8,16,128]{3,2,1,0:T(8,128)S(1)}, f32[2,8,16,128]{3,2,1,0:T(8,128)S(1)}, f32[8,24,128]{2,1,0:T(8,128)S(1)}, f32[8,16,128]{2,1,0:T(8,128)S(1)}, ...) custom-call(f32[1]{0:T(128)} %bitcast.5.dt_ref, f32[152,128]{1,0:T(8,128)S(1)} %collective-permute-done.2.refs_0_, ...), custom_call_target="tpu_custom_call" | custom-call | tf_op jit(solution)/shard_map/outer/pallas_call | solution.py:514
  16.3 4.9 %all-to-all-start = ((f32[32,1,128]{2,1,0:T(1,128)}), f32[32,1,128]{2,1,0:T(1,128)S(1)}, u32[]{:S(2)}, u32[]{:S(2)}) async-start(f32[32,1,128]{2,1,0:T(1,128)} %bitcast.2), calls=%async_computation | async-start | bytes 32768 | tf_op jit(solution)/shard_map/all_to_all | solution.py:548
  21.2 2.2 %carry.1 = (f32[12,12,128]{2,1,0:T(8,128)}, f32[12,12,128]{2,1,0:T(8,128)}, f32[12,12,128]{2,1,0:T(8,128)}, f32[12,12,128]{2,1,0:T(8,128)}, f32[12,12,128]{2,1,0:T(8,128)}) custom-call(f32[1]{0:T(128)} %bitcast.6.dt_ref, f32[3,8,16,128]{3,2,1,0:T(8,128)S(1)} %get-tuple-element.36.refs_6_.refs_0_, f32[2,8,16,128]{3,2,1,0:T(8,128)S(1)} %get-tuple-element.37.refs_1_, ...), custom_call_target="tpu_custom_call" | custom-call | flops 10000000 | bytes 4000000 | tf_op jit(solution)/shard_map/carry/pallas_call | solution.py:534
  23.4 4.9 %all-to-all-done = f32[32,1,128]{2,1,0:T(1,128)S(1)} async-done(((f32[32,1,128]{2,1,0:T(1,128)}), f32[32,1,128]{2,1,0:T(1,128)S(1)}, u32[]{:S(2)}, u32[]{:S(2)}) %all-to-all-start) | async-done | bytes 16416 | tf_op jit(solution)/shard_map/all_to_all | solution.py:548
  28.3 0.6 %reduce_min.9 = f32[]{:T(128)} reduce(f32[32,1,128]{2,1,0:T(1,128)S(1)} %all-to-all-done, f32[]{:T(128)} %constant.0.clone.1), dimensions={0,1,2}, to_apply=%region_0.0 | reduce | flops 4095 | bytes 16392 | tf_op jit(solution)/shard_map/reduce_min | solution.py:548
  (1 shorter events, 0.0 us)
Async XLA Ops:
  1.6 9.0 %collective-permute-start.2 = (f32[152,128]{1,0:T(8,128)S(1)}, f32[152,128]{1,0:T(8,128)S(1)}, u32[]{:S(2)}, u32[]{:S(2)}) collective-permute-start(f32[152,128]{1,0:T(8,128)S(1)} %get-tuple-element.41), channel_id=1, source_target_pairs={{28,0},{0,4},{4,8},{8,12},{12,16},{16,20},{20,24},{24,28},{29,1},{... | collective-permute-start | bytes 233480 | tf_op jit(solution)/shard_map/ppermute | solution.py:62
  4.7 6.1 %collective-permute-start.3 = (f32[152,128]{1,0:T(8,128)S(1)}, f32[152,128]{1,0:T(8,128)S(1)}, u32[]{:S(2)}, u32[]{:S(2)}) collective-permute-start(f32[152,128]{1,0:T(8,128)S(1)} %get-tuple-element.42), channel_id=1, source_target_pairs={{4,0},{8,4},{12,8},{16,12},{20,16},{24,20},{28,24},{0,28},{5,1},{9... | collective-permute-start | bytes 233480 | tf_op jit(solution)/shard_map/ppermute | solution.py:62
  8.9 5.2 %collective-permute-start = (f32[208,128]{1,0:T(8,128)S(1)}, f32[208,128]{1,0:T(8,128)S(1)}, u32[]{:S(2)}, u32[]{:S(2)}) collective-permute-start(f32[208,128]{1,0:T(8,128)S(1)} %get-tuple-element.34), channel_id=1, source_target_pairs={{0,3},{1,2},{2,1},{3,0},{4,7},{5,6},{6,5},{7,4},{8,11},{9,10},{10,... | collective-permute-start | bytes 319496 | tf_op jit(solution)/shard_map/ppermute | solution.py:68
  9.6 4.5 %collective-permute-start.1 = (f32[208,128]{1,0:T(8,128)S(1)}, f32[208,128]{1,0:T(8,128)S(1)}, u32[]{:S(2)}, u32[]{:S(2)}) collective-permute-start(f32[208,128]{1,0:T(8,128)S(1)} %get-tuple-element.35), channel_id=1, source_target_pairs={{0,1},{1,0},{2,3},{3,2},{4,5},{5,4},{6,7},{7,6},{8,9},{9,8},{10,11... | collective-permute-start | bytes 319496 | tf_op jit(solution)/shard_map/ppermute | solution.py:68
  10.8 4.2 %collective-permute-start.4 = (f32[80,128]{1,0:T(8,128)S(1)}, f32[80,128]{1,0:T(8,128)S(1)}, u32[]{:S(2)}, u32[]{:S(2)}) collective-permute-start(f32[80,128]{1,0:T(8,128)S(1)} %get-tuple-element.43), channel_id=1, source_target_pairs={{0,3},{1,2},{2,1},{3,0},{4,7},{5,6},{6,5},{7,4},{8,11},{9,10},{10,... | collective-permute-start | bytes 122888 | tf_op jit(solution)/shard_map/ppermute | solution.py:68
  10.8 4.1 %collective-permute-start.5 = (f32[80,128]{1,0:T(8,128)S(1)}, f32[80,128]{1,0:T(8,128)S(1)}, u32[]{:S(2)}, u32[]{:S(2)}) collective-permute-start(f32[80,128]{1,0:T(8,128)S(1)} %get-tuple-element.44), channel_id=1, source_target_pairs={{0,1},{1,0},{2,3},{3,2},{4,5},{5,4},{6,7},{7,6},{8,9},{9,8},{10,11... | collective-permute-start | bytes 122888 | tf_op jit(solution)/shard_map/ppermute | solution.py:68
  16.3 12.0 %all-to-all-start = ((f32[32,1,128]{2,1,0:T(1,128)}), f32[32,1,128]{2,1,0:T(1,128)S(1)}, u32[]{:S(2)}, u32[]{:S(2)}) async-start(f32[32,1,128]{2,1,0:T(1,128)} %bitcast.2), calls=%async_computation | async-start | bytes 32768 | tf_op jit(solution)/shard_map/all_to_all | solution.py:548
